TPU v7x, 128 devices: a whole 4x4x4 slice. The times are simulated.
128 devices in a mesh: row: 16 (over y, x_lo, core), col: 8 (over x_hi, z).
Axes of the slice: x: 4 (x_hi: 2, x_lo: 2; x = x_hi * 2 + x_lo), y: 4, z: 4, core: 2. Of those that a mesh axis runs over, the one named last changes fastest.
Arguments:
- tokens: bfloat16 [1024, 8192], P('col', 'row'), may hold values from -6 to 6
- gate_weight: bfloat16 [8192, 14336], P('row', 'col'), may hold values from -0.0625 to 0.0625
- up_weight: bfloat16 [8192, 14336], P('row', 'col'), may hold values from -0.0625 to 0.0625
- down_weight: bfloat16 [14336, 8192], P('col', 'row'), may hold values from -0.046875 to 0.046875
- grad_output: bfloat16 [1024, 8192], P('col', 'row'), may hold values from -6 to 6
Outputs:
- layer_output: bfloat16 [1024, 8192], P('col', 'row')
- grad_input: bfloat16 [1024, 8192], P('col', 'row')
- grad_gate: bfloat16 [8192, 14336], P('row', 'col')
- grad_up: bfloat16 [8192, 14336], P('row', 'col')
- grad_down: bfloat16 [14336, 8192], P('col', 'row')
All inputs are finite; a program needn't handle non-finite values.
Results may differ from a plain program's by a relative error of at most 0.005.
Values may be sent and summed in bfloat16 or wider, within the bound.
No kernel may reach another device: no remote copies, remote signals or barrier semaphores. Data moves between devices by JAX's collectives and lax.ppermute only.
A program may use at most 128 MiB of HBM per device.

v0:
```python
import jax
import jax.numpy as jnp
from jax import lax
from jax.sharding import PartitionSpec as P


def share_sum(term_fn, row_count):
    return lax.psum_scatter(
        term_fn(jnp.int32(0), lax.axis_size("row") * row_count),
        "row",
        scatter_dimension=0,
        tiled=True,
    )


def row_gather(values):
    return lax.all_gather(values, "row", axis=0, tiled=True)


def col_sum(term_fn, row_count):
    return lax.psum_scatter(
        term_fn(jnp.int32(0), lax.axis_size("col") * row_count),
        "col",
        scatter_dimension=0,
        tiled=True,
    )


def swiglu(gate_value, up_value):
    sig_gate = jax.nn.sigmoid(gate_value)
    return (gate_value * sig_gate * up_value).astype(jnp.bfloat16)


def derivatives(d_hidden, gate_value, up_value):
    sig_gate = jax.nn.sigmoid(gate_value)
    d_gate = (d_hidden * up_value * sig_gate * (1.0 + gate_value * (1.0 - sig_gate))).astype(
        jnp.bfloat16
    )
    d_up = (d_hidden * gate_value * sig_gate).astype(jnp.bfloat16)
    return jnp.concatenate([d_gate, d_up], axis=1)


def body(tokens, gate_weight, up_weight, down_weight, grad_output):
    tok_all, grad_all = (
        lax.all_gather(tokens, "col", axis=0, tiled=True),
        lax.all_gather(grad_output, "col", axis=0, tiled=True),
    )
    total_rows = tok_all.shape[0]
    share_rows = total_rows // lax.axis_size("row")
    ff_width = gate_weight.shape[1]
    contract_last = (((1,), (1,)), ((), ()))
    contract_first = (((0,), (0,)), ((), ()))

    def gate_terms(begin_row, row_count):
        gate_part = jnp.dot(tok_all, gate_weight, preferred_element_type=jnp.float32)
        up_part = jnp.dot(tok_all, up_weight, preferred_element_type=jnp.float32)
        return jnp.concatenate([gate_part, up_part], axis=1)

    def back_terms(begin_row, row_count):
        return lax.dot_general(
            grad_all, down_weight, contract_last, preferred_element_type=jnp.float32
        )

    both_sums = share_sum(gate_terms, share_rows)
    gate_value = both_sums[:, :ff_width]
    up_value = both_sums[:, ff_width:]
    hidden = row_gather(swiglu(gate_value, up_value))
    d_hidden = share_sum(back_terms, share_rows)
    d_both = row_gather(derivatives(d_hidden, gate_value, up_value))
    local_rows = tokens.shape[0]

    def output_terms(begin_row, row_count):
        return jnp.dot(hidden, down_weight, preferred_element_type=jnp.float32)

    layer_output = col_sum(output_terms, local_rows).astype(jnp.bfloat16)
    d_gate = d_both[:, :ff_width]
    d_up = d_both[:, ff_width:]
    grad_down = lax.dot_general(
        hidden, grad_all, contract_first, preferred_element_type=jnp.float32
    ).astype(jnp.bfloat16)
    grad_gate = lax.dot_general(
        tok_all, d_gate, contract_first, preferred_element_type=jnp.float32
    ).astype(jnp.bfloat16)
    grad_up = lax.dot_general(
        tok_all, d_up, contract_first, preferred_element_type=jnp.float32
    ).astype(jnp.bfloat16)

    def input_terms(begin_row, row_count):
        first_term = lax.dot_general(
            d_gate, gate_weight, contract_last, preferred_element_type=jnp.float32
        )
        second_term = lax.dot_general(
            d_up, up_weight, contract_last, preferred_element_type=jnp.float32
        )
        return first_term + second_term

    grad_input = col_sum(input_terms, local_rows).astype(jnp.bfloat16)
    return (layer_output, grad_input, grad_gate, grad_up, grad_down)


def solution(mesh):
    placed = (P("col", "row"), P("row", "col"), P("row", "col"), P("col", "row"), P("col", "row"))
    return jax.shard_map(
        body,
        mesh=mesh,
        in_specs=placed,
        out_specs=(
            P("col", "row"),
            P("col", "row"),
            P("row", "col"),
            P("row", "col"),
            P("col", "row"),
        ),
        check_vma=False,
    )
```

profile of v0, /device:TPU:17, one launch (start us, length us, event | category | flops | bytes accessed | tf_op | source)
XLA Modules:
  0.0 609.1 jit_solution(16831235166229149662)
XLA Ops:
  8.7 49.1 %all-gather.9.cloned.1.call-done = bf16[1024,512]{1,0:T(8,128)(2,1)} async-done(((bf16[128,512]{1,0:T(8,128)(2,1)}), bf16[1024,512]{1,0:T(8,128)(2,1)}) %all-gather.9.cloned.1.call-update) | async-done | bytes 1048592 | tf_op jit(solution)/shard_map/all_gather | solution.py:46
  57.8 6.3 %fusion.26 = f32[1024,1792]{1,0:T(8,128)} fusion(bf16[1024,512]{1,0:T(8,128)(2,1)} %all-gather.9.cloned.1.call-done, bf16[1792,512]{1,0:T(8,128)(2,1)S(1)} %copy-done), kind=kOutput, calls=%fused_computation.23 | convolution fusion | flops 1879048192 | bytes 10223616 | tf_op jit(solution)/shard_map/dot_general | solution.py:60
  64.1 41.2 %all-gather.5.cloned.1.call-done = bf16[1024,512]{1,0:T(8,128)(2,1)} async-done(((bf16[128,512]{1,0:T(8,128)(2,1)}), bf16[1024,512]{1,0:T(8,128)(2,1)}) %all-gather.5.cloned.1.call-update) | async-done | bytes 1048592 | tf_op jit(solution)/shard_map/all_gather | solution.py:45
  105.4 4.0 fusion.23
  109.4 2.1 fusion.24
  111.5 5.9 pad_maximum_fusion
  117.5 75.6 %reduce-scatter.9.cloned.1.call-done = f32[64,1792]{1,0:T(8,128)} async-done(((f32[1024,1792]{1,0:T(8,128)}), f32[64,1792]{1,0:T(8,128)}) %reduce-scatter.9.cloned.1.call-update) | async-done | bytes 458768 | tf_op jit(solution)/shard_map/reduce_scatter | solution.py:8
  193.1 162.3 %reduce-scatter.5.cloned.1.call-done = f32[64,3584]{1,0:T(8,128)} async-done(((f32[1024,3584]{1,0:T(8,128)}), f32[64,3584]{1,0:T(8,128)}) %reduce-scatter.5.cloned.1.call-update) | async-done | bytes 917520 | tf_op jit(solution)/shard_map/reduce_scatter | solution.py:8
  355.4 2.2 multiply_convert_fusion.1
  357.7 0.8 pad_maximum_fusion.1
  358.5 36.1 %all-gather.7.cloned.1.call-done = bf16[1024,1792]{1,0:T(8,128)(2,1)} async-done(((bf16[64,1792]{1,0:T(8,128)(2,1)}), bf16[1024,1792]{1,0:T(8,128)(2,1)}) %all-gather.7.cloned.1.call-update) | async-done | bytes 3670032 | tf_op jit(solution)/shard_map/all_gather | solution.py:17
  394.7 5.4 fusion.25
  400.3 44.4 %all-gather.11.cloned.1.call-done = bf16[1024,3584]{1,0:T(8,128)(2,1)} async-done(((bf16[64,3584]{1,0:T(8,128)(2,1)}), bf16[1024,3584]{1,0:T(8,128)(2,1)}) %all-gather.11.cloned.1.call-update) | async-done | bytes 7340048 | tf_op jit(solution)/shard_map/all_gather | solution.py:17
  444.7 4.8 fusion.2
  449.6 3.5 fusion.20
  453.1 5.7 convolution_convert_fusion
  458.8 64.3 %reduce-scatter.7.cloned.1.call-done = f32[128,512]{1,0:T(8,128)} async-done(((f32[1024,512]{1,0:T(8,128)}), f32[128,512]{1,0:T(8,128)}) %reduce-scatter.7.cloned.1.call-update) | async-done | bytes 262160 | tf_op jit(solution)/shard_map/reduce_scatter | solution.py:21
  523.1 1.6 convert_element_type.31
  524.7 4.1 fusion.17
  528.8 2.4 copy.10
  531.2 5.6 fusion.14
  536.8 3.8 copy.11
  540.6 60.0 %reduce-scatter.11.cloned.1.call-done = f32[128,512]{1,0:T(8,128)} async-done(((f32[1024,512]{1,0:T(8,128)}), f32[128,512]{1,0:T(8,128)}) %reduce-scatter.11.cloned.1.call-update) | async-done | bytes 262160 | tf_op jit(solution)/shard_map/reduce_scatter | solution.py:21
  600.6 1.6 convert_element_type.34
  (28 shorter events, 2.0 us)
Async XLA Ops:
  7.2 50.6 %copy-start = (bf16[1792,512]{1,0:T(8,128)(2,1)S(1)}, bf16[1792,512]{1,0:T(8,128)(2,1)}, u32[]{:S(2)}) copy-start(bf16[1792,512]{1,0:T(8,128)(2,1)} %param.8) | copy-start | bytes 5505028
  7.2 50.6 %all-gather.9.cloned.1.call-start = ((), (), s32[]{:S(2)}) async-start(), calls=%async_computation.8 | async-start | bytes 1179648 | tf_op jit(solution)/shard_map/all_gather | solution.py:46
  7.9 97.5 %all-gather.5.cloned.1.call-start = ((), (), s32[]{:S(2)}) async-start(), calls=%async_computation.4 | async-start | bytes 1179648 | tf_op jit(solution)/shard_map/all_gather | solution.py:45
  8.7 184.4 %reduce-scatter.9.cloned.1.call-start = ((), (), s32[]{:S(2)}) async-start(), calls=%async_computation.9 | async-start | bytes 7798784 | tf_op jit(solution)/shard_map/reduce_scatter | solution.py:8
  64.1 291.3 %reduce-scatter.5.cloned.1.call-start = ((), (), s32[]{:S(2)}) async-start(), calls=%async_computation.5 | async-start | bytes 15597568 | tf_op jit(solution)/shard_map/reduce_scatter | solution.py:8
  105.4 4.0 copy-start.3
  105.4 4.0 copy-start.5
  117.5 277.2 %all-gather.7.cloned.1.call-start = ((), (), s32[]{:S(2)}) async-start(), calls=%async_computation.6 | async-start | bytes 3899392 | tf_op jit(solution)/shard_map/all_gather | solution.py:17
  357.6 87.1 %all-gather.11.cloned.1.call-start = ((), (), s32[]{:S(2)}) async-start(), calls=%async_computation.10 | async-start | bytes 7798784 | tf_op jit(solution)/shard_map/all_gather | solution.py:17
  358.5 164.6 %reduce-scatter.7.cloned.1.call-start = ((), (), s32[]{:S(2)}) async-start(), calls=%async_computation.7 | async-start | bytes 2359296 | tf_op jit(solution)/shard_map/reduce_scatter | solution.py:21
  400.1 49.5 %copy-start.4 = (bf16[512,1792]{1,0:T(8,128)(2,1)S(1)}, bf16[512,1792]{1,0:T(8,128)(2,1)}, u32[]{:S(2)}) copy-start(bf16[512,1792]{1,0:T(8,128)(2,1)} %param.6) | copy-start | bytes 5505028
  400.1 200.5 %reduce-scatter.11.cloned.1.call-start = ((), (), s32[]{:S(2)}) async-start(), calls=%async_computation.11 | async-start | bytes 2359296 | tf_op jit(solution)/shard_map/reduce_scatter | solution.py:21
  444.7 4.9 copy-start.2
  531.2 71.0 %copy-start.1 = (bf16[1792,512]{1,0:T(8,128)(2,1)S(1)}, bf16[1792,512]{1,0:T(8,128)(2,1)}, u32[]{:S(2)}) copy-start(bf16[1792,512]{1,0:T(8,128)(2,1)} %param.8) | copy-start | bytes 5505028
Sparse Core Ops, SparseCore 0:
  10.4 47.3 all-gather.8
  60.2 45.1 all-gather.4
  107.8 85.2 reduce-scatter.8
  195.4 159.9 reduce-scatter.4
  357.7 36.8 all-gather.6
  396.8 47.8 all-gather.10
  448.4 74.6 reduce-scatter.6
  526.8 73.7 reduce-scatter.10
where the time goes:
time: 611 us; the launch traced here: 609 us
  waiting for transfers between devices  535 us (88%)
  matrix products  41.5 us (7%)
  between operations  14.2 us (2%)
  other arithmetic  12.2 us (2%)
  local copies, waits for them, and re-layouts  6.23 us (1%)
    reduce_scatter x2, waiting for transfers between devices, share_sum(): lax.psum_scatter(term_fn(jnp.int32(0), lax.axis_size('row') * row_count),...  238 us
    reduce_scatter x2, waiting for transfers between devices, col_sum(): lax.psum_scatter(term_fn(jnp.int32(0), lax.axis_size('col') * row_count),...  124 us
    all_gather x2, waiting for transfers between devices, row_gather(): return lax.all_gather(values, 'row', axis=0, tiled=True)  80.5 us
    all_gather x1, waiting for transfers between devices, body(): lax.all_gather(grad_output, 'col', axis=0, tiled=True)  49.1 us
    all_gather x1, waiting for transfers between devices, body(): lax.all_gather(tokens, 'col', axis=0, tiled=True)  41.2 us
  transfers between devices with their start and end apart: 8, of which 8 were waited for; matrix products, arithmetic and copies ran while one was open for 9% of the time, Pallas kernels for 0%

commit v1 on v0

v1 whole, which is shorter than its diff:
```python
import functools

import jax
import jax.numpy as jnp
from jax import lax
from jax.experimental import pallas as pl
from jax.experimental.pallas import tpu as pltpu
from jax.sharding import PartitionSpec as P

NY, NX, NC, NZ = 4, 2, 2, 4
PIECE = 64
BOTH = ("row", "col")


def row_at(y, x, core):
    return ((y % NY) * NX + x) * NC + core


def row_perm(core0, core1):
    pairs = []
    for y in range(NY):
        for x in range(NX):
            for core, move in ((0, core0), (1, core1)):
                if move is not None:
                    to_y, to_x = move(y, x)
                    pairs.append((row_at(y, x, core), row_at(to_y, to_x, core)))
    return pairs


def over_x(y, x):
    return y, 1 - x


def over_y(step):
    return lambda y, x: (y + step, x)


CORE_FLIP = [(i, i ^ 1) for i in range(NY * NX * NC)]


def gather_perm(step):
    pairs = []
    for row in range(NY * NX * NC):
        core = row % NC
        if core == 0 and step == 0:
            continue
        for hi in range(2):
            for z in range(NZ):
                source = (hi ^ core) * NZ + (z + step) % NZ
                pairs.append((row * 8 + source, row * 8 + hi * NZ + z))
    return pairs


def col_perm(flip, step):
    return [(hi * NZ + z, (hi ^ flip) * NZ + (z + step) % NZ) for hi in range(2) for z in range(NZ)]


def product(left, right, transposed):
    dims = (((1,), (1 if transposed else 0,)), ((), ()))
    return lax.dot_general(left, right, dims, preferred_element_type=jnp.float32)


def first_kernel(count, transposed, table, acts, *refs):
    weights, outs, held = refs[: 2 * count], refs[2 * count : 2 * count + 3], refs[-1]

    @pl.when(pl.program_id(0) == 0)
    def _():
        for slot in range(6):
            held[slot * PIECE : (slot + 1) * PIECE, :] = acts[table[slot]]

    half = held.shape[1] // 2
    for which in range(count):
        total = product(held[:, :half], weights[2 * which][...], transposed)
        total += product(held[:, half:], weights[2 * which + 1][...], transposed)
        total = total.astype(jnp.bfloat16)
        for message in range(3):
            outs[message][which] = total[message * 2 * PIECE : (message + 1) * 2 * PIECE]


def second_kernel(count, transposed, table, acts, *refs):
    weights, heard, outs, held = (
        refs[: 2 * count],
        refs[2 * count : 2 * count + 3],
        refs[2 * count + 3 : 2 * count + 7],
        refs[-1],
    )

    @pl.when(pl.program_id(0) == 0)
    def _():
        for slot in range(4):
            held[slot * PIECE : (slot + 1) * PIECE, :] = acts[table[slot]]

    core, x = table[4], table[5]
    near = pl.ds(pl.multiple_of(x * PIECE, PIECE), PIECE)
    far = pl.ds(pl.multiple_of((1 - x) * PIECE, PIECE), PIECE)
    half = held.shape[1] // 2
    for which in range(count):
        total = product(held[:, :half], weights[2 * which][...], transposed)
        total += product(held[:, half:], weights[2 * which + 1][...], transposed)
        near1, near2, near3 = [h[which, near].astype(jnp.float32) for h in heard]
        far1, far2, far3 = [h[which, far].astype(jnp.float32) for h in heard]
        more_near = jnp.where(core == 1, near2 + near3, 0.0)
        more_far = jnp.where(core == 1, far2 + far3, 0.0)
        outs[0][which] = (total[:PIECE] + far1 + more_far).astype(jnp.bfloat16)
        outs[1][which] = (total[PIECE : 2 * PIECE] + near2).astype(jnp.bfloat16)
        outs[2][which] = (total[2 * PIECE : 3 * PIECE] + far2).astype(jnp.bfloat16)
        outs[3][which] = total[3 * PIECE :] + near1 + more_near


def stage(kernel, table, acts, weights, transposed, heard=()):
    count = len(weights)
    depth = weights[0][0].shape[1 if transposed else 0]
    width = weights[0][0].shape[0 if transposed else 1]
    block = 256
    if transposed:
        weight_spec = pl.BlockSpec((block, depth), lambda i, t: (i, 0))
    else:
        weight_spec = pl.BlockSpec((depth, block), lambda i, t: (0, i))
    if heard:
        rows, slots = [PIECE] * 4, 4
        types = [jnp.bfloat16] * 3 + [jnp.float32]
    else:
        rows, slots = [2 * PIECE] * 3, 6
        types = [jnp.bfloat16] * 3
    out_block = lambda n: pl.BlockSpec((count, n, block), lambda i, t: (0, 0, i))
    flops = 2 * slots * PIECE * 2 * depth * width * count
    return pl.pallas_call(
        functools.partial(kernel, count, transposed),
        grid_spec=pltpu.PrefetchScalarGridSpec(
            num_scalar_prefetch=1,
            grid=(width // block,),
            in_specs=[pl.BlockSpec(acts.shape, lambda i, t: (0, 0, 0))]
            + [weight_spec] * (2 * count)
            + [out_block(2 * PIECE)] * len(heard),
            out_specs=[out_block(n) for n in rows],
            scratch_shapes=[pltpu.VMEM((slots * PIECE, acts.shape[2]), jnp.bfloat16)],
        ),
        out_shape=[jax.ShapeDtypeStruct((count, n, width), d) for n, d in zip(rows, types)],
        compiler_params=pltpu.CompilerParams(vmem_limit_bytes=32 * 2**20),
        cost_estimate=pl.CostEstimate(
            flops=flops, bytes_accessed=4 * depth * width * count, transcendentals=0
        ),
    )(table, acts, *[w for pair in weights for w in pair], *heard)


def row_sum(acts, weights, transposed, first_table, second_table):
    sent = stage(first_kernel, first_table, acts, weights, transposed)
    heard = (
        lax.ppermute(sent[0], "row", row_perm(over_x, over_y(1))),
        lax.ppermute(sent[1], "row", row_perm(over_x, over_y(-1))),
        lax.ppermute(sent[2], "row", row_perm(None, over_y(2))),
    )
    *sent, kept = stage(second_kernel, second_table, acts, weights, transposed, heard)
    heard = (
        lax.ppermute(sent[0], "row", row_perm(over_y(1), over_x)),
        lax.ppermute(sent[1], "row", row_perm(over_y(-1), None)),
        lax.ppermute(sent[2], "row", row_perm(over_y(2), None)),
    )
    for term in heard:
        kept = kept + term.astype(jnp.float32)
    return kept


def col_sum(total):
    blocks = total.reshape(NY, NX, NC, PIECE, total.shape[1])
    away = blocks[:, :, 1].astype(jnp.bfloat16)
    heard = lax.ppermute(away, "col", col_perm(1, 0))
    near = blocks[:, :, 0] + heard.astype(jnp.float32)
    result = near[0]
    send = near[1:].astype(jnp.bfloat16)
    for step in range(1, NZ):
        result = result + lax.ppermute(send[step - 1], "col", col_perm(0, step)).astype(jnp.float32)
    return result.astype(jnp.bfloat16).reshape(NX * PIECE, total.shape[1])


def body(tokens, gate_weight, up_weight, down_weight, grad_output):
    row = lax.axis_index("row")
    core, x, y = row % NC, (row // NC) % NX, row // (NC * NX)
    piece = lambda y_at, x_at: (y_at % NY) * NX + x_at
    other = 1 - x
    first0 = [
        jnp.where(other == 0, piece(y, other), piece(y + 1, other)),
        jnp.where(other == 0, piece(y + 1, other), piece(y, other)),
        jnp.where(other == 0, piece(y + 3, other), piece(y + 2, other)),
        jnp.where(other == 0, piece(y + 2, other), piece(y + 3, other)),
        piece(y, x),
        piece(y, x),
    ]
    first1 = [piece(y + step, x_at) for step in (1, 3, 2) for x_at in (0, 1)]
    second0 = [piece(y + 1, x), piece(y + 3, x), piece(y + 2, x), piece(y, x)]
    second1 = [piece(y, other), piece(y, x), piece(y, x), piece(y, x)]
    choose = lambda zero, one: [jnp.where(core == 0, a, b) for a, b in zip(zero, one)]
    first_table = jnp.stack(choose(first0, first1)).astype(jnp.int32)
    second_table = jnp.stack(choose(second0, second1) + [core, x]).astype(jnp.int32)

    flip = lambda value: lax.ppermute(value, "row", CORE_FLIP)
    width = tokens.shape[1]
    mine = jnp.stack([tokens, grad_output])
    theirs = flip(mine)

    def gather(own, partner):
        block = jnp.concatenate([own, partner], axis=1)
        blocks = [lax.ppermute(block, BOTH, gather_perm(step)) for step in range(NZ)]
        blocks[0] = jnp.where(core == 0, block, blocks[0])
        return jnp.concatenate(blocks, axis=0).reshape(NY * NX, PIECE, 2 * width)

    tok_half = gather(tokens, theirs[0])
    gate_pair = (gate_weight, flip(gate_weight))
    up_pair = (up_weight, flip(up_weight))
    down_pair = (down_weight, flip(down_weight))
    grad_half = gather(grad_output, theirs[1])

    both = row_sum(tok_half, [gate_pair, up_pair], False, first_table, second_table)
    d_hidden = row_sum(grad_half, [down_pair], True, first_table, second_table)[0]
    gate_value, up_value = both[0], both[1]
    sig_gate = jax.nn.sigmoid(gate_value)
    hidden = (gate_value * sig_gate * up_value).astype(jnp.bfloat16)
    hidden = lax.all_gather(hidden, "row", axis=0, tiled=True)
    d_gate = (d_hidden * up_value * sig_gate * (1.0 + gate_value * (1.0 - sig_gate))).astype(
        jnp.bfloat16
    )
    d_up = (d_hidden * gate_value * sig_gate).astype(jnp.bfloat16)
    d_both = lax.all_gather(jnp.concatenate([d_gate, d_up], axis=1), "row", axis=0, tiled=True)
    ff_width = gate_weight.shape[1]
    d_gate, d_up = d_both[:, :ff_width], d_both[:, ff_width:]

    others = flip(jnp.stack([tok_half[:, :, width:], grad_half[:, :, width:]]))

    def all_rows(half, received):
        own = half[:, :, :width]
        pair = jnp.where(
            core == 0, jnp.stack([own, received], axis=1), jnp.stack([received, own], axis=1)
        )
        return pair.reshape(-1, width)

    tok_all, grad_all = all_rows(tok_half, others[0]), all_rows(grad_half, others[1])

    layer_output = col_sum(jnp.dot(hidden, down_weight, preferred_element_type=jnp.float32))
    last = (((1,), (1,)), ((), ()))
    first = (((0,), (0,)), ((), ()))
    dot = functools.partial(lax.dot_general, preferred_element_type=jnp.float32)
    grad_input = col_sum(dot(d_gate, gate_weight, last) + dot(d_up, up_weight, last))
    grad_down = dot(hidden, grad_all, first).astype(jnp.bfloat16)
    grad_gate = dot(tok_all, d_gate, first).astype(jnp.bfloat16)
    grad_up = dot(tok_all, d_up, first).astype(jnp.bfloat16)
    return (layer_output, grad_input, grad_gate, grad_up, grad_down)


def solution(mesh):
    placed = (P("col", "row"), P("row", "col"), P("row", "col"), P("col", "row"), P("col", "row"))
    return jax.shard_map(
        body,
        mesh=mesh,
        in_specs=placed,
        out_specs=(
            P("col", "row"),
            P("col", "row"),
            P("row", "col"),
            P("row", "col"),
            P("col", "row"),
        ),
        check_vma=False,
    )
```

time: 611 us -> 254 us (0.42)
  waiting for transfers between devices: 535 us -> 102 us
  starting transfers between devices: 0.5 us -> 67.2 us
  Pallas kernels: 0 us -> 27.7 us
  matrix products: 41.5 us -> 20.4 us
    reduce_scatter x4 -> x0, waiting for transfers between devices: 362 us -> none  [the longest x2 238 us: share_sum(): lax.psum_scatter(term_fn(jnp.int32(0), lax.axis_size('row') * row_count),...]
    all_gather x4 -> x2, waiting for transfers between devices: 171 us -> 58.6 us  [the longest x1 34.4 us: body(): hidden = lax.all_gather(hidden, 'row', axis=0, tiled=True)]
    ppermute x0 -> x33, starting transfers between devices: none -> 67.1 us  [the longest x8 25.1 us: gather(): lax.ppermute(block, BOTH, gather_perm(step))]
    ppermute x0 -> x33, waiting for transfers between devices: none -> 43 us  [the longest x2 20.4 us: col_sum(): heard = lax.ppermute(away, 'col', col_perm(1, 0))]
    pallas_call x0 -> x4, Pallas kernels: none -> 27.7 us  [stage(): pl.pallas_call(functools.partial(kernel, count, transposed), grid_spec=pl...]
    dot_general x9 -> x6, matrix products: 41.5 us -> 20.4 us  [the longest x1 4.27 us: body(): dot(d_up, up_weight, last)]
  transfers between devices with their start and end apart: 8 -> 35, of which waited for: 8 -> 12; matrix products, arithmetic and copies ran while one was open for 9% -> 9% of each run, Pallas kernels for 0% -> 11%
where the time goes in v1:
time: 254 us; the launch traced here: 250 us
  waiting for transfers between devices  102 us (40%)
  starting transfers between devices  67.2 us (26%)
  Pallas kernels  27.7 us (11%)
  matrix products  20.4 us (8%)
  between operations  14.6 us (6%)
  local copies, waits for them, and re-layouts  10.1 us (4%)
  other arithmetic  8.4 us (3%)
    all_gather x1, waiting for transfers between devices, body(): hidden = lax.all_gather(hidden, 'row', axis=0, tiled=True)  34.4 us
    pallas_call x4, Pallas kernels, stage(): pl.pallas_call(functools.partial(kernel, count, transposed), grid_spec=pl...  27.7 us
    ppermute x8, starting transfers between devices, gather(): lax.ppermute(block, BOTH, gather_perm(step))  25.1 us
    all_gather x1, waiting for transfers between devices, body(): lax.all_gather(jnp.concatenate([d_gate, d_up], axis=1), 'row', axis=0, ti...  24.2 us
    ppermute x2, waiting for transfers between devices, col_sum(): heard = lax.ppermute(away, 'col', col_perm(1, 0))  20.4 us
    ppermute x5, starting transfers between devices, body(): flip = lambda value: lax.ppermute(value, 'row', CORE_FLIP)  13.6 us
    ppermute x8, waiting for transfers between devices, gather(): lax.ppermute(block, BOTH, gather_perm(step))  13.5 us
    ppermute x6, starting transfers between devices, col_sum(): lax.ppermute(send[step - 1], 'col', col_perm(0, step)).astype(jnp.float32)  9 us
  transfers between devices with their start and end apart: 35, of which 12 were waited for; matrix products, arithmetic and copies ran while one was open for 9% of the time, Pallas kernels for 11%

profile of v1, /device:TPU:17, one launch (start us, length us, event | category | flops | bytes accessed | tf_op | source)
XLA Modules:
  0.0 250.1 jit_solution(3249362834897283826)
XLA Ops:
  9.7 2.5 collective-permute-done
  13.1 6.1 %collective-permute-start.3 = (bf16[128,1024]{1,0:T(8,128)(2,1)S(1)}, bf16[128,1024]{1,0:T(8,128)(2,1)S(1)}, u32[]{:S(2)}, u32[]{:S(2)}) collective-permute-start(bf16[128,1024]{1,0:T(8,128)(2,1)S(1)} %pad_maximum_fusion.5), channel_id=1, source_target_pairs={{2,0},{3,1},{0,2},{1,3},{6,4},{7,5},{4,6},{5,7},{14,8},{15,9},{12,... | collective-permute-start | bytes 786440 | tf_op jit(solution)/shard_map/ppermute | solution.py:203
  23.1 5.5 %collective-permute-start.2 = (bf16[128,1024]{1,0:T(8,128)(2,1)S(1)}, bf16[128,1024]{1,0:T(8,128)(2,1)S(1)}, u32[]{:S(2)}, u32[]{:S(2)}) collective-permute-start(bf16[128,1024]{1,0:T(8,128)(2,1)S(1)} %pad_maximum_fusion.5), channel_id=1, source_target_pairs={{1,0},{2,1},{3,2},{0,3},{5,4},{6,5},{7,6},{4,7},{13,8},{14,9},{15,... | collective-permute-start | bytes 786440 | tf_op jit(solution)/shard_map/ppermute | solution.py:203
  31.9 4.3 %collective-permute-start.19 = (bf16[128,1024]{1,0:T(8,128)(2,1)S(1)}, bf16[128,1024]{1,0:T(8,128)(2,1)S(1)}, u32[]{:S(2)}, u32[]{:S(2)}) collective-permute-start(bf16[128,1024]{1,0:T(8,128)(2,1)S(1)} %pad_maximum_fusion.6), channel_id=1, source_target_pairs={{2,0},{3,1},{0,2},{1,3},{6,4},{7,5},{4,6},{5,7},{14,8},{15,9},{12,... | collective-permute-start | bytes 786440 | tf_op jit(solution)/shard_map/ppermute | solution.py:203
  37.8 3.5 %collective-permute-start.17 = (bf16[128,1024]{1,0:T(8,128)(2,1)S(1)}, bf16[128,1024]{1,0:T(8,128)(2,1)S(1)}, u32[]{:S(2)}, u32[]{:S(2)}) collective-permute-start(bf16[128,1024]{1,0:T(8,128)(2,1)S(1)} %pad_maximum_fusion.6), channel_id=1, source_target_pairs={{12,8},{13,9},{14,10},{15,11},{8,12},{9,13},{10,14},{11,15},{28,24... | collective-permute-start | bytes 786440 | tf_op jit(solution)/shard_map/ppermute | solution.py:203
  44.3 8.0 %shard_map.92 = (bf16[2,128,1792]{2,1,0:T(8,128)(2,1)}, bf16[2,128,1792]{2,1,0:T(8,128)(2,1)}, bf16[2,128,1792]{2,1,0:T(8,128)(2,1)}) custom-call(s32[6]{0:T(128)S(1)} %stack.96.table, bf16[8,64,1024]{2,1,0:T(8,128)(2,1)S(1)} %bitcast.126, bf16[512,1792]{1,0:T(8,128)(2,1)S(1)} %copy-done.6, bf16[512,1792]{1,0:T(8,128)(2,1)} %collective-permute-done.5.refs_1_, ...), custom_call_target="tpu_custom_call" | custom-call | flops 2818572288 | bytes 7340032 | tf_op jit(solution)/shard_map/pallas_call | solution.py:127
  53.8 3.3 %collective-permute-start.9 = (bf16[2,128,1792]{2,1,0:T(8,128)(2,1)}, bf16[2,128,1792]{2,1,0:T(8,128)(2,1)}, u32[]{:S(2)}, u32[]{:S(2)}) collective-permute-start(bf16[2,128,1792]{2,1,0:T(8,128)(2,1)} %get-tuple-element.21), channel_id=1, source_target_pairs={{8,72},{24,88},{40,104},{56,120},{72,8},{88,24},{104,40},{120,56},... | collective-permute-start | bytes 2752520 | tf_op jit(solution)/shard_map/ppermute | solution.py:151
  57.2 2.8 %collective-permute-start.20 = (bf16[128,1024]{1,0:T(8,128)(2,1)S(1)}, bf16[128,1024]{1,0:T(8,128)(2,1)S(1)}, u32[]{:S(2)}, u32[]{:S(2)}) collective-permute-start(bf16[128,1024]{1,0:T(8,128)(2,1)S(1)} %pad_maximum_fusion.6), channel_id=1, source_target_pairs={{3,0},{0,1},{1,2},{2,3},{7,4},{4,5},{5,6},{6,7},{15,8},{12,9},{13,... | collective-permute-start | bytes 786440 | tf_op jit(solution)/shard_map/ppermute | solution.py:203
  60.0 8.9 %collective-permute-done.20 = bf16[128,1024]{1,0:T(8,128)(2,1)S(1)} collective-permute-done((bf16[128,1024]{1,0:T(8,128)(2,1)S(1)}, bf16[128,1024]{1,0:T(8,128)(2,1)S(1)}, u32[]{:S(2)}, u32[]{:S(2)}) %collective-permute-start.20) | collective-permute-done | bytes 262176 | tf_op jit(solution)/shard_map/ppermute | solution.py:203
  69.0 6.7 %shard_map.94 = (bf16[1,128,1792]{2,1,0:T(8,128)(2,1)}, bf16[1,128,1792]{2,1,0:T(8,128)(2,1)S(1)}, bf16[1,128,1792]{2,1,0:T(8,128)(2,1)S(1)}) custom-call(s32[6]{0:T(128)S(1)} %stack.96.table, bf16[8,64,1024]{2,1,0:T(8,128)(2,1)S(1)} %bitcast.123, bf16[1792,512]{1,0:T(8,128)(2,1)S(1)} %copy-done, bf16[1792,512]{1,0:T(8,128)(2,1)} %collective-permute-done.21.refs_1_), custom_call_target="tpu_custom_call" | custom-call | flops 1409286144 | bytes 3670016 | tf_op jit(solution)/shard_map/pallas_call | solution.py:127
  78.8 4.8 %collective-permute-start.24 = (bf16[1,128,1792]{2,1,0:T(8,128)(2,1)}, bf16[1,128,1792]{2,1,0:T(8,128)(2,1)S(1)}, u32[]{:S(2)}, u32[]{:S(2)}) collective-permute-start(bf16[1,128,1792]{2,1,0:T(8,128)(2,1)} %copy-done.9), channel_id=1, source_target_pairs={{8,72},{24,88},{40,104},{56,120},{72,8},{88,24},{104,40},{120,56},... | collective-permute-start | bytes 1376264 | tf_op jit(solution)/shard_map/ppermute | solution.py:151
  86.7 7.1 %shard_map.93 = (bf16[2,64,1792]{2,1,0:T(8,128)(2,1)S(1)}, bf16[2,64,1792]{2,1,0:T(8,128)(2,1)S(1)}, bf16[2,64,1792]{2,1,0:T(8,128)(2,1)S(1)}, f32[2,64,1792]{2,1,0:T(8,128)S(1)}) custom-call(s32[6]{0:T(128)S(1)} %stack.86.table, bf16[8,64,1024]{2,1,0:T(8,128)(2,1)S(1)} %bitcast.127, bf16[512,1792]{1,0:T(8,128)(2,1)S(1)} %copy-done.7, ...), custom_call_target="tpu_custom_call" | custom-call | flops 1879048192 | bytes 7340032 | tf_op jit(solution)/shard_map/pallas_call | solution.py:127
  95.6 5.9 %shard_map.95 = (bf16[1,64,1792]{2,1,0:T(8,128)(2,1)S(1)}, bf16[1,64,1792]{2,1,0:T(8,128)(2,1)S(1)}, bf16[1,64,1792]{2,1,0:T(8,128)(2,1)S(1)}, f32[1,64,1792]{2,1,0:T(8,128)S(1)}) custom-call(s32[6]{0:T(128)S(1)} %stack.86.table, bf16[8,64,1024]{2,1,0:T(8,128)(2,1)S(1)} %bitcast.124, bf16[1792,512]{1,0:T(8,128)(2,1)S(1)} %copy-done.1, ...), custom_call_target="tpu_custom_call" | custom-call | flops 939524096 | bytes 3670016 | tf_op jit(solution)/shard_map/pallas_call | solution.py:127
  109.9 12.1 %collective-permute-start.32 = (bf16[2,8,64,512]{3,2,1,0:T(8,128)(2,1)}, bf16[2,8,64,512]{3,2,1,0:T(8,128)(2,1)}, u32[]{:S(2)}, u32[]{:S(2)}) collective-permute-start(bf16[2,8,64,512]{3,2,1,0:T(8,128)(2,1)} %pad_maximum_fusion.2), channel_id=1, source_target_pairs={{0,8},{8,0},{16,24},{24,16},{32,40},{40,32},{48,56},{56,48},{64,72... | collective-permute-start | bytes 3145736 | tf_op jit(solution)/shard_map/ppermute | solution.py:196
  122.1 34.4 %all-gather.3.cloned.1.call-done = bf16[1024,1792]{1,0:T(8,128)(2,1)} async-done(((bf16[64,1792]{1,0:T(8,128)(2,1)}), bf16[1024,1792]{1,0:T(8,128)(2,1)}) %all-gather.3.cloned.1.call-update) | async-done | bytes 3670032 | tf_op jit(solution)/shard_map/all_gather | solution.py:218
  156.5 4.1 %fusion.38 = f32[1024,512]{1,0:T(8,128)S(1)} fusion(bf16[1024,1792]{1,0:T(8,128)(2,1)} %all-gather.3.cloned.1.call-done, bf16[1792,512]{1,0:T(8,128)(2,1)S(1)} %copy-done.2), kind=kOutput, calls=%fused_computation.70 | convolution fusion | flops 1879048192 | bytes 7602176 | tf_op jit(solution)/shard_map/dot_general | solution.py:238
  160.6 2.5 %collective-permute-start.13 = (bf16[4,2,64,512]{3,2,1,0:T(8,128)(2,1)S(1)}, bf16[4,2,64,512]{3,2,1,0:T(8,128)(2,1)S(1)}, u32[]{:S(2)}, u32[]{:S(2)}) collective-permute-start(bf16[4,2,64,512]{3,2,1,0:T(8,128)(2,1)S(1)} %fusion.19), channel_id=1, source_target_pairs={{0,4},{1,5},{2,6},{3,7},{4,0},{5,1},{6,2},{7,3},{8,12},{9,13},{10,... | collective-permute-start | bytes 1572872 | tf_op jit(solution)/shard_map/ppermute | solution.py:167
  165.0 10.5 %collective-permute-done.13 = bf16[4,2,64,512]{3,2,1,0:T(8,128)(2,1)S(1)} collective-permute-done((bf16[4,2,64,512]{3,2,1,0:T(8,128)(2,1)S(1)}, bf16[4,2,64,512]{3,2,1,0:T(8,128)(2,1)S(1)}, u32[]{:S(2)}, u32[]{:S(2)}) %collective-permute-start.13) | collective-permute-done | bytes 524320 | tf_op jit(solution)/shard_map/ppermute | solution.py:167
  180.3 3.4 %convolution_convert_fusion = bf16[1792,512]{1,0:T(8,128)(2,1)} fusion(bf16[1024,1792]{1,0:T(8,128)(2,1)S(1)} %copy-done.14, bf16[1024,512]{1,0:T(8,128)(2,1)S(1)} %bitcast.137), kind=kOutput, calls=%fused_computation.10 | convolution fusion | flops 1879965696 | bytes 6553600 | tf_op jit(solution)/shard_map/dot_general | solution.py:243
  186.4 24.2 %all-gather.5.cloned.1.call-done = bf16[1024,3584]{1,0:T(8,128)(2,1)} async-done(((bf16[64,3584]{1,0:T(8,128)(2,1)}), bf16[1024,3584]{1,0:T(8,128)(2,1)}) %all-gather.5.cloned.1.call-update) | async-done | bytes 7340048 | tf_op jit(solution)/shard_map/all_gather | solution.py:223
  210.6 4.3 %fusion.2 = f32[1024,512]{1,0:T(8,128)S(1)} fusion(bf16[512,1792]{1,0:T(8,128)(2,1)S(1)} %copy-done.5, bf16[1024,3584]{1,0:T(8,128)(2,1)} %all-gather.5.cloned.1.call-done), kind=kOutput, calls=%fused_computation.2 | convolution fusion | flops 1879048192 | bytes 7602176 | tf_op jit(solution)/shard_map/dot_general | solution.py:242
  219.1 3.3 %fusion.8 = bf16[512,1792]{1,0:T(8,128)(2,1)} fusion(bf16[1024,512]{1,0:T(8,128)(2,1)S(1)} %bitcast.135, bf16[1024,3584]{1,0:T(8,128)(2,1)S(1)} %copy-done.13), kind=kOutput, calls=%fused_computation.8 | convolution fusion | flops 1879965696 | bytes 6553600 | tf_op jit(solution)/shard_map/dot_general | solution.py:244
  222.4 10.0 %collective-permute-done.28 = bf16[4,2,64,512]{3,2,1,0:T(8,128)(2,1)S(1)} collective-permute-done((bf16[4,2,64,512]{3,2,1,0:T(8,128)(2,1)S(1)}, bf16[4,2,64,512]{3,2,1,0:T(8,128)(2,1)S(1)}, u32[]{:S(2)}, u32[]{:S(2)}) %collective-permute-start.28) | collective-permute-done | bytes 524320 | tf_op jit(solution)/shard_map/ppermute | solution.py:167
  237.1 3.3 %fusion.11 = bf16[512,1792]{1,0:T(8,128)(2,1)} fusion(bf16[1024,512]{1,0:T(8,128)(2,1)S(1)} %bitcast.136, bf16[1024,3584]{1,0:T(8,128)(2,1)S(1)} %copy-done.13), kind=kOutput, calls=%fused_computation.9 | convolution fusion | flops 1879965696 | bytes 6553600 | tf_op jit(solution)/shard_map/dot_general | solution.py:245
  (116 shorter events, 54.0 us)
Async XLA Ops:
  7.2 149.3 %all-gather.3.cloned.1.call-start = ((), (), s32[]{:S(2)}) async-start(), calls=%async_computation | async-start | bytes 3899392 | tf_op jit(solution)/shard_map/all_gather | solution.py:218
  7.2 30.6 %collective-permute-start.5 = (bf16[512,1792]{1,0:T(8,128)(2,1)}, bf16[512,1792]{1,0:T(8,128)(2,1)}, u32[]{:S(2)}, u32[]{:S(2)}) collective-permute-start(bf16[512,1792]{1,0:T(8,128)(2,1)} %refs_0_.5), channel_id=1, source_target_pairs={{0,8},{8,0},{16,24},{24,16},{32,40},{40,32},{48,56},{56,48},{64,72... | collective-permute-start | bytes 5505032 | tf_op jit(solution)/shard_map/ppermute | solution.py:196
  8.0 33.3 %collective-permute-start.6 = (bf16[512,1792]{1,0:T(8,128)(2,1)}, bf16[512,1792]{1,0:T(8,128)(2,1)}, u32[]{:S(2)}, u32[]{:S(2)}) collective-permute-start(bf16[512,1792]{1,0:T(8,128)(2,1)} %refs_2_.3), channel_id=1, source_target_pairs={{0,8},{8,0},{16,24},{24,16},{32,40},{40,32},{48,56},{56,48},{64,72... | collective-permute-start | bytes 5505032 | tf_op jit(solution)/shard_map/ppermute | solution.py:196
  9.6 59.4 %collective-permute-start.21 = (bf16[1792,512]{1,0:T(8,128)(2,1)}, bf16[1792,512]{1,0:T(8,128)(2,1)}, u32[]{:S(2)}, u32[]{:S(2)}) collective-permute-start(bf16[1792,512]{1,0:T(8,128)(2,1)} %refs_0_.7), channel_id=1, source_target_pairs={{0,8},{8,0},{16,24},{24,16},{32,40},{40,32},{48,56},{56,48},{64,72... | collective-permute-start | bytes 5505032 | tf_op jit(solution)/shard_map/ppermute | solution.py:196
  13.1 10.0 %collective-permute-start.3 = (bf16[128,1024]{1,0:T(8,128)(2,1)S(1)}, bf16[128,1024]{1,0:T(8,128)(2,1)S(1)}, u32[]{:S(2)}, u32[]{:S(2)}) collective-permute-start(bf16[128,1024]{1,0:T(8,128)(2,1)S(1)} %pad_maximum_fusion.5), channel_id=1, source_target_pairs={{2,0},{3,1},{0,2},{1,3},{6,4},{7,5},{4,6},{5,7},{14,8},{15,9},{12,... | collective-permute-start | bytes 786440 | tf_op jit(solution)/shard_map/ppermute | solution.py:203
  19.2 9.4 %collective-permute-start.1 = (bf16[128,1024]{1,0:T(8,128)(2,1)S(1)}, bf16[128,1024]{1,0:T(8,128)(2,1)S(1)}, u32[]{:S(2)}, u32[]{:S(2)}) collective-permute-start(bf16[128,1024]{1,0:T(8,128)(2,1)S(1)} %pad_maximum_fusion.5), channel_id=1, source_target_pairs={{12,8},{13,9},{14,10},{15,11},{8,12},{9,13},{10,14},{11,15},{28,24... | collective-permute-start | bytes 786440 | tf_op jit(solution)/shard_map/ppermute | solution.py:203
  28.6 8.9 %collective-permute-start.4 = (bf16[128,1024]{1,0:T(8,128)(2,1)S(1)}, bf16[128,1024]{1,0:T(8,128)(2,1)S(1)}, u32[]{:S(2)}, u32[]{:S(2)}) collective-permute-start(bf16[128,1024]{1,0:T(8,128)(2,1)S(1)} %pad_maximum_fusion.5), channel_id=1, source_target_pairs={{3,0},{0,1},{1,2},{2,3},{7,4},{4,5},{5,6},{6,7},{15,8},{12,9},{13,... | collective-permute-start | bytes 786440 | tf_op jit(solution)/shard_map/ppermute | solution.py:203
  31.9 21.4 %collective-permute-start.19 = (bf16[128,1024]{1,0:T(8,128)(2,1)S(1)}, bf16[128,1024]{1,0:T(8,128)(2,1)S(1)}, u32[]{:S(2)}, u32[]{:S(2)}) collective-permute-start(bf16[128,1024]{1,0:T(8,128)(2,1)S(1)} %pad_maximum_fusion.6), channel_id=1, source_target_pairs={{2,0},{3,1},{0,2},{1,3},{6,4},{7,5},{4,6},{5,7},{14,8},{15,9},{12,... | collective-permute-start | bytes 786440 | tf_op jit(solution)/shard_map/ppermute | solution.py:203
  37.6 16.3 %collective-permute-start.18 = (bf16[128,1024]{1,0:T(8,128)(2,1)S(1)}, bf16[128,1024]{1,0:T(8,128)(2,1)S(1)}, u32[]{:S(2)}, u32[]{:S(2)}) collective-permute-start(bf16[128,1024]{1,0:T(8,128)(2,1)S(1)} %pad_maximum_fusion.6), channel_id=1, source_target_pairs={{1,0},{2,1},{3,2},{0,3},{5,4},{6,5},{7,6},{4,7},{13,8},{14,9},{15,... | collective-permute-start | bytes 786440 | tf_op jit(solution)/shard_map/ppermute | solution.py:203
  37.8 19.4 %collective-permute-start.17 = (bf16[128,1024]{1,0:T(8,128)(2,1)S(1)}, bf16[128,1024]{1,0:T(8,128)(2,1)S(1)}, u32[]{:S(2)}, u32[]{:S(2)}) collective-permute-start(bf16[128,1024]{1,0:T(8,128)(2,1)S(1)} %pad_maximum_fusion.6), channel_id=1, source_target_pairs={{12,8},{13,9},{14,10},{15,11},{8,12},{9,13},{10,14},{11,15},{28,24... | collective-permute-start | bytes 786440 | tf_op jit(solution)/shard_map/ppermute | solution.py:203
  52.4 26.5 %collective-permute-start.7 = (bf16[2,128,1792]{2,1,0:T(8,128)(2,1)}, bf16[2,128,1792]{2,1,0:T(8,128)(2,1)S(1)}, u32[]{:S(2)}, u32[]{:S(2)}) collective-permute-start(bf16[2,128,1792]{2,1,0:T(8,128)(2,1)} %get-tuple-element.19), channel_id=1, source_target_pairs={{0,16},{8,40},{16,0},{24,56},{32,48},{40,72},{48,32},{56,88},{64,8... | collective-permute-start | bytes 2752520 | tf_op jit(solution)/shard_map/ppermute | solution.py:149
  53.4 30.3 %collective-permute-start.8 = (bf16[2,128,1792]{2,1,0:T(8,128)(2,1)}, bf16[2,128,1792]{2,1,0:T(8,128)(2,1)}, u32[]{:S(2)}, u32[]{:S(2)}) collective-permute-start(bf16[2,128,1792]{2,1,0:T(8,128)(2,1)} %get-tuple-element.20), channel_id=1, source_target_pairs={{0,16},{8,104},{16,0},{24,120},{32,48},{40,8},{48,32},{56,24},{64,... | collective-permute-start | bytes 2752520 | tf_op jit(solution)/shard_map/ppermute | solution.py:150
  53.8 29.8 %collective-permute-start.9 = (bf16[2,128,1792]{2,1,0:T(8,128)(2,1)}, bf16[2,128,1792]{2,1,0:T(8,128)(2,1)}, u32[]{:S(2)}, u32[]{:S(2)}) collective-permute-start(bf16[2,128,1792]{2,1,0:T(8,128)(2,1)} %get-tuple-element.21), channel_id=1, source_target_pairs={{8,72},{24,88},{40,104},{56,120},{72,8},{88,24},{104,40},{120,56},... | collective-permute-start | bytes 2752520 | tf_op jit(solution)/shard_map/ppermute | solution.py:151
  57.2 11.8 %collective-permute-start.20 = (bf16[128,1024]{1,0:T(8,128)(2,1)S(1)}, bf16[128,1024]{1,0:T(8,128)(2,1)S(1)}, u32[]{:S(2)}, u32[]{:S(2)}) collective-permute-start(bf16[128,1024]{1,0:T(8,128)(2,1)S(1)} %pad_maximum_fusion.6), channel_id=1, source_target_pairs={{3,0},{0,1},{1,2},{2,3},{7,4},{4,5},{5,6},{6,7},{15,8},{12,9},{13,... | collective-permute-start | bytes 786440 | tf_op jit(solution)/shard_map/ppermute | solution.py:203
  77.3 17.6 %collective-permute-start.22 = (bf16[1,128,1792]{2,1,0:T(8,128)(2,1)}, bf16[1,128,1792]{2,1,0:T(8,128)(2,1)S(1)}, u32[]{:S(2)}, u32[]{:S(2)}) collective-permute-start(bf16[1,128,1792]{2,1,0:T(8,128)(2,1)} %get-tuple-element.26), channel_id=1, source_target_pairs={{0,16},{8,40},{16,0},{24,56},{32,48},{40,72},{48,32},{56,88},{64,8... | collective-permute-start | bytes 1376264 | tf_op jit(solution)/shard_map/ppermute | solution.py:149
  77.9 17.6 %collective-permute-start.23 = (bf16[1,128,1792]{2,1,0:T(8,128)(2,1)}, bf16[1,128,1792]{2,1,0:T(8,128)(2,1)S(1)}, u32[]{:S(2)}, u32[]{:S(2)}) collective-permute-start(bf16[1,128,1792]{2,1,0:T(8,128)(2,1)} %copy-done.10), channel_id=1, source_target_pairs={{0,16},{8,104},{16,0},{24,120},{32,48},{40,8},{48,32},{56,24},{64,... | collective-permute-start | bytes 1376264 | tf_op jit(solution)/shard_map/ppermute | solution.py:150
  78.8 16.7 %collective-permute-start.24 = (bf16[1,128,1792]{2,1,0:T(8,128)(2,1)}, bf16[1,128,1792]{2,1,0:T(8,128)(2,1)S(1)}, u32[]{:S(2)}, u32[]{:S(2)}) collective-permute-start(bf16[1,128,1792]{2,1,0:T(8,128)(2,1)} %copy-done.9), channel_id=1, source_target_pairs={{8,72},{24,88},{40,104},{56,120},{72,8},{88,24},{104,40},{120,56},... | collective-permute-start | bytes 1376264 | tf_op jit(solution)/shard_map/ppermute | solution.py:151
  93.8 9.6 %collective-permute-start.10 = (bf16[2,64,1792]{2,1,0:T(8,128)(2,1)S(1)}, bf16[2,64,1792]{2,1,0:T(8,128)(2,1)S(1)}, u32[]{:S(2)}, u32[]{:S(2)}) collective-permute-start(bf16[2,64,1792]{2,1,0:T(8,128)(2,1)S(1)} %get-tuple-element.23), channel_id=1, source_target_pairs={{0,32},{8,24},{16,48},{24,8},{32,64},{40,56},{48,80},{56,40},{64,9... | collective-permute-start | bytes 1376264 | tf_op jit(solution)/shard_map/ppermute | solution.py:155
  94.2 9.9 %collective-permute-start.11 = (bf16[2,64,1792]{2,1,0:T(8,128)(2,1)S(1)}, bf16[2,64,1792]{2,1,0:T(8,128)(2,1)S(1)}, u32[]{:S(2)}, u32[]{:S(2)}) collective-permute-start(bf16[2,64,1792]{2,1,0:T(8,128)(2,1)S(1)} %get-tuple-element.24), channel_id=1, source_target_pairs={{0,96},{16,112},{32,0},{48,16},{64,32},{80,48},{96,64},{112,80},{1... | collective-permute-start | bytes 1376264 | tf_op jit(solution)/shard_map/ppermute | solution.py:156
  94.9 9.2 %collective-permute-start.12 = (bf16[2,64,1792]{2,1,0:T(8,128)(2,1)S(1)}, bf16[2,64,1792]{2,1,0:T(8,128)(2,1)S(1)}, u32[]{:S(2)}, u32[]{:S(2)}) collective-permute-start(bf16[2,64,1792]{2,1,0:T(8,128)(2,1)S(1)} %get-tuple-element.25), channel_id=1, source_target_pairs={{0,64},{16,80},{32,96},{48,112},{64,0},{80,16},{96,32},{112,48},{1... | collective-permute-start | bytes 1376264 | tf_op jit(solution)/shard_map/ppermute | solution.py:157
  107.7 102.9 %all-gather.5.cloned.1.call-start = ((), (), s32[]{:S(2)}) async-start(), calls=%async_computation.1 | async-start | bytes 7798784 | tf_op jit(solution)/shard_map/all_gather | solution.py:223
  109.9 53.2 %collective-permute-start.32 = (bf16[2,8,64,512]{3,2,1,0:T(8,128)(2,1)}, bf16[2,8,64,512]{3,2,1,0:T(8,128)(2,1)}, u32[]{:S(2)}, u32[]{:S(2)}) collective-permute-start(bf16[2,8,64,512]{3,2,1,0:T(8,128)(2,1)} %pad_maximum_fusion.2), channel_id=1, source_target_pairs={{0,8},{8,0},{16,24},{24,16},{32,40},{40,32},{48,56},{56,48},{64,72... | collective-permute-start | bytes 3145736 | tf_op jit(solution)/shard_map/ppermute | solution.py:196
  160.6 14.8 %collective-permute-start.13 = (bf16[4,2,64,512]{3,2,1,0:T(8,128)(2,1)S(1)}, bf16[4,2,64,512]{3,2,1,0:T(8,128)(2,1)S(1)}, u32[]{:S(2)}, u32[]{:S(2)}) collective-permute-start(bf16[4,2,64,512]{3,2,1,0:T(8,128)(2,1)S(1)} %fusion.19), channel_id=1, source_target_pairs={{0,4},{1,5},{2,6},{3,7},{4,0},{5,1},{6,2},{7,3},{8,12},{9,13},{10,... | collective-permute-start | bytes 1572872 | tf_op jit(solution)/shard_map/ppermute | solution.py:167
  217.5 14.8 %collective-permute-start.28 = (bf16[4,2,64,512]{3,2,1,0:T(8,128)(2,1)S(1)}, bf16[4,2,64,512]{3,2,1,0:T(8,128)(2,1)S(1)}, u32[]{:S(2)}, u32[]{:S(2)}) collective-permute-start(bf16[4,2,64,512]{3,2,1,0:T(8,128)(2,1)S(1)} %fusion.20), channel_id=1, source_target_pairs={{0,4},{1,5},{2,6},{3,7},{4,0},{5,1},{6,2},{7,3},{8,12},{9,13},{10,... | collective-permute-start | bytes 1572872 | tf_op jit(solution)/shard_map/ppermute | solution.py:167
  (26 other events, 249.0 us)
Sparse Core Ops, SparseCore 0:
  107.9 48.5 all-gather.2
  158.7 51.8 all-gather.4

commit v2 on v1

v2 whole, which is shorter than its diff:
```python
import functools

import jax
import jax.numpy as jnp
from jax import lax
from jax.experimental import pallas as pl
from jax.experimental.pallas import tpu as pltpu
from jax.sharding import PartitionSpec as P

NY, NX, NC, NZ = 4, 2, 2, 4
PIECE = 64
BOTH = ("row", "col")


def row_at(y, x, core):
    return ((y % NY) * NX + x) * NC + core


def row_perm(core0, core1):
    pairs = []
    for y in range(NY):
        for x in range(NX):
            for core, move in ((0, core0), (1, core1)):
                if move is not None:
                    to_y, to_x = move(y, x)
                    pairs.append((row_at(y, x, core), row_at(to_y, to_x, core)))
    return pairs


def over_x(y, x):
    return y, 1 - x


def over_y(step):
    return lambda y, x: (y + step, x)


CORE_FLIP = [(i, i ^ 1) for i in range(NY * NX * NC)]


def gather_perm(step):
    pairs = []
    for row in range(NY * NX * NC):
        core = row % NC
        if core == 0 and step == 0:
            continue
        for hi in range(2):
            for z in range(NZ):
                source = (hi ^ core) * NZ + (z + step) % NZ
                pairs.append((row * 8 + source, row * 8 + hi * NZ + z))
    return pairs


def col_perm(flip, step):
    return [(hi * NZ + z, (hi ^ flip) * NZ + (z + step) % NZ) for hi in range(2) for z in range(NZ)]


def product(left, right, transposed):
    dims = (((1,), (1 if transposed else 0,)), ((), ()))
    return lax.dot_general(left, right, dims, preferred_element_type=jnp.float32)


def spans(width):
    return [(at, min(at + 256, width)) for at in range(0, width, 256)]


def pair_product(held, pair, at, end, transposed):
    half = held.shape[1] // 2
    own, other = pair
    if transposed:
        own, other = own[at:end, :], other[at:end, :]
    else:
        own, other = own[:, at:end], other[:, at:end]
    return product(held[:, :half], own, transposed) + product(held[:, half:], other, transposed)


def first_kernel(count, transposed, table, *refs):
    blocks, weights = refs[: NZ + 1], refs[NZ + 1 : NZ + 1 + 2 * count]
    acts, *outs, held = refs[NZ + 1 + 2 * count :]
    width = outs[0].shape[2]
    rows = blocks[0].shape[0]
    acts[:rows] = jnp.where(table[CORE] == 0, blocks[0][...], blocks[1][...])
    for k in range(1, NZ):
        acts[k * rows : (k + 1) * rows] = blocks[k + 1][...]
    for slot in range(6):
        start = pl.multiple_of(table[FIRST + slot] * PIECE, PIECE)
        held[slot * PIECE : (slot + 1) * PIECE, :] = acts[pl.ds(start, PIECE), :]
    for at, end in spans(width):
        for which in range(count):
            pair = weights[2 * which : 2 * which + 2]
            total = pair_product(held, pair, at, end, transposed).astype(jnp.bfloat16)
            for message in range(3):
                outs[message][which, :, at:end] = total[
                    message * 2 * PIECE : (message + 1) * 2 * PIECE
                ]


def second_kernel(count, transposed, table, acts, *refs):
    weights, heard = refs[: 2 * count], refs[2 * count : 2 * count + 3]
    *outs, held = refs[2 * count + 3 :]
    width = outs[0].shape[2]
    core, x = table[CORE], table[AT_X]
    for slot in range(4):
        start = pl.multiple_of(table[SECOND + slot] * PIECE, PIECE)
        held[slot * PIECE : (slot + 1) * PIECE, :] = acts[pl.ds(start, PIECE), :]
    near = pl.ds(pl.multiple_of(x * PIECE, PIECE), PIECE)
    far = pl.ds(pl.multiple_of((1 - x) * PIECE, PIECE), PIECE)
    for at, end in spans(width):
        for which in range(count):
            pair = weights[2 * which : 2 * which + 2]
            total = pair_product(held, pair, at, end, transposed)
            near1, near2, near3 = [h[which, near, at:end].astype(jnp.float32) for h in heard]
            far1, far2, far3 = [h[which, far, at:end].astype(jnp.float32) for h in heard]
            sum1 = total[:PIECE] + far1 + jnp.where(core == 1, far2 + far3, 0.0)
            high = sum1.astype(jnp.bfloat16)
            rest = sum1 - high.astype(jnp.float32)
            sum2 = jnp.where(core == 1, rest, total[PIECE : 2 * PIECE] + near2)
            outs[0][which, :, at:end] = high
            outs[1][which, :, at:end] = sum2.astype(jnp.bfloat16)
            outs[2][which, :, at:end] = (total[2 * PIECE : 3 * PIECE] + far2).astype(jnp.bfloat16)
            outs[3][which, :, at:end] = (
                total[3 * PIECE :] + near1 + jnp.where(core == 1, near2 + near3, 0.0)
            )


def call(kernel, table, operands, out_shape, held_rows, depth, flops):
    vmem = pl.BlockSpec(memory_space=pltpu.VMEM)
    moved = sum(o.size * o.dtype.itemsize for o in [*operands, *out_shape])
    return pl.pallas_call(
        kernel,
        in_specs=[pl.BlockSpec(memory_space=pltpu.SMEM)] + [vmem] * len(operands),
        out_specs=[vmem] * len(out_shape),
        out_shape=out_shape,
        scratch_shapes=[pltpu.VMEM((held_rows, depth), jnp.bfloat16)],
        compiler_params=pltpu.CompilerParams(vmem_limit_bytes=40 * 2**20),
        cost_estimate=pl.CostEstimate(flops=flops, bytes_accessed=moved, transcendentals=0),
    )(table, *operands)


def first_stage(table, blocks, weights, transposed):
    count = len(weights)
    width = weights[0][0].shape[0 if transposed else 1]
    rows, depth = blocks[0].shape
    message = jax.ShapeDtypeStruct((count, 2 * PIECE, width), jnp.bfloat16)
    return call(
        functools.partial(first_kernel, count, transposed),
        table,
        [*blocks, *[w for pair in weights for w in pair]],
        [jax.ShapeDtypeStruct((NZ * rows, depth), jnp.bfloat16)] + [message] * 3,
        6 * PIECE,
        depth,
        2 * 6 * PIECE * depth * width * count,
    )


def second_stage(table, acts, weights, transposed, heard):
    count = len(weights)
    width = weights[0][0].shape[0 if transposed else 1]
    message = jax.ShapeDtypeStruct((count, PIECE, width), jnp.bfloat16)
    return call(
        functools.partial(second_kernel, count, transposed),
        table,
        [acts, *[w for pair in weights for w in pair], *heard],
        [message] * 3 + [jax.ShapeDtypeStruct((count, PIECE, width), jnp.float32)],
        4 * PIECE,
        acts.shape[1],
        2 * 4 * PIECE * acts.shape[1] * width * count,
    )


def send_first(sent):
    return (
        lax.ppermute(sent[0], "row", row_perm(over_x, over_y(1))),
        lax.ppermute(sent[1], "row", row_perm(over_x, over_y(-1))),
        lax.ppermute(sent[2], "row", row_perm(None, over_y(2))),
    )


def send_second(sent):
    return (
        lax.ppermute(sent[0], "row", row_perm(over_y(1), over_x)),
        lax.ppermute(sent[1], "row", row_perm(over_y(-1), over_x)),
        lax.ppermute(sent[2], "row", row_perm(over_y(2), None)),
    )


def add_all(kept, heard):
    for term in heard:
        kept = kept + term.astype(jnp.float32)
    return kept


FIRST, SECOND, CORE, AT_X = 0, 6, 10, 11


def table_rows():
    piece = lambda y_at, x_at: (y_at % NY) * NX + x_at
    rows = []
    for y in range(NY):
        for x in range(NX):
            other = 1 - x
            pair1 = [piece(y, other), piece(y + 1, other)]
            pair2 = [piece(y - 1, other), piece(y + 2, other)]
            if other == 1:
                pair1, pair2 = pair1[::-1], pair2[::-1]
            here = piece(y, x)
            first0 = pair1 + pair2 + [here, here]
            second0 = [piece(y + 1, x), piece(y - 1, x), piece(y + 2, x), here]
            first1 = [piece(y + step, x_at) for step in (1, -1, 2) for x_at in (0, 1)]
            second1 = [piece(y, other), here, here, here]
            rows.append(first0 + second0 + [0, x])
            rows.append(first1 + second1 + [1, x])
    return rows


def col_sum(total):
    blocks = total.reshape(NY, NX, NC, PIECE, total.shape[1])
    away = blocks[:, :, 1].astype(jnp.bfloat16)
    heard = lax.ppermute(away, "col", col_perm(1, 0))
    near = blocks[:, :, 0] + heard.astype(jnp.float32)
    result = near[0]
    send = near[1:].astype(jnp.bfloat16)
    for step in range(1, NZ):
        result = result + lax.ppermute(send[step - 1], "col", col_perm(0, step)).astype(jnp.float32)
    return result.astype(jnp.bfloat16).reshape(NX * PIECE, total.shape[1])


def body(tokens, gate_weight, up_weight, down_weight, grad_output):
    row = lax.axis_index("row")
    table = lax.dynamic_index_in_dim(jnp.array(table_rows(), jnp.int32), row, 0, keepdims=False)
    core = table[CORE]
    flip = lambda value: lax.ppermute(value, "row", CORE_FLIP)
    after = lambda value, *others: lax.optimization_barrier((value, *others))[0]
    width = tokens.shape[1]

    def gather(block, steps):
        return [lax.ppermute(block, BOTH, gather_perm(step)) for step in steps]

    tok_block = jnp.concatenate([tokens, flip(tokens)], axis=1)
    tok_blocks = gather(tok_block, range(NZ))
    gate_pair = (gate_weight, flip(after(gate_weight, tok_block)))
    up_pair = (up_weight, flip(after(up_weight, tok_blocks[1])))
    tok_half, *sent = first_stage(table, [tok_block, *tok_blocks], [gate_pair, up_pair], False)
    heard = send_first(sent)

    grad_own, down_own, _ = lax.optimization_barrier((grad_output, down_weight, sent[0]))
    grad_block = jnp.concatenate([grad_own, flip(grad_own)], axis=1)
    grad_blocks = gather(grad_block, range(NZ))
    down_pair = (down_weight, flip(down_own))
    grad_half, *sent_d = first_stage(table, [grad_block, *grad_blocks], [down_pair], True)
    heard_d = send_first(sent_d)

    *sent, kept = second_stage(table, tok_half, [gate_pair, up_pair], False, heard)
    both = add_all(kept, send_second(sent))
    gate_value, up_value = both[0], both[1]
    sig_gate = jax.nn.sigmoid(gate_value)
    hidden = (gate_value * sig_gate * up_value).astype(jnp.bfloat16)
    hidden, gate_value, up_value, sig_gate = lax.optimization_barrier(
        (hidden, gate_value, up_value, sig_gate)
    )
    hidden = lax.all_gather(hidden, "row", axis=0, tiled=True)

    *sent_d, kept_d = second_stage(table, grad_half, [down_pair], True, heard_d)
    d_hidden = add_all(kept_d, send_second(sent_d))[0]
    d_gate = (d_hidden * up_value * sig_gate * (1.0 + gate_value * (1.0 - sig_gate))).astype(
        jnp.bfloat16
    )
    d_up = (d_hidden * gate_value * sig_gate).astype(jnp.bfloat16)
    d_both = lax.all_gather(jnp.concatenate([d_gate, d_up], axis=1), "row", axis=0, tiled=True)
    ff_width = gate_weight.shape[1]
    d_gate, d_up = d_both[:, :ff_width], d_both[:, ff_width:]

    tok_half = tok_half.reshape(NY * NX, PIECE, 2 * width)
    grad_half = grad_half.reshape(NY * NX, PIECE, 2 * width)
    others = flip(jnp.stack([tok_half[:, :, width:], grad_half[:, :, width:]]))

    def all_rows(half, received):
        own = half[:, :, :width]
        pair = jnp.where(
            core == 0, jnp.stack([own, received], axis=1), jnp.stack([received, own], axis=1)
        )
        return pair.reshape(-1, width)

    tok_all, grad_all = all_rows(tok_half, others[0]), all_rows(grad_half, others[1])

    layer_output = col_sum(jnp.dot(hidden, down_weight, preferred_element_type=jnp.float32))
    last = (((1,), (1,)), ((), ()))
    first = (((0,), (0,)), ((), ()))
    dot = functools.partial(lax.dot_general, preferred_element_type=jnp.float32)
    grad_input = col_sum(dot(d_gate, gate_weight, last) + dot(d_up, up_weight, last))
    grad_down = dot(hidden, grad_all, first).astype(jnp.bfloat16)
    grad_gate = dot(tok_all, d_gate, first).astype(jnp.bfloat16)
    grad_up = dot(tok_all, d_up, first).astype(jnp.bfloat16)
    return (layer_output, grad_input, grad_gate, grad_up, grad_down)


def solution(mesh):
    placed = (P("col", "row"), P("row", "col"), P("row", "col"), P("col", "row"), P("col", "row"))
    return jax.shard_map(
        body,
        mesh=mesh,
        in_specs=placed,
        out_specs=(
            P("col", "row"),
            P("col", "row"),
            P("row", "col"),
            P("row", "col"),
            P("col", "row"),
        ),
        check_vma=False,
    )
```

time: 254 us -> 269 us (1.059)
  starting transfers between devices: 67.2 us -> 85.8 us
  Pallas kernels: 27.7 us -> 12.3 us
  waiting for transfers between devices: 102 us -> 111 us
  local copies, waits for them, and re-layouts: 10.1 us -> 15 us
    ppermute x20, waiting for transfers between devices: 16 us -> 60.4 us  [the longest x8 13.1 us: gather(): return [lax.ppermute(block, BOTH, gather_perm(step)) for step in steps]]
    all_gather x1, waiting for transfers between devices: 34.4 us -> 0.02 us  [body(): hidden = lax.all_gather(hidden, 'row', axis=0, tiled=True)]
    ppermute x20, starting transfers between devices: 40.5 us -> 61.6 us  [the longest x8 27.7 us: gather(): return [lax.ppermute(block, BOTH, gather_perm(step)) for step in steps]]
    pallas_call x4, Pallas kernels: 27.7 us -> 12.3 us  [call(): pl.pallas_call(kernel, in_specs=[pl.BlockSpec(memory_space=pltpu.SMEM)] +...]
    ppermute x5 -> x6, starting transfers between devices: 13.6 us -> 3.51 us  [body(): flip = lambda value: lax.ppermute(value, 'row', CORE_FLIP)]
    ppermute x6, starting transfers between devices: 9 us -> 16.9 us  [col_sum(): lax.ppermute(send[step - 1], 'col', col_perm(0, step)).astype(jnp.float32)]
    all_gather x1, waiting for transfers between devices: 24.2 us -> 21.3 us  [body(): lax.all_gather(jnp.concatenate([d_gate, d_up], axis=1), 'row', axis=0, ti...]
    unnamed x30 -> x42, local copies, waits for them, and re-layouts: 8.07 us -> 10.9 us
  transfers between devices with their start and end apart: 35 -> 36, of which waited for: 12 -> 22; matrix products, arithmetic and copies ran while one was open for 9% -> 8% of each run, Pallas kernels for 11% -> 1%
where the time goes in v2:
time: 269 us; the launch traced here: 266 us
  waiting for transfers between devices  111 us (41%)
  starting transfers between devices  85.8 us (32%)
  matrix products  20.5 us (8%)
  between operations  15.1 us (6%)
  local copies, waits for them, and re-layouts  15 us (6%)
  Pallas kernels  12.3 us (5%)
  other arithmetic  6.38 us (2%)
    ppermute x8, starting transfers between devices, gather(): return [lax.ppermute(block, BOTH, gather_perm(step)) for step in steps]  27.7 us
    all_gather x1, waiting for transfers between devices, body(): lax.all_gather(jnp.concatenate([d_gate, d_up], axis=1), 'row', axis=0, ti...  21.3 us
    ppermute x2, waiting for transfers between devices, col_sum(): heard = lax.ppermute(away, 'col', col_perm(1, 0))  20.6 us
    ppermute x2, starting transfers between devices, send_first(): lax.ppermute(sent[0], 'row', row_perm(over_x, over_y(1)))  18.7 us
    ppermute x6, starting transfers between devices, col_sum(): lax.ppermute(send[step - 1], 'col', col_perm(0, step)).astype(jnp.float32)  16.9 us
    ppermute x8, waiting for transfers between devices, gather(): return [lax.ppermute(block, BOTH, gather_perm(step)) for step in steps]  13.1 us
    pallas_call x4, Pallas kernels, call(): pl.pallas_call(kernel, in_specs=[pl.BlockSpec(memory_space=pltpu.SMEM)] +...  12.3 us
    ppermute x2, waiting for transfers between devices, send_first(): lax.ppermute(sent[2], 'row', row_perm(None, over_y(2)))  12.2 us
  transfers between devices with their start and end apart: 36, of which 22 were waited for; matrix products, arithmetic and copies ran while one was open for 8% of the time, Pallas kernels for 1%

profile of v2, /device:TPU:17, one launch (start us, length us, event | category | flops | bytes accessed | tf_op | source)
XLA Modules:
  0.0 266.1 jit_solution(18219825316458080929)
XLA Ops:
  9.2 6.3 %collective-permute-start.2 = (bf16[128,1024]{1,0:T(8,128)(2,1)S(1)}, bf16[128,1024]{1,0:T(8,128)(2,1)S(1)}, u32[]{:S(2)}, u32[]{:S(2)}) collective-permute-start(bf16[128,1024]{1,0:T(8,128)(2,1)S(1)} %constant_dynamic-update-slice_fusion.refs_0_), channel_id=1, source_target_pairs={{1,0},{2,1},{3,2},{0,3},{5,4},{6,5},{7,6},{4,7},{13,8},{14,9},{15,... | collective-permute-start | bytes 786440 | tf_op jit(solution)/shard_map/ppermute | solution.py:237
  22.9 4.5 %collective-permute-start.3 = (bf16[128,1024]{1,0:T(8,128)(2,1)S(1)}, bf16[128,1024]{1,0:T(8,128)(2,1)S(1)}, u32[]{:S(2)}, u32[]{:S(2)}) collective-permute-start(bf16[128,1024]{1,0:T(8,128)(2,1)S(1)} %constant_dynamic-update-slice_fusion.refs_0_), channel_id=1, source_target_pairs={{2,0},{3,1},{0,2},{1,3},{6,4},{7,5},{4,6},{5,7},{14,8},{15,9},{12,... | collective-permute-start | bytes 786440 | tf_op jit(solution)/shard_map/ppermute | solution.py:237
  27.3 4.6 %collective-permute-start.1 = (bf16[128,1024]{1,0:T(8,128)(2,1)S(1)}, bf16[128,1024]{1,0:T(8,128)(2,1)S(1)}, u32[]{:S(2)}, u32[]{:S(2)}) collective-permute-start(bf16[128,1024]{1,0:T(8,128)(2,1)S(1)} %constant_dynamic-update-slice_fusion.refs_0_), channel_id=1, source_target_pairs={{12,8},{13,9},{14,10},{15,11},{8,12},{9,13},{10,14},{11,15},{28,24... | collective-permute-start | bytes 786440 | tf_op jit(solution)/shard_map/ppermute | solution.py:237
  43.5 4.6 %shard_map.101 = (bf16[512,1024]{1,0:T(8,128)(2,1)S(1)}, bf16[2,128,1792]{2,1,0:T(8,128)(2,1)S(1)}, bf16[2,128,1792]{2,1,0:T(8,128)(2,1)S(1)}, bf16[2,128,1792]{2,1,0:T(8,128)(2,1)S(1)}) custom-call(s32[12]{0:T(128)S(1)} %get-tuple-element.76.table, bf16[128,1024]{1,0:T(8,128)(2,1)S(1)} %constant_dynamic-update-slice_fusion.refs_0_, ...), custom_call_target="tpu_custom_call" | custom-call | flops 2818572288 | bytes 12451840 | tf_op jit(solution)/shard_map/pallas_call | solution.py:129
  48.3 4.5 %collective-permute-start.9 = (bf16[2,128,1792]{2,1,0:T(8,128)(2,1)S(1)}, bf16[2,128,1792]{2,1,0:T(8,128)(2,1)S(1)}, u32[]{:S(2)}, u32[]{:S(2)}) collective-permute-start(bf16[2,128,1792]{2,1,0:T(8,128)(2,1)S(1)} %get-tuple-element.34), channel_id=1, source_target_pairs={{8,72},{24,88},{40,104},{56,120},{72,8},{88,24},{104,40},{120,56},... | collective-permute-start | bytes 2752520 | tf_op jit(solution)/shard_map/ppermute | solution.py:175
  52.9 7.8 %collective-permute-done.8.refs_5_ = bf16[2,128,1792]{2,1,0:T(8,128)(2,1)S(1)} collective-permute-done((bf16[2,128,1792]{2,1,0:T(8,128)(2,1)S(1)}, bf16[2,128,1792]{2,1,0:T(8,128)(2,1)S(1)}, u32[]{:S(2)}, u32[]{:S(2)}) %collective-permute-start.8) | collective-permute-done | bytes 917536 | tf_op jit(solution)/shard_map/ppermute | solution.py:174
  64.1 9.7 %collective-permute-done.7.refs_4_ = bf16[2,128,1792]{2,1,0:T(8,128)(2,1)S(1)} collective-permute-done((bf16[2,128,1792]{2,1,0:T(8,128)(2,1)S(1)}, bf16[2,128,1792]{2,1,0:T(8,128)(2,1)S(1)}, u32[]{:S(2)}, u32[]{:S(2)}) %collective-permute-start.7) | collective-permute-done | bytes 917536 | tf_op jit(solution)/shard_map/ppermute | solution.py:173
  73.8 3.7 %shard_map.102 = (bf16[2,64,1792]{2,1,0:T(8,128)(2,1)S(1)}, bf16[2,64,1792]{2,1,0:T(8,128)(2,1)S(1)}, bf16[2,64,1792]{2,1,0:T(8,128)(2,1)S(1)}, f32[2,64,1792]{2,1,0:T(8,128)S(1)}) custom-call(s32[12]{0:T(128)S(1)} %get-tuple-element.76.table, bf16[512,1024]{1,0:T(8,128)(2,1)S(1)} %get-tuple-element.31.acts, bf16[512,1792]{1,0:T(8,128)(2,1)S(1)} %copy-done.5, ...), custom_call_target="tpu_custom_call" | custom-call | flops 1879048192 | bytes 13434880 | tf_op jit(solution)/shard_map/pallas_call | solution.py:129
  79.7 5.5 %collective-permute-done.10 = bf16[2,64,1792]{2,1,0:T(8,128)(2,1)S(1)} collective-permute-done((bf16[2,64,1792]{2,1,0:T(8,128)(2,1)S(1)}, bf16[2,64,1792]{2,1,0:T(8,128)(2,1)S(1)}, u32[]{:S(2)}, u32[]{:S(2)}) %collective-permute-start.10) | collective-permute-done | bytes 458784 | tf_op jit(solution)/shard_map/ppermute | solution.py:181
  85.2 4.9 %collective-permute-done.11 = bf16[2,64,1792]{2,1,0:T(8,128)(2,1)S(1)} collective-permute-done((bf16[2,64,1792]{2,1,0:T(8,128)(2,1)S(1)}, bf16[2,64,1792]{2,1,0:T(8,128)(2,1)S(1)}, u32[]{:S(2)}, u32[]{:S(2)}) %collective-permute-start.11) | collective-permute-done | bytes 458784 | tf_op jit(solution)/shard_map/ppermute | solution.py:182
  93.6 3.5 %collective-permute-done.17 = bf16[128,512]{1,0:T(8,128)(2,1)S(1)} collective-permute-done((bf16[128,512]{1,0:T(8,128)(2,1)S(1)}, bf16[128,512]{1,0:T(8,128)(2,1)S(1)}, u32[]{:S(2)}, u32[]{:S(2)}) %collective-permute-start.17) | collective-permute-done | bytes 131104 | tf_op jit(solution)/shard_map/ppermute | solution.py:232
  99.3 4.4 %collective-permute-start.19 = (bf16[128,1024]{1,0:T(8,128)(2,1)S(1)}, bf16[128,1024]{1,0:T(8,128)(2,1)S(1)}, u32[]{:S(2)}, u32[]{:S(2)}) collective-permute-start(bf16[128,1024]{1,0:T(8,128)(2,1)S(1)} %constant_dynamic-update-slice_fusion.2.refs_0_), channel_id=1, source_target_pairs={{1,0},{2,1},{3,2},{0,3},{5,4},{6,5},{7,6},{4,7},{13,8},{14,9},{15,... | collective-permute-start | bytes 786440 | tf_op jit(solution)/shard_map/ppermute | solution.py:237
  108.9 4.9 %collective-permute-done.19.refs_2_ = bf16[128,1024]{1,0:T(8,128)(2,1)S(1)} collective-permute-done((bf16[128,1024]{1,0:T(8,128)(2,1)S(1)}, bf16[128,1024]{1,0:T(8,128)(2,1)S(1)}, u32[]{:S(2)}, u32[]{:S(2)}) %collective-permute-start.19) | collective-permute-done | bytes 262176 | tf_op jit(solution)/shard_map/ppermute | solution.py:237
  117.6 18.6 %collective-permute-start.23 = (bf16[1,128,1792]{2,1,0:T(8,128)(2,1)S(1)}, bf16[1,128,1792]{2,1,0:T(8,128)(2,1)S(1)}, u32[]{:S(2)}, u32[]{:S(2)}) collective-permute-start(bf16[1,128,1792]{2,1,0:T(8,128)(2,1)S(1)} %get-tuple-element.43), channel_id=1, source_target_pairs={{0,16},{8,40},{16,0},{24,56},{32,48},{40,72},{48,32},{56,88},{64,8... | collective-permute-start | bytes 1376264 | tf_op jit(solution)/shard_map/ppermute | solution.py:173
  136.2 6.1 %collective-permute-start.25 = (bf16[1,128,1792]{2,1,0:T(8,128)(2,1)S(1)}, bf16[1,128,1792]{2,1,0:T(8,128)(2,1)S(1)}, u32[]{:S(2)}, u32[]{:S(2)}) collective-permute-start(bf16[1,128,1792]{2,1,0:T(8,128)(2,1)S(1)} %get-tuple-element.45), channel_id=1, source_target_pairs={{8,72},{24,88},{40,104},{56,120},{72,8},{88,24},{104,40},{120,56},... | collective-permute-start | bytes 1376264 | tf_op jit(solution)/shard_map/ppermute | solution.py:175
  144.3 8.8 %collective-permute-done.25.refs_4_ = bf16[1,128,1792]{2,1,0:T(8,128)(2,1)S(1)} collective-permute-done((bf16[1,128,1792]{2,1,0:T(8,128)(2,1)S(1)}, bf16[1,128,1792]{2,1,0:T(8,128)(2,1)S(1)}, u32[]{:S(2)}, u32[]{:S(2)}) %collective-permute-start.25) | collective-permute-done | bytes 458784 | tf_op jit(solution)/shard_map/ppermute | solution.py:175
  166.0 4.1 %fusion.39 = f32[1024,512]{1,0:T(8,128)S(1)} fusion(bf16[1024,1792]{1,0:T(8,128)(2,1)} %all-gather.3.cloned.1.call-done, bf16[1792,512]{1,0:T(8,128)(2,1)S(1)} %copy-done.2), kind=kOutput, calls=%fused_computation.67 | convolution fusion | flops 1879048192 | bytes 7602176 | tf_op jit(solution)/shard_map/dot_general | solution.py:286
  172.8 11.9 %collective-permute-done.13 = bf16[4,2,64,512]{3,2,1,0:T(8,128)(2,1)S(1)} collective-permute-done((bf16[4,2,64,512]{3,2,1,0:T(8,128)(2,1)S(1)}, bf16[4,2,64,512]{3,2,1,0:T(8,128)(2,1)S(1)}, u32[]{:S(2)}, u32[]{:S(2)}) %collective-permute-start.13) | collective-permute-done | bytes 524320 | tf_op jit(solution)/shard_map/ppermute | solution.py:219
  192.2 3.4 %convolution_convert_fusion = bf16[1792,512]{1,0:T(8,128)(2,1)} fusion(bf16[1024,1792]{1,0:T(8,128)(2,1)S(1)} %copy-done.19, bf16[1024,512]{1,0:T(8,128)(2,1)S(1)} %bitcast.114), kind=kOutput, calls=%fused_computation.10 | convolution fusion | flops 1879965696 | bytes 6553600 | tf_op jit(solution)/shard_map/dot_general | solution.py:291
  198.7 21.3 %all-gather.5.cloned.1.call-done = bf16[1024,3584]{1,0:T(8,128)(2,1)} async-done(((bf16[64,3584]{1,0:T(8,128)(2,1)}), bf16[1024,3584]{1,0:T(8,128)(2,1)}) %all-gather.5.cloned.1.call-update) | async-done | bytes 7340048 | tf_op jit(solution)/shard_map/all_gather | solution.py:269
  220.0 4.3 %fusion.2 = f32[1024,512]{1,0:T(8,128)S(1)} fusion(bf16[512,1792]{1,0:T(8,128)(2,1)S(1)} %copy-done.4, bf16[1024,3584]{1,0:T(8,128)(2,1)} %all-gather.5.cloned.1.call-done), kind=kOutput, calls=%fused_computation.2 | convolution fusion | flops 1879048192 | bytes 7602176 | tf_op jit(solution)/shard_map/dot_general | solution.py:290
  227.0 3.6 %collective-permute-start.29 = (bf16[4,2,64,512]{3,2,1,0:T(8,128)(2,1)S(1)}, bf16[4,2,64,512]{3,2,1,0:T(8,128)(2,1)S(1)}, u32[]{:S(2)}, u32[]{:S(2)}) collective-permute-start(bf16[4,2,64,512]{3,2,1,0:T(8,128)(2,1)S(1)} %fusion.20), channel_id=1, source_target_pairs={{0,4},{1,5},{2,6},{3,7},{4,0},{5,1},{6,2},{7,3},{8,12},{9,13},{10,... | collective-permute-start | bytes 1572872 | tf_op jit(solution)/shard_map/ppermute | solution.py:219
  233.9 8.8 %collective-permute-done.29 = bf16[4,2,64,512]{3,2,1,0:T(8,128)(2,1)S(1)} collective-permute-done((bf16[4,2,64,512]{3,2,1,0:T(8,128)(2,1)S(1)}, bf16[4,2,64,512]{3,2,1,0:T(8,128)(2,1)S(1)}, u32[]{:S(2)}, u32[]{:S(2)}) %collective-permute-start.29) | collective-permute-done | bytes 524320 | tf_op jit(solution)/shard_map/ppermute | solution.py:219
  245.9 5.7 %collective-permute-start.32 = (bf16[2,64,512]{2,1,0:T(8,128)(2,1)S(1)}, bf16[2,64,512]{2,1,0:T(8,128)(2,1)S(1)}, u32[]{:S(2)}, u32[]{:S(2)}) collective-permute-start(bf16[2,64,512]{2,1,0:T(8,128)(2,1)S(1)} %get-tuple-element.70), channel_id=1, source_target_pairs={{0,3},{1,0},{2,1},{3,2},{4,7},{5,4},{6,5},{7,6},{8,11},{9,8},{10,9... | collective-permute-start | bytes 393224 | tf_op jit(solution)/shard_map/ppermute | solution.py:224
  (126 shorter events, 85.7 us)
Async XLA Ops:
  7.2 158.8 %all-gather.3.cloned.1.call-start = ((), (), s32[]{:S(2)}) async-start(), calls=%async_computation | async-start | bytes 3899392 | tf_op jit(solution)/shard_map/all_gather | solution.py:261
  15.5 22.2 %collective-permute-start.5 = (bf16[512,1792]{1,0:T(8,128)(2,1)}, bf16[512,1792]{1,0:T(8,128)(2,1)S(1)}, u32[]{:S(2)}, u32[]{:S(2)}) collective-permute-start(bf16[512,1792]{1,0:T(8,128)(2,1)} %refs_0_.2), channel_id=1, source_target_pairs={{0,8},{8,0},{16,24},{24,16},{32,40},{40,32},{48,56},{56,48},{64,72... | collective-permute-start | bytes 5505032 | tf_op jit(solution)/shard_map/ppermute | solution.py:232
  18.8 18.9 %collective-permute-start.6 = (bf16[512,1792]{1,0:T(8,128)(2,1)}, bf16[512,1792]{1,0:T(8,128)(2,1)}, u32[]{:S(2)}, u32[]{:S(2)}) collective-permute-start(bf16[512,1792]{1,0:T(8,128)(2,1)} %refs_2_.1), channel_id=1, source_target_pairs={{0,8},{8,0},{16,24},{24,16},{32,40},{40,32},{48,56},{56,48},{64,72... | collective-permute-start | bytes 5505032 | tf_op jit(solution)/shard_map/ppermute | solution.py:232
  20.4 12.3 %collective-permute-start.4 = (bf16[128,1024]{1,0:T(8,128)(2,1)S(1)}, bf16[128,1024]{1,0:T(8,128)(2,1)S(1)}, u32[]{:S(2)}, u32[]{:S(2)}) collective-permute-start(bf16[128,1024]{1,0:T(8,128)(2,1)S(1)} %constant_dynamic-update-slice_fusion.refs_0_), channel_id=1, source_target_pairs={{3,0},{0,1},{1,2},{2,3},{7,4},{4,5},{5,6},{6,7},{15,8},{12,9},{13,... | collective-permute-start | bytes 786440 | tf_op jit(solution)/shard_map/ppermute | solution.py:237
  22.9 11.1 %collective-permute-start.3 = (bf16[128,1024]{1,0:T(8,128)(2,1)S(1)}, bf16[128,1024]{1,0:T(8,128)(2,1)S(1)}, u32[]{:S(2)}, u32[]{:S(2)}) collective-permute-start(bf16[128,1024]{1,0:T(8,128)(2,1)S(1)} %constant_dynamic-update-slice_fusion.refs_0_), channel_id=1, source_target_pairs={{2,0},{3,1},{0,2},{1,3},{6,4},{7,5},{4,6},{5,7},{14,8},{15,9},{12,... | collective-permute-start | bytes 786440 | tf_op jit(solution)/shard_map/ppermute | solution.py:237
  27.3 9.6 %collective-permute-start.1 = (bf16[128,1024]{1,0:T(8,128)(2,1)S(1)}, bf16[128,1024]{1,0:T(8,128)(2,1)S(1)}, u32[]{:S(2)}, u32[]{:S(2)}) collective-permute-start(bf16[128,1024]{1,0:T(8,128)(2,1)S(1)} %constant_dynamic-update-slice_fusion.refs_0_), channel_id=1, source_target_pairs={{12,8},{13,9},{14,10},{15,11},{8,12},{9,13},{10,14},{11,15},{28,24... | collective-permute-start | bytes 786440 | tf_op jit(solution)/shard_map/ppermute | solution.py:237
  48.1 12.6 %collective-permute-start.8 = (bf16[2,128,1792]{2,1,0:T(8,128)(2,1)S(1)}, bf16[2,128,1792]{2,1,0:T(8,128)(2,1)S(1)}, u32[]{:S(2)}, u32[]{:S(2)}) collective-permute-start(bf16[2,128,1792]{2,1,0:T(8,128)(2,1)S(1)} %get-tuple-element.33), channel_id=1, source_target_pairs={{0,16},{8,104},{16,0},{24,120},{32,48},{40,8},{48,32},{56,24},{64,... | collective-permute-start | bytes 2752520 | tf_op jit(solution)/shard_map/ppermute | solution.py:174
  48.3 15.7 %collective-permute-start.9 = (bf16[2,128,1792]{2,1,0:T(8,128)(2,1)S(1)}, bf16[2,128,1792]{2,1,0:T(8,128)(2,1)S(1)}, u32[]{:S(2)}, u32[]{:S(2)}) collective-permute-start(bf16[2,128,1792]{2,1,0:T(8,128)(2,1)S(1)} %get-tuple-element.34), channel_id=1, source_target_pairs={{8,72},{24,88},{40,104},{56,120},{72,8},{88,24},{104,40},{120,56},... | collective-permute-start | bytes 2752520 | tf_op jit(solution)/shard_map/ppermute | solution.py:175
  52.9 20.9 %collective-permute-start.7 = (bf16[2,128,1792]{2,1,0:T(8,128)(2,1)S(1)}, bf16[2,128,1792]{2,1,0:T(8,128)(2,1)S(1)}, u32[]{:S(2)}, u32[]{:S(2)}) collective-permute-start(bf16[2,128,1792]{2,1,0:T(8,128)(2,1)S(1)} %get-tuple-element.32), channel_id=1, source_target_pairs={{0,16},{8,40},{16,0},{24,56},{32,48},{40,72},{48,32},{56,88},{64,8... | collective-permute-start | bytes 2752520 | tf_op jit(solution)/shard_map/ppermute | solution.py:173
  78.1 12.0 %collective-permute-start.11 = (bf16[2,64,1792]{2,1,0:T(8,128)(2,1)S(1)}, bf16[2,64,1792]{2,1,0:T(8,128)(2,1)S(1)}, u32[]{:S(2)}, u32[]{:S(2)}) collective-permute-start(bf16[2,64,1792]{2,1,0:T(8,128)(2,1)S(1)} %get-tuple-element.37), channel_id=1, source_target_pairs={{0,96},{8,24},{16,112},{24,8},{32,0},{40,56},{48,16},{56,40},{64,3... | collective-permute-start | bytes 1376264 | tf_op jit(solution)/shard_map/ppermute | solution.py:182
  79.1 11.1 %collective-permute-start.12 = (bf16[2,64,1792]{2,1,0:T(8,128)(2,1)S(1)}, bf16[2,64,1792]{2,1,0:T(8,128)(2,1)S(1)}, u32[]{:S(2)}, u32[]{:S(2)}) collective-permute-start(bf16[2,64,1792]{2,1,0:T(8,128)(2,1)S(1)} %get-tuple-element.38), channel_id=1, source_target_pairs={{0,64},{16,80},{32,96},{48,112},{64,0},{80,16},{96,32},{112,48},{1... | collective-permute-start | bytes 1376264 | tf_op jit(solution)/shard_map/ppermute | solution.py:183
  92.3 127.7 %all-gather.5.cloned.1.call-start = ((), (), s32[]{:S(2)}) async-start(), calls=%async_computation.1 | async-start | bytes 7798784 | tf_op jit(solution)/shard_map/all_gather | solution.py:269
  92.4 21.4 %collective-permute-start.22 = (bf16[1792,512]{1,0:T(8,128)(2,1)S(1)}, bf16[1792,512]{1,0:T(8,128)(2,1)S(1)}, u32[]{:S(2)}, u32[]{:S(2)}) collective-permute-start(bf16[1792,512]{1,0:T(8,128)(2,1)S(1)} %copy-done), channel_id=1, source_target_pairs={{0,8},{8,0},{16,24},{24,16},{32,40},{40,32},{48,56},{56,48},{64,72... | collective-permute-start | bytes 5505032 | tf_op jit(solution)/shard_map/ppermute | solution.py:232
  97.1 11.0 %collective-permute-start.21 = (bf16[128,1024]{1,0:T(8,128)(2,1)S(1)}, bf16[128,1024]{1,0:T(8,128)(2,1)S(1)}, u32[]{:S(2)}, u32[]{:S(2)}) collective-permute-start(bf16[128,1024]{1,0:T(8,128)(2,1)S(1)} %constant_dynamic-update-slice_fusion.2.refs_0_), channel_id=1, source_target_pairs={{3,0},{0,1},{1,2},{2,3},{7,4},{4,5},{5,6},{6,7},{15,8},{12,9},{13,... | collective-permute-start | bytes 786440 | tf_op jit(solution)/shard_map/ppermute | solution.py:237
  97.1 11.7 %collective-permute-start.20 = (bf16[128,1024]{1,0:T(8,128)(2,1)S(1)}, bf16[128,1024]{1,0:T(8,128)(2,1)S(1)}, u32[]{:S(2)}, u32[]{:S(2)}) collective-permute-start(bf16[128,1024]{1,0:T(8,128)(2,1)S(1)} %constant_dynamic-update-slice_fusion.2.refs_0_), channel_id=1, source_target_pairs={{2,0},{3,1},{0,2},{1,3},{6,4},{7,5},{4,6},{5,7},{14,8},{15,9},{12,... | collective-permute-start | bytes 786440 | tf_op jit(solution)/shard_map/ppermute | solution.py:237
  99.3 14.5 %collective-permute-start.19 = (bf16[128,1024]{1,0:T(8,128)(2,1)S(1)}, bf16[128,1024]{1,0:T(8,128)(2,1)S(1)}, u32[]{:S(2)}, u32[]{:S(2)}) collective-permute-start(bf16[128,1024]{1,0:T(8,128)(2,1)S(1)} %constant_dynamic-update-slice_fusion.2.refs_0_), channel_id=1, source_target_pairs={{1,0},{2,1},{3,2},{0,3},{5,4},{6,5},{7,6},{4,7},{13,8},{14,9},{15,... | collective-permute-start | bytes 786440 | tf_op jit(solution)/shard_map/ppermute | solution.py:237
  103.7 10.1 %collective-permute-start.18 = (bf16[128,1024]{1,0:T(8,128)(2,1)S(1)}, bf16[128,1024]{1,0:T(8,128)(2,1)S(1)}, u32[]{:S(2)}, u32[]{:S(2)}) collective-permute-start(bf16[128,1024]{1,0:T(8,128)(2,1)S(1)} %constant_dynamic-update-slice_fusion.2.refs_0_), channel_id=1, source_target_pairs={{12,8},{13,9},{14,10},{15,11},{8,12},{9,13},{10,14},{11,15},{28,24... | collective-permute-start | bytes 786440 | tf_op jit(solution)/shard_map/ppermute | solution.py:237
  117.6 24.7 %collective-permute-start.23 = (bf16[1,128,1792]{2,1,0:T(8,128)(2,1)S(1)}, bf16[1,128,1792]{2,1,0:T(8,128)(2,1)S(1)}, u32[]{:S(2)}, u32[]{:S(2)}) collective-permute-start(bf16[1,128,1792]{2,1,0:T(8,128)(2,1)S(1)} %get-tuple-element.43), channel_id=1, source_target_pairs={{0,16},{8,40},{16,0},{24,56},{32,48},{40,72},{48,32},{56,88},{64,8... | collective-permute-start | bytes 1376264 | tf_op jit(solution)/shard_map/ppermute | solution.py:173
  136.2 16.9 %collective-permute-start.25 = (bf16[1,128,1792]{2,1,0:T(8,128)(2,1)S(1)}, bf16[1,128,1792]{2,1,0:T(8,128)(2,1)S(1)}, u32[]{:S(2)}, u32[]{:S(2)}) collective-permute-start(bf16[1,128,1792]{2,1,0:T(8,128)(2,1)S(1)} %get-tuple-element.45), channel_id=1, source_target_pairs={{8,72},{24,88},{40,104},{56,120},{72,8},{88,24},{104,40},{120,56},... | collective-permute-start | bytes 1376264 | tf_op jit(solution)/shard_map/ppermute | solution.py:175
  170.1 14.6 %collective-permute-start.13 = (bf16[4,2,64,512]{3,2,1,0:T(8,128)(2,1)S(1)}, bf16[4,2,64,512]{3,2,1,0:T(8,128)(2,1)S(1)}, u32[]{:S(2)}, u32[]{:S(2)}) collective-permute-start(bf16[4,2,64,512]{3,2,1,0:T(8,128)(2,1)S(1)} %fusion.19), channel_id=1, source_target_pairs={{0,4},{1,5},{2,6},{3,7},{4,0},{5,1},{6,2},{7,3},{8,12},{9,13},{10,... | collective-permute-start | bytes 1572872 | tf_op jit(solution)/shard_map/ppermute | solution.py:219
  185.0 10.6 %collective-permute-start.14 = (bf16[2,64,512]{2,1,0:T(8,128)(2,1)S(1)}, bf16[2,64,512]{2,1,0:T(8,128)(2,1)S(1)}, u32[]{:S(2)}, u32[]{:S(2)}) collective-permute-start(bf16[2,64,512]{2,1,0:T(8,128)(2,1)S(1)} %get-tuple-element.72), channel_id=1, source_target_pairs={{0,1},{1,2},{2,3},{3,0},{4,5},{5,6},{6,7},{7,4},{8,9},{9,10},{10,1... | collective-permute-start | bytes 393224 | tf_op jit(solution)/shard_map/ppermute | solution.py:224
  227.0 15.7 %collective-permute-start.29 = (bf16[4,2,64,512]{3,2,1,0:T(8,128)(2,1)S(1)}, bf16[4,2,64,512]{3,2,1,0:T(8,128)(2,1)S(1)}, u32[]{:S(2)}, u32[]{:S(2)}) collective-permute-start(bf16[4,2,64,512]{3,2,1,0:T(8,128)(2,1)S(1)} %fusion.20), channel_id=1, source_target_pairs={{0,4},{1,5},{2,6},{3,7},{4,0},{5,1},{6,2},{7,3},{8,12},{9,13},{10,... | collective-permute-start | bytes 1572872 | tf_op jit(solution)/shard_map/ppermute | solution.py:219
  242.9 13.0 %collective-permute-start.30 = (bf16[2,64,512]{2,1,0:T(8,128)(2,1)S(1)}, bf16[2,64,512]{2,1,0:T(8,128)(2,1)S(1)}, u32[]{:S(2)}, u32[]{:S(2)}) collective-permute-start(bf16[2,64,512]{2,1,0:T(8,128)(2,1)S(1)} %get-tuple-element.69), channel_id=1, source_target_pairs={{0,1},{1,2},{2,3},{3,0},{4,5},{5,6},{6,7},{7,4},{8,9},{9,10},{10,1... | collective-permute-start | bytes 393224 | tf_op jit(solution)/shard_map/ppermute | solution.py:224
  245.9 10.1 %collective-permute-start.32 = (bf16[2,64,512]{2,1,0:T(8,128)(2,1)S(1)}, bf16[2,64,512]{2,1,0:T(8,128)(2,1)S(1)}, u32[]{:S(2)}, u32[]{:S(2)}) collective-permute-start(bf16[2,64,512]{2,1,0:T(8,128)(2,1)S(1)} %get-tuple-element.70), channel_id=1, source_target_pairs={{0,3},{1,0},{2,1},{3,2},{4,7},{5,4},{6,5},{7,6},{8,11},{9,8},{10,9... | collective-permute-start | bytes 393224 | tf_op jit(solution)/shard_map/ppermute | solution.py:224
  (32 other events, 182.2 us)
Sparse Core Ops, SparseCore 0:
  92.5 39.8 all-gather.2
  163.5 56.4 all-gather.4

commit v3 on v2

v3 whole, which is shorter than its diff:
```python
import functools

import jax
import jax.numpy as jnp
from jax import lax
from jax.experimental import pallas as pl
from jax.experimental.pallas import tpu as pltpu
from jax.sharding import PartitionSpec as P

NY, NX, NC, NZ = 4, 2, 2, 4
PIECE = 64
BOTH = ("row", "col")


def row_at(y, x, core):
    return ((y % NY) * NX + x) * NC + core


def row_perm(core0, core1):
    pairs = []
    for y in range(NY):
        for x in range(NX):
            for core, move in ((0, core0), (1, core1)):
                if move is not None:
                    to_y, to_x = move(y, x)
                    pairs.append((row_at(y, x, core), row_at(to_y, to_x, core)))
    return pairs


def over_x(y, x):
    return y, 1 - x


def over_y(step):
    return lambda y, x: (y + step, x)


CORE_FLIP = [(i, i ^ 1) for i in range(NY * NX * NC)]


def gather_perm(step):
    pairs = []
    for row in range(NY * NX * NC):
        core = row % NC
        if core == 0 and step == 0:
            continue
        for hi in range(2):
            for z in range(NZ):
                source = (hi ^ core) * NZ + (z + step) % NZ
                pairs.append((row * 8 + source, row * 8 + hi * NZ + z))
    return pairs


def scatter_perm(step):
    return [(to, source) for source, to in gather_perm(step)]


def place_rows():
    return [
        [(hi ^ cc) * NZ + (z + k) % NZ for cc in range(NC) for k in range(NZ)]
        for hi in range(2)
        for z in range(NZ)
    ]


def col_perm(flip, step):
    return [(hi * NZ + z, (hi ^ flip) * NZ + (z + step) % NZ) for hi in range(2) for z in range(NZ)]


def product(left, right, transposed):
    dims = (((1,), (1 if transposed else 0,)), ((), ()))
    return lax.dot_general(left, right, dims, preferred_element_type=jnp.float32)


def spans(width):
    return [(at, min(at + 256, width)) for at in range(0, width, 256)]


class Fetch:
    def __init__(self, source, target, sems, chunks=None, first_sem=0):
        self.target, self.waiting = target, {}
        for i, chunk in enumerate(chunks or [slice(None)]):
            sem = sems.at[first_sem + i]
            copy = pltpu.make_async_copy(source.at[chunk], target.at[chunk], sem)
            copy.start()
            self.waiting[str(chunk)] = copy

    def get(self, chunk=slice(None)):
        copy = self.waiting.pop(str(chunk), None)
        if copy is not None:
            copy.wait()
        return self.target


def weight_chunk(at, end, transposed):
    return (slice(at, end), slice(None)) if transposed else (slice(None), slice(at, end))


def pair_product(held, pair, at, end, transposed):
    half = held.shape[1] // 2
    chunk = weight_chunk(at, end, transposed)
    own, other = [fetch.get(chunk)[chunk] for fetch in pair]
    return product(held[:, :half], own, transposed) + product(held[:, half:], other, transposed)


def fetch_all(refs, buffers, sems):
    return [Fetch(*three) for three in zip(refs, buffers, sems)]


def fetch_weights(refs, buffers, sems, transposed):
    count = len(refs) - 1
    width = refs[0].shape[0 if transposed else 1]
    chunks = [weight_chunk(at, end, transposed) for at, end in spans(width)]
    result = []
    for i in range(count):
        result.append(Fetch(refs[i], buffers[i], sems[i], chunks))
        other, to = refs[count].at[i], buffers[count].at[i]
        result.append(Fetch(other, to, sems[count], chunks, i * len(chunks)))
    return result


def weight_copies(weights, transposed):
    steps = len(spans(weights[0].shape[0 if transposed else 1]))
    return [steps] * (len(weights) - 1) + [steps * (len(weights) - 1)]


def fill_tokens(table, blocks, acts):
    blocks = [block.get() for block in blocks]
    rows = blocks[0].shape[0]
    acts[:rows] = jnp.where(table[CORE] == 0, blocks[0][...], blocks[1][...])
    for k in range(1, NZ):
        acts[k * rows : (k + 1) * rows] = blocks[k + 1][...]


def fill_halves(table, halves, acts):
    width = halves[0].target.shape[1]
    acts[:, :width] = halves[0].get()[...]
    acts[:, width:] = halves[1].get()[...]


def first_kernel(count, transposed, fill, sources, table, *refs):
    n = sources + count + 1
    ins, (acts, *outs), (held, *more) = refs[:n], refs[n : n + 4], refs[n + 4 :]
    buffers, sems = more[:n], more[n:]
    blocks = fetch_all(ins[:sources], buffers, sems)
    weights = fetch_weights(ins[sources:], buffers[sources:], sems[sources:], transposed)
    fill(table, blocks, acts)
    for slot in range(6):
        start = pl.multiple_of(table[FIRST + slot] * PIECE, PIECE)
        held[slot * PIECE : (slot + 1) * PIECE, :] = acts[pl.ds(start, PIECE), :]
    for at, end in spans(outs[0].shape[2]):
        for which in range(count):
            pair = weights[2 * which : 2 * which + 2]
            total = pair_product(held, pair, at, end, transposed).astype(jnp.bfloat16)
            for message in range(3):
                outs[message][which, :, at:end] = total[
                    message * 2 * PIECE : (message + 1) * 2 * PIECE
                ]


def second_kernel(count, transposed, table, *refs):
    n = 1 + count + 1 + 3
    ins, outs, (held, *more) = refs[:n], refs[n : n + 4], refs[n + 4 :]
    buffers, sems = more[:n], more[n:]
    (acts,) = fetch_all(ins[:1], buffers, sems)
    weights = fetch_weights(ins[1:-3], buffers[1:-3], sems[1:-3], transposed)
    heard = fetch_all(ins[-3:], buffers[-3:], sems[-3:])
    core, x = table[CORE], table[AT_X]
    rows = acts.get()
    for slot in range(4):
        start = pl.multiple_of(table[SECOND + slot] * PIECE, PIECE)
        held[slot * PIECE : (slot + 1) * PIECE, :] = rows[pl.ds(start, PIECE), :]
    near = pl.ds(pl.multiple_of(x * PIECE, PIECE), PIECE)
    far = pl.ds(pl.multiple_of((1 - x) * PIECE, PIECE), PIECE)
    for at, end in spans(outs[0].shape[2]):
        for which in range(count):
            pair = weights[2 * which : 2 * which + 2]
            total = pair_product(held, pair, at, end, transposed)
            terms = [h.get() for h in heard]
            near1, near2, near3 = [h[which, near, at:end].astype(jnp.float32) for h in terms]
            far1, far2, far3 = [h[which, far, at:end].astype(jnp.float32) for h in terms]
            sum1 = total[:PIECE] + far1 + jnp.where(core == 1, far2 + far3, 0.0)
            high = sum1.astype(jnp.bfloat16)
            rest = sum1 - high.astype(jnp.float32)
            sum2 = jnp.where(core == 1, rest, total[PIECE : 2 * PIECE] + near2)
            outs[0][which, :, at:end] = high
            outs[1][which, :, at:end] = sum2.astype(jnp.bfloat16)
            outs[2][which, :, at:end] = (total[2 * PIECE : 3 * PIECE] + far2).astype(jnp.bfloat16)
            outs[3][which, :, at:end] = (
                total[3 * PIECE :] + near1 + jnp.where(core == 1, near2 + near3, 0.0)
            )


def join_kernel(first, second, both, sems):
    copies = [
        pltpu.make_async_copy(source, both.at[i], sems.at[i])
        for i, source in enumerate((first, second))
    ]
    for copy in copies:
        copy.start()
    for copy in copies:
        copy.wait()


def join(first, second):
    anywhere = pl.BlockSpec(memory_space=pl.ANY)
    return pl.pallas_call(
        join_kernel,
        in_specs=[anywhere] * 2,
        out_specs=anywhere,
        out_shape=shape((2, *first.shape)),
        scratch_shapes=[pltpu.SemaphoreType.DMA((2,))],
    )(first, second)


def order_kernel(table, place, every, full, own, other):
    block = NX * PIECE
    for k in range(NZ):
        for cc in range(NC):
            start = pl.multiple_of(place[cc * NZ + k] * block, block)
            for x in range(NX):
                at = ((k * NX + x) * NC + cc) * PIECE
                full[at : at + PIECE] = every[pl.ds(start + x * PIECE, PIECE), :]
        mine = pl.multiple_of(place[table[CORE] * NZ + k] * block, block)
        theirs = pl.multiple_of(place[(1 - table[CORE]) * NZ + k] * block, block)
        own[k * block : (k + 1) * block] = every[pl.ds(mine, block), :]
        other[k * block : (k + 1) * block] = every[pl.ds(theirs, block), :]


def hidden_kernel(kept, heard1, heard2, heard3, hidden, gate, up):
    for which, out in ((0, gate), (1, up)):
        out[...] = kept[which] + sum(
            h[which].astype(jnp.float32) for h in (heard1, heard2, heard3)
        )
    gate_value = gate[...]
    hidden[...] = (gate_value * jax.nn.sigmoid(gate_value) * up[...]).astype(jnp.bfloat16)


def derivative_kernel(kept, heard1, heard2, heard3, gate, up, both):
    d_hidden = kept[0] + sum(h[0].astype(jnp.float32) for h in (heard1, heard2, heard3))
    gate_value = gate[...]
    sig_gate = jax.nn.sigmoid(gate_value)
    slope = d_hidden * up[...] * sig_gate * (1.0 + gate_value * (1.0 - sig_gate))
    both[0] = slope.astype(jnp.bfloat16)
    both[1] = (d_hidden * gate_value * sig_gate).astype(jnp.bfloat16)


def pack_kernel(table, own, near1, near2, near3, first, second):
    core0 = table[CORE] == 0
    first[:, :PIECE] = own[...]
    first[:, PIECE:] = near1[...]
    second[:, :PIECE] = jnp.where(core0, near2[...], own[...])
    second[:, PIECE:] = jnp.where(core0, near3[...], near1[...])


def input_kernel(table, *refs):
    n = 10
    ins, outs, more = refs[:n], refs[n : n + 6], refs[n + 6 :]
    buffers, sems = more[:n], more[n:]
    moved = fetch_all(ins[:7], buffers, sems)
    weights = fetch_weights(ins[7:], buffers[7:], sems[7:], True)
    own, near1, near2, near3, far1, far2, far3 = [fetch.get() for fetch in moved]
    d_set, messages, kept = outs[0], outs[1:5], outs[5]

    def put(slot, value):
        start = pl.multiple_of(table[GATHER + slot] * PIECE, PIECE)
        d_set[:, pl.ds(start, PIECE), :] = value

    put(0, own[...])
    put(1, near1[...])
    put(2, far1[:, :PIECE])
    put(3, far1[:, PIECE:])
    put(4, far2[:, :PIECE])
    put(5, far2[:, PIECE:])
    core0 = table[CORE] == 0
    put(6, jnp.where(core0, near2[...], far3[:, :PIECE]))
    put(7, jnp.where(core0, near3[...], far3[:, PIECE:]))
    depth = weights[0].target.shape[0]
    block = NX * PIECE
    for side in range(2):
        for at, end in spans(depth):
            chunk = weight_chunk(at, end, True)
            gate, up = [weights[side + i].get(chunk)[chunk] for i in (0, 2)]
            total = product(d_set[0], gate, True) + product(d_set[1], up, True)
            columns = slice(side * depth + at, side * depth + end)
            kept[:, columns] = total[:block]
            for k in range(NZ):
                messages[k][:, columns] = total[k * block : (k + 1) * block].astype(jnp.bfloat16)


def call(kernel, tables, operands, out_shape, scratch=(), flops=0, fetched=None):
    vmem = pl.BlockSpec(memory_space=pltpu.VMEM)
    smem = pl.BlockSpec(memory_space=pltpu.SMEM)
    moved = sum(o.size * o.dtype.itemsize for o in [*operands, *out_shape])
    place = vmem
    if fetched is not None:
        place = pl.BlockSpec(memory_space=pltpu.HBM)
        scratch = [
            *scratch,
            *[pltpu.VMEM(o.shape, o.dtype) for o in operands],
            *[pltpu.SemaphoreType.DMA((n,)) for n in fetched],
        ]
    return pl.pallas_call(
        kernel,
        in_specs=[smem] * len(tables) + [place] * len(operands),
        out_specs=[vmem] * len(out_shape),
        out_shape=out_shape,
        scratch_shapes=scratch,
        compiler_params=pltpu.CompilerParams(vmem_limit_bytes=36 * 2**20),
        cost_estimate=pl.CostEstimate(flops=flops, bytes_accessed=moved, transcendentals=0),
    )(*tables, *operands)


def shape(dims, dtype=jnp.bfloat16):
    return jax.ShapeDtypeStruct(dims, dtype)


def first_stage(table, fill, sources, weights, transposed):
    count = len(weights) - 1
    width, depth = weights[0].shape[:: -1 if not transposed else 1]
    message = shape((count, 2 * PIECE, width))
    return call(
        functools.partial(first_kernel, count, transposed, fill, len(sources)),
        [table],
        [*sources, *weights],
        [shape((NY * NX * PIECE, 2 * depth))] + [message] * 3,
        [pltpu.VMEM((6 * PIECE, 2 * depth), jnp.bfloat16)],
        2 * 6 * PIECE * 2 * depth * width * count,
        [1] * len(sources) + weight_copies(weights, transposed),
    )


def second_stage(table, acts, weights, transposed, heard):
    count = len(weights) - 1
    width, depth = weights[0].shape[:: -1 if not transposed else 1]
    message = shape((count, PIECE, width))
    return call(
        functools.partial(second_kernel, count, transposed),
        [table],
        [acts, *weights, *heard],
        [message] * 3 + [shape((count, PIECE, width), jnp.float32)],
        [pltpu.VMEM((4 * PIECE, 2 * depth), jnp.bfloat16)],
        2 * 4 * PIECE * 2 * depth * width * count,
        [1] + weight_copies(weights, transposed) + [1] * 3,
    )


def send_first(sent):
    return (
        lax.ppermute(sent[0], "row", row_perm(over_x, over_y(1))),
        lax.ppermute(sent[1], "row", row_perm(over_x, over_y(-1))),
        lax.ppermute(sent[2], "row", row_perm(None, over_y(2))),
    )


def send_second(sent):
    return (
        lax.ppermute(sent[0], "row", row_perm(over_y(1), over_x)),
        lax.ppermute(sent[1], "row", row_perm(over_y(-1), over_x)),
        lax.ppermute(sent[2], "row", row_perm(over_y(2), None)),
    )


FIRST, SECOND, CORE, AT_X, GATHER = 0, 6, 10, 11, 12


def table_rows():
    piece = lambda y_at, x_at: (y_at % NY) * NX + x_at
    rows = []
    for y in range(NY):
        for x in range(NX):
            other = 1 - x
            pair1 = [piece(y, other), piece(y + 1, other)]
            pair2 = [piece(y - 1, other), piece(y + 2, other)]
            if other == 1:
                pair1, pair2 = pair1[::-1], pair2[::-1]
            here = piece(y, x)
            first0 = pair1 + pair2 + [here, here]
            second0 = [piece(y + 1, x), piece(y - 1, x), piece(y + 2, x), here]
            first1 = [piece(y + step, x_at) for step in (1, -1, 2) for x_at in (0, 1)]
            second1 = [piece(y, other), here, here, here]
            gather0 = [here, piece(y - 1, x), piece(y, other), piece(y - 1, other)]
            gather0 += [piece(y + 1, other), piece(y + 2, other), piece(y + 1, x), piece(y + 2, x)]
            gather1 = [here, piece(y, other)]
            gather1 += [piece(y + step, x_at) for step in (-1, 1, 2) for x_at in (x, other)]
            rows.append(first0 + second0 + [0, x] + gather0)
            rows.append(first1 + second1 + [1, x] + gather1)
    return rows


def col_first(total):
    blocks = total.reshape(NY, NX, NC, PIECE, total.shape[1])
    heard = lax.ppermute(blocks[:, :, 1].astype(jnp.bfloat16), "col", col_perm(1, 0))
    near = blocks[:, :, 0] + heard.astype(jnp.float32)
    return near[0], near[1:].astype(jnp.bfloat16)


def col_second(result, send):
    for step in range(1, NZ):
        result = result + lax.ppermute(send[step - 1], "col", col_perm(0, step)).astype(jnp.float32)
    return result.astype(jnp.bfloat16).reshape(NX * PIECE, result.shape[-1])


def body(tokens, gate_weight, up_weight, down_weight, grad_output):
    pick = lambda rows, axis: lax.dynamic_index_in_dim(
        jnp.array(rows, jnp.int32), lax.axis_index(axis), 0, keepdims=False
    )
    table, place = pick(table_rows(), "row"), pick(place_rows(), "col")
    core = table[CORE]
    flip = lambda value: lax.ppermute(value, "row", CORE_FLIP)
    after = lambda value, *others: lax.optimization_barrier((value, *others))[0]
    width, ff_width = gate_weight.shape
    half_rows = NY * NX * PIECE

    grad_every = lax.all_gather(grad_output, "col", axis=0, tiled=True)
    others = flip(join(gate_weight, up_weight))
    tok_block = jnp.concatenate([tokens, flip(tokens)], axis=1)
    tok_blocks = [lax.ppermute(tok_block, BOTH, gather_perm(step)) for step in (0, 1, 2, 3)]
    both_weights = [gate_weight, up_weight, others]
    tok_half, *sent = first_stage(
        table, fill_tokens, [tok_block, *tok_blocks], both_weights, False
    )
    heard = send_first(sent)
    down_own, _ = lax.optimization_barrier((down_weight, sent[0]))
    down_weights = [down_weight, flip(down_own)[None]]

    *sent, kept = second_stage(table, tok_half, both_weights, False, heard)
    heard = send_second(sent)
    grad_all, grad_own, grad_other = call(
        order_kernel,
        [table, place],
        [after(grad_every, sent[0])],
        [shape(grad_every.shape), shape((half_rows, width)), shape((half_rows, width))],
    )
    grad_half, *sent_d = first_stage(
        table, fill_halves, [grad_own, flip(grad_other)], down_weights, True
    )
    heard_d = send_first(sent_d)
    *heard, _ = lax.optimization_barrier((*heard, sent_d[0]))
    hidden, gate_value, up_value = call(
        hidden_kernel,
        [],
        [kept, *heard],
        [shape((PIECE, ff_width))] + [shape((PIECE, ff_width), jnp.float32)] * 2,
    )
    hidden = lax.all_gather(hidden, "row", axis=0, tiled=True)

    *sent_d, kept_d = second_stage(table, grad_half, down_weights, True, heard_d)
    piece = shape((2, PIECE, ff_width))
    (d_own,) = call(
        derivative_kernel, [], [kept_d, *send_second(sent_d), gate_value, up_value], [piece]
    )

    near = send_second([d_own] * 3)
    first, second = call(
        pack_kernel, [table], [d_own, *near], [shape((2, 2 * PIECE, ff_width))] * 2
    )
    far = send_first([first, second, first])
    dot = functools.partial(lax.dot_general, preferred_element_type=jnp.float32)
    contract_first = (((0,), (0,)), ((), ()))
    near_sum, near_send = col_first(
        jnp.dot(hidden, down_weight, preferred_element_type=jnp.float32)
    )
    tok_own, tok_other = tok_half[:, :width], flip(tok_half[:, width:])
    *far, near_send, tok_other = lax.optimization_barrier((*far, near_send, tok_other))
    block = shape((NX * PIECE, 2 * width))
    d_set, *messages, kept = call(
        input_kernel,
        [table],
        [d_own, *near, *far, *both_weights],
        [shape((2, half_rows, ff_width))] + [block] * 4 + [shape(block.shape, jnp.float32)],
        flops=2 * half_rows * 2 * width * 2 * ff_width,
        fetched=[1] * 7 + weight_copies(both_weights, True),
    )
    total = jnp.where(core == 0, kept, 0.0)
    for step in range(NZ):
        message = lax.ppermute(messages[step], BOTH, scatter_perm(step))
        total = total + message.astype(jnp.float32)
    grad_input = (total[:, :width] + flip(total[:, width:])).astype(jnp.bfloat16)
    layer_output = col_second(near_sum, after(near_send, messages[0]))

    grad_down = dot(hidden, grad_all, contract_first).astype(jnp.bfloat16)
    d_other = flip(d_set)

    def weight_gradient(which):
        total = dot(tok_own, d_set[which], contract_first)
        return (total + dot(tok_other, d_other[which], contract_first)).astype(jnp.bfloat16)

    return (layer_output, grad_input, weight_gradient(0), weight_gradient(1), grad_down)


def solution(mesh):
    placed = (P("col", "row"), P("row", "col"), P("row", "col"), P("col", "row"), P("col", "row"))
    return jax.shard_map(
        body,
        mesh=mesh,
        in_specs=placed,
        out_specs=(
            P("col", "row"),
            P("col", "row"),
            P("row", "col"),
            P("row", "col"),
            P("col", "row"),
        ),
        check_vma=False,
    )
```

time: 269 us -> 395 us (1.47); the launches traced: 266 us -> 387 us
  Pallas kernels: 12.3 us -> 162 us
  waiting for transfers between devices: 111 us -> 67.9 us
  starting transfers between devices: 85.8 us -> 108 us
  matrix products: 20.5 us -> 15.3 us
  other arithmetic: 6.38 us -> 1.8 us
    pallas_call x4 -> x10, Pallas kernels: 12.3 us -> 162 us  [the longest x1 112 us: join(): pl.pallas_call(join_kernel, in_specs=[anywhere] * 2, out_specs=anywhere,...]
    ppermute x6 -> x7, starting transfers between devices: 3.51 us -> 47 us  [body(): flip = lambda value: lax.ppermute(value, 'row', CORE_FLIP)]
    ppermute x16 -> x12, waiting for transfers between devices: 38.8 us -> 4.91 us  [the longest x4 4.7 us: body(): lax.ppermute(tok_block, BOTH, gather_perm(step))]
    all_gather x1, waiting for transfers between devices: 21.3 us -> 0.01 us  [body(): grad_every = lax.all_gather(grad_output, 'col', axis=0, tiled=True)]
    ppermute x2 -> x3, starting transfers between devices: 18.7 us -> 0.22 us  [send_first(): lax.ppermute(sent[0], 'row', row_perm(over_x, over_y(1)))]
    ppermute x16 -> x12, starting transfers between devices: 48.3 us -> 32.3 us  [the longest x4 12.7 us: body(): lax.ppermute(tok_block, BOTH, gather_perm(step))]
    ppermute x2 -> x3, starting transfers between devices: 10.6 us -> 19.6 us  [send_first(): lax.ppermute(sent[2], 'row', row_perm(None, over_y(2)))]
    ppermute x2 -> x3, waiting for transfers between devices: 9.73 us -> 18 us  [send_first(): lax.ppermute(sent[0], 'row', row_perm(over_x, over_y(1)))]
  transfers between devices with their start and end apart: 36 -> 39, of which waited for: 22 -> 17; matrix products, arithmetic and copies ran while one was open for 8% -> 3% of each run, Pallas kernels for 1% -> 9%
where the time goes in v3:
time: 395 us; the launch traced here: 387 us
  Pallas kernels  162 us (41%)
  starting transfers between devices  108 us (27%)
  waiting for transfers between devices  67.9 us (17%)
  local copies, waits for them, and re-layouts  17.9 us (5%)
  matrix products  15.3 us (4%)
  between operations  15.1 us (4%)
    pallas_call x1, Pallas kernels, join(): pl.pallas_call(join_kernel, in_specs=[anywhere] * 2, out_specs=anywhere,...  112 us
    pallas_call x9, Pallas kernels, call(): pl.pallas_call(kernel, in_specs=[smem] * len(tables) + [place] * len(oper...  49.4 us
    ppermute x7, starting transfers between devices, body(): flip = lambda value: lax.ppermute(value, 'row', CORE_FLIP)  47 us
    ppermute x3, starting transfers between devices, send_first(): lax.ppermute(sent[2], 'row', row_perm(None, over_y(2)))  19.6 us
    ppermute x3, waiting for transfers between devices, send_first(): lax.ppermute(sent[0], 'row', row_perm(over_x, over_y(1)))  18 us
    unnamed x63, local copies, waits for them, and re-layouts  15.7 us
    ppermute x4, starting transfers between devices, body(): lax.ppermute(tok_block, BOTH, gather_perm(step))  12.7 us
    ppermute x3, waiting for transfers between devices, send_second(): lax.ppermute(sent[0], 'row', row_perm(over_y(1), over_x))  11.7 us
  transfers between devices with their start and end apart: 39, of which 17 were waited for; matrix products, arithmetic and copies ran while one was open for 3% of the time, Pallas kernels for 9%

profile of v3, /device:TPU:17, one launch (start us, length us, event | category | flops | bytes accessed | tf_op | source)
XLA Modules:
  0.0 387.4 jit_solution(8697202183792596291)
XLA Ops:
  7.2 112.3 %shard_map.110 = bf16[2,512,1792]{2,1,0:T(8,128)(2,1)} custom-call(bf16[512,1792]{1,0:T(8,128)(2,1)} %refs_7_.1, bf16[512,1792]{1,0:T(8,128)(2,1)} %refs_8_.1), custom_call_target="tpu_custom_call" | custom-call | tf_op jit(solution)/shard_map/pallas_call | solution.py:207
  120.4 6.0 %collective-permute-done = bf16[128,512]{1,0:T(8,128)(2,1)S(1)} collective-permute-done((bf16[128,512]{1,0:T(8,128)(2,1)S(1)}, bf16[128,512]{1,0:T(8,128)(2,1)S(1)}, u32[]{:S(2)}, u32[]{:S(2)}) %collective-permute-start) | collective-permute-done | bytes 131104 | tf_op jit(solution)/shard_map/ppermute | solution.py:410
  126.4 4.2 %collective-permute-start.4 = (bf16[128,1024]{1,0:T(8,128)(2,1)S(1)}, bf16[128,1024]{1,0:T(8,128)(2,1)S(1)}, u32[]{:S(2)}, u32[]{:S(2)}) collective-permute-start(bf16[128,1024]{1,0:T(8,128)(2,1)S(1)} %constant_dynamic-update-slice_fusion.refs_0_), channel_id=1, source_target_pairs={{3,0},{0,1},{1,2},{2,3},{7,4},{4,5},{5,6},{6,7},{15,8},{12,9},{13,... | collective-permute-start | bytes 786440 | tf_op jit(solution)/shard_map/ppermute | solution.py:418
  151.1 11.5 %shard_map.111 = (bf16[512,1024]{1,0:T(8,128)(2,1)S(1)}, bf16[2,128,1792]{2,1,0:T(8,128)(2,1)}, bf16[2,128,1792]{2,1,0:T(8,128)(2,1)}, bf16[2,128,1792]{2,1,0:T(8,128)(2,1)}) custom-call(s32[20]{0:T(128)S(1)} %get-tuple-element.91.table, bf16[128,1024]{1,0:T(8,128)(2,1)S(1)} %constant_dynamic-update-slice_fusion.refs_0_, bf16[128,1024]{1,0:T(8,128)(2,1)S(1)} %copy-done.28, ...), custom_call_target="tpu_custom_call" | custom-call | flops 2818572288 | bytes 12451840 | tf_op jit(solution)/shard_map/pallas_call | solution.py:303
  163.2 4.5 %collective-permute-start.8 = (bf16[2,128,1792]{2,1,0:T(8,128)(2,1)}, bf16[2,128,1792]{2,1,0:T(8,128)(2,1)}, u32[]{:S(2)}, u32[]{:S(2)}) collective-permute-start(bf16[2,128,1792]{2,1,0:T(8,128)(2,1)} %get-tuple-element.49), channel_id=1, source_target_pairs={{8,72},{24,88},{40,104},{56,120},{72,8},{88,24},{104,40},{120,56},... | collective-permute-start | bytes 2752520 | tf_op jit(solution)/shard_map/ppermute | solution.py:352
  168.5 7.4 %collective-permute-done.7.refs_5_ = bf16[2,128,1792]{2,1,0:T(8,128)(2,1)} collective-permute-done((bf16[2,128,1792]{2,1,0:T(8,128)(2,1)}, bf16[2,128,1792]{2,1,0:T(8,128)(2,1)}, u32[]{:S(2)}, u32[]{:S(2)}) %collective-permute-start.7) | collective-permute-done | bytes 917536 | tf_op jit(solution)/shard_map/ppermute | solution.py:351
  179.4 9.8 %collective-permute-done.6.refs_4_ = bf16[2,128,1792]{2,1,0:T(8,128)(2,1)} collective-permute-done((bf16[2,128,1792]{2,1,0:T(8,128)(2,1)}, bf16[2,128,1792]{2,1,0:T(8,128)(2,1)}, u32[]{:S(2)}, u32[]{:S(2)}) %collective-permute-start.6) | collective-permute-done | bytes 917536 | tf_op jit(solution)/shard_map/ppermute | solution.py:350
  190.7 10.7 %shard_map.112 = (bf16[2,64,1792]{2,1,0:T(8,128)(2,1)}, bf16[2,64,1792]{2,1,0:T(8,128)(2,1)}, bf16[2,64,1792]{2,1,0:T(8,128)(2,1)}, f32[2,64,1792]{2,1,0:T(8,128)S(1)}) custom-call(s32[20]{0:T(128)S(1)} %get-tuple-element.91.table, bf16[512,1024]{1,0:T(8,128)(2,1)S(1)} %get-tuple-element.46.refs_0_, bf16[512,1792]{1,0:T(8,128)(2,1)S(1)} %copy-done, ...), custom_call_target="tpu_custom_call" | custom-call | flops 1879048192 | bytes 13434880 | tf_op jit(solution)/shard_map/pallas_call | solution.py:303
  210.7 5.8 %shard_map.114 = (bf16[512,1024]{1,0:T(8,128)(2,1)S(1)}, bf16[1,128,1792]{2,1,0:T(8,128)(2,1)S(1)}, bf16[1,128,1792]{2,1,0:T(8,128)(2,1)S(1)}, bf16[1,128,1792]{2,1,0:T(8,128)(2,1)S(1)}) custom-call(s32[20]{0:T(128)S(1)} %get-tuple-element.91.table, bf16[512,512]{1,0:T(8,128)(2,1)S(1)} %get-tuple-element.55.refs_0_, ...), custom_call_target="tpu_custom_call" | custom-call | flops 1409286144 | bytes 7143424 | tf_op jit(solution)/shard_map/pallas_call | solution.py:303
  217.5 3.7 collective-permute-done.9.heard1
  224.1 4.5 %collective-permute-start.17 = (bf16[1,128,1792]{2,1,0:T(8,128)(2,1)}, bf16[1,128,1792]{2,1,0:T(8,128)(2,1)S(1)}, u32[]{:S(2)}, u32[]{:S(2)}) collective-permute-start(bf16[1,128,1792]{2,1,0:T(8,128)(2,1)} %copy-done.21), channel_id=1, source_target_pairs={{8,72},{24,88},{40,104},{56,120},{72,8},{88,24},{104,40},{120,56},... | collective-permute-start | bytes 1376264 | tf_op jit(solution)/shard_map/ppermute | solution.py:352
  231.5 3.7 collective-permute-done.17.refs_5_
  235.2 8.2 %collective-permute-done.15.refs_3_ = bf16[1,128,1792]{2,1,0:T(8,128)(2,1)S(1)} collective-permute-done((bf16[1,128,1792]{2,1,0:T(8,128)(2,1)S(1)}, bf16[1,128,1792]{2,1,0:T(8,128)(2,1)S(1)}, u32[]{:S(2)}, u32[]{:S(2)}) %collective-permute-start.15) | collective-permute-done | bytes 458784 | tf_op jit(solution)/shard_map/ppermute | solution.py:350
  244.6 5.0 %shard_map.116 = (bf16[1,64,1792]{2,1,0:T(8,128)(2,1)S(1)}, bf16[1,64,1792]{2,1,0:T(8,128)(2,1)S(1)}, bf16[1,64,1792]{2,1,0:T(8,128)(2,1)S(1)}, f32[1,64,1792]{2,1,0:T(8,128)S(1)}) custom-call(s32[20]{0:T(128)S(1)} %get-tuple-element.91.table, bf16[512,1024]{1,0:T(8,128)(2,1)S(1)} %copy-done.5, bf16[1792,512]{1,0:T(8,128)(2,1)} %refs_1_.3, ...), custom_call_target="tpu_custom_call" | custom-call | flops 939524096 | bytes 7241728 | tf_op jit(solution)/shard_map/pallas_call | solution.py:303
  259.9 6.2 %collective-permute-done.22.near2.refs_2_ = bf16[2,64,1792]{2,1,0:T(8,128)(2,1)S(1)} collective-permute-done((bf16[2,64,1792]{2,1,0:T(8,128)(2,1)S(1)}, bf16[2,64,1792]{2,1,0:T(8,128)(2,1)S(1)}, u32[]{:S(2)}, u32[]{:S(2)}) %collective-permute-start.22) | collective-permute-done | bytes 458784 | tf_op jit(solution)/shard_map/ppermute | solution.py:359
  266.1 4.9 %collective-permute-done.21.near1.refs_1_ = bf16[2,64,1792]{2,1,0:T(8,128)(2,1)S(1)} collective-permute-done((bf16[2,64,1792]{2,1,0:T(8,128)(2,1)S(1)}, bf16[2,64,1792]{2,1,0:T(8,128)(2,1)S(1)}, u32[]{:S(2)}, u32[]{:S(2)}) %collective-permute-start.21) | collective-permute-done | bytes 458784 | tf_op jit(solution)/shard_map/ppermute | solution.py:358
  273.7 10.6 %collective-permute-start.26 = (bf16[2,128,1792]{2,1,0:T(8,128)(2,1)}, bf16[2,128,1792]{2,1,0:T(8,128)(2,1)}, u32[]{:S(2)}, u32[]{:S(2)}) collective-permute-start(bf16[2,128,1792]{2,1,0:T(8,128)(2,1)} %get-tuple-element.72), channel_id=1, source_target_pairs={{8,72},{24,88},{40,104},{56,120},{72,8},{88,24},{104,40},{120,56},... | collective-permute-start | bytes 2752520 | tf_op jit(solution)/shard_map/ppermute | solution.py:352
  285.8 4.7 %fusion.16 = f32[1024,512]{1,0:T(8,128)S(1)} fusion(bf16[1024,1792]{1,0:T(8,128)(2,1)} %all-gather.5.cloned.1.call-done, bf16[1792,512]{1,0:T(8,128)(2,1)} %refs_1_.3), kind=kOutput, calls=%fused_computation.34 | convolution fusion | flops 1879048192 | bytes 7602176 | tf_op jit(solution)/shard_map/dot_general | solution.py:462
  293.5 20.1 %collective-permute-start.27 = (bf16[512,512]{1,0:T(8,128)(2,1)S(1)}, bf16[512,512]{1,0:T(8,128)(2,1)S(1)}, u32[]{:S(2)}, u32[]{:S(2)}) collective-permute-start(bf16[512,512]{1,0:T(8,128)(2,1)S(1)} %slice.55), channel_id=1, source_target_pairs={{0,8},{8,0},{16,24},{24,16},{32,40},{40,32},{48,56},{56,48},{64,72... | collective-permute-start | bytes 1572872 | tf_op jit(solution)/shard_map/ppermute | solution.py:410
  315.2 12.3 %shard_map.119 = (bf16[2,512,1792]{2,1,0:T(8,128)(2,1)S(1)}, bf16[128,1024]{1,0:T(8,128)(2,1)S(1)}, bf16[128,1024]{1,0:T(8,128)(2,1)S(1)}, bf16[128,1024]{1,0:T(...) custom-call(s32[20]{0:T(128)S(1)} %get-tuple-element.91.table, ...), custom_call_target="tpu_custom_call" | custom-call | flops 3758096384 | bytes 17170432 | tf_op jit(solution)/shard_map/pallas_call | solution.py:303
  327.5 20.6 %collective-permute-start.36 = (bf16[2,512,1792]{2,1,0:T(8,128)(2,1)S(1)}, bf16[2,512,1792]{2,1,0:T(8,128)(2,1)S(1)}, u32[]{:S(2)}, u32[]{:S(2)}) collective-permute-start(bf16[2,512,1792]{2,1,0:T(8,128)(2,1)S(1)} %get-tuple-element.84), channel_id=1, source_target_pairs={{0,8},{8,0},{16,24},{24,16},{32,40},{40,32},{48,56},{56,48},{64,72... | collective-permute-start | bytes 11010056 | tf_op jit(solution)/shard_map/ppermute | solution.py:410
  348.2 5.1 %collective-permute-start.34 = (bf16[128,1024]{1,0:T(8,128)(2,1)S(1)}, bf16[128,1024]{1,0:T(8,128)(2,1)S(1)}, u32[]{:S(2)}, u32[]{:S(2)}) collective-permute-start(bf16[128,1024]{1,0:T(8,128)(2,1)S(1)} %get-tuple-element.83), channel_id=1, source_target_pairs={{0,3},{1,0},{2,1},{3,2},{4,7},{5,4},{6,5},{7,6},{8,15},{9,12},{10,... | collective-permute-start | bytes 786440 | tf_op jit(solution)/shard_map/ppermute | solution.py:477
  353.2 4.9 %collective-permute-start.31 = (bf16[128,1024]{1,0:T(8,128)(2,1)S(1)}, bf16[128,1024]{1,0:T(8,128)(2,1)S(1)}, u32[]{:S(2)}, u32[]{:S(2)}) collective-permute-start(bf16[128,1024]{1,0:T(8,128)(2,1)S(1)} %get-tuple-element.78), channel_id=1, source_target_pairs={{8,12},{9,13},{10,14},{11,15},{12,8},{13,9},{14,10},{15,11},{24,28... | collective-permute-start | bytes 786440 | tf_op jit(solution)/shard_map/ppermute | solution.py:477
  360.3 5.4 %collective-permute-start.30 = (bf16[2,64,512]{2,1,0:T(8,128)(2,1)S(1)}, bf16[2,64,512]{2,1,0:T(8,128)(2,1)S(1)}, u32[]{:S(2)}, u32[]{:S(2)}) collective-permute-start(bf16[2,64,512]{2,1,0:T(8,128)(2,1)S(1)} %get-tuple-element.88), channel_id=1, source_target_pairs={{0,3},{1,0},{2,1},{3,2},{4,7},{5,4},{6,5},{7,6},{8,11},{9,8},{10,9... | collective-permute-start | bytes 393224 | tf_op jit(solution)/shard_map/ppermute | solution.py:400
  (148 shorter events, 80.4 us)
Async XLA Ops:
  7.2 195.2 %all-gather.3.cloned.1.call-start = ((), (), s32[]{:S(2)}) async-start(), calls=%async_computation | async-start | bytes 1179648 | tf_op jit(solution)/shard_map/all_gather | solution.py:415
  119.5 27.2 %collective-permute-start.5 = (bf16[2,512,1792]{2,1,0:T(8,128)(2,1)}, bf16[2,512,1792]{2,1,0:T(8,128)(2,1)}, u32[]{:S(2)}, u32[]{:S(2)}) collective-permute-start(bf16[2,512,1792]{2,1,0:T(8,128)(2,1)} %shard_map.110), channel_id=1, source_target_pairs={{0,8},{8,0},{16,24},{24,16},{32,40},{40,32},{48,56},{56,48},{64,72... | collective-permute-start | bytes 11010056 | tf_op jit(solution)/shard_map/ppermute | solution.py:410
  126.4 13.5 %collective-permute-start.4 = (bf16[128,1024]{1,0:T(8,128)(2,1)S(1)}, bf16[128,1024]{1,0:T(8,128)(2,1)S(1)}, u32[]{:S(2)}, u32[]{:S(2)}) collective-permute-start(bf16[128,1024]{1,0:T(8,128)(2,1)S(1)} %constant_dynamic-update-slice_fusion.refs_0_), channel_id=1, source_target_pairs={{3,0},{0,1},{1,2},{2,3},{7,4},{4,5},{5,6},{6,7},{15,8},{12,9},{13,... | collective-permute-start | bytes 786440 | tf_op jit(solution)/shard_map/ppermute | solution.py:418
  139.2 146.6 %all-gather.5.cloned.1.call-start = ((), (), s32[]{:S(2)}) async-start(), calls=%async_computation.1 | async-start | bytes 3899392 | tf_op jit(solution)/shard_map/all_gather | solution.py:446
  162.6 48.0 %collective-permute-start.13 = (bf16[1792,512]{1,0:T(8,128)(2,1)}, bf16[1792,512]{1,0:T(8,128)(2,1)}, u32[]{:S(2)}, u32[]{:S(2)}) collective-permute-start(bf16[1792,512]{1,0:T(8,128)(2,1)} %refs_1_.3), channel_id=1, source_target_pairs={{0,8},{8,0},{16,24},{24,16},{32,40},{40,32},{48,56},{56,48},{64,72... | collective-permute-start | bytes 5505032 | tf_op jit(solution)/shard_map/ppermute | solution.py:410
  163.0 12.9 %collective-permute-start.7 = (bf16[2,128,1792]{2,1,0:T(8,128)(2,1)}, bf16[2,128,1792]{2,1,0:T(8,128)(2,1)}, u32[]{:S(2)}, u32[]{:S(2)}) collective-permute-start(bf16[2,128,1792]{2,1,0:T(8,128)(2,1)} %get-tuple-element.48), channel_id=1, source_target_pairs={{0,16},{8,104},{16,0},{24,120},{32,48},{40,8},{48,32},{56,24},{64,... | collective-permute-start | bytes 2752520 | tf_op jit(solution)/shard_map/ppermute | solution.py:351
  163.2 16.3 %collective-permute-start.8 = (bf16[2,128,1792]{2,1,0:T(8,128)(2,1)}, bf16[2,128,1792]{2,1,0:T(8,128)(2,1)}, u32[]{:S(2)}, u32[]{:S(2)}) collective-permute-start(bf16[2,128,1792]{2,1,0:T(8,128)(2,1)} %get-tuple-element.49), channel_id=1, source_target_pairs={{8,72},{24,88},{40,104},{56,120},{72,8},{88,24},{104,40},{120,56},... | collective-permute-start | bytes 2752520 | tf_op jit(solution)/shard_map/ppermute | solution.py:352
  167.7 21.5 %collective-permute-start.6 = (bf16[2,128,1792]{2,1,0:T(8,128)(2,1)}, bf16[2,128,1792]{2,1,0:T(8,128)(2,1)}, u32[]{:S(2)}, u32[]{:S(2)}) collective-permute-start(bf16[2,128,1792]{2,1,0:T(8,128)(2,1)} %get-tuple-element.47), channel_id=1, source_target_pairs={{0,16},{8,40},{16,0},{24,56},{32,48},{40,72},{48,32},{56,88},{64,8... | collective-permute-start | bytes 2752520 | tf_op jit(solution)/shard_map/ppermute | solution.py:350
  210.2 11.0 %collective-permute-start.9 = (bf16[2,64,1792]{2,1,0:T(8,128)(2,1)}, bf16[2,64,1792]{2,1,0:T(8,128)(2,1)S(1)}, u32[]{:S(2)}, u32[]{:S(2)}) collective-permute-start(bf16[2,64,1792]{2,1,0:T(8,128)(2,1)} %get-tuple-element.51), channel_id=1, source_target_pairs={{0,32},{8,24},{16,48},{24,8},{32,64},{40,56},{48,80},{56,40},{64,9... | collective-permute-start | bytes 1376264 | tf_op jit(solution)/shard_map/ppermute | solution.py:358
  224.1 11.0 %collective-permute-start.17 = (bf16[1,128,1792]{2,1,0:T(8,128)(2,1)}, bf16[1,128,1792]{2,1,0:T(8,128)(2,1)S(1)}, u32[]{:S(2)}, u32[]{:S(2)}) collective-permute-start(bf16[1,128,1792]{2,1,0:T(8,128)(2,1)} %copy-done.21), channel_id=1, source_target_pairs={{8,72},{24,88},{40,104},{56,120},{72,8},{88,24},{104,40},{120,56},... | collective-permute-start | bytes 1376264 | tf_op jit(solution)/shard_map/ppermute | solution.py:352
  228.7 14.7 %collective-permute-start.15 = (bf16[1,128,1792]{2,1,0:T(8,128)(2,1)S(1)}, bf16[1,128,1792]{2,1,0:T(8,128)(2,1)S(1)}, u32[]{:S(2)}, u32[]{:S(2)}) collective-permute-start(bf16[1,128,1792]{2,1,0:T(8,128)(2,1)S(1)} %get-tuple-element.58), channel_id=1, source_target_pairs={{0,16},{8,40},{16,0},{24,56},{32,48},{40,72},{48,32},{56,88},{64,8... | collective-permute-start | bytes 1376264 | tf_op jit(solution)/shard_map/ppermute | solution.py:350
  259.5 11.5 %collective-permute-start.21 = (bf16[2,64,1792]{2,1,0:T(8,128)(2,1)S(1)}, bf16[2,64,1792]{2,1,0:T(8,128)(2,1)S(1)}, u32[]{:S(2)}, u32[]{:S(2)}) collective-permute-start(bf16[2,64,1792]{2,1,0:T(8,128)(2,1)S(1)} %shard_map.117.own.refs_0_), channel_id=1, source_target_pairs={{0,32},{8,24},{16,48},{24,8},{32,64},{40,56},{48,80},{56,40},{64,9... | collective-permute-start | bytes 1376264 | tf_op jit(solution)/shard_map/ppermute | solution.py:358
  273.7 41.5 %collective-permute-start.26 = (bf16[2,128,1792]{2,1,0:T(8,128)(2,1)}, bf16[2,128,1792]{2,1,0:T(8,128)(2,1)}, u32[]{:S(2)}, u32[]{:S(2)}) collective-permute-start(bf16[2,128,1792]{2,1,0:T(8,128)(2,1)} %get-tuple-element.72), channel_id=1, source_target_pairs={{8,72},{24,88},{40,104},{56,120},{72,8},{88,24},{104,40},{120,56},... | collective-permute-start | bytes 2752520 | tf_op jit(solution)/shard_map/ppermute | solution.py:352
  284.2 31.0 %collective-permute-start.24 = (bf16[2,128,1792]{2,1,0:T(8,128)(2,1)}, bf16[2,128,1792]{2,1,0:T(8,128)(2,1)}, u32[]{:S(2)}, u32[]{:S(2)}) collective-permute-start(bf16[2,128,1792]{2,1,0:T(8,128)(2,1)} %get-tuple-element.72), channel_id=1, source_target_pairs={{0,16},{8,40},{16,0},{24,56},{32,48},{40,72},{48,32},{56,88},{64,8... | collective-permute-start | bytes 2752520 | tf_op jit(solution)/shard_map/ppermute | solution.py:350
  284.3 30.9 %collective-permute-start.25 = (bf16[2,128,1792]{2,1,0:T(8,128)(2,1)}, bf16[2,128,1792]{2,1,0:T(8,128)(2,1)}, u32[]{:S(2)}, u32[]{:S(2)}) collective-permute-start(bf16[2,128,1792]{2,1,0:T(8,128)(2,1)} %get-tuple-element.73), channel_id=1, source_target_pairs={{0,16},{8,104},{16,0},{24,120},{32,48},{40,8},{48,32},{56,24},{64,... | collective-permute-start | bytes 2752520 | tf_op jit(solution)/shard_map/ppermute | solution.py:351
  290.6 23.1 %collective-permute-start.14 = (bf16[4,2,64,512]{3,2,1,0:T(8,128)(2,1)S(1)}, bf16[4,2,64,512]{3,2,1,0:T(8,128)(2,1)S(1)}, u32[]{:S(2)}, u32[]{:S(2)}) collective-permute-start(bf16[4,2,64,512]{3,2,1,0:T(8,128)(2,1)S(1)} %fusion.7), channel_id=1, source_target_pairs={{0,4},{1,5},{2,6},{3,7},{4,0},{5,1},{6,2},{7,3},{8,12},{9,13},{10,... | collective-permute-start | bytes 1572872 | tf_op jit(solution)/shard_map/ppermute | solution.py:393
  293.5 21.7 %collective-permute-start.27 = (bf16[512,512]{1,0:T(8,128)(2,1)S(1)}, bf16[512,512]{1,0:T(8,128)(2,1)S(1)}, u32[]{:S(2)}, u32[]{:S(2)}) collective-permute-start(bf16[512,512]{1,0:T(8,128)(2,1)S(1)} %slice.55), channel_id=1, source_target_pairs={{0,8},{8,0},{16,24},{24,16},{32,40},{40,32},{48,56},{56,48},{64,72... | collective-permute-start | bytes 1572872 | tf_op jit(solution)/shard_map/ppermute | solution.py:410
  327.5 45.7 %collective-permute-start.36 = (bf16[2,512,1792]{2,1,0:T(8,128)(2,1)S(1)}, bf16[2,512,1792]{2,1,0:T(8,128)(2,1)S(1)}, u32[]{:S(2)}, u32[]{:S(2)}) collective-permute-start(bf16[2,512,1792]{2,1,0:T(8,128)(2,1)S(1)} %get-tuple-element.84), channel_id=1, source_target_pairs={{0,8},{8,0},{16,24},{24,16},{32,40},{40,32},{48,56},{56,48},{64,72... | collective-permute-start | bytes 11010056 | tf_op jit(solution)/shard_map/ppermute | solution.py:410
  348.2 11.3 %collective-permute-start.32 = (bf16[128,1024]{1,0:T(8,128)(2,1)S(1)}, bf16[128,1024]{1,0:T(8,128)(2,1)S(1)}, u32[]{:S(2)}, u32[]{:S(2)}) collective-permute-start(bf16[128,1024]{1,0:T(8,128)(2,1)S(1)} %get-tuple-element.81), channel_id=1, source_target_pairs={{0,1},{1,2},{2,3},{3,0},{4,5},{5,6},{6,7},{7,4},{8,13},{9,14},{10,... | collective-permute-start | bytes 786440 | tf_op jit(solution)/shard_map/ppermute | solution.py:477
  348.2 12.1 %collective-permute-start.33 = (bf16[128,1024]{1,0:T(8,128)(2,1)S(1)}, bf16[128,1024]{1,0:T(8,128)(2,1)S(1)}, u32[]{:S(2)}, u32[]{:S(2)}) collective-permute-start(bf16[128,1024]{1,0:T(8,128)(2,1)S(1)} %get-tuple-element.82), channel_id=1, source_target_pairs={{0,2},{1,3},{2,0},{3,1},{4,6},{5,7},{6,4},{7,5},{8,14},{9,15},{10,... | collective-permute-start | bytes 786440 | tf_op jit(solution)/shard_map/ppermute | solution.py:477
  348.2 17.5 %collective-permute-start.34 = (bf16[128,1024]{1,0:T(8,128)(2,1)S(1)}, bf16[128,1024]{1,0:T(8,128)(2,1)S(1)}, u32[]{:S(2)}, u32[]{:S(2)}) collective-permute-start(bf16[128,1024]{1,0:T(8,128)(2,1)S(1)} %get-tuple-element.83), channel_id=1, source_target_pairs={{0,3},{1,0},{2,1},{3,2},{4,7},{5,4},{6,5},{7,6},{8,15},{9,12},{10,... | collective-permute-start | bytes 786440 | tf_op jit(solution)/shard_map/ppermute | solution.py:477
  353.2 13.1 %collective-permute-start.31 = (bf16[128,1024]{1,0:T(8,128)(2,1)S(1)}, bf16[128,1024]{1,0:T(8,128)(2,1)S(1)}, u32[]{:S(2)}, u32[]{:S(2)}) collective-permute-start(bf16[128,1024]{1,0:T(8,128)(2,1)S(1)} %get-tuple-element.78), channel_id=1, source_target_pairs={{8,12},{9,13},{10,14},{11,15},{12,8},{13,9},{14,10},{15,11},{24,28... | collective-permute-start | bytes 786440 | tf_op jit(solution)/shard_map/ppermute | solution.py:477
  359.4 12.4 %collective-permute-start.28 = (bf16[2,64,512]{2,1,0:T(8,128)(2,1)S(1)}, bf16[2,64,512]{2,1,0:T(8,128)(2,1)S(1)}, u32[]{:S(2)}, u32[]{:S(2)}) collective-permute-start(bf16[2,64,512]{2,1,0:T(8,128)(2,1)S(1)} %get-tuple-element.87), channel_id=1, source_target_pairs={{0,1},{1,2},{2,3},{3,0},{4,5},{5,6},{6,7},{7,4},{8,9},{9,10},{10,1... | collective-permute-start | bytes 393224 | tf_op jit(solution)/shard_map/ppermute | solution.py:400
  360.3 11.6 %collective-permute-start.30 = (bf16[2,64,512]{2,1,0:T(8,128)(2,1)S(1)}, bf16[2,64,512]{2,1,0:T(8,128)(2,1)S(1)}, u32[]{:S(2)}, u32[]{:S(2)}) collective-permute-start(bf16[2,64,512]{2,1,0:T(8,128)(2,1)S(1)} %get-tuple-element.88), channel_id=1, source_target_pairs={{0,3},{1,0},{2,1},{3,2},{4,7},{5,4},{6,5},{7,6},{8,11},{9,8},{10,9... | collective-permute-start | bytes 393224 | tf_op jit(solution)/shard_map/ppermute | solution.py:400
  (46 other events, 642.2 us)
Sparse Core Ops, SparseCore 0:
  139.3 46.8 all-gather.2
  224.0 42.6 all-gather.4

commit v4 on v2

v4 whole, which is shorter than its diff:
```python
import functools

import jax
import jax.numpy as jnp
from jax import lax
from jax.experimental import pallas as pl
from jax.experimental.pallas import tpu as pltpu
from jax.sharding import PartitionSpec as P

NY, NX, NC, NZ = 4, 2, 2, 4
PIECE = 64
BOTH = ("row", "col")


def row_at(y, x, core):
    return ((y % NY) * NX + x) * NC + core


def row_perm(core0, core1):
    pairs = []
    for y in range(NY):
        for x in range(NX):
            for core, move in ((0, core0), (1, core1)):
                if move is not None:
                    to_y, to_x = move(y, x)
                    pairs.append((row_at(y, x, core), row_at(to_y, to_x, core)))
    return pairs


def over_x(y, x):
    return y, 1 - x


def over_y(step):
    return lambda y, x: (y + step, x)


CORE_FLIP = [(i, i ^ 1) for i in range(NY * NX * NC)]


def gather_perm(step):
    pairs = []
    for row in range(NY * NX * NC):
        core = row % NC
        if core == 0 and step == 0:
            continue
        for hi in range(2):
            for z in range(NZ):
                source = (hi ^ core) * NZ + (z + step) % NZ
                pairs.append((row * 8 + source, row * 8 + hi * NZ + z))
    return pairs


def scatter_perm(step):
    return [(to, source) for source, to in gather_perm(step)]


def col_perm(flip, step):
    return [(hi * NZ + z, (hi ^ flip) * NZ + (z + step) % NZ) for hi in range(2) for z in range(NZ)]


def product(left, right, transposed):
    dims = (((1,), (1 if transposed else 0,)), ((), ()))
    return lax.dot_general(left, right, dims, preferred_element_type=jnp.float32)


def spans(width):
    return [(at, min(at + 256, width)) for at in range(0, width, 256)]


class Load:
    def __init__(self, source, target, sem):
        self.target, self.copy = target, pltpu.make_async_copy(source, target, sem)
        self.copy.start()

    def get(self):
        if self.copy is not None:
            self.copy.wait()
            self.copy = None
        return self.target


class Store:
    def __init__(self, source, target, sem):
        self.ref, self.copy, self.sent = source, pltpu.make_async_copy(source, target, sem), False

    def send(self):
        self.copy.start()
        self.sent = True


class OfOther:
    def __init__(self, value):
        self.value = value


def call(kernel, tables, operands, out_shape, scratch=()):
    parts = [shape(o.value.shape[1:]) if isinstance(o, OfOther) else o for o in operands]
    operands = [o.value if isinstance(o, OfOther) else o for o in operands]
    any_space = pl.BlockSpec(memory_space=pl.ANY)
    smem = pl.BlockSpec(memory_space=pltpu.SMEM)
    n_tables, n_in, n_out, n_own = len(tables), len(operands), len(out_shape), len(scratch)

    def run(*refs):
        refs = list(refs)
        take = lambda count: [refs.pop(0) for _ in range(count)]
        table_refs, ins, outs, own = take(n_tables), take(n_in), take(n_out), take(n_own)
        in_buffers, out_buffers, (in_sems, out_sems) = take(n_in), take(n_out), take(2)
        ins = [
            ref.at[1 - table_refs[0][CORE]] if len(ref.shape) > len(to.shape) else ref
            for ref, to in zip(ins, in_buffers)
        ]
        loads = [Load(ins[i], in_buffers[i], in_sems.at[i]) for i in range(n_in)]
        stores = [Store(out_buffers[i], outs[i], out_sems.at[i]) for i in range(n_out)]
        kernel(table_refs, loads, stores, *own)
        for load in loads:
            load.get()
        for store in stores:
            if not store.sent:
                store.send()
        for store in stores:
            store.copy.wait()

    return pl.pallas_call(
        run,
        in_specs=[smem] * n_tables + [any_space] * n_in,
        out_specs=[any_space] * n_out,
        out_shape=out_shape,
        scratch_shapes=[
            *scratch,
            *[pltpu.VMEM(o.shape, o.dtype) for o in [*parts, *out_shape]],
            pltpu.SemaphoreType.DMA((n_in,)),
            pltpu.SemaphoreType.DMA((n_out,)),
        ],
        compiler_params=pltpu.CompilerParams(vmem_limit_bytes=56 * 2**20),
        cost_estimate=pl.CostEstimate(flops=1, bytes_accessed=1, transcendentals=0),
    )(*tables, *operands)


def pair_product(held, pair, at, end, transposed):
    half = held.shape[1] // 2
    chunk = (slice(at, end), slice(None)) if transposed else (slice(None), slice(at, end))
    own, other = [load.get()[chunk] for load in pair]
    return product(held[:, :half], own, transposed) + product(held[:, half:], other, transposed)


def first_kernel(tables, loads, stores, tok_held, grad_held):
    (table,) = tables
    block, *blocks = [load.get() for load in loads[:-6]]
    weights, messages, halves = loads[-6:], stores[2:], [store.ref for store in stores[:2]]
    rows = block.shape[1]
    for i, (acts, held) in enumerate(zip(halves, (tok_held, grad_held))):
        acts[:rows] = jnp.where(table[CORE] == 0, block[i], blocks[0][i])
        for k in range(1, NZ):
            acts[k * rows : (k + 1) * rows] = blocks[k][i]
        stores[i].send()
        for slot in range(6):
            start = pl.multiple_of(table[FIRST + slot] * PIECE, PIECE)
            held[slot * PIECE : (slot + 1) * PIECE, :] = acts[pl.ds(start, PIECE), :]
    for which in range(3):
        held, transposed = ((tok_held, False), (grad_held, True))[which // 2]
        pair = weights[2 * which : 2 * which + 2]
        for at, end in spans(messages[0].ref.shape[2]):
            total = pair_product(held, pair, at, end, transposed).astype(jnp.bfloat16)
            for i, message in enumerate(messages):
                message.ref[which, :, at:end] = total[i * 2 * PIECE : (i + 1) * 2 * PIECE]


def second_kernel(tables, loads, stores, tok_held, grad_held):
    (table,) = tables
    weights, heard = loads[2:8], loads[8:]
    outs = [store.ref for store in stores]
    core, x = table[CORE], table[AT_X]
    near = pl.ds(pl.multiple_of(x * PIECE, PIECE), PIECE)
    far = pl.ds(pl.multiple_of((1 - x) * PIECE, PIECE), PIECE)
    for acts, held in zip(loads[:2], (tok_held, grad_held)):
        rows = acts.get()
        for slot in range(4):
            start = pl.multiple_of(table[SECOND + slot] * PIECE, PIECE)
            held[slot * PIECE : (slot + 1) * PIECE, :] = rows[pl.ds(start, PIECE), :]
    for which in range(3):
        held, transposed = ((tok_held, False), (grad_held, True))[which // 2]
        pair = weights[2 * which : 2 * which + 2]
        for at, end in spans(outs[0].shape[2]):
            total = pair_product(held, pair, at, end, transposed)
            terms = [h.get() for h in heard]
            near1, near2, near3 = [h[which, near, at:end].astype(jnp.float32) for h in terms]
            far1, far2, far3 = [h[which, far, at:end].astype(jnp.float32) for h in terms]
            sum1 = total[:PIECE] + far1 + jnp.where(core == 1, far2 + far3, 0.0)
            high = sum1.astype(jnp.bfloat16)
            rest = sum1 - high.astype(jnp.float32)
            sum2 = jnp.where(core == 1, rest, total[PIECE : 2 * PIECE] + near2)
            outs[0][which, :, at:end] = high
            outs[1][which, :, at:end] = sum2.astype(jnp.bfloat16)
            outs[2][which, :, at:end] = (total[2 * PIECE : 3 * PIECE] + far2).astype(jnp.bfloat16)
            outs[3][which, :, at:end] = (
                total[3 * PIECE :] + near1 + jnp.where(core == 1, near2 + near3, 0.0)
            )


def weave_kernel(tables, loads, stores):
    core = tables[0][CORE]
    full = stores[0].ref
    for load, at_core in zip(loads, (core, 1 - core)):
        rows = load.get()
        for piece in range(NY * NX):
            start = pl.multiple_of((piece * NC + at_core) * PIECE, PIECE)
            full[pl.ds(start, PIECE), :] = rows[piece * PIECE : (piece + 1) * PIECE, :]


def unit_kernel(tables, loads, stores):
    kept, *heard = [load.get() for load in loads]
    gate, up, d_hidden = [
        kept[which] + sum(h[which].astype(jnp.float32) for h in heard) for which in range(3)
    ]
    sig_gate = jax.nn.sigmoid(gate)
    hidden, both = [store.ref for store in stores]
    hidden[...] = (gate * sig_gate * up).astype(jnp.bfloat16)
    slope = d_hidden * up * sig_gate * (1.0 + gate * (1.0 - sig_gate))
    both[0] = slope.astype(jnp.bfloat16)
    both[1] = (d_hidden * gate * sig_gate).astype(jnp.bfloat16)


def pack_kernel(tables, loads, stores):
    own, near1, near2, near3 = [load.get() for load in loads]
    first, second = [store.ref for store in stores]
    core0 = tables[0][CORE] == 0
    first[:, :PIECE] = own[...]
    first[:, PIECE:] = near1[...]
    stores[0].send()
    second[:, :PIECE] = jnp.where(core0, near2[...], own[...])
    second[:, PIECE:] = jnp.where(core0, near3[...], near1[...])


def input_kernel(tables, loads, stores):
    (table,) = tables
    own, near1, near2, near3, far1, far2, far3 = [load.get() for load in loads[:7]]
    weights = loads[7:]
    *messages, d_set, kept = [store.ref for store in stores]

    def put(slot, value):
        start = pl.multiple_of(table[GATHER + slot] * PIECE, PIECE)
        d_set[:, pl.ds(start, PIECE), :] = value

    put(0, own[...])
    put(1, near1[...])
    put(2, far1[:, :PIECE])
    put(3, far1[:, PIECE:])
    put(4, far2[:, :PIECE])
    put(5, far2[:, PIECE:])
    core0 = table[CORE] == 0
    put(6, jnp.where(core0, near2[...], far3[:, :PIECE]))
    put(7, jnp.where(core0, near3[...], far3[:, PIECE:]))
    stores[NZ].send()
    depth = weights[0].target.shape[0]
    block = NX * PIECE
    for side in range(2):
        for at, end in spans(depth):
            gate, up = [weights[2 * side + i].get()[at:end, :] for i in range(2)]
            total = product(d_set[0], gate, True) + product(d_set[1], up, True)
            columns = slice(side * depth + at, side * depth + end)
            kept[:, columns] = total[:block]
            for k in range(NZ):
                messages[k][:, columns] = total[k * block : (k + 1) * block].astype(jnp.bfloat16)


def shape(dims, dtype=jnp.bfloat16):
    return jax.ShapeDtypeStruct(dims, dtype)


def first_stage(table, blocks, weights):
    depth, width = weights[0].shape
    rows = shape((NY * NX * PIECE, 2 * depth))
    return call(
        first_kernel,
        [table],
        [*blocks, *weights],
        [rows] * 2 + [shape((3, 2 * PIECE, width))] * 3,
        [pltpu.VMEM((6 * PIECE, 2 * depth), jnp.bfloat16)] * 2,
    )


def second_stage(table, tok_half, grad_half, weights, heard):
    width, depth = weights[0].shape[1], weights[0].shape[0]
    message = shape((3, PIECE, width))
    return call(
        second_kernel,
        [table],
        [tok_half, grad_half, *weights, *heard],
        [message] * 3 + [shape(message.shape, jnp.float32)],
        [pltpu.VMEM((4 * PIECE, 2 * depth), jnp.bfloat16)] * 2,
    )


def send_first(sent):
    return (
        lax.ppermute(sent[0], "row", row_perm(over_x, over_y(1))),
        lax.ppermute(sent[1], "row", row_perm(over_x, over_y(-1))),
        lax.ppermute(sent[2], "row", row_perm(None, over_y(2))),
    )


def send_second(sent):
    return (
        lax.ppermute(sent[0], "row", row_perm(over_y(1), over_x)),
        lax.ppermute(sent[1], "row", row_perm(over_y(-1), over_x)),
        lax.ppermute(sent[2], "row", row_perm(over_y(2), None)),
    )


FIRST, SECOND, CORE, AT_X, GATHER = 0, 6, 10, 11, 12


def table_rows():
    piece = lambda y_at, x_at: (y_at % NY) * NX + x_at
    rows = []
    for y in range(NY):
        for x in range(NX):
            other = 1 - x
            pair1 = [piece(y, other), piece(y + 1, other)]
            pair2 = [piece(y - 1, other), piece(y + 2, other)]
            if other == 1:
                pair1, pair2 = pair1[::-1], pair2[::-1]
            here = piece(y, x)
            first0 = pair1 + pair2 + [here, here]
            second0 = [piece(y + 1, x), piece(y - 1, x), piece(y + 2, x), here]
            first1 = [piece(y + step, x_at) for step in (1, -1, 2) for x_at in (0, 1)]
            second1 = [piece(y, other), here, here, here]
            gather0 = [here, piece(y - 1, x), piece(y, other), piece(y - 1, other)]
            gather0 += [piece(y + 1, other), piece(y + 2, other), piece(y + 1, x), piece(y + 2, x)]
            gather1 = [here, piece(y, other)]
            gather1 += [piece(y + step, x_at) for step in (-1, 1, 2) for x_at in (x, other)]
            rows.append(first0 + second0 + [0, x] + gather0)
            rows.append(first1 + second1 + [1, x] + gather1)
    return rows


def col_blocks(total):
    blocks = total.reshape(NY, NX, NC, PIECE, total.shape[1])
    return blocks[0], blocks[1:].astype(jnp.bfloat16)


def col_first(near, send):
    for step in range(1, NZ):
        near = near + lax.ppermute(send[step - 1], "col", col_perm(0, step)).astype(jnp.float32)
    return near[:, 0], near[:, 1].astype(jnp.bfloat16)


def col_second(result, send):
    result = result + lax.ppermute(send, "col", col_perm(1, 0)).astype(jnp.float32)
    return result.astype(jnp.bfloat16).reshape(NX * PIECE, result.shape[-1])


def body(tokens, gate_weight, up_weight, down_weight, grad_output):
    table = lax.dynamic_index_in_dim(
        jnp.array(table_rows(), jnp.int32), lax.axis_index("row"), 0, keepdims=False
    )
    core = table[CORE]
    flip = lambda value: lax.ppermute(value, "row", CORE_FLIP)
    after = lambda value, *others: lax.optimization_barrier((value, *others))[0]
    width, ff_width = gate_weight.shape
    half_rows = NY * NX * PIECE

    pairs = [[i, i + 1] for i in range(0, NY * NX * NC, NC)]
    gate_other, up_other, down_other = [
        OfOther(lax.all_gather(weight, "row", axis_index_groups=pairs))
        for weight in (gate_weight, up_weight, down_weight)
    ]
    mine = jnp.stack([tokens, grad_output])
    own_block = jnp.concatenate([mine, flip(mine)], axis=2)
    blocks = [lax.ppermute(own_block, BOTH, gather_perm(step)) for step in range(NZ)]

    both_weights = [gate_weight, gate_other, up_weight, up_other]
    weights = [*both_weights, down_weight, down_other]
    tok_half, grad_half, *sent = first_stage(table, [own_block, *blocks], weights)
    heard = send_first(sent)
    halves = after(jnp.stack([tok_half[:, width:], grad_half[:, width:]]), sent[0])
    tok_other, grad_other = flip(halves)
    tok_own = tok_half[:, :width]
    (grad_all,) = call(
        weave_kernel,
        [table],
        [grad_half[:, :width], grad_other],
        [shape((2 * half_rows, width))],
    )
    *heard, grad_all, tok_other = lax.optimization_barrier((*heard, grad_all, tok_other))
    *sent, kept = second_stage(table, tok_half, grad_half, weights, heard)
    hidden, d_own = call(
        unit_kernel,
        [],
        [kept, *send_second(sent)],
        [shape((PIECE, ff_width)), shape((2, PIECE, ff_width))],
    )
    hidden = lax.all_gather(hidden, "row", axis=0, tiled=True)

    near = send_second([d_own] * 3)
    first, second = call(
        pack_kernel, [table], [d_own, *near], [shape((2, 2 * PIECE, ff_width))] * 2
    )
    far = send_first([first, second, first])
    block = shape((NX * PIECE, 2 * width))
    *messages, d_set, kept = call(
        input_kernel,
        [table],
        [d_own, *near, *far, gate_weight, up_weight, gate_other, up_other],
        [block] * 4 + [shape((2, half_rows, ff_width)), shape(block.shape, jnp.float32)],
    )
    hidden = after(hidden, kept)
    messages = [lax.ppermute(messages[k], BOTH, scatter_perm(k)) for k in range(NZ)]
    d_other = flip(d_set)
    dot = functools.partial(lax.dot_general, preferred_element_type=jnp.float32)
    contract_first = (((0,), (0,)), ((), ()))
    near_sum, send = col_blocks(jnp.dot(hidden, down_weight, preferred_element_type=jnp.float32))
    layer_output = col_second(*col_first(near_sum, send))
    grad_down = dot(hidden, grad_all, contract_first).astype(jnp.bfloat16)

    def weight_gradient(which):
        total = dot(tok_own, d_set[which], contract_first)
        return (total + dot(tok_other, d_other[which], contract_first)).astype(jnp.bfloat16)

    grad_gate, grad_up = weight_gradient(0), weight_gradient(1)
    *messages, grad_gate, grad_up = lax.optimization_barrier((*messages, grad_gate, grad_up))
    total = jnp.where(core == 0, kept, 0.0)
    for message in messages:
        total = total + message.astype(jnp.float32)
    grad_input = (total[:, :width] + flip(total[:, width:])).astype(jnp.bfloat16)
    return (layer_output, grad_input, grad_gate, grad_up, grad_down)


def solution(mesh):
    placed = (P("col", "row"), P("row", "col"), P("row", "col"), P("col", "row"), P("col", "row"))
    return jax.shard_map(
        body,
        mesh=mesh,
        in_specs=placed,
        out_specs=(
            P("col", "row"),
            P("col", "row"),
            P("row", "col"),
            P("row", "col"),
            P("col", "row"),
        ),
        check_vma=False,
    )
```

time: 269 us -> 281 us (1.045)
  the two profiles are of different devices: /device:TPU:17 before, /device:TPU:0 now
where the time goes in v4:
time: 281 us; the launch traced here: 280 us
  waiting for transfers between devices  147 us (52%)
  starting transfers between devices  47.3 us (17%)
  Pallas kernels  42.5 us (15%)
  between operations  14.8 us (5%)
  matrix products  14.7 us (5%)
  local copies, waits for them, and re-layouts  12.2 us (4%)
    pallas_call x6, Pallas kernels, call(): pl.pallas_call(run, in_specs=[smem] * n_tables + [any_space] * n_in, out_...  42.5 us
    ppermute x2, waiting for transfers between devices, send_first(): lax.ppermute(sent[0], 'row', row_perm(over_x, over_y(1)))  30.4 us
    all_gather x3, waiting for transfers between devices, body(): lax.all_gather(weight, 'row', axis_index_groups=pairs)  25.3 us
    ppermute x2, waiting for transfers between devices, send_first(): lax.ppermute(sent[1], 'row', row_perm(over_x, over_y(-1)))  24.6 us
    ppermute x4, waiting for transfers between devices, body(): lax.ppermute(own_block, BOTH, gather_perm(step))  21.1 us
    ppermute x2, waiting for transfers between devices, send_second(): lax.ppermute(sent[1], 'row', row_perm(over_y(-1), over_x))  16.9 us
    ppermute x3, waiting for transfers between devices, col_first(): lax.ppermute(send[step - 1], 'col', col_perm(0, step)).astype(jnp.float32)  11.2 us
    ppermute x2, waiting for transfers between devices, send_second(): lax.ppermute(sent[0], 'row', row_perm(over_y(1), over_x))  10.5 us
  transfers between devices with their start and end apart: 32, of which 17 were waited for; matrix products, arithmetic and copies ran while one was open for 7% of the time, Pallas kernels for 6%

profile of v4, /device:TPU:0, one launch (start us, length us, event | category | flops | bytes accessed | tf_op | source)
XLA Modules:
  0.0 280.4 jit_solution(7923985259279991919)
XLA Ops:
  11.9 4.2 %collective-permute-start.2 = (bf16[2,128,1024]{2,1,0:T(8,128)(2,1)S(1)}, bf16[2,128,1024]{2,1,0:T(8,128)(2,1)S(1)}, u32[]{:S(2)}, u32[]{:S(2)}) collective-permute-start(bf16[2,128,1024]{2,1,0:T(8,128)(2,1)S(1)} %pad_maximum_fusion.1.refs_1_), channel_id=1, source_target_pairs={{1,0},{2,1},{3,2},{0,3},{5,4},{6,5},{7,6},{4,7},{13,8},{14,9},{15,... | collective-permute-start | bytes 1572872 | tf_op jit(solution)/shard_map/ppermute | solution.py:371
  18.6 21.1 %collective-permute-done.2.refs_3_ = bf16[2,128,1024]{2,1,0:T(8,128)(2,1)S(1)} collective-permute-done((bf16[2,128,1024]{2,1,0:T(8,128)(2,1)S(1)}, bf16[2,128,1024]{2,1,0:T(8,128)(2,1)S(1)}, u32[]{:S(2)}, u32[]{:S(2)}) %collective-permute-start.2) | collective-permute-done | bytes 524320 | tf_op jit(solution)/shard_map/ppermute | solution.py:371
  39.7 6.7 %all-gather.12.cloned.1.call-done = bf16[1024,1792]{1,0:T(8,128)(2,1)} async-done(((bf16[512,1792]{1,0:T(8,128)(2,1)}), bf16[1024,1792]{1,0:T(8,128)(2,1)}) %all-gather.12.cloned.1.call-update) | async-done | bytes 3670032 | tf_op jit(solution)/shard_map/all_gather | solution.py:366
  46.4 18.6 %all-gather.14.cloned.1.call-done = bf16[3584,512]{1,0:T(8,128)(2,1)} async-done(((bf16[1792,512]{1,0:T(8,128)(2,1)}), bf16[3584,512]{1,0:T(8,128)(2,1)}) %all-gather.14.cloned.1.call-update) | async-done | bytes 3670032 | tf_op jit(solution)/shard_map/all_gather | solution.py:366
  65.0 11.1 %shard_map.101 = (bf16[512,1024]{1,0:T(8,128)(2,1)}, bf16[512,1024]{1,0:T(8,128)(2,1)}, bf16[3,128,1792]{2,1,0:T(8,128)(2,1)}, bf16[3,128,1792]{2,1,0:T(8,128)(2,1)}, bf16[3,128,1792]{2,1,0:T(8,128)(2,1)}) custom-call(s32[20]{0:T(128)} %get-tuple-element.77.refs_0_, bf16[2,128,1024]{2,1,0:T(8,128)(2,1)} %copy-done.3, bf16[2,128,1024]{2,1,0:T(8,128)(2,1)} %copy-done.18, ...), custom_call_target="tpu_custom_call" | custom-call | flops 1 | bytes 1 | tf_op jit(solution)/shard_map/pallas_call | solution.py:124
  82.1 3.8 %collective-permute-start.8 = (bf16[2,512,512]{2,1,0:T(8,128)(2,1)S(1)}, bf16[2,512,512]{2,1,0:T(8,128)(2,1)S(1)}, u32[]{:S(2)}, u32[]{:S(2)}) collective-permute-start(bf16[2,512,512]{2,1,0:T(8,128)(2,1)S(1)} %pad_maximum_fusion), channel_id=1, source_target_pairs={{0,8},{8,0},{16,24},{24,16},{32,40},{40,32},{48,56},{56,48},{64,72... | collective-permute-start | bytes 3145736 | tf_op jit(solution)/shard_map/ppermute | solution.py:359
  92.0 5.7 %collective-permute-done.5.refs_9_ = bf16[3,128,1792]{2,1,0:T(8,128)(2,1)S(1)} collective-permute-done((bf16[3,128,1792]{2,1,0:T(8,128)(2,1)}, bf16[3,128,1792]{2,1,0:T(8,128)(2,1)S(1)}, u32[]{:S(2)}, u32[]{:S(2)}) %collective-permute-start.5) | collective-permute-done | bytes 1376288 | tf_op jit(solution)/shard_map/ppermute | solution.py:297
  97.8 14.7 %collective-permute-done.6.refs_10_ = bf16[3,128,1792]{2,1,0:T(8,128)(2,1)S(1)} collective-permute-done((bf16[3,128,1792]{2,1,0:T(8,128)(2,1)}, bf16[3,128,1792]{2,1,0:T(8,128)(2,1)S(1)}, u32[]{:S(2)}, u32[]{:S(2)}) %collective-permute-start.6) | collective-permute-done | bytes 1376288 | tf_op jit(solution)/shard_map/ppermute | solution.py:298
  114.1 12.1 %shard_map.103 = (bf16[3,64,1792]{2,1,0:T(8,128)(2,1)}, bf16[3,64,1792]{2,1,0:T(8,128)(2,1)}, bf16[3,64,1792]{2,1,0:T(8,128)(2,1)}, f32[3,64,1792]{2,1,0:T(8,128)}) custom-call(s32[20]{0:T(128)} %get-tuple-element.77.refs_0_, bf16[512,1024]{1,0:T(8,128)(2,1)} %get-tuple-element.37.refs_1_, bf16[512,1024]{1,0:T(8,128)(2,1)} %get-tuple-element.38.refs_2_, ...), custom_call_target="tpu_custom_call" | custom-call | flops 1 | bytes 1 | tf_op jit(solution)/shard_map/pallas_call | solution.py:124
  126.2 2.9 %collective-permute-start.10 = (bf16[3,64,1792]{2,1,0:T(8,128)(2,1)}, bf16[3,64,1792]{2,1,0:T(8,128)(2,1)S(1)}, u32[]{:S(2)}, u32[]{:S(2)}) collective-permute-start(bf16[3,64,1792]{2,1,0:T(8,128)(2,1)} %get-tuple-element.48), channel_id=1, source_target_pairs={{0,96},{8,24},{16,112},{24,8},{32,0},{40,56},{48,16},{56,40},{64,3... | collective-permute-start | bytes 2064392 | tf_op jit(solution)/shard_map/ppermute | solution.py:306
  132.9 12.3 %collective-permute-done.10.refs_2_ = bf16[3,64,1792]{2,1,0:T(8,128)(2,1)S(1)} collective-permute-done((bf16[3,64,1792]{2,1,0:T(8,128)(2,1)}, bf16[3,64,1792]{2,1,0:T(8,128)(2,1)S(1)}, u32[]{:S(2)}, u32[]{:S(2)}) %collective-permute-start.10) | collective-permute-done | bytes 688160 | tf_op jit(solution)/shard_map/ppermute | solution.py:306
  145.2 5.8 %collective-permute-done.9.refs_1_ = bf16[3,64,1792]{2,1,0:T(8,128)(2,1)S(1)} collective-permute-done((bf16[3,64,1792]{2,1,0:T(8,128)(2,1)}, bf16[3,64,1792]{2,1,0:T(8,128)(2,1)S(1)}, u32[]{:S(2)}, u32[]{:S(2)}) %collective-permute-start.9) | collective-permute-done | bytes 688160 | tf_op jit(solution)/shard_map/ppermute | solution.py:305
  151.8 3.3 %shard_map.104 = (bf16[64,1792]{1,0:T(8,128)(2,1)}, bf16[2,64,1792]{2,1,0:T(8,128)(2,1)}) custom-call(f32[3,64,1792]{2,1,0:T(8,128)} %get-tuple-element.46.refs_0_, bf16[3,64,1792]{2,1,0:T(8,128)(2,1)} %copy-done.16, bf16[3,64,1792]{2,1,0:T(8,128)(2,1)} %copy-done.14, bf16[3,64,1792]{2,1,0:T(8,128)(2,1)} %copy-done.15), custom_call_target="tpu_custom_call" | custom-call | flops 1 | bytes 1 | tf_op jit(solution)/shard_map/pallas_call | solution.py:124
  155.2 3.2 %collective-permute-start.13 = (bf16[2,64,1792]{2,1,0:T(8,128)(2,1)}, bf16[2,64,1792]{2,1,0:T(8,128)(2,1)S(1)}, u32[]{:S(2)}, u32[]{:S(2)}) collective-permute-start(bf16[2,64,1792]{2,1,0:T(8,128)(2,1)} %get-tuple-element.51.refs_1_), channel_id=1, source_target_pairs={{0,96},{8,24},{16,112},{24,8},{32,0},{40,56},{48,16},{56,40},{64,3... | collective-permute-start | bytes 1376264 | tf_op jit(solution)/shard_map/ppermute | solution.py:306
  160.4 4.7 %collective-permute-done.12.refs_2_ = bf16[2,64,1792]{2,1,0:T(8,128)(2,1)S(1)} collective-permute-done((bf16[2,64,1792]{2,1,0:T(8,128)(2,1)}, bf16[2,64,1792]{2,1,0:T(8,128)(2,1)S(1)}, u32[]{:S(2)}, u32[]{:S(2)}) %collective-permute-start.12) | collective-permute-done | bytes 458784 | tf_op jit(solution)/shard_map/ppermute | solution.py:305
  165.1 4.6 %collective-permute-done.13.refs_3_ = bf16[2,64,1792]{2,1,0:T(8,128)(2,1)S(1)} collective-permute-done((bf16[2,64,1792]{2,1,0:T(8,128)(2,1)}, bf16[2,64,1792]{2,1,0:T(8,128)(2,1)S(1)}, u32[]{:S(2)}, u32[]{:S(2)}) %collective-permute-start.13) | collective-permute-done | bytes 458784 | tf_op jit(solution)/shard_map/ppermute | solution.py:306
  171.3 3.4 %shard_map.105 = (bf16[2,128,1792]{2,1,0:T(8,128)(2,1)}, bf16[2,128,1792]{2,1,0:T(8,128)(2,1)}) custom-call(s32[20]{0:T(128)} %get-tuple-element.77.refs_0_, bf16[2,64,1792]{2,1,0:T(8,128)(2,1)} %get-tuple-element.51.refs_1_, bf16[2,64,1792]{2,1,0:T(8,128)(2,1)} %copy-done.4, bf16[2,64,1792]{2,1,0:T(8,128)(2,1)} %copy-done.5, bf16[2,64,1792]{2,1,0:T(8,128)(2,1)} %copy-done.6), custom_call_target="tpu_custom_call" | custom-call | flops 1 | bytes 1 | tf_op jit(solution)/shard_map/pallas_call | solution.py:124
  177.5 24.7 %collective-permute-done.15.refs_5_ = bf16[2,128,1792]{2,1,0:T(8,128)(2,1)S(1)} collective-permute-done((bf16[2,128,1792]{2,1,0:T(8,128)(2,1)}, bf16[2,128,1792]{2,1,0:T(8,128)(2,1)S(1)}, u32[]{:S(2)}, u32[]{:S(2)}) %collective-permute-start.15) | collective-permute-done | bytes 917536 | tf_op jit(solution)/shard_map/ppermute | solution.py:297
  202.2 9.8 %collective-permute-done.16.refs_6_ = bf16[2,128,1792]{2,1,0:T(8,128)(2,1)S(1)} collective-permute-done((bf16[2,128,1792]{2,1,0:T(8,128)(2,1)}, bf16[2,128,1792]{2,1,0:T(8,128)(2,1)S(1)}, u32[]{:S(2)}, u32[]{:S(2)}) %collective-permute-start.16) | collective-permute-done | bytes 917536 | tf_op jit(solution)/shard_map/ppermute | solution.py:298
  213.9 9.8 %shard_map.106 = (bf16[128,1024]{1,0:T(8,128)(2,1)}, bf16[128,1024]{1,0:T(8,128)(2,1)}, bf16[128,1024]{1,0:T(8,128)(2,1)}, bf16[128,1024]{1,0:T(8,128)(2,1)}, bf...) custom-call(s32[20]{0:T(128)} %get-tuple-element.77.refs_0_, bf16[2,64,1792]{2,1,0:T(8,128)(2,1)} %get-tuple-element.51.refs_1_, ...), custom_call_target="tpu_custom_call" | custom-call | flops 1 | bytes 1 | tf_op jit(solution)/shard_map/pallas_call | solution.py:124
  240.3 6.3 %collective-permute-start.27 = (f32[128,512]{1,0:T(8,128)S(1)}, f32[128,512]{1,0:T(8,128)S(1)}, u32[]{:S(2)}, u32[]{:S(2)}) collective-permute-start(f32[128,512]{1,0:T(8,128)S(1)} %slice.89), channel_id=1, source_target_pairs={{0,8},{8,0},{16,24},{24,16},{32,40},{40,32},{48,56},{56,48},{64,72... | collective-permute-start | bytes 786440 | tf_op jit(solution)/shard_map/ppermute | solution.py:359
  246.6 4.1 %fusion.14 = (bf16[1024,512]{1,0:T(8,128)(2,1)S(1)}, f32[1024,512]{1,0:T(8,128)S(1)}) fusion(bf16[1024,1792]{1,0:T(8,128)(2,1)} %all-gather.8.cloned.1.call-done, bf16[1792,512]{1,0:T(8,128)(2,1)S(1)} %copy-done), kind=kOutput, calls=%fused_computation.32 | convolution fusion | flops 1879572480 | bytes 8650752 | tf_op jit(solution)/shard_map/dot_general | solution.py:413
  255.3 10.6 %collective-permute-done.18 = bf16[2,2,64,512]{3,2,1,0:T(8,128)(2,1)S(1)} collective-permute-done((bf16[2,2,64,512]{3,2,1,0:T(8,128)(2,1)S(1)}, bf16[2,2,64,512]{3,2,1,0:T(8,128)(2,1)S(1)}, u32[]{:S(2)}, u32[]{:S(2)}) %collective-permute-start.18) | collective-permute-done | bytes 262176 | tf_op jit(solution)/shard_map/ppermute | solution.py:345
  269.5 3.4 %convolution_convert_fusion = bf16[1792,512]{1,0:T(8,128)(2,1)} fusion(bf16[1024,1792]{1,0:T(8,128)(2,1)S(1)} %copy-done.24, bf16[1024,512]{1,0:T(8,128)(2,1)S(1)} %copy-done.10), kind=kOutput, calls=%fused_computation.2 | convolution fusion | flops 1879965696 | bytes 6553600 | tf_op jit(solution)/shard_map/dot_general | solution.py:415
  (122 shorter events, 58.8 us)
Async XLA Ops:
  7.2 32.5 %all-gather.10.cloned.1.call-start = ((), (), s32[]{:S(2)}) async-start(), calls=%async_computation.1 | async-start | bytes 5505024 | tf_op jit(solution)/shard_map/all_gather | solution.py:366
  7.9 38.4 %all-gather.12.cloned.1.call-start = ((), (), s32[]{:S(2)}) async-start(), calls=%async_computation.2 | async-start | bytes 5505024 | tf_op jit(solution)/shard_map/all_gather | solution.py:366
  8.7 56.3 %all-gather.14.cloned.1.call-start = ((), (), s32[]{:S(2)}) async-start(), calls=%async_computation.3 | async-start | bytes 5505024 | tf_op jit(solution)/shard_map/all_gather | solution.py:366
  9.4 237.1 %all-gather.8.cloned.1.call-start = ((), (), s32[]{:S(2)}) async-start(), calls=%async_computation | async-start | bytes 3899392 | tf_op jit(solution)/shard_map/all_gather | solution.py:394
  11.9 27.7 %collective-permute-start.2 = (bf16[2,128,1024]{2,1,0:T(8,128)(2,1)S(1)}, bf16[2,128,1024]{2,1,0:T(8,128)(2,1)S(1)}, u32[]{:S(2)}, u32[]{:S(2)}) collective-permute-start(bf16[2,128,1024]{2,1,0:T(8,128)(2,1)S(1)} %pad_maximum_fusion.1.refs_1_), channel_id=1, source_target_pairs={{1,0},{2,1},{3,2},{0,3},{5,4},{6,5},{7,6},{4,7},{13,8},{14,9},{15,... | collective-permute-start | bytes 1572872 | tf_op jit(solution)/shard_map/ppermute | solution.py:371
  16.1 23.6 %collective-permute-start.3 = (bf16[2,128,1024]{2,1,0:T(8,128)(2,1)S(1)}, bf16[2,128,1024]{2,1,0:T(8,128)(2,1)S(1)}, u32[]{:S(2)}, u32[]{:S(2)}) collective-permute-start(bf16[2,128,1024]{2,1,0:T(8,128)(2,1)S(1)} %pad_maximum_fusion.1.refs_1_), channel_id=1, source_target_pairs={{2,0},{3,1},{0,2},{1,3},{6,4},{7,5},{4,6},{5,7},{14,8},{15,9},{12,... | collective-permute-start | bytes 1572872 | tf_op jit(solution)/shard_map/ppermute | solution.py:371
  16.1 23.6 %collective-permute-start.4 = (bf16[2,128,1024]{2,1,0:T(8,128)(2,1)S(1)}, bf16[2,128,1024]{2,1,0:T(8,128)(2,1)S(1)}, u32[]{:S(2)}, u32[]{:S(2)}) collective-permute-start(bf16[2,128,1024]{2,1,0:T(8,128)(2,1)S(1)} %pad_maximum_fusion.1.refs_1_), channel_id=1, source_target_pairs={{3,0},{0,1},{1,2},{2,3},{7,4},{4,5},{5,6},{6,7},{15,8},{12,9},{13,... | collective-permute-start | bytes 1572872 | tf_op jit(solution)/shard_map/ppermute | solution.py:371
  79.3 18.5 %collective-permute-start.5 = (bf16[3,128,1792]{2,1,0:T(8,128)(2,1)}, bf16[3,128,1792]{2,1,0:T(8,128)(2,1)S(1)}, u32[]{:S(2)}, u32[]{:S(2)}) collective-permute-start(bf16[3,128,1792]{2,1,0:T(8,128)(2,1)} %get-tuple-element.39), channel_id=1, source_target_pairs={{0,16},{8,40},{16,0},{24,56},{32,48},{40,72},{48,32},{56,88},{64,8... | collective-permute-start | bytes 4128776 | tf_op jit(solution)/shard_map/ppermute | solution.py:297
  80.8 31.7 %collective-permute-start.6 = (bf16[3,128,1792]{2,1,0:T(8,128)(2,1)}, bf16[3,128,1792]{2,1,0:T(8,128)(2,1)S(1)}, u32[]{:S(2)}, u32[]{:S(2)}) collective-permute-start(bf16[3,128,1792]{2,1,0:T(8,128)(2,1)} %get-tuple-element.40), channel_id=1, source_target_pairs={{0,16},{8,104},{16,0},{24,120},{32,48},{40,8},{48,32},{56,24},{64,... | collective-permute-start | bytes 4128776 | tf_op jit(solution)/shard_map/ppermute | solution.py:298
  81.3 31.2 %collective-permute-start.7 = (bf16[3,128,1792]{2,1,0:T(8,128)(2,1)}, bf16[3,128,1792]{2,1,0:T(8,128)(2,1)S(1)}, u32[]{:S(2)}, u32[]{:S(2)}) collective-permute-start(bf16[3,128,1792]{2,1,0:T(8,128)(2,1)} %get-tuple-element.41), channel_id=1, source_target_pairs={{8,72},{24,88},{40,104},{56,120},{72,8},{88,24},{104,40},{120,56},... | collective-permute-start | bytes 4128776 | tf_op jit(solution)/shard_map/ppermute | solution.py:299
  126.2 19.1 %collective-permute-start.10 = (bf16[3,64,1792]{2,1,0:T(8,128)(2,1)}, bf16[3,64,1792]{2,1,0:T(8,128)(2,1)S(1)}, u32[]{:S(2)}, u32[]{:S(2)}) collective-permute-start(bf16[3,64,1792]{2,1,0:T(8,128)(2,1)} %get-tuple-element.48), channel_id=1, source_target_pairs={{0,96},{8,24},{16,112},{24,8},{32,0},{40,56},{48,16},{56,40},{64,3... | collective-permute-start | bytes 2064392 | tf_op jit(solution)/shard_map/ppermute | solution.py:306
  129.1 16.1 %collective-permute-start.11 = (bf16[3,64,1792]{2,1,0:T(8,128)(2,1)}, bf16[3,64,1792]{2,1,0:T(8,128)(2,1)S(1)}, u32[]{:S(2)}, u32[]{:S(2)}) collective-permute-start(bf16[3,64,1792]{2,1,0:T(8,128)(2,1)} %get-tuple-element.49), channel_id=1, source_target_pairs={{0,64},{16,80},{32,96},{48,112},{64,0},{80,16},{96,32},{112,48},{1... | collective-permute-start | bytes 2064392 | tf_op jit(solution)/shard_map/ppermute | solution.py:307
  131.8 19.2 %collective-permute-start.9 = (bf16[3,64,1792]{2,1,0:T(8,128)(2,1)}, bf16[3,64,1792]{2,1,0:T(8,128)(2,1)S(1)}, u32[]{:S(2)}, u32[]{:S(2)}) collective-permute-start(bf16[3,64,1792]{2,1,0:T(8,128)(2,1)} %get-tuple-element.47), channel_id=1, source_target_pairs={{0,32},{8,24},{16,48},{24,8},{32,64},{40,56},{48,80},{56,40},{64,9... | collective-permute-start | bytes 2064392 | tf_op jit(solution)/shard_map/ppermute | solution.py:305
  155.2 14.5 %collective-permute-start.13 = (bf16[2,64,1792]{2,1,0:T(8,128)(2,1)}, bf16[2,64,1792]{2,1,0:T(8,128)(2,1)S(1)}, u32[]{:S(2)}, u32[]{:S(2)}) collective-permute-start(bf16[2,64,1792]{2,1,0:T(8,128)(2,1)} %get-tuple-element.51.refs_1_), channel_id=1, source_target_pairs={{0,96},{8,24},{16,112},{24,8},{32,0},{40,56},{48,16},{56,40},{64,3... | collective-permute-start | bytes 1376264 | tf_op jit(solution)/shard_map/ppermute | solution.py:306
  174.7 27.5 %collective-permute-start.15 = (bf16[2,128,1792]{2,1,0:T(8,128)(2,1)}, bf16[2,128,1792]{2,1,0:T(8,128)(2,1)S(1)}, u32[]{:S(2)}, u32[]{:S(2)}) collective-permute-start(bf16[2,128,1792]{2,1,0:T(8,128)(2,1)} %get-tuple-element.52), channel_id=1, source_target_pairs={{0,16},{8,40},{16,0},{24,56},{32,48},{40,72},{48,32},{56,88},{64,8... | collective-permute-start | bytes 2752520 | tf_op jit(solution)/shard_map/ppermute | solution.py:297
  176.2 35.8 %collective-permute-start.16 = (bf16[2,128,1792]{2,1,0:T(8,128)(2,1)}, bf16[2,128,1792]{2,1,0:T(8,128)(2,1)S(1)}, u32[]{:S(2)}, u32[]{:S(2)}) collective-permute-start(bf16[2,128,1792]{2,1,0:T(8,128)(2,1)} %get-tuple-element.53), channel_id=1, source_target_pairs={{0,16},{8,104},{16,0},{24,120},{32,48},{40,8},{48,32},{56,24},{64,... | collective-permute-start | bytes 2752520 | tf_op jit(solution)/shard_map/ppermute | solution.py:298
  176.8 35.2 %collective-permute-start.17 = (bf16[2,128,1792]{2,1,0:T(8,128)(2,1)}, bf16[2,128,1792]{2,1,0:T(8,128)(2,1)S(1)}, u32[]{:S(2)}, u32[]{:S(2)}) collective-permute-start(bf16[2,128,1792]{2,1,0:T(8,128)(2,1)} %get-tuple-element.52), channel_id=1, source_target_pairs={{8,72},{24,88},{40,104},{56,120},{72,8},{88,24},{104,40},{120,56},... | collective-permute-start | bytes 2752520 | tf_op jit(solution)/shard_map/ppermute | solution.py:299
  225.0 15.0 %collective-permute-start.22 = (bf16[128,1024]{1,0:T(8,128)(2,1)}, bf16[128,1024]{1,0:T(8,128)(2,1)S(1)}, u32[]{:S(2)}, u32[]{:S(2)}) collective-permute-start(bf16[128,1024]{1,0:T(8,128)(2,1)} %get-tuple-element.56), channel_id=1, source_target_pairs={{8,12},{9,13},{10,14},{11,15},{12,8},{13,9},{14,10},{15,11},{24,28... | collective-permute-start | bytes 786440 | tf_op jit(solution)/shard_map/ppermute | solution.py:409
  225.7 14.3 %collective-permute-start.23 = (bf16[128,1024]{1,0:T(8,128)(2,1)}, bf16[128,1024]{1,0:T(8,128)(2,1)S(1)}, u32[]{:S(2)}, u32[]{:S(2)}) collective-permute-start(bf16[128,1024]{1,0:T(8,128)(2,1)} %get-tuple-element.57), channel_id=1, source_target_pairs={{0,1},{1,2},{2,3},{3,0},{4,5},{5,6},{6,7},{7,4},{8,13},{9,14},{10,... | collective-permute-start | bytes 786440 | tf_op jit(solution)/shard_map/ppermute | solution.py:409
  227.3 12.7 %collective-permute-start.24 = (bf16[128,1024]{1,0:T(8,128)(2,1)}, bf16[128,1024]{1,0:T(8,128)(2,1)S(1)}, u32[]{:S(2)}, u32[]{:S(2)}) collective-permute-start(bf16[128,1024]{1,0:T(8,128)(2,1)} %get-tuple-element.58), channel_id=1, source_target_pairs={{0,2},{1,3},{2,0},{3,1},{4,6},{5,7},{6,4},{7,5},{8,14},{9,15},{10,... | collective-permute-start | bytes 786440 | tf_op jit(solution)/shard_map/ppermute | solution.py:409
  240.3 14.3 %collective-permute-start.27 = (f32[128,512]{1,0:T(8,128)S(1)}, f32[128,512]{1,0:T(8,128)S(1)}, u32[]{:S(2)}, u32[]{:S(2)}) collective-permute-start(f32[128,512]{1,0:T(8,128)S(1)} %slice.89), channel_id=1, source_target_pairs={{0,8},{8,0},{16,24},{24,16},{32,40},{40,32},{48,56},{56,48},{64,72... | collective-permute-start | bytes 786440 | tf_op jit(solution)/shard_map/ppermute | solution.py:359
  250.7 15.2 %collective-permute-start.18 = (bf16[2,2,64,512]{3,2,1,0:T(8,128)(2,1)S(1)}, bf16[2,2,64,512]{3,2,1,0:T(8,128)(2,1)S(1)}, u32[]{:S(2)}, u32[]{:S(2)}) collective-permute-start(bf16[2,2,64,512]{3,2,1,0:T(8,128)(2,1)S(1)} %bitcast.64), channel_id=1, source_target_pairs={{0,1},{1,2},{2,3},{3,0},{4,5},{5,6},{6,7},{7,4},{8,9},{9,10},{10,1... | collective-permute-start | bytes 786440 | tf_op jit(solution)/shard_map/ppermute | solution.py:345
  251.4 14.4 %collective-permute-start.19 = (bf16[2,2,64,512]{3,2,1,0:T(8,128)(2,1)S(1)}, bf16[2,2,64,512]{3,2,1,0:T(8,128)(2,1)S(1)}, u32[]{:S(2)}, u32[]{:S(2)}) collective-permute-start(bf16[2,2,64,512]{3,2,1,0:T(8,128)(2,1)S(1)} %bitcast.63), channel_id=1, source_target_pairs={{0,2},{1,3},{2,0},{3,1},{4,6},{5,7},{6,4},{7,5},{8,10},{9,11},{10,... | collective-permute-start | bytes 786440 | tf_op jit(solution)/shard_map/ppermute | solution.py:345
  253.4 13.1 %collective-permute-start.20 = (bf16[2,2,64,512]{3,2,1,0:T(8,128)(2,1)S(1)}, bf16[2,2,64,512]{3,2,1,0:T(8,128)(2,1)S(1)}, u32[]{:S(2)}, u32[]{:S(2)}) collective-permute-start(bf16[2,2,64,512]{3,2,1,0:T(8,128)(2,1)S(1)} %bitcast.62), channel_id=1, source_target_pairs={{0,3},{1,0},{2,1},{3,2},{4,7},{5,4},{6,5},{7,6},{8,11},{9,8},{10,9... | collective-permute-start | bytes 786440 | tf_op jit(solution)/shard_map/ppermute | solution.py:345
  (33 other events, 343.6 us)
Sparse Core Ops, SparseCore 0:
  9.7 18.0 all-gather.9
  29.4 16.9 all-gather.11
  48.0 16.9 all-gather.13
  160.5 41.5 all-gather.7

commit v5 on v4

--- a/solution.py
+++ b/solution.py
@@ -89,14 +89,7 @@
         self.sent = True
 
 
-class OfOther:
-    def __init__(self, value):
-        self.value = value
-
-
 def call(kernel, tables, operands, out_shape, scratch=()):
-    parts = [shape(o.value.shape[1:]) if isinstance(o, OfOther) else o for o in operands]
-    operands = [o.value if isinstance(o, OfOther) else o for o in operands]
     any_space = pl.BlockSpec(memory_space=pl.ANY)
     smem = pl.BlockSpec(memory_space=pltpu.SMEM)
     n_tables, n_in, n_out, n_own = len(tables), len(operands), len(out_shape), len(scratch)
@@ -106,10 +99,6 @@
         take = lambda count: [refs.pop(0) for _ in range(count)]
         table_refs, ins, outs, own = take(n_tables), take(n_in), take(n_out), take(n_own)
         in_buffers, out_buffers, (in_sems, out_sems) = take(n_in), take(n_out), take(2)
-        ins = [
-            ref.at[1 - table_refs[0][CORE]] if len(ref.shape) > len(to.shape) else ref
-            for ref, to in zip(ins, in_buffers)
-        ]
         loads = [Load(ins[i], in_buffers[i], in_sems.at[i]) for i in range(n_in)]
         stores = [Store(out_buffers[i], outs[i], out_sems.at[i]) for i in range(n_out)]
         kernel(table_refs, loads, stores, *own)
@@ -128,7 +117,7 @@
         out_shape=out_shape,
         scratch_shapes=[
             *scratch,
-            *[pltpu.VMEM(o.shape, o.dtype) for o in [*parts, *out_shape]],
+            *[pltpu.VMEM(o.shape, o.dtype) for o in [*operands, *out_shape]],
             pltpu.SemaphoreType.DMA((n_in,)),
             pltpu.SemaphoreType.DMA((n_out,)),
         ],
@@ -147,9 +136,11 @@
 def first_kernel(tables, loads, stores, tok_held, grad_held):
     (table,) = tables
     block, *blocks = [load.get() for load in loads[:-6]]
-    weights, messages, halves = loads[-6:], stores[2:], [store.ref for store in stores[:2]]
+    weights, messages = loads[-6:], stores[6:]
     rows = block.shape[1]
-    for i, (acts, held) in enumerate(zip(halves, (tok_held, grad_held))):
+    for i, held in enumerate((tok_held, grad_held)):
+        acts, own, away = [store.ref for store in stores[i:6:2]]
+        half = own.shape[1]
         acts[:rows] = jnp.where(table[CORE] == 0, block[i], blocks[0][i])
         for k in range(1, NZ):
             acts[k * rows : (k + 1) * rows] = blocks[k][i]
@@ -164,15 +155,17 @@
             total = pair_product(held, pair, at, end, transposed).astype(jnp.bfloat16)
             for i, message in enumerate(messages):
                 message.ref[which, :, at:end] = total[i * 2 * PIECE : (i + 1) * 2 * PIECE]
-
-
-def second_kernel(tables, loads, stores, tok_held, grad_held):
+    for message in messages:
+        message.send()
+    for i in range(2):
+        acts, own, away = [store.ref for store in stores[i:6:2]]
+        half = own.shape[1]
+        own[...] = acts[:, :half]
+        away[...] = acts[:, half:]
+
+
+def partial_kernel(tables, loads, stores, tok_held, grad_held):
     (table,) = tables
-    weights, heard = loads[2:8], loads[8:]
-    outs = [store.ref for store in stores]
-    core, x = table[CORE], table[AT_X]
-    near = pl.ds(pl.multiple_of(x * PIECE, PIECE), PIECE)
-    far = pl.ds(pl.multiple_of((1 - x) * PIECE, PIECE), PIECE)
     for acts, held in zip(loads[:2], (tok_held, grad_held)):
         rows = acts.get()
         for slot in range(4):
@@ -180,22 +173,37 @@
             held[slot * PIECE : (slot + 1) * PIECE, :] = rows[pl.ds(start, PIECE), :]
     for which in range(3):
         held, transposed = ((tok_held, False), (grad_held, True))[which // 2]
-        pair = weights[2 * which : 2 * which + 2]
+        pair = loads[2 + 2 * which : 4 + 2 * which]
+        out = stores[which].ref
+        for at, end in spans(out.shape[1]):
+            out[:, at:end] = pair_product(held, pair, at, end, transposed)
+        stores[which].send()
+
+
+def second_kernel(tables, loads, stores):
+    (table,) = tables
+    heard = loads[3:]
+    outs = [store.ref for store in stores]
+    core, x = table[CORE], table[AT_X]
+    near = pl.ds(pl.multiple_of(x * PIECE, PIECE), PIECE)
+    far = pl.ds(pl.multiple_of((1 - x) * PIECE, PIECE), PIECE)
+    one = core == 1
+    terms = [h.get() for h in heard]
+    for which in range(3):
+        total = loads[which].get()
         for at, end in spans(outs[0].shape[2]):
-            total = pair_product(held, pair, at, end, transposed)
-            terms = [h.get() for h in heard]
             near1, near2, near3 = [h[which, near, at:end].astype(jnp.float32) for h in terms]
             far1, far2, far3 = [h[which, far, at:end].astype(jnp.float32) for h in terms]
-            sum1 = total[:PIECE] + far1 + jnp.where(core == 1, far2 + far3, 0.0)
+            part1, part2, part3, part4 = [
+                total[slot * PIECE : (slot + 1) * PIECE, at:end] for slot in range(4)
+            ]
+            sum1 = part1 + far1 + jnp.where(one, far2 + far3, 0.0)
             high = sum1.astype(jnp.bfloat16)
             rest = sum1 - high.astype(jnp.float32)
-            sum2 = jnp.where(core == 1, rest, total[PIECE : 2 * PIECE] + near2)
             outs[0][which, :, at:end] = high
-            outs[1][which, :, at:end] = sum2.astype(jnp.bfloat16)
-            outs[2][which, :, at:end] = (total[2 * PIECE : 3 * PIECE] + far2).astype(jnp.bfloat16)
-            outs[3][which, :, at:end] = (
-                total[3 * PIECE :] + near1 + jnp.where(core == 1, near2 + near3, 0.0)
-            )
+            outs[1][which, :, at:end] = jnp.where(one, rest, part2 + near2).astype(jnp.bfloat16)
+            outs[2][which, :, at:end] = (part3 + far2).astype(jnp.bfloat16)
+            outs[3][which, :, at:end] = part4 + near1 + jnp.where(one, near2 + near3, 0.0)
 
 
 def weave_kernel(tables, loads, stores):
@@ -270,25 +278,36 @@
 
 def first_stage(table, blocks, weights):
     depth, width = weights[0].shape
-    rows = shape((NY * NX * PIECE, 2 * depth))
+    rows = NY * NX * PIECE
     return call(
         first_kernel,
         [table],
         [*blocks, *weights],
-        [rows] * 2 + [shape((3, 2 * PIECE, width))] * 3,
+        [shape((rows, 2 * depth))] * 2
+        + [shape((rows, depth))] * 4
+        + [shape((3, 2 * PIECE, width))] * 3,
         [pltpu.VMEM((6 * PIECE, 2 * depth), jnp.bfloat16)] * 2,
     )
 
 
-def second_stage(table, tok_half, grad_half, weights, heard):
-    width, depth = weights[0].shape[1], weights[0].shape[0]
-    message = shape((3, PIECE, width))
+def partial_stage(table, tok_half, grad_half, weights):
+    depth, width = weights[0].shape
+    return call(
+        partial_kernel,
+        [table],
+        [tok_half, grad_half, *weights],
+        [shape((4 * PIECE, width), jnp.float32)] * 3,
+        [pltpu.VMEM((4 * PIECE, 2 * depth), jnp.bfloat16)] * 2,
+    )
+
+
+def second_stage(table, products, heard):
+    message = shape((3, PIECE, products[0].shape[1]))
     return call(
         second_kernel,
         [table],
-        [tok_half, grad_half, *weights, *heard],
+        [*products, *heard],
         [message] * 3 + [shape(message.shape, jnp.float32)],
-        [pltpu.VMEM((4 * PIECE, 2 * depth), jnp.bfloat16)] * 2,
     )
 
 
@@ -361,30 +380,26 @@
     width, ff_width = gate_weight.shape
     half_rows = NY * NX * PIECE
 
-    pairs = [[i, i + 1] for i in range(0, NY * NX * NC, NC)]
-    gate_other, up_other, down_other = [
-        OfOther(lax.all_gather(weight, "row", axis_index_groups=pairs))
-        for weight in (gate_weight, up_weight, down_weight)
-    ]
+    gate_other, up_other, down_other = flip(gate_weight), flip(up_weight), flip(down_weight)
     mine = jnp.stack([tokens, grad_output])
     own_block = jnp.concatenate([mine, flip(mine)], axis=2)
-    blocks = [lax.ppermute(own_block, BOTH, gather_perm(step)) for step in range(NZ)]
+    starts = [own_block, own_block, after(own_block, gate_other), after(own_block, up_other)]
+    blocks = [lax.ppermute(starts[step], BOTH, gather_perm(step)) for step in range(NZ)]
 
     both_weights = [gate_weight, gate_other, up_weight, up_other]
     weights = [*both_weights, down_weight, down_other]
-    tok_half, grad_half, *sent = first_stage(table, [own_block, *blocks], weights)
+    tok_half, grad_half, tok_own, grad_own, tok_away, grad_away, *sent = first_stage(
+        table, [own_block, *blocks], weights
+    )
     heard = send_first(sent)
-    halves = after(jnp.stack([tok_half[:, width:], grad_half[:, width:]]), sent[0])
-    tok_other, grad_other = flip(halves)
-    tok_own = tok_half[:, :width]
+    products = partial_stage(table, tok_half, grad_half, weights)
+    tok_other = flip(after(tok_away, products[0]))
+    grad_other = flip(after(grad_away, products[0]))
     (grad_all,) = call(
-        weave_kernel,
-        [table],
-        [grad_half[:, :width], grad_other],
-        [shape((2 * half_rows, width))],
+        weave_kernel, [table], [grad_own, grad_other], [shape((2 * half_rows, width))]
     )
     *heard, grad_all, tok_other = lax.optimization_barrier((*heard, grad_all, tok_other))
-    *sent, kept = second_stage(table, tok_half, grad_half, weights, heard)
+    *sent, kept = second_stage(table, products, heard)
     hidden, d_own = call(
         unit_kernel,
         [],
@@ -398,6 +413,13 @@
         pack_kernel, [table], [d_own, *near], [shape((2, 2 * PIECE, ff_width))] * 2
     )
     far = send_first([first, second, first])
+    dot = functools.partial(lax.dot_general, preferred_element_type=jnp.float32)
+    contract_first = (((0,), (0,)), ((), ()))
+    hidden = after(hidden, far[0])
+    near_sum, send = col_blocks(jnp.dot(hidden, down_weight, preferred_element_type=jnp.float32))
+    near_sum, send = lax.optimization_barrier((near_sum, send))
+    layer_output = col_second(*col_first(near_sum, send))
+    *far, _ = lax.optimization_barrier((*far, send))
     block = shape((NX * PIECE, 2 * width))
     *messages, d_set, kept = call(
         input_kernel,
@@ -405,13 +427,8 @@
         [d_own, *near, *far, gate_weight, up_weight, gate_other, up_other],
         [block] * 4 + [shape((2, half_rows, ff_width)), shape(block.shape, jnp.float32)],
     )
-    hidden = after(hidden, kept)
     messages = [lax.ppermute(messages[k], BOTH, scatter_perm(k)) for k in range(NZ)]
     d_other = flip(d_set)
-    dot = functools.partial(lax.dot_general, preferred_element_type=jnp.float32)
-    contract_first = (((0,), (0,)), ((), ()))
-    near_sum, send = col_blocks(jnp.dot(hidden, down_weight, preferred_element_type=jnp.float32))
-    layer_output = col_second(*col_first(near_sum, send))
     grad_down = dot(hidden, grad_all, contract_first).astype(jnp.bfloat16)
 
     def weight_gradient(which):

time: 281 us -> 247 us (0.88)
  the two profiles are of different devices: /device:TPU:0 before, /device:TPU:17 now
where the time goes in v5:
time: 247 us; the launch traced here: 243 us
  waiting for transfers between devices  95.1 us (39%)
  starting transfers between devices  60.4 us (24%)
  Pallas kernels  46.7 us (19%)
  between operations  15.1 us (6%)
  matrix products  15 us (6%)
  local copies, waits for them, and re-layouts  6.89 us (3%)
  other arithmetic  3.73 us (2%)
    pallas_call x7, Pallas kernels, call(): pl.pallas_call(run, in_specs=[smem] * n_tables + [any_space] * n_in, out_...  46.7 us
    ppermute x2, waiting for transfers between devices, send_first(): lax.ppermute(sent[0], 'row', row_perm(over_x, over_y(1)))  33.6 us
    ppermute x4, waiting for transfers between devices, body(): lax.ppermute(starts[step], BOTH, gather_perm(step))  18.7 us
    ppermute x2, waiting for transfers between devices, send_second(): lax.ppermute(sent[1], 'row', row_perm(over_y(-1), over_x))  13.4 us
    ppermute x2, waiting for transfers between devices, send_second(): lax.ppermute(sent[0], 'row', row_perm(over_y(1), over_x))  13.4 us
    ppermute x4, starting transfers between devices, body(): lax.ppermute(messages[k], BOTH, scatter_perm(k))  12.7 us
    ppermute x8, starting transfers between devices, body(): flip = lambda value: lax.ppermute(value, 'row', CORE_FLIP)  12.3 us
    ppermute x4, starting transfers between devices, body(): lax.ppermute(starts[step], BOTH, gather_perm(step))  11.6 us
  transfers between devices with their start and end apart: 33, of which 14 were waited for; matrix products, arithmetic and copies ran while one was open for 8% of the time, Pallas kernels for 6%

profile of v5, /device:TPU:17, one launch (start us, length us, event | category | flops | bytes accessed | tf_op | source)
XLA Modules:
  0.0 242.9 jit_solution(7425205629875353241)
XLA Ops:
  9.6 4.2 %collective-permute-done = bf16[2,128,512]{2,1,0:T(8,128)(2,1)S(1)} collective-permute-done((bf16[2,128,512]{2,1,0:T(8,128)(2,1)S(1)}, bf16[2,128,512]{2,1,0:T(8,128)(2,1)S(1)}, u32[]{:S(2)}, u32[]{:S(2)}) %collective-permute-start) | collective-permute-done | bytes 262176 | tf_op jit(solution)/shard_map/ppermute | solution.py:378
  14.8 6.3 %collective-permute-start.2 = (bf16[2,128,1024]{2,1,0:T(8,128)(2,1)S(1)}, bf16[2,128,1024]{2,1,0:T(8,128)(2,1)S(1)}, u32[]{:S(2)}, u32[]{:S(2)}) collective-permute-start(bf16[2,128,1024]{2,1,0:T(8,128)(2,1)S(1)} %pad_maximum_fusion.refs_1_), channel_id=1, source_target_pairs={{1,0},{2,1},{3,2},{0,3},{5,4},{6,5},{7,6},{4,7},{13,8},{14,9},{15,... | collective-permute-start | bytes 1572872 | tf_op jit(solution)/shard_map/ppermute | solution.py:387
  27.7 5.9 %collective-permute-done.1.refs_2_ = bf16[2,128,1024]{2,1,0:T(8,128)(2,1)S(1)} collective-permute-done((bf16[2,128,1024]{2,1,0:T(8,128)(2,1)S(1)}, bf16[2,128,1024]{2,1,0:T(8,128)(2,1)S(1)}, u32[]{:S(2)}, u32[]{:S(2)}) %collective-permute-start.1) | collective-permute-done | bytes 524320 | tf_op jit(solution)/shard_map/ppermute | solution.py:387
  33.6 5.5 %collective-permute-done.4.refs_4_ = bf16[2,128,1024]{2,1,0:T(8,128)(2,1)} collective-permute-done((bf16[2,128,1024]{2,1,0:T(8,128)(2,1)S(1)}, bf16[2,128,1024]{2,1,0:T(8,128)(2,1)}, u32[]{:S(2)}, u32[]{:S(2)}) %collective-permute-start.4) | collective-permute-done | bytes 524320 | tf_op jit(solution)/shard_map/ppermute | solution.py:387
  39.1 7.3 %collective-permute-done.6.refs_5_ = bf16[2,128,1024]{2,1,0:T(8,128)(2,1)} collective-permute-done((bf16[2,128,1024]{2,1,0:T(8,128)(2,1)S(1)}, bf16[2,128,1024]{2,1,0:T(8,128)(2,1)}, u32[]{:S(2)}, u32[]{:S(2)}) %collective-permute-start.6) | collective-permute-done | bytes 524320 | tf_op jit(solution)/shard_map/ppermute | solution.py:387
  46.4 11.7 %shard_map.101 = (bf16[512,1024]{1,0:T(8,128)(2,1)}, bf16[512,1024]{1,0:T(8,128)(2,1)}, bf16[512,512]{1,0:T(8,128)(2,1)}, bf16[512,512]{1,0:T(8,128)(2,1)}, bf16...) custom-call(s32[20]{0:T(128)} %get-tuple-element.103.refs_0_, ...), custom_call_target="tpu_custom_call" | custom-call | flops 1 | bytes 1 | tf_op jit(solution)/shard_map/pallas_call | solution.py:113
  62.9 8.5 %shard_map.102 = (f32[256,1792]{1,0:T(8,128)}, f32[256,1792]{1,0:T(8,128)}, f32[256,1792]{1,0:T(8,128)}) custom-call(s32[20]{0:T(128)} %get-tuple-element.103.refs_0_, bf16[512,1024]{1,0:T(8,128)(2,1)} %get-tuple-element.54.refs_1_, bf16[512,1024]{1,0:T(8,128)(2,1)} %get-tuple-element.55.refs_2_, bf16[512,1792]{1,0:T(8,128)(2,1)} %refs_8_.3, ...), custom_call_target="tpu_custom_call" | custom-call | flops 1 | bytes 1 | tf_op jit(solution)/shard_map/pallas_call | solution.py:113
  77.3 13.2 %collective-permute-done.8.refs_4_ = bf16[3,128,1792]{2,1,0:T(8,128)(2,1)S(1)} collective-permute-done((bf16[3,128,1792]{2,1,0:T(8,128)(2,1)}, bf16[3,128,1792]{2,1,0:T(8,128)(2,1)S(1)}, u32[]{:S(2)}, u32[]{:S(2)}) %collective-permute-start.8) | collective-permute-done | bytes 1376288 | tf_op jit(solution)/shard_map/ppermute | solution.py:316
  92.6 7.0 %shard_map.104 = (bf16[3,64,1792]{2,1,0:T(8,128)(2,1)}, bf16[3,64,1792]{2,1,0:T(8,128)(2,1)}, bf16[3,64,1792]{2,1,0:T(8,128)(2,1)}, f32[3,64,1792]{2,1,0:T(8,128)}) custom-call(s32[20]{0:T(128)} %get-tuple-element.103.refs_0_, f32[256,1792]{1,0:T(8,128)} %get-tuple-element.56.refs_1_, f32[256,1792]{1,0:T(8,128)} %get-tuple-element.57.refs_2_, ...), custom_call_target="tpu_custom_call" | custom-call | flops 1 | bytes 1 | tf_op jit(solution)/shard_map/pallas_call | solution.py:113
  101.8 8.1 %collective-permute-done.13.refs_1_ = bf16[3,64,1792]{2,1,0:T(8,128)(2,1)S(1)} collective-permute-done((bf16[3,64,1792]{2,1,0:T(8,128)(2,1)}, bf16[3,64,1792]{2,1,0:T(8,128)(2,1)S(1)}, u32[]{:S(2)}, u32[]{:S(2)}) %collective-permute-start.13) | collective-permute-done | bytes 688160 | tf_op jit(solution)/shard_map/ppermute | solution.py:324
  109.9 7.4 %collective-permute-done.14.refs_2_ = bf16[3,64,1792]{2,1,0:T(8,128)(2,1)S(1)} collective-permute-done((bf16[3,64,1792]{2,1,0:T(8,128)(2,1)}, bf16[3,64,1792]{2,1,0:T(8,128)(2,1)S(1)}, u32[]{:S(2)}, u32[]{:S(2)}) %collective-permute-start.14) | collective-permute-done | bytes 688160 | tf_op jit(solution)/shard_map/ppermute | solution.py:325
  124.1 6.1 %collective-permute-done.17.refs_3_ = bf16[2,64,1792]{2,1,0:T(8,128)(2,1)S(1)} collective-permute-done((bf16[2,64,1792]{2,1,0:T(8,128)(2,1)}, bf16[2,64,1792]{2,1,0:T(8,128)(2,1)S(1)}, u32[]{:S(2)}, u32[]{:S(2)}) %collective-permute-start.17) | collective-permute-done | bytes 458784 | tf_op jit(solution)/shard_map/ppermute | solution.py:325
  130.2 5.3 %collective-permute-done.16.refs_2_ = bf16[2,64,1792]{2,1,0:T(8,128)(2,1)S(1)} collective-permute-done((bf16[2,64,1792]{2,1,0:T(8,128)(2,1)}, bf16[2,64,1792]{2,1,0:T(8,128)(2,1)S(1)}, u32[]{:S(2)}, u32[]{:S(2)}) %collective-permute-start.16) | collective-permute-done | bytes 458784 | tf_op jit(solution)/shard_map/ppermute | solution.py:324
  136.3 3.4 %shard_map.106 = (bf16[2,128,1792]{2,1,0:T(8,128)(2,1)}, bf16[2,128,1792]{2,1,0:T(8,128)(2,1)}) custom-call(s32[20]{0:T(128)} %get-tuple-element.103.refs_0_, bf16[2,64,1792]{2,1,0:T(8,128)(2,1)} %get-tuple-element.75.refs_1_, bf16[2,64,1792]{2,1,0:T(8,128)(2,1)} %copy-done.8, bf16[2,64,1792]{2,1,0:T(8,128)(2,1)} %copy-done.7, bf16[2,64,1792]{2,1,0:T(8,128)(2,1)} %copy-done.6), custom_call_target="tpu_custom_call" | custom-call | flops 1 | bytes 1 | tf_op jit(solution)/shard_map/pallas_call | solution.py:113
  142.9 5.1 %collective-permute-start.25 = (bf16[2,128,1792]{2,1,0:T(8,128)(2,1)}, bf16[2,128,1792]{2,1,0:T(8,128)(2,1)}, u32[]{:S(2)}, u32[]{:S(2)}) collective-permute-start(bf16[2,128,1792]{2,1,0:T(8,128)(2,1)} %get-tuple-element.76), channel_id=1, source_target_pairs={{8,72},{24,88},{40,104},{56,120},{72,8},{88,24},{104,40},{120,56},... | collective-permute-start | bytes 2752520 | tf_op jit(solution)/shard_map/ppermute | solution.py:318
  148.0 20.3 %collective-permute-done.19.refs_5_ = bf16[2,128,1792]{2,1,0:T(8,128)(2,1)S(1)} collective-permute-done((bf16[2,128,1792]{2,1,0:T(8,128)(2,1)}, bf16[2,128,1792]{2,1,0:T(8,128)(2,1)S(1)}, u32[]{:S(2)}, u32[]{:S(2)}) %collective-permute-start.19) | collective-permute-done | bytes 917536 | tf_op jit(solution)/shard_map/ppermute | solution.py:316
  168.3 4.4 %fusion.11 = f32[1024,512]{1,0:T(8,128)S(1)} fusion(bf16[1024,1792]{1,0:T(8,128)(2,1)} %all-gather.2.cloned.1.call-done, bf16[1792,512]{1,0:T(8,128)(2,1)S(1)} %copy-done.1), kind=kOutput, calls=%fused_computation.28 | convolution fusion | flops 1879048192 | bytes 7602176 | tf_op jit(solution)/shard_map/dot_general | solution.py:419
  172.9 5.1 %collective-permute-done.25.refs_7_ = bf16[2,128,1792]{2,1,0:T(8,128)(2,1)} collective-permute-done((bf16[2,128,1792]{2,1,0:T(8,128)(2,1)}, bf16[2,128,1792]{2,1,0:T(8,128)(2,1)}, u32[]{:S(2)}, u32[]{:S(2)}) %collective-permute-start.25) | collective-permute-done | bytes 917536 | tf_op jit(solution)/shard_map/ppermute | solution.py:318
  177.9 9.7 %shard_map.107 = (bf16[128,1024]{1,0:T(8,128)(2,1)}, bf16[128,1024]{1,0:T(8,128)(2,1)}, bf16[128,1024]{1,0:T(8,128)(2,1)}, bf16[128,1024]{1,0:T(8,128)(2,1)}, bf...) custom-call(s32[20]{0:T(128)} %get-tuple-element.103.refs_0_, bf16[2,64,1792]{2,1,0:T(8,128)(2,1)} %get-tuple-element.75.refs_1_, ...), custom_call_target="tpu_custom_call" | custom-call | flops 1 | bytes 1 | tf_op jit(solution)/shard_map/pallas_call | solution.py:113
  187.7 10.2 %collective-permute-start.30 = (bf16[2,512,1792]{2,1,0:T(8,128)(2,1)}, bf16[2,512,1792]{2,1,0:T(8,128)(2,1)S(1)}, u32[]{:S(2)}, u32[]{:S(2)}) collective-permute-start(bf16[2,512,1792]{2,1,0:T(8,128)(2,1)} %get-tuple-element.90), channel_id=1, source_target_pairs={{0,8},{8,0},{16,24},{24,16},{32,40},{40,32},{48,56},{56,48},{64,72... | collective-permute-start | bytes 11010056 | tf_op jit(solution)/shard_map/ppermute | solution.py:378
  201.9 6.3 %collective-permute-start.26 = (bf16[128,1024]{1,0:T(8,128)(2,1)}, bf16[128,1024]{1,0:T(8,128)(2,1)S(1)}, u32[]{:S(2)}, u32[]{:S(2)}) collective-permute-start(bf16[128,1024]{1,0:T(8,128)(2,1)} %get-tuple-element.85), channel_id=1, source_target_pairs={{8,12},{9,13},{10,14},{11,15},{12,8},{13,9},{14,10},{15,11},{24,28... | collective-permute-start | bytes 786440 | tf_op jit(solution)/shard_map/ppermute | solution.py:430
  208.2 4.6 %collective-permute-done.20 = bf16[2,2,64,512]{3,2,1,0:T(8,128)(2,1)S(1)} collective-permute-done((bf16[2,2,64,512]{3,2,1,0:T(8,128)(2,1)S(1)}, bf16[2,2,64,512]{3,2,1,0:T(8,128)(2,1)S(1)}, u32[]{:S(2)}, u32[]{:S(2)}) %collective-permute-start.20) | collective-permute-done | bytes 262176 | tf_op jit(solution)/shard_map/ppermute | solution.py:364
  215.6 3.6 %collective-permute-start.29 = (bf16[128,1024]{1,0:T(8,128)(2,1)}, bf16[128,1024]{1,0:T(8,128)(2,1)S(1)}, u32[]{:S(2)}, u32[]{:S(2)}) collective-permute-start(bf16[128,1024]{1,0:T(8,128)(2,1)} %get-tuple-element.88), channel_id=1, source_target_pairs={{0,3},{1,0},{2,1},{3,2},{4,7},{5,4},{6,5},{7,6},{8,15},{9,12},{10,... | collective-permute-start | bytes 786440 | tf_op jit(solution)/shard_map/ppermute | solution.py:430
  219.4 3.4 %collective-permute-start.23 = (bf16[2,64,512]{2,1,0:T(8,128)(2,1)S(1)}, bf16[2,64,512]{2,1,0:T(8,128)(2,1)S(1)}, u32[]{:S(2)}, u32[]{:S(2)}) collective-permute-start(bf16[2,64,512]{2,1,0:T(8,128)(2,1)S(1)} %fusion.9), channel_id=1, source_target_pairs={{0,4},{1,5},{2,6},{3,7},{4,0},{5,1},{6,2},{7,3},{8,12},{9,13},{10,... | collective-permute-start | bytes 393224 | tf_op jit(solution)/shard_map/ppermute | solution.py:369
  (118 shorter events, 55.2 us)
Async XLA Ops:
  7.2 161.1 %all-gather.2.cloned.1.call-start = ((), (), s32[]{:S(2)}) async-start(), calls=%async_computation | async-start | bytes 3899392 | tf_op jit(solution)/shard_map/all_gather | solution.py:409
  7.2 16.1 %collective-permute-start.3 = (bf16[512,1792]{1,0:T(8,128)(2,1)}, bf16[512,1792]{1,0:T(8,128)(2,1)S(1)}, u32[]{:S(2)}, u32[]{:S(2)}) collective-permute-start(bf16[512,1792]{1,0:T(8,128)(2,1)} %refs_8_.3), channel_id=1, source_target_pairs={{0,8},{8,0},{16,24},{24,16},{32,40},{40,32},{48,56},{56,48},{64,72... | collective-permute-start | bytes 5505032 | tf_op jit(solution)/shard_map/ppermute | solution.py:378
  8.0 17.5 %collective-permute-start.5 = (bf16[512,1792]{1,0:T(8,128)(2,1)}, bf16[512,1792]{1,0:T(8,128)(2,1)}, u32[]{:S(2)}, u32[]{:S(2)}) collective-permute-start(bf16[512,1792]{1,0:T(8,128)(2,1)} %refs_9_.1), channel_id=1, source_target_pairs={{0,8},{8,0},{16,24},{24,16},{32,40},{40,32},{48,56},{56,48},{64,72... | collective-permute-start | bytes 5505032 | tf_op jit(solution)/shard_map/ppermute | solution.py:378
  8.1 25.5 %collective-permute-start.7 = (bf16[1792,512]{1,0:T(8,128)(2,1)}, bf16[1792,512]{1,0:T(8,128)(2,1)}, u32[]{:S(2)}, u32[]{:S(2)}) collective-permute-start(bf16[1792,512]{1,0:T(8,128)(2,1)} %refs_7_.1), channel_id=1, source_target_pairs={{0,8},{8,0},{16,24},{24,16},{32,40},{40,32},{48,56},{56,48},{64,72... | collective-permute-start | bytes 5505032 | tf_op jit(solution)/shard_map/ppermute | solution.py:378
  14.8 12.8 %collective-permute-start.2 = (bf16[2,128,1024]{2,1,0:T(8,128)(2,1)S(1)}, bf16[2,128,1024]{2,1,0:T(8,128)(2,1)S(1)}, u32[]{:S(2)}, u32[]{:S(2)}) collective-permute-start(bf16[2,128,1024]{2,1,0:T(8,128)(2,1)S(1)} %pad_maximum_fusion.refs_1_), channel_id=1, source_target_pairs={{1,0},{2,1},{3,2},{0,3},{5,4},{6,5},{7,6},{4,7},{13,8},{14,9},{15,... | collective-permute-start | bytes 1572872 | tf_op jit(solution)/shard_map/ppermute | solution.py:387
  23.3 15.8 %collective-permute-start.4 = (bf16[2,128,1024]{2,1,0:T(8,128)(2,1)S(1)}, bf16[2,128,1024]{2,1,0:T(8,128)(2,1)}, u32[]{:S(2)}, u32[]{:S(2)}) collective-permute-start(bf16[2,128,1024]{2,1,0:T(8,128)(2,1)S(1)} %pad_maximum_fusion.refs_1_), channel_id=1, source_target_pairs={{2,0},{3,1},{0,2},{1,3},{6,4},{7,5},{4,6},{5,7},{14,8},{15,9},{12,... | collective-permute-start | bytes 1572872 | tf_op jit(solution)/shard_map/ppermute | solution.py:387
  25.5 20.8 %collective-permute-start.6 = (bf16[2,128,1024]{2,1,0:T(8,128)(2,1)S(1)}, bf16[2,128,1024]{2,1,0:T(8,128)(2,1)}, u32[]{:S(2)}, u32[]{:S(2)}) collective-permute-start(bf16[2,128,1024]{2,1,0:T(8,128)(2,1)S(1)} %pad_maximum_fusion.refs_1_), channel_id=1, source_target_pairs={{3,0},{0,1},{1,2},{2,3},{7,4},{4,5},{5,6},{6,7},{15,8},{12,9},{13,... | collective-permute-start | bytes 1572872 | tf_op jit(solution)/shard_map/ppermute | solution.py:387
  58.1 32.5 %collective-permute-start.8 = (bf16[3,128,1792]{2,1,0:T(8,128)(2,1)}, bf16[3,128,1792]{2,1,0:T(8,128)(2,1)S(1)}, u32[]{:S(2)}, u32[]{:S(2)}) collective-permute-start(bf16[3,128,1792]{2,1,0:T(8,128)(2,1)} %get-tuple-element.59), channel_id=1, source_target_pairs={{0,16},{8,40},{16,0},{24,56},{32,48},{40,72},{48,32},{56,88},{64,8... | collective-permute-start | bytes 4128776 | tf_op jit(solution)/shard_map/ppermute | solution.py:316
  59.1 31.4 %collective-permute-start.9 = (bf16[3,128,1792]{2,1,0:T(8,128)(2,1)}, bf16[3,128,1792]{2,1,0:T(8,128)(2,1)S(1)}, u32[]{:S(2)}, u32[]{:S(2)}) collective-permute-start(bf16[3,128,1792]{2,1,0:T(8,128)(2,1)} %get-tuple-element.60), channel_id=1, source_target_pairs={{0,16},{8,104},{16,0},{24,120},{32,48},{40,8},{48,32},{56,24},{64,... | collective-permute-start | bytes 4128776 | tf_op jit(solution)/shard_map/ppermute | solution.py:317
  59.6 31.0 %collective-permute-start.10 = (bf16[3,128,1792]{2,1,0:T(8,128)(2,1)}, bf16[3,128,1792]{2,1,0:T(8,128)(2,1)S(1)}, u32[]{:S(2)}, u32[]{:S(2)}) collective-permute-start(bf16[3,128,1792]{2,1,0:T(8,128)(2,1)} %get-tuple-element.61), channel_id=1, source_target_pairs={{8,72},{24,88},{40,104},{56,120},{72,8},{88,24},{104,40},{120,56},... | collective-permute-start | bytes 4128776 | tf_op jit(solution)/shard_map/ppermute | solution.py:318
  100.6 16.7 %collective-permute-start.14 = (bf16[3,64,1792]{2,1,0:T(8,128)(2,1)}, bf16[3,64,1792]{2,1,0:T(8,128)(2,1)S(1)}, u32[]{:S(2)}, u32[]{:S(2)}) collective-permute-start(bf16[3,64,1792]{2,1,0:T(8,128)(2,1)} %get-tuple-element.72), channel_id=1, source_target_pairs={{0,96},{8,24},{16,112},{24,8},{32,0},{40,56},{48,16},{56,40},{64,3... | collective-permute-start | bytes 2064392 | tf_op jit(solution)/shard_map/ppermute | solution.py:325
  101.1 16.2 %collective-permute-start.15 = (bf16[3,64,1792]{2,1,0:T(8,128)(2,1)}, bf16[3,64,1792]{2,1,0:T(8,128)(2,1)S(1)}, u32[]{:S(2)}, u32[]{:S(2)}) collective-permute-start(bf16[3,64,1792]{2,1,0:T(8,128)(2,1)} %get-tuple-element.73), channel_id=1, source_target_pairs={{0,64},{16,80},{32,96},{48,112},{64,0},{80,16},{96,32},{112,48},{1... | collective-permute-start | bytes 2064392 | tf_op jit(solution)/shard_map/ppermute | solution.py:326
  139.8 28.5 %collective-permute-start.19 = (bf16[2,128,1792]{2,1,0:T(8,128)(2,1)}, bf16[2,128,1792]{2,1,0:T(8,128)(2,1)S(1)}, u32[]{:S(2)}, u32[]{:S(2)}) collective-permute-start(bf16[2,128,1792]{2,1,0:T(8,128)(2,1)} %get-tuple-element.76), channel_id=1, source_target_pairs={{0,16},{8,40},{16,0},{24,56},{32,48},{40,72},{48,32},{56,88},{64,8... | collective-permute-start | bytes 2752520 | tf_op jit(solution)/shard_map/ppermute | solution.py:316
  142.9 30.0 %collective-permute-start.24 = (bf16[2,128,1792]{2,1,0:T(8,128)(2,1)}, bf16[2,128,1792]{2,1,0:T(8,128)(2,1)}, u32[]{:S(2)}, u32[]{:S(2)}) collective-permute-start(bf16[2,128,1792]{2,1,0:T(8,128)(2,1)} %get-tuple-element.80), channel_id=1, source_target_pairs={{0,16},{8,104},{16,0},{24,120},{32,48},{40,8},{48,32},{56,24},{64,... | collective-permute-start | bytes 2752520 | tf_op jit(solution)/shard_map/ppermute | solution.py:317
  142.9 35.1 %collective-permute-start.25 = (bf16[2,128,1792]{2,1,0:T(8,128)(2,1)}, bf16[2,128,1792]{2,1,0:T(8,128)(2,1)}, u32[]{:S(2)}, u32[]{:S(2)}) collective-permute-start(bf16[2,128,1792]{2,1,0:T(8,128)(2,1)} %get-tuple-element.76), channel_id=1, source_target_pairs={{8,72},{24,88},{40,104},{56,120},{72,8},{88,24},{104,40},{120,56},... | collective-permute-start | bytes 2752520 | tf_op jit(solution)/shard_map/ppermute | solution.py:318
  187.7 31.7 %collective-permute-start.30 = (bf16[2,512,1792]{2,1,0:T(8,128)(2,1)}, bf16[2,512,1792]{2,1,0:T(8,128)(2,1)S(1)}, u32[]{:S(2)}, u32[]{:S(2)}) collective-permute-start(bf16[2,512,1792]{2,1,0:T(8,128)(2,1)} %get-tuple-element.90), channel_id=1, source_target_pairs={{0,8},{8,0},{16,24},{24,16},{32,40},{40,32},{48,56},{56,48},{64,72... | collective-permute-start | bytes 11010056 | tf_op jit(solution)/shard_map/ppermute | solution.py:378
  198.0 14.8 %collective-permute-start.20 = (bf16[2,2,64,512]{3,2,1,0:T(8,128)(2,1)S(1)}, bf16[2,2,64,512]{3,2,1,0:T(8,128)(2,1)S(1)}, u32[]{:S(2)}, u32[]{:S(2)}) collective-permute-start(bf16[2,2,64,512]{3,2,1,0:T(8,128)(2,1)S(1)} %get-tuple-element.99), channel_id=1, source_target_pairs={{0,1},{1,2},{2,3},{3,0},{4,5},{5,6},{6,7},{7,4},{8,9},{9,10},{10,1... | collective-permute-start | bytes 786440 | tf_op jit(solution)/shard_map/ppermute | solution.py:364
  198.0 14.7 %collective-permute-start.22 = (bf16[2,2,64,512]{3,2,1,0:T(8,128)(2,1)S(1)}, bf16[2,2,64,512]{3,2,1,0:T(8,128)(2,1)S(1)}, u32[]{:S(2)}, u32[]{:S(2)}) collective-permute-start(bf16[2,2,64,512]{3,2,1,0:T(8,128)(2,1)S(1)} %get-tuple-element.100), channel_id=1, source_target_pairs={{0,3},{1,0},{2,1},{3,2},{4,7},{5,4},{6,5},{7,6},{8,11},{9,8},{10,9... | collective-permute-start | bytes 786440 | tf_op jit(solution)/shard_map/ppermute | solution.py:364
  200.7 14.9 %collective-permute-start.21 = (bf16[2,2,64,512]{3,2,1,0:T(8,128)(2,1)S(1)}, bf16[2,2,64,512]{3,2,1,0:T(8,128)(2,1)S(1)}, u32[]{:S(2)}, u32[]{:S(2)}) collective-permute-start(bf16[2,2,64,512]{3,2,1,0:T(8,128)(2,1)S(1)} %get-tuple-element.101), channel_id=1, source_target_pairs={{0,2},{1,3},{2,0},{3,1},{4,6},{5,7},{6,4},{7,5},{8,10},{9,11},{10,... | collective-permute-start | bytes 786440 | tf_op jit(solution)/shard_map/ppermute | solution.py:364
  201.9 28.1 %collective-permute-start.26 = (bf16[128,1024]{1,0:T(8,128)(2,1)}, bf16[128,1024]{1,0:T(8,128)(2,1)S(1)}, u32[]{:S(2)}, u32[]{:S(2)}) collective-permute-start(bf16[128,1024]{1,0:T(8,128)(2,1)} %get-tuple-element.85), channel_id=1, source_target_pairs={{8,12},{9,13},{10,14},{11,15},{12,8},{13,9},{14,10},{15,11},{24,28... | collective-permute-start | bytes 786440 | tf_op jit(solution)/shard_map/ppermute | solution.py:430
  212.8 17.3 %collective-permute-start.27 = (bf16[128,1024]{1,0:T(8,128)(2,1)}, bf16[128,1024]{1,0:T(8,128)(2,1)S(1)}, u32[]{:S(2)}, u32[]{:S(2)}) collective-permute-start(bf16[128,1024]{1,0:T(8,128)(2,1)} %get-tuple-element.86), channel_id=1, source_target_pairs={{0,1},{1,2},{2,3},{3,0},{4,5},{5,6},{6,7},{7,4},{8,13},{9,14},{10,... | collective-permute-start | bytes 786440 | tf_op jit(solution)/shard_map/ppermute | solution.py:430
  212.8 17.3 %collective-permute-start.28 = (bf16[128,1024]{1,0:T(8,128)(2,1)}, bf16[128,1024]{1,0:T(8,128)(2,1)S(1)}, u32[]{:S(2)}, u32[]{:S(2)}) collective-permute-start(bf16[128,1024]{1,0:T(8,128)(2,1)} %get-tuple-element.87), channel_id=1, source_target_pairs={{0,2},{1,3},{2,0},{3,1},{4,6},{5,7},{6,4},{7,5},{8,14},{9,15},{10,... | collective-permute-start | bytes 786440 | tf_op jit(solution)/shard_map/ppermute | solution.py:430
  215.6 15.2 %collective-permute-start.29 = (bf16[128,1024]{1,0:T(8,128)(2,1)}, bf16[128,1024]{1,0:T(8,128)(2,1)S(1)}, u32[]{:S(2)}, u32[]{:S(2)}) collective-permute-start(bf16[128,1024]{1,0:T(8,128)(2,1)} %get-tuple-element.88), channel_id=1, source_target_pairs={{0,3},{1,0},{2,1},{3,2},{4,7},{5,4},{6,5},{7,6},{8,15},{9,12},{10,... | collective-permute-start | bytes 786440 | tf_op jit(solution)/shard_map/ppermute | solution.py:430
  219.4 15.2 %collective-permute-start.23 = (bf16[2,64,512]{2,1,0:T(8,128)(2,1)S(1)}, bf16[2,64,512]{2,1,0:T(8,128)(2,1)S(1)}, u32[]{:S(2)}, u32[]{:S(2)}) collective-permute-start(bf16[2,64,512]{2,1,0:T(8,128)(2,1)S(1)} %fusion.9), channel_id=1, source_target_pairs={{0,4},{1,5},{2,6},{3,7},{4,0},{5,1},{6,2},{7,3},{8,12},{9,13},{10,... | collective-permute-start | bytes 393224 | tf_op jit(solution)/shard_map/ppermute | solution.py:369
  (34 other events, 311.3 us)
Sparse Core Ops, SparseCore 0:
  121.9 45.4 all-gather.1

commit v6 on v5

--- a/solution.py
+++ b/solution.py
@@ -81,34 +81,51 @@
 
 
 class Store:
-    def __init__(self, source, target, sem):
-        self.ref, self.copy, self.sent = source, pltpu.make_async_copy(source, target, sem), False
-
-    def send(self):
-        self.copy.start()
-        self.sent = True
-
-
-def call(kernel, tables, operands, out_shape, scratch=()):
+    def __init__(self, source, target, sems):
+        self.ref, self.target, self.sems, self.copies = source, target, sems, []
+
+    def send(self, part=None):
+        i = len(self.copies)
+        source, target = self.ref, self.target
+        if part is not None:
+            source, target = source.at[part], target.at[part]
+        self.copies.append(pltpu.make_async_copy(source, target, self.sems.at[i]))
+        self.copies[-1].start()
+
+
+class Raw:
+    def __init__(self, value):
+        self.value = value
+
+
+def call(kernel, tables, operands, out_shape, scratch=(), limit=56):
+    raw = [isinstance(o, Raw) for o in operands]
+    operands = [o.value if isinstance(o, Raw) else o for o in operands]
     any_space = pl.BlockSpec(memory_space=pl.ANY)
     smem = pl.BlockSpec(memory_space=pltpu.SMEM)
     n_tables, n_in, n_out, n_own = len(tables), len(operands), len(out_shape), len(scratch)
+    buffers = [o for o, is_raw in zip(operands, raw) if not is_raw]
 
     def run(*refs):
         refs = list(refs)
         take = lambda count: [refs.pop(0) for _ in range(count)]
         table_refs, ins, outs, own = take(n_tables), take(n_in), take(n_out), take(n_own)
-        in_buffers, out_buffers, (in_sems, out_sems) = take(n_in), take(n_out), take(2)
-        loads = [Load(ins[i], in_buffers[i], in_sems.at[i]) for i in range(n_in)]
-        stores = [Store(out_buffers[i], outs[i], out_sems.at[i]) for i in range(n_out)]
+        in_buffers, out_buffers = take(len(buffers)), take(n_out)
+        (in_sems,), out_sems = take(1), take(n_out)
+        loads = []
+        for i, ref in enumerate(ins):
+            loads.append(ref if raw[i] else Load(ref, in_buffers.pop(0), in_sems.at[i]))
+        stores = [Store(*three) for three in zip(out_buffers, outs, out_sems)]
         kernel(table_refs, loads, stores, *own)
         for load in loads:
-            load.get()
+            if isinstance(load, Load):
+                load.get()
         for store in stores:
-            if not store.sent:
+            if not store.copies:
                 store.send()
         for store in stores:
-            store.copy.wait()
+            for copy in store.copies:
+                copy.wait()
 
     return pl.pallas_call(
         run,
@@ -117,11 +134,11 @@
         out_shape=out_shape,
         scratch_shapes=[
             *scratch,
-            *[pltpu.VMEM(o.shape, o.dtype) for o in [*operands, *out_shape]],
+            *[pltpu.VMEM(o.shape, o.dtype) for o in [*buffers, *out_shape]],
             pltpu.SemaphoreType.DMA((n_in,)),
-            pltpu.SemaphoreType.DMA((n_out,)),
+            *[pltpu.SemaphoreType.DMA((3,))] * n_out,
         ],
-        compiler_params=pltpu.CompilerParams(vmem_limit_bytes=56 * 2**20),
+        compiler_params=pltpu.CompilerParams(vmem_limit_bytes=limit * 2**20),
         cost_estimate=pl.CostEstimate(flops=1, bytes_accessed=1, transcendentals=0),
     )(*tables, *operands)
 
@@ -133,17 +150,23 @@
     return product(held[:, :half], own, transposed) + product(held[:, half:], other, transposed)
 
 
-def first_kernel(tables, loads, stores, tok_held, grad_held):
+def first_kernel(tables, loads, stores, tok_held, grad_held, sems):
     (table,) = tables
-    block, *blocks = [load.get() for load in loads[:-6]]
-    weights, messages = loads[-6:], stores[6:]
-    rows = block.shape[1]
+    (block, heard), blocks = loads[:2], loads[2 : NZ + 1]
+    weights, messages = loads[NZ + 1 :], stores[2:]
+    rows = block.target.shape[1]
+    landing = [
+        [
+            Load(source.at[i], stores[i].ref.at[pl.ds(k * rows, rows)], sems.at[i * (NZ - 1) + k - 1])
+            for k, source in enumerate(blocks, 1)
+        ]
+        for i in range(2)
+    ]
     for i, held in enumerate((tok_held, grad_held)):
-        acts, own, away = [store.ref for store in stores[i:6:2]]
-        half = own.shape[1]
-        acts[:rows] = jnp.where(table[CORE] == 0, block[i], blocks[0][i])
-        for k in range(1, NZ):
-            acts[k * rows : (k + 1) * rows] = blocks[k][i]
+        acts = stores[i].ref
+        acts[:rows] = jnp.where(table[CORE] == 0, block.get()[i], heard.get()[i])
+        for load in landing[i]:
+            load.get()
         stores[i].send()
         for slot in range(6):
             start = pl.multiple_of(table[FIRST + slot] * PIECE, PIECE)
@@ -155,22 +178,23 @@
             total = pair_product(held, pair, at, end, transposed).astype(jnp.bfloat16)
             for i, message in enumerate(messages):
                 message.ref[which, :, at:end] = total[i * 2 * PIECE : (i + 1) * 2 * PIECE]
-    for message in messages:
-        message.send()
-    for i in range(2):
-        acts, own, away = [store.ref for store in stores[i:6:2]]
-        half = own.shape[1]
-        own[...] = acts[:, :half]
-        away[...] = acts[:, half:]
+        for message in messages:
+            message.send(which)
 
 
 def partial_kernel(tables, loads, stores, tok_held, grad_held):
     (table,) = tables
-    for acts, held in zip(loads[:2], (tok_held, grad_held)):
-        rows = acts.get()
+    for i, held in enumerate((tok_held, grad_held)):
+        rows = loads[i].get()
         for slot in range(4):
             start = pl.multiple_of(table[SECOND + slot] * PIECE, PIECE)
             held[slot * PIECE : (slot + 1) * PIECE, :] = rows[pl.ds(start, PIECE), :]
+        own, away = stores[3 + i], stores[5 + i]
+        half = own.ref.shape[1]
+        own.ref[...] = rows[:, :half]
+        away.ref[...] = rows[:, half:]
+        own.send()
+        away.send()
     for which in range(3):
         held, transposed = ((tok_held, False), (grad_held, True))[which // 2]
         pair = loads[2 + 2 * which : 4 + 2 * which]
@@ -182,20 +206,19 @@
 
 def second_kernel(tables, loads, stores):
     (table,) = tables
-    heard = loads[3:]
     outs = [store.ref for store in stores]
     core, x = table[CORE], table[AT_X]
     near = pl.ds(pl.multiple_of(x * PIECE, PIECE), PIECE)
     far = pl.ds(pl.multiple_of((1 - x) * PIECE, PIECE), PIECE)
     one = core == 1
-    terms = [h.get() for h in heard]
+    terms = [load.get() for load in loads[3:]]
     for which in range(3):
         total = loads[which].get()
         for at, end in spans(outs[0].shape[2]):
-            near1, near2, near3 = [h[which, near, at:end].astype(jnp.float32) for h in terms]
+            _, near2, _ = [h[which, near, at:end].astype(jnp.float32) for h in terms]
             far1, far2, far3 = [h[which, far, at:end].astype(jnp.float32) for h in terms]
-            part1, part2, part3, part4 = [
-                total[slot * PIECE : (slot + 1) * PIECE, at:end] for slot in range(4)
+            part1, part2, part3 = [
+                total[slot * PIECE : (slot + 1) * PIECE, at:end] for slot in range(3)
             ]
             sum1 = part1 + far1 + jnp.where(one, far2 + far3, 0.0)
             high = sum1.astype(jnp.bfloat16)
@@ -203,7 +226,18 @@
             outs[0][which, :, at:end] = high
             outs[1][which, :, at:end] = jnp.where(one, rest, part2 + near2).astype(jnp.bfloat16)
             outs[2][which, :, at:end] = (part3 + far2).astype(jnp.bfloat16)
-            outs[3][which, :, at:end] = part4 + near1 + jnp.where(one, near2 + near3, 0.0)
+        for store in stores:
+            store.send(which)
+
+
+def kept_kernel(tables, loads, stores):
+    (table,) = tables
+    near = pl.ds(pl.multiple_of(table[AT_X] * PIECE, PIECE), PIECE)
+    one = table[CORE] == 1
+    for which in range(3):
+        near1, near2, near3 = [h.get()[which, near].astype(jnp.float32) for h in loads[3:]]
+        total = loads[which].get()[...] + near1
+        stores[0].ref[which] = total + jnp.where(one, near2 + near3, 0.0)
 
 
 def weave_kernel(tables, loads, stores):
@@ -229,36 +263,43 @@
     both[1] = (d_hidden * gate * sig_gate).astype(jnp.bfloat16)
 
 
-def pack_kernel(tables, loads, stores):
-    own, near1, near2, near3 = [load.get() for load in loads]
+def pack_kernel(tables, loads, stores, sems):
+    own, near1, near2, near3 = loads
     first, second = [store.ref for store in stores]
+    landing = [
+        Load(source, first.at[:, pl.ds(i * PIECE, PIECE)], sems.at[i])
+        for i, source in enumerate((own, near1))
+    ]
+    for load in landing:
+        load.get()
+    stores[0].send()
     core0 = tables[0][CORE] == 0
-    first[:, :PIECE] = own[...]
-    first[:, PIECE:] = near1[...]
-    stores[0].send()
-    second[:, :PIECE] = jnp.where(core0, near2[...], own[...])
-    second[:, PIECE:] = jnp.where(core0, near3[...], near1[...])
-
-
-def input_kernel(tables, loads, stores):
+    second[:, :PIECE] = jnp.where(core0, near2.get()[...], first[:, :PIECE])
+    second[:, PIECE:] = jnp.where(core0, near3.get()[...], first[:, PIECE:])
+
+
+def input_kernel(tables, loads, stores, sems):
     (table,) = tables
-    own, near1, near2, near3, far1, far2, far3 = [load.get() for load in loads[:7]]
+    own, near1, far1, far2, near2, near3, far3 = loads[:7]
     weights = loads[7:]
     *messages, d_set, kept = [store.ref for store in stores]
 
-    def put(slot, value):
-        start = pl.multiple_of(table[GATHER + slot] * PIECE, PIECE)
-        d_set[:, pl.ds(start, PIECE), :] = value
-
-    put(0, own[...])
-    put(1, near1[...])
-    put(2, far1[:, :PIECE])
-    put(3, far1[:, PIECE:])
-    put(4, far2[:, :PIECE])
-    put(5, far2[:, PIECE:])
+    def at_slot(slot):
+        return pl.ds(pl.multiple_of(table[GATHER + slot] * PIECE, PIECE), PIECE)
+
+    front, back = pl.ds(0, PIECE), pl.ds(PIECE, PIECE)
+    sources = [own, near1]
+    for both in (far1, far2):
+        sources += [both.at[:, front], both.at[:, back]]
+    landing = [
+        Load(source, d_set.at[:, at_slot(slot)], sems.at[slot])
+        for slot, source in enumerate(sources)
+    ]
     core0 = table[CORE] == 0
-    put(6, jnp.where(core0, near2[...], far3[:, :PIECE]))
-    put(7, jnp.where(core0, near3[...], far3[:, PIECE:]))
+    d_set[:, at_slot(6)] = jnp.where(core0, near2.get()[...], far3.get()[:, :PIECE])
+    d_set[:, at_slot(7)] = jnp.where(core0, near3.get()[...], far3.get()[:, PIECE:])
+    for load in landing:
+        load.get()
     stores[NZ].send()
     depth = weights[0].target.shape[0]
     block = NX * PIECE
@@ -279,14 +320,13 @@
 def first_stage(table, blocks, weights):
     depth, width = weights[0].shape
     rows = NY * NX * PIECE
+    held = pltpu.VMEM((6 * PIECE, 2 * depth), jnp.bfloat16)
     return call(
         first_kernel,
         [table],
-        [*blocks, *weights],
-        [shape((rows, 2 * depth))] * 2
-        + [shape((rows, depth))] * 4
-        + [shape((3, 2 * PIECE, width))] * 3,
-        [pltpu.VMEM((6 * PIECE, 2 * depth), jnp.bfloat16)] * 2,
+        [*blocks[:2], *[Raw(block) for block in blocks[2:]], *weights],
+        [shape((rows, 2 * depth))] * 2 + [shape((3, 2 * PIECE, width))] * 3,
+        [held, held, pltpu.SemaphoreType.DMA((2 * (NZ - 1),))],
     )
 
 
@@ -296,19 +336,14 @@
         partial_kernel,
         [table],
         [tok_half, grad_half, *weights],
-        [shape((4 * PIECE, width), jnp.float32)] * 3,
+        [shape((4 * PIECE, width), jnp.float32)] * 3 + [shape((NY * NX * PIECE, depth))] * 4,
         [pltpu.VMEM((4 * PIECE, 2 * depth), jnp.bfloat16)] * 2,
     )
 
 
 def second_stage(table, products, heard):
     message = shape((3, PIECE, products[0].shape[1]))
-    return call(
-        second_kernel,
-        [table],
-        [*products, *heard],
-        [message] * 3 + [shape(message.shape, jnp.float32)],
-    )
+    return call(second_kernel, [table], [*products, *heard], [message] * 3)
 
 
 def send_first(sent):
@@ -360,8 +395,9 @@
 
 
 def col_first(near, send):
-    for step in range(1, NZ):
-        near = near + lax.ppermute(send[step - 1], "col", col_perm(0, step)).astype(jnp.float32)
+    heard = [lax.ppermute(send[step - 1], "col", col_perm(0, step)) for step in range(1, NZ)]
+    for term in heard:
+        near = near + term.astype(jnp.float32)
     return near[:, 0], near[:, 1].astype(jnp.bfloat16)
 
 
@@ -388,18 +424,22 @@
 
     both_weights = [gate_weight, gate_other, up_weight, up_other]
     weights = [*both_weights, down_weight, down_other]
-    tok_half, grad_half, tok_own, grad_own, tok_away, grad_away, *sent = first_stage(
-        table, [own_block, *blocks], weights
-    )
+    tok_half, grad_half, *sent = first_stage(table, [own_block, *blocks], weights)
     heard = send_first(sent)
-    products = partial_stage(table, tok_half, grad_half, weights)
+    *products, tok_own, grad_own, tok_away, grad_away = partial_stage(
+        table, tok_half, grad_half, weights
+    )
     tok_other = flip(after(tok_away, products[0]))
     grad_other = flip(after(grad_away, products[0]))
     (grad_all,) = call(
         weave_kernel, [table], [grad_own, grad_other], [shape((2 * half_rows, width))]
     )
     *heard, grad_all, tok_other = lax.optimization_barrier((*heard, grad_all, tok_other))
-    *sent, kept = second_stage(table, products, heard)
+    sent = second_stage(table, products, heard)
+    last = [after(product, sent[0])[3 * PIECE :] for product in products]
+    (kept,) = call(
+        kept_kernel, [table], [*last, *heard], [shape((3, PIECE, ff_width), jnp.float32)]
+    )
     hidden, d_own = call(
         unit_kernel,
         [],
@@ -410,7 +450,11 @@
 
     near = send_second([d_own] * 3)
     first, second = call(
-        pack_kernel, [table], [d_own, *near], [shape((2, 2 * PIECE, ff_width))] * 2
+        pack_kernel,
+        [table],
+        [Raw(d_own), Raw(near[0]), *near[1:]],
+        [shape((2, 2 * PIECE, ff_width))] * 2,
+        [pltpu.SemaphoreType.DMA((2,))],
     )
     far = send_first([first, second, first])
     dot = functools.partial(lax.dot_general, preferred_element_type=jnp.float32)
@@ -418,14 +462,19 @@
     hidden = after(hidden, far[0])
     near_sum, send = col_blocks(jnp.dot(hidden, down_weight, preferred_element_type=jnp.float32))
     near_sum, send = lax.optimization_barrier((near_sum, send))
-    layer_output = col_second(*col_first(near_sum, send))
-    *far, _ = lax.optimization_barrier((*far, send))
+    near_sum, near_send = col_first(near_sum, send)
+    *far, near_sum, near_send = lax.optimization_barrier((*far, near_sum, near_send))
+    layer_output = col_second(near_sum, near_send)
     block = shape((NX * PIECE, 2 * width))
     *messages, d_set, kept = call(
         input_kernel,
         [table],
-        [d_own, *near, *far, gate_weight, up_weight, gate_other, up_other],
+        [
+            *[Raw(d_own), Raw(near[0]), Raw(far[0]), Raw(far[1])],
+            *[near[1], near[2], far[2], gate_weight, up_weight, gate_other, up_other],
+        ],
         [block] * 4 + [shape((2, half_rows, ff_width)), shape(block.shape, jnp.float32)],
+        [pltpu.SemaphoreType.DMA((6,))],
     )
     messages = [lax.ppermute(messages[k], BOTH, scatter_perm(k)) for k in range(NZ)]
     d_other = flip(d_set)

time: 247 us -> 256 us (1.036)
  local copies, waits for them, and re-layouts: 6.89 us -> 13.8 us
  Pallas kernels: 46.7 us -> 53.2 us
  starting transfers between devices: 60.4 us -> 57 us
    ppermute x2, waiting for transfers between devices: 33.6 us -> 43 us  [send_first(): lax.ppermute(sent[0], 'row', row_perm(over_x, over_y(1)))]
    ppermute x2, waiting for transfers between devices: 13.4 us -> 6.07 us  [send_second(): lax.ppermute(sent[1], 'row', row_perm(over_y(-1), over_x))]
    pallas_call x7 -> x8, Pallas kernels: 46.7 us -> 53.2 us  [call(): pl.pallas_call(run, in_specs=[smem] * n_tables + [any_space] * n_in, out_...]
    ppermute x2, waiting for transfers between devices: 0.01 us -> 5.63 us  [send_first(): lax.ppermute(sent[1], 'row', row_perm(over_x, over_y(-1)))]
    slice x0 -> x3, local copies, waits for them, and re-layouts: none -> 5.51 us  [body(): last = [after(product, sent[0])[3 * PIECE:] for product in products]]
    ppermute x2, waiting for transfers between devices: 13.4 us -> 10.2 us  [send_second(): lax.ppermute(sent[0], 'row', row_perm(over_y(1), over_x))]
    ppermute x3, waiting for transfers between devices: 4.56 us -> 1.91 us  [col_first(): lax.ppermute(send[step - 1], 'col', col_perm(0, step))]
    unnamed x48 -> x50, local copies, waits for them, and re-layouts: 4.91 us -> 6.26 us
  transfers between devices with their start and end apart: 33 -> 33, of which waited for: 14 -> 14; matrix products, arithmetic and copies ran while one was open for 8% -> 8% of each run, Pallas kernels for 6% -> 8%
where the time goes in v6:
time: 256 us; the launch traced here: 253 us
  waiting for transfers between devices  94.7 us (37%)
  starting transfers between devices  57 us (22%)
  Pallas kernels  53.2 us (21%)
  between operations  15.1 us (6%)
  matrix products  15 us (6%)
  local copies, waits for them, and re-layouts  13.8 us (5%)
  other arithmetic  3.73 us (1%)
    pallas_call x8, Pallas kernels, call(): pl.pallas_call(run, in_specs=[smem] * n_tables + [any_space] * n_in, out_...  53.2 us
    ppermute x2, waiting for transfers between devices, send_first(): lax.ppermute(sent[0], 'row', row_perm(over_x, over_y(1)))  43 us
    ppermute x4, waiting for transfers between devices, body(): lax.ppermute(starts[step], BOTH, gather_perm(step))  18.7 us
    ppermute x4, starting transfers between devices, body(): lax.ppermute(messages[k], BOTH, scatter_perm(k))  12.4 us
    ppermute x4, starting transfers between devices, body(): lax.ppermute(starts[step], BOTH, gather_perm(step))  11.6 us
    ppermute x2, waiting for transfers between devices, send_second(): lax.ppermute(sent[0], 'row', row_perm(over_y(1), over_x))  10.2 us
    ppermute x8, starting transfers between devices, body(): flip = lambda value: lax.ppermute(value, 'row', CORE_FLIP)  10.2 us
    ppermute x2, starting transfers between devices, send_first(): lax.ppermute(sent[2], 'row', row_perm(None, over_y(2)))  8.07 us
  transfers between devices with their start and end apart: 33, of which 14 were waited for; matrix products, arithmetic and copies ran while one was open for 8% of the time, Pallas kernels for 8%

profile of v6, /device:TPU:17, one launch (start us, length us, event | category | flops | bytes accessed | tf_op | source)
XLA Modules:
  0.0 252.7 jit_solution(5301257586489268608)
XLA Ops:
  9.6 4.2 %collective-permute-done = bf16[2,128,512]{2,1,0:T(8,128)(2,1)S(1)} collective-permute-done((bf16[2,128,512]{2,1,0:T(8,128)(2,1)S(1)}, bf16[2,128,512]{2,1,0:T(8,128)(2,1)S(1)}, u32[]{:S(2)}, u32[]{:S(2)}) %collective-permute-start) | collective-permute-done | bytes 262176 | tf_op jit(solution)/shard_map/ppermute | solution.py:414
  14.8 6.3 %collective-permute-start.2 = (bf16[2,128,1024]{2,1,0:T(8,128)(2,1)S(1)}, bf16[2,128,1024]{2,1,0:T(8,128)(2,1)S(1)}, u32[]{:S(2)}, u32[]{:S(2)}) collective-permute-start(bf16[2,128,1024]{2,1,0:T(8,128)(2,1)S(1)} %pad_maximum_fusion.refs_1_), channel_id=1, source_target_pairs={{1,0},{2,1},{3,2},{0,3},{5,4},{6,5},{7,6},{4,7},{13,8},{14,9},{15,... | collective-permute-start | bytes 1572872 | tf_op jit(solution)/shard_map/ppermute | solution.py:423
  27.7 5.9 %collective-permute-done.1.refs_2_ = bf16[2,128,1024]{2,1,0:T(8,128)(2,1)S(1)} collective-permute-done((bf16[2,128,1024]{2,1,0:T(8,128)(2,1)S(1)}, bf16[2,128,1024]{2,1,0:T(8,128)(2,1)S(1)}, u32[]{:S(2)}, u32[]{:S(2)}) %collective-permute-start.1) | collective-permute-done | bytes 524320 | tf_op jit(solution)/shard_map/ppermute | solution.py:423
  33.6 5.5 %collective-permute-done.4.refs_4_ = bf16[2,128,1024]{2,1,0:T(8,128)(2,1)} collective-permute-done((bf16[2,128,1024]{2,1,0:T(8,128)(2,1)S(1)}, bf16[2,128,1024]{2,1,0:T(8,128)(2,1)}, u32[]{:S(2)}, u32[]{:S(2)}) %collective-permute-start.4) | collective-permute-done | bytes 524320 | tf_op jit(solution)/shard_map/ppermute | solution.py:423
  39.1 7.3 %collective-permute-done.6.refs_5_ = bf16[2,128,1024]{2,1,0:T(8,128)(2,1)} collective-permute-done((bf16[2,128,1024]{2,1,0:T(8,128)(2,1)S(1)}, bf16[2,128,1024]{2,1,0:T(8,128)(2,1)}, u32[]{:S(2)}, u32[]{:S(2)}) %collective-permute-start.6) | collective-permute-done | bytes 524320 | tf_op jit(solution)/shard_map/ppermute | solution.py:423
  46.3 12.5 %shard_map.101 = (bf16[512,1024]{1,0:T(8,128)(2,1)}, bf16[512,1024]{1,0:T(8,128)(2,1)}, bf16[3,128,1792]{2,1,0:T(8,128)(2,1)}, bf16[3,128,1792]{2,1,0:T(8,128)(2,1)}, bf16[3,128,1792]{2,1,0:T(8,128)(2,1)}) custom-call(s32[20]{0:T(128)} %get-tuple-element.111.refs_0_, bf16[2,128,1024]{2,1,0:T(8,128)(2,1)} %copy-done.6, bf16[2,128,1024]{2,1,0:T(8,128)(2,1)} %copy-done.21, ...), custom_call_target="tpu_custom_call" | custom-call | flops 1 | bytes 1 | tf_op jit(solution)/shard_map/pallas_call | solution.py:130
  63.7 9.3 %shard_map.102 = (f32[256,1792]{1,0:T(8,128)}, f32[256,1792]{1,0:T(8,128)}, f32[256,1792]{1,0:T(8,128)}, bf16[512,512]{1,0:T(8,128)(2,1)}, bf16[512,512]{1,0:T(8...) custom-call(s32[20]{0:T(128)} %get-tuple-element.111.refs_0_, ...), custom_call_target="tpu_custom_call" | custom-call | flops 1 | bytes 1 | tf_op jit(solution)/shard_map/pallas_call | solution.py:130
  79.0 12.4 %collective-permute-done.8.refs_4_ = bf16[3,128,1792]{2,1,0:T(8,128)(2,1)S(1)} collective-permute-done((bf16[3,128,1792]{2,1,0:T(8,128)(2,1)}, bf16[3,128,1792]{2,1,0:T(8,128)(2,1)S(1)}, u32[]{:S(2)}, u32[]{:S(2)}) %collective-permute-start.8) | collective-permute-done | bytes 1376288 | tf_op jit(solution)/shard_map/ppermute | solution.py:351
  93.3 6.2 %shard_map.104 = (bf16[3,64,1792]{2,1,0:T(8,128)(2,1)}, bf16[3,64,1792]{2,1,0:T(8,128)(2,1)}, bf16[3,64,1792]{2,1,0:T(8,128)(2,1)}) custom-call(s32[20]{0:T(128)} %get-tuple-element.111.refs_0_, f32[256,1792]{1,0:T(8,128)} %get-tuple-element.75.refs_1_, f32[256,1792]{1,0:T(8,128)} %get-tuple-element.76.refs_2_, f32[256,1792]{1,0:T(8,128)} %get-tuple-element.77.refs_3_, ...), custom_call_target="tpu_custom_call" | custom-call | flops 1 | bytes 1 | tf_op jit(solution)/shard_map/pallas_call | solution.py:130
  107.3 4.9 %shard_map.105.refs_0_ = f32[3,64,1792]{2,1,0:T(8,128)} custom-call(s32[20]{0:T(128)} %get-tuple-element.111.refs_0_, f32[64,1792]{1,0:T(8,128)} %slice.56.refs_1_, f32[64,1792]{1,0:T(8,128)} %slice.57.refs_2_, f32[64,1792]{1,0:T(8,128)} %slice.58.refs_3_, bf16[3,128,1792]{2,1,0:T(8,128)(2,1)} %copy-done.2, bf16[3,128,1792]{2,1,0:T(8,128)(2,1)} %copy-done.3, ...), custom_call_target="tpu_custom_call" | custom-call | flops 1 | bytes 1 | tf_op jit(solution)/shard_map/pallas_call | solution.py:130
  112.2 5.0 %collective-permute-done.13.refs_1_ = bf16[3,64,1792]{2,1,0:T(8,128)(2,1)S(1)} collective-permute-done((bf16[3,64,1792]{2,1,0:T(8,128)(2,1)}, bf16[3,64,1792]{2,1,0:T(8,128)(2,1)S(1)}, u32[]{:S(2)}, u32[]{:S(2)}) %collective-permute-start.13) | collective-permute-done | bytes 688160 | tf_op jit(solution)/shard_map/ppermute | solution.py:359
  123.9 6.1 %collective-permute-done.17.refs_3_.refs_5_ = bf16[2,64,1792]{2,1,0:T(8,128)(2,1)S(1)} collective-permute-done((bf16[2,64,1792]{2,1,0:T(8,128)(2,1)}, bf16[2,64,1792]{2,1,0:T(8,128)(2,1)S(1)}, u32[]{:S(2)}, u32[]{:S(2)}) %collective-permute-start.17) | collective-permute-done | bytes 458784 | tf_op jit(solution)/shard_map/ppermute | solution.py:360
  129.9 5.2 %collective-permute-done.16.refs_2_ = bf16[2,64,1792]{2,1,0:T(8,128)(2,1)S(1)} collective-permute-done((bf16[2,64,1792]{2,1,0:T(8,128)(2,1)}, bf16[2,64,1792]{2,1,0:T(8,128)(2,1)S(1)}, u32[]{:S(2)}, u32[]{:S(2)}) %collective-permute-start.16) | collective-permute-done | bytes 458784 | tf_op jit(solution)/shard_map/ppermute | solution.py:359
  135.9 3.4 %shard_map.107 = (bf16[2,128,1792]{2,1,0:T(8,128)(2,1)}, bf16[2,128,1792]{2,1,0:T(8,128)(2,1)}) custom-call(s32[20]{0:T(128)} %get-tuple-element.111.refs_0_, bf16[2,64,1792]{2,1,0:T(8,128)(2,1)} %get-tuple-element.80.refs_1_, bf16[2,64,1792]{2,1,0:T(8,128)(2,1)} %copy-done.10, bf16[2,64,1792]{2,1,0:T(8,128)(2,1)} %copy-done.9, bf16[2,64,1792]{2,1,0:T(8,128)(2,1)} %copy-done.8), custom_call_target="tpu_custom_call" | custom-call | flops 1 | bytes 1 | tf_op jit(solution)/shard_map/pallas_call | solution.py:130
  141.0 30.6 %collective-permute-done.19.refs_3_ = bf16[2,128,1792]{2,1,0:T(8,128)(2,1)S(1)} collective-permute-done((bf16[2,128,1792]{2,1,0:T(8,128)(2,1)}, bf16[2,128,1792]{2,1,0:T(8,128)(2,1)S(1)}, u32[]{:S(2)}, u32[]{:S(2)}) %collective-permute-start.19) | collective-permute-done | bytes 917536 | tf_op jit(solution)/shard_map/ppermute | solution.py:351
  171.6 4.4 %fusion.9 = f32[1024,512]{1,0:T(8,128)S(1)} fusion(bf16[1024,1792]{1,0:T(8,128)(2,1)} %all-gather.2.cloned.1.call-done, bf16[1792,512]{1,0:T(8,128)(2,1)S(1)} %copy-done.1), kind=kOutput, calls=%fused_computation.27 | convolution fusion | flops 1879048192 | bytes 7602176 | tf_op jit(solution)/shard_map/dot_general | solution.py:463
  179.1 4.8 %collective-permute-start.21 = (bf16[2,128,1792]{2,1,0:T(8,128)(2,1)S(1)}, bf16[2,128,1792]{2,1,0:T(8,128)(2,1)S(1)}, u32[]{:S(2)}, u32[]{:S(2)}) collective-permute-start(bf16[2,128,1792]{2,1,0:T(8,128)(2,1)S(1)} %copy-done.23), channel_id=1, source_target_pairs={{8,72},{24,88},{40,104},{56,120},{72,8},{88,24},{104,40},{120,56},... | collective-permute-start | bytes 2752520 | tf_op jit(solution)/shard_map/ppermute | solution.py:353
  186.0 5.6 %collective-permute-done.20.refs_4_ = bf16[2,128,1792]{2,1,0:T(8,128)(2,1)S(1)} collective-permute-done((bf16[2,128,1792]{2,1,0:T(8,128)(2,1)S(1)}, bf16[2,128,1792]{2,1,0:T(8,128)(2,1)S(1)}, u32[]{:S(2)}, u32[]{:S(2)}) %collective-permute-start.20) | collective-permute-done | bytes 917536 | tf_op jit(solution)/shard_map/ppermute | solution.py:352
  191.6 3.4 %collective-permute-done.21.refs_7_ = bf16[2,128,1792]{2,1,0:T(8,128)(2,1)S(1)} collective-permute-done((bf16[2,128,1792]{2,1,0:T(8,128)(2,1)S(1)}, bf16[2,128,1792]{2,1,0:T(8,128)(2,1)S(1)}, u32[]{:S(2)}, u32[]{:S(2)}) %collective-permute-start.21) | collective-permute-done | bytes 917536 | tf_op jit(solution)/shard_map/ppermute | solution.py:353
  196.0 10.7 %shard_map.108 = (bf16[128,1024]{1,0:T(8,128)(2,1)}, bf16[128,1024]{1,0:T(8,128)(2,1)}, bf16[128,1024]{1,0:T(8,128)(2,1)}, bf16[128,1024]{1,0:T(8,128)(2,1)}, bf...) custom-call(s32[20]{0:T(128)} %get-tuple-element.111.refs_0_, bf16[2,64,1792]{2,1,0:T(8,128)(2,1)} %get-tuple-element.80.refs_1_, ...), custom_call_target="tpu_custom_call" | custom-call | flops 1 | bytes 1 | tf_op jit(solution)/shard_map/pallas_call | solution.py:130
  206.6 8.1 %collective-permute-start.30 = (bf16[2,512,1792]{2,1,0:T(8,128)(2,1)}, bf16[2,512,1792]{2,1,0:T(8,128)(2,1)S(1)}, u32[]{:S(2)}, u32[]{:S(2)}) collective-permute-start(bf16[2,512,1792]{2,1,0:T(8,128)(2,1)} %get-tuple-element.98), channel_id=1, source_target_pairs={{0,8},{8,0},{16,24},{24,16},{32,40},{40,32},{48,56},{56,48},{64,72... | collective-permute-start | bytes 11010056 | tf_op jit(solution)/shard_map/ppermute | solution.py:414
  216.0 4.2 %collective-permute-start.25 = (bf16[2,64,512]{2,1,0:T(8,128)(2,1)S(1)}, bf16[2,64,512]{2,1,0:T(8,128)(2,1)S(1)}, u32[]{:S(2)}, u32[]{:S(2)}) collective-permute-start(bf16[2,64,512]{2,1,0:T(8,128)(2,1)S(1)} %fusion.7), channel_id=1, source_target_pairs={{0,4},{1,5},{2,6},{3,7},{4,0},{5,1},{6,2},{7,3},{8,12},{9,13},{10,... | collective-permute-start | bytes 393224 | tf_op jit(solution)/shard_map/ppermute | solution.py:405
  228.2 4.4 %collective-permute-start.29 = (bf16[128,1024]{1,0:T(8,128)(2,1)}, bf16[128,1024]{1,0:T(8,128)(2,1)S(1)}, u32[]{:S(2)}, u32[]{:S(2)}) collective-permute-start(bf16[128,1024]{1,0:T(8,128)(2,1)} %get-tuple-element.96), channel_id=1, source_target_pairs={{0,3},{1,0},{2,1},{3,2},{4,7},{5,4},{6,5},{7,6},{8,15},{9,12},{10,... | collective-permute-start | bytes 786440 | tf_op jit(solution)/shard_map/ppermute | solution.py:479
  241.1 3.4 %convolution_convert_fusion = bf16[1792,512]{1,0:T(8,128)(2,1)} fusion(bf16[1024,1792]{1,0:T(8,128)(2,1)S(1)} %copy-done.22, bf16[1024,512]{1,0:T(8,128)(2,1)S(1)} %copy-done.11), kind=kOutput, calls=%fused_computation.2 | convolution fusion | flops 1879965696 | bytes 6553600 | tf_op jit(solution)/shard_map/dot_general | solution.py:481
  (124 shorter events, 63.9 us)
Async XLA Ops:
  7.2 164.5 %all-gather.2.cloned.1.call-start = ((), (), s32[]{:S(2)}) async-start(), calls=%async_computation | async-start | bytes 3899392 | tf_op jit(solution)/shard_map/all_gather | solution.py:449
  7.2 16.1 %collective-permute-start.3 = (bf16[512,1792]{1,0:T(8,128)(2,1)}, bf16[512,1792]{1,0:T(8,128)(2,1)S(1)}, u32[]{:S(2)}, u32[]{:S(2)}) collective-permute-start(bf16[512,1792]{1,0:T(8,128)(2,1)} %refs_8_.3), channel_id=1, source_target_pairs={{0,8},{8,0},{16,24},{24,16},{32,40},{40,32},{48,56},{56,48},{64,72... | collective-permute-start | bytes 5505032 | tf_op jit(solution)/shard_map/ppermute | solution.py:414
  8.0 17.5 %collective-permute-start.5 = (bf16[512,1792]{1,0:T(8,128)(2,1)}, bf16[512,1792]{1,0:T(8,128)(2,1)}, u32[]{:S(2)}, u32[]{:S(2)}) collective-permute-start(bf16[512,1792]{1,0:T(8,128)(2,1)} %refs_9_.1), channel_id=1, source_target_pairs={{0,8},{8,0},{16,24},{24,16},{32,40},{40,32},{48,56},{56,48},{64,72... | collective-permute-start | bytes 5505032 | tf_op jit(solution)/shard_map/ppermute | solution.py:414
  8.1 25.5 %collective-permute-start.7 = (bf16[1792,512]{1,0:T(8,128)(2,1)}, bf16[1792,512]{1,0:T(8,128)(2,1)}, u32[]{:S(2)}, u32[]{:S(2)}) collective-permute-start(bf16[1792,512]{1,0:T(8,128)(2,1)} %refs_7_.1), channel_id=1, source_target_pairs={{0,8},{8,0},{16,24},{24,16},{32,40},{40,32},{48,56},{56,48},{64,72... | collective-permute-start | bytes 5505032 | tf_op jit(solution)/shard_map/ppermute | solution.py:414
  14.8 12.8 %collective-permute-start.2 = (bf16[2,128,1024]{2,1,0:T(8,128)(2,1)S(1)}, bf16[2,128,1024]{2,1,0:T(8,128)(2,1)S(1)}, u32[]{:S(2)}, u32[]{:S(2)}) collective-permute-start(bf16[2,128,1024]{2,1,0:T(8,128)(2,1)S(1)} %pad_maximum_fusion.refs_1_), channel_id=1, source_target_pairs={{1,0},{2,1},{3,2},{0,3},{5,4},{6,5},{7,6},{4,7},{13,8},{14,9},{15,... | collective-permute-start | bytes 1572872 | tf_op jit(solution)/shard_map/ppermute | solution.py:423
  21.1 12.5 %collective-permute-start.1 = (bf16[2,128,1024]{2,1,0:T(8,128)(2,1)S(1)}, bf16[2,128,1024]{2,1,0:T(8,128)(2,1)S(1)}, u32[]{:S(2)}, u32[]{:S(2)}) collective-permute-start(bf16[2,128,1024]{2,1,0:T(8,128)(2,1)S(1)} %pad_maximum_fusion.refs_1_), channel_id=1, source_target_pairs={{12,8},{13,9},{14,10},{15,11},{8,12},{9,13},{10,14},{11,15},{28,24... | collective-permute-start | bytes 1572872 | tf_op jit(solution)/shard_map/ppermute | solution.py:423
  23.3 15.8 %collective-permute-start.4 = (bf16[2,128,1024]{2,1,0:T(8,128)(2,1)S(1)}, bf16[2,128,1024]{2,1,0:T(8,128)(2,1)}, u32[]{:S(2)}, u32[]{:S(2)}) collective-permute-start(bf16[2,128,1024]{2,1,0:T(8,128)(2,1)S(1)} %pad_maximum_fusion.refs_1_), channel_id=1, source_target_pairs={{2,0},{3,1},{0,2},{1,3},{6,4},{7,5},{4,6},{5,7},{14,8},{15,9},{12,... | collective-permute-start | bytes 1572872 | tf_op jit(solution)/shard_map/ppermute | solution.py:423
  25.5 20.8 %collective-permute-start.6 = (bf16[2,128,1024]{2,1,0:T(8,128)(2,1)S(1)}, bf16[2,128,1024]{2,1,0:T(8,128)(2,1)}, u32[]{:S(2)}, u32[]{:S(2)}) collective-permute-start(bf16[2,128,1024]{2,1,0:T(8,128)(2,1)S(1)} %pad_maximum_fusion.refs_1_), channel_id=1, source_target_pairs={{3,0},{0,1},{1,2},{2,3},{7,4},{4,5},{5,6},{6,7},{15,8},{12,9},{13,... | collective-permute-start | bytes 1572872 | tf_op jit(solution)/shard_map/ppermute | solution.py:423
  58.8 32.5 %collective-permute-start.8 = (bf16[3,128,1792]{2,1,0:T(8,128)(2,1)}, bf16[3,128,1792]{2,1,0:T(8,128)(2,1)S(1)}, u32[]{:S(2)}, u32[]{:S(2)}) collective-permute-start(bf16[3,128,1792]{2,1,0:T(8,128)(2,1)} %get-tuple-element.63), channel_id=1, source_target_pairs={{0,16},{8,40},{16,0},{24,56},{32,48},{40,72},{48,32},{56,88},{64,8... | collective-permute-start | bytes 4128776 | tf_op jit(solution)/shard_map/ppermute | solution.py:351
  59.9 31.4 %collective-permute-start.9 = (bf16[3,128,1792]{2,1,0:T(8,128)(2,1)}, bf16[3,128,1792]{2,1,0:T(8,128)(2,1)S(1)}, u32[]{:S(2)}, u32[]{:S(2)}) collective-permute-start(bf16[3,128,1792]{2,1,0:T(8,128)(2,1)} %get-tuple-element.64), channel_id=1, source_target_pairs={{0,16},{8,104},{16,0},{24,120},{32,48},{40,8},{48,32},{56,24},{64,... | collective-permute-start | bytes 4128776 | tf_op jit(solution)/shard_map/ppermute | solution.py:352
  60.4 31.0 %collective-permute-start.10 = (bf16[3,128,1792]{2,1,0:T(8,128)(2,1)}, bf16[3,128,1792]{2,1,0:T(8,128)(2,1)S(1)}, u32[]{:S(2)}, u32[]{:S(2)}) collective-permute-start(bf16[3,128,1792]{2,1,0:T(8,128)(2,1)} %get-tuple-element.65), channel_id=1, source_target_pairs={{8,72},{24,88},{40,104},{56,120},{72,8},{88,24},{104,40},{120,56},... | collective-permute-start | bytes 4128776 | tf_op jit(solution)/shard_map/ppermute | solution.py:353
  99.5 12.7 %collective-permute-start.14 = (bf16[3,64,1792]{2,1,0:T(8,128)(2,1)}, bf16[3,64,1792]{2,1,0:T(8,128)(2,1)S(1)}, u32[]{:S(2)}, u32[]{:S(2)}) collective-permute-start(bf16[3,64,1792]{2,1,0:T(8,128)(2,1)} %get-tuple-element.78), channel_id=1, source_target_pairs={{0,96},{8,24},{16,112},{24,8},{32,0},{40,56},{48,16},{56,40},{64,3... | collective-permute-start | bytes 2064392 | tf_op jit(solution)/shard_map/ppermute | solution.py:360
  100.5 11.7 %collective-permute-start.15 = (bf16[3,64,1792]{2,1,0:T(8,128)(2,1)}, bf16[3,64,1792]{2,1,0:T(8,128)(2,1)S(1)}, u32[]{:S(2)}, u32[]{:S(2)}) collective-permute-start(bf16[3,64,1792]{2,1,0:T(8,128)(2,1)} %get-tuple-element.79), channel_id=1, source_target_pairs={{0,64},{16,80},{32,96},{48,112},{64,0},{80,16},{96,32},{112,48},{1... | collective-permute-start | bytes 2064392 | tf_op jit(solution)/shard_map/ppermute | solution.py:361
  101.2 16.0 %collective-permute-start.13 = (bf16[3,64,1792]{2,1,0:T(8,128)(2,1)}, bf16[3,64,1792]{2,1,0:T(8,128)(2,1)S(1)}, u32[]{:S(2)}, u32[]{:S(2)}) collective-permute-start(bf16[3,64,1792]{2,1,0:T(8,128)(2,1)} %get-tuple-element.74), channel_id=1, source_target_pairs={{0,32},{8,24},{16,48},{24,8},{32,64},{40,56},{48,80},{56,40},{64,9... | collective-permute-start | bytes 2064392 | tf_op jit(solution)/shard_map/ppermute | solution.py:359
  123.3 11.8 %collective-permute-start.16 = (bf16[2,64,1792]{2,1,0:T(8,128)(2,1)}, bf16[2,64,1792]{2,1,0:T(8,128)(2,1)S(1)}, u32[]{:S(2)}, u32[]{:S(2)}) collective-permute-start(bf16[2,64,1792]{2,1,0:T(8,128)(2,1)} %get-tuple-element.80.refs_1_), channel_id=1, source_target_pairs={{0,32},{8,24},{16,48},{24,8},{32,64},{40,56},{48,80},{56,40},{64,9... | collective-permute-start | bytes 1376264 | tf_op jit(solution)/shard_map/ppermute | solution.py:359
  139.3 32.3 %collective-permute-start.19 = (bf16[2,128,1792]{2,1,0:T(8,128)(2,1)}, bf16[2,128,1792]{2,1,0:T(8,128)(2,1)S(1)}, u32[]{:S(2)}, u32[]{:S(2)}) collective-permute-start(bf16[2,128,1792]{2,1,0:T(8,128)(2,1)} %get-tuple-element.81), channel_id=1, source_target_pairs={{0,16},{8,40},{16,0},{24,56},{32,48},{40,72},{48,32},{56,88},{64,8... | collective-permute-start | bytes 2752520 | tf_op jit(solution)/shard_map/ppermute | solution.py:351
  179.1 12.5 %collective-permute-start.20 = (bf16[2,128,1792]{2,1,0:T(8,128)(2,1)S(1)}, bf16[2,128,1792]{2,1,0:T(8,128)(2,1)S(1)}, u32[]{:S(2)}, u32[]{:S(2)}) collective-permute-start(bf16[2,128,1792]{2,1,0:T(8,128)(2,1)S(1)} %copy-done.24), channel_id=1, source_target_pairs={{0,16},{8,104},{16,0},{24,120},{32,48},{40,8},{48,32},{56,24},{64,... | collective-permute-start | bytes 2752520 | tf_op jit(solution)/shard_map/ppermute | solution.py:352
  179.1 15.9 %collective-permute-start.21 = (bf16[2,128,1792]{2,1,0:T(8,128)(2,1)S(1)}, bf16[2,128,1792]{2,1,0:T(8,128)(2,1)S(1)}, u32[]{:S(2)}, u32[]{:S(2)}) collective-permute-start(bf16[2,128,1792]{2,1,0:T(8,128)(2,1)S(1)} %copy-done.23), channel_id=1, source_target_pairs={{8,72},{24,88},{40,104},{56,120},{72,8},{88,24},{104,40},{120,56},... | collective-permute-start | bytes 2752520 | tf_op jit(solution)/shard_map/ppermute | solution.py:353
  206.6 21.5 %collective-permute-start.30 = (bf16[2,512,1792]{2,1,0:T(8,128)(2,1)}, bf16[2,512,1792]{2,1,0:T(8,128)(2,1)S(1)}, u32[]{:S(2)}, u32[]{:S(2)}) collective-permute-start(bf16[2,512,1792]{2,1,0:T(8,128)(2,1)} %get-tuple-element.98), channel_id=1, source_target_pairs={{0,8},{8,0},{16,24},{24,16},{32,40},{40,32},{48,56},{56,48},{64,72... | collective-permute-start | bytes 11010056 | tf_op jit(solution)/shard_map/ppermute | solution.py:414
  216.0 28.5 %collective-permute-start.25 = (bf16[2,64,512]{2,1,0:T(8,128)(2,1)S(1)}, bf16[2,64,512]{2,1,0:T(8,128)(2,1)S(1)}, u32[]{:S(2)}, u32[]{:S(2)}) collective-permute-start(bf16[2,64,512]{2,1,0:T(8,128)(2,1)S(1)} %fusion.7), channel_id=1, source_target_pairs={{0,4},{1,5},{2,6},{3,7},{4,0},{5,1},{6,2},{7,3},{8,12},{9,13},{10,... | collective-permute-start | bytes 393224 | tf_op jit(solution)/shard_map/ppermute | solution.py:405
  220.2 19.7 %collective-permute-start.26 = (bf16[128,1024]{1,0:T(8,128)(2,1)}, bf16[128,1024]{1,0:T(8,128)(2,1)S(1)}, u32[]{:S(2)}, u32[]{:S(2)}) collective-permute-start(bf16[128,1024]{1,0:T(8,128)(2,1)} %get-tuple-element.93), channel_id=1, source_target_pairs={{8,12},{9,13},{10,14},{11,15},{12,8},{13,9},{14,10},{15,11},{24,28... | collective-permute-start | bytes 786440 | tf_op jit(solution)/shard_map/ppermute | solution.py:479
  222.1 17.7 %collective-permute-start.27 = (bf16[128,1024]{1,0:T(8,128)(2,1)}, bf16[128,1024]{1,0:T(8,128)(2,1)S(1)}, u32[]{:S(2)}, u32[]{:S(2)}) collective-permute-start(bf16[128,1024]{1,0:T(8,128)(2,1)} %get-tuple-element.94), channel_id=1, source_target_pairs={{0,1},{1,2},{2,3},{3,0},{4,5},{5,6},{6,7},{7,4},{8,13},{9,14},{10,... | collective-permute-start | bytes 786440 | tf_op jit(solution)/shard_map/ppermute | solution.py:479
  225.4 14.4 %collective-permute-start.28 = (bf16[128,1024]{1,0:T(8,128)(2,1)}, bf16[128,1024]{1,0:T(8,128)(2,1)S(1)}, u32[]{:S(2)}, u32[]{:S(2)}) collective-permute-start(bf16[128,1024]{1,0:T(8,128)(2,1)} %get-tuple-element.95), channel_id=1, source_target_pairs={{0,2},{1,3},{2,0},{3,1},{4,6},{5,7},{6,4},{7,5},{8,14},{9,15},{10,... | collective-permute-start | bytes 786440 | tf_op jit(solution)/shard_map/ppermute | solution.py:479
  228.2 11.7 %collective-permute-start.29 = (bf16[128,1024]{1,0:T(8,128)(2,1)}, bf16[128,1024]{1,0:T(8,128)(2,1)S(1)}, u32[]{:S(2)}, u32[]{:S(2)}) collective-permute-start(bf16[128,1024]{1,0:T(8,128)(2,1)} %get-tuple-element.96), channel_id=1, source_target_pairs={{0,3},{1,0},{2,1},{3,2},{4,7},{5,4},{6,5},{7,6},{8,15},{9,12},{10,... | collective-permute-start | bytes 786440 | tf_op jit(solution)/shard_map/ppermute | solution.py:479
  (34 other events, 252.7 us)
Sparse Core Ops, SparseCore 0:
  121.6 49.6 all-gather.1

commit v7 on v0

v7 whole, which is shorter than its diff:
```python
import functools

import jax
import jax.numpy as jnp
from jax import lax
from jax.experimental import pallas as pl
from jax.experimental.pallas import tpu as pltpu
from jax.sharding import PartitionSpec as P

NY, NX, NC, NZ = 4, 2, 2, 4
PIECE = 64
BOTH = ("row", "col")


def row_at(y, x, core):
    return ((y % NY) * NX + x) * NC + core


def row_perm(core0, core1):
    pairs = []
    for y in range(NY):
        for x in range(NX):
            for core, move in ((0, core0), (1, core1)):
                if move is not None:
                    to_y, to_x = move(y, x)
                    pairs.append((row_at(y, x, core), row_at(to_y, to_x, core)))
    return pairs


def over_x(y, x):
    return y, 1 - x


def over_y(step):
    return lambda y, x: (y + step, x)


CORE_FLIP = [(i, i ^ 1) for i in range(NY * NX * NC)]


def gather_perm(step):
    pairs = []
    for row in range(NY * NX * NC):
        core = row % NC
        if core == 0 and step == 0:
            continue
        for hi in range(2):
            for z in range(NZ):
                source = (hi ^ core) * NZ + (z + step) % NZ
                pairs.append((row * 8 + source, row * 8 + hi * NZ + z))
    return pairs


def scatter_perm(step):
    return [(to, source) for source, to in gather_perm(step)]


def product(left, right, transposed):
    dims = (((1,), (1 if transposed else 0,)), ((), ()))
    return lax.dot_general(left, right, dims, preferred_element_type=jnp.float32)


def spans(width):
    return [(at, min(at + 256, width)) for at in range(0, width, 256)]


def shape(dims, dtype=jnp.bfloat16):
    return jax.ShapeDtypeStruct(dims, dtype)


def call(kernel, operands, out_shape, scratch=()):
    n_in, n_out = len(operands), len(out_shape)

    def run(*refs):
        kernel(refs[:n_in], refs[n_in : n_in + n_out], *refs[n_in + n_out :])

    vmem = pl.BlockSpec(memory_space=pltpu.VMEM)
    return pl.pallas_call(
        run,
        in_specs=[vmem] * n_in,
        out_specs=[vmem] * n_out,
        out_shape=out_shape,
        scratch_shapes=scratch,
        compiler_params=pltpu.CompilerParams(vmem_limit_bytes=12 * 2**20),
        cost_estimate=pl.CostEstimate(flops=1, bytes_accessed=1, transcendentals=0),
    )(*operands)


class Place:
    def __init__(self):
        row = lax.axis_index("row")
        self.core, self.x, self.y = row % NC, (row // NC) % NX, row // (NC * NX)
        self.other = 1 - self.x

    def piece(self, step, x):
        return ((self.y + step) % NY) * NX + x

    def choose(self, core0, core1):
        pieces = [jnp.where(self.core == 0, self.piece(*a), self.piece(*b)) for a, b in zip(core0, core1)]
        return [pl.ds(pl.multiple_of(piece * PIECE, PIECE), PIECE) for piece in pieces]

    def first(self):
        o = self.other
        core0 = [(o, o), (1 - o, o), (3 - o, o), (2 + o, o), (0, self.x), (0, self.x)]
        return self.choose(core0, [(step, x) for step in (1, 3, 2) for x in (0, 1)])

    def second(self):
        x, o = self.x, self.other
        return self.choose([(1, x), (3, x), (2, x), (0, x)], [(0, o), (0, x), (0, x), (0, x)])

    def gathered(self):
        x, o = self.x, self.other
        core0 = [(0, x), (3, x), (0, o), (3, o), (1, o), (2, o), (1, x), (2, x)]
        return self.choose(core0, [(0, x), (0, o)] + [(step, at) for step in (3, 1, 2) for at in (x, o)])

    def half(self, x):
        return pl.ds(pl.multiple_of(x * PIECE, PIECE), PIECE)


def pair_product(held, pair, at, end, transposed):
    half = held.shape[1] // 2
    chunk = (slice(at, end), slice(None)) if transposed else (slice(None), slice(at, end))
    own, other = [ref[chunk] for ref in pair]
    return product(held[:, :half], own, transposed) + product(held[:, half:], other, transposed)


def block_kernel(ins, outs):
    (block,) = outs
    half = block.shape[2] // 2
    for i in range(2):
        block[i, :, :half] = ins[i][...]
        block[i, :, half:] = ins[2 + i][...]


def first_kernel(ins, outs, tok_held, grad_held):
    place = Place()
    block, *blocks = ins[: NZ + 1]
    weights, messages = ins[NZ + 1 :], outs[2:]
    rows = block.shape[1]
    pieces = place.first()
    for i, held in enumerate((tok_held, grad_held)):
        acts = outs[i]
        acts[:rows] = jnp.where(place.core == 0, block[i], blocks[0][i])
        for k in range(1, NZ):
            acts[k * rows : (k + 1) * rows] = blocks[k][i]
        for slot, rows_at in enumerate(pieces):
            held[slot * PIECE : (slot + 1) * PIECE, :] = acts[rows_at, :]
    for which in range(3):
        held, transposed = ((tok_held, False), (grad_held, True))[which // 2]
        pair = weights[2 * which : 2 * which + 2]
        for at, end in spans(messages[0].shape[2]):
            total = pair_product(held, pair, at, end, transposed).astype(jnp.bfloat16)
            for i, message in enumerate(messages):
                message[which, :, at:end] = total[i * 2 * PIECE : (i + 1) * 2 * PIECE]


def partial_kernel(ins, outs, tok_held, grad_held):
    pieces = Place().second()
    for i, held in enumerate((tok_held, grad_held)):
        rows = ins[i]
        for slot, rows_at in enumerate(pieces):
            held[slot * PIECE : (slot + 1) * PIECE, :] = rows[rows_at, :]
        own, away = outs[1 + i], outs[3 + i]
        half = own.shape[1]
        own[...] = rows[:, :half]
        away[...] = rows[:, half:]
    for which in range(3):
        held, transposed = ((tok_held, False), (grad_held, True))[which // 2]
        pair = ins[2 + 2 * which : 4 + 2 * which]
        for at, end in spans(outs[0].shape[2]):
            outs[0][which, :, at:end] = pair_product(held, pair, at, end, transposed)


def second_kernel(ins, outs):
    place = Place()
    products, *heard = ins
    near, far = place.half(place.x), place.half(place.other)
    one = place.core == 1
    for which in range(3):
        for at, end in spans(outs[0].shape[2]):
            near2 = heard[1][which, near, at:end].astype(jnp.float32)
            far1, far2, far3 = [h[which, far, at:end].astype(jnp.float32) for h in heard]
            part1, part2, part3 = [
                products[which, slot * PIECE : (slot + 1) * PIECE, at:end] for slot in range(3)
            ]
            sum1 = part1 + far1 + jnp.where(one, far2 + far3, 0.0)
            high = sum1.astype(jnp.bfloat16)
            rest = sum1 - high.astype(jnp.float32)
            outs[0][which, :, at:end] = high
            outs[1][which, :, at:end] = jnp.where(one, rest, part2 + near2).astype(jnp.bfloat16)
            outs[2][which, :, at:end] = (part3 + far2).astype(jnp.bfloat16)


def unit_kernel(ins, outs):
    place = Place()
    products, first, second = ins[0], ins[1:4], ins[4:7]
    hidden, both = outs
    near, one = place.half(place.x), place.core == 1
    for at, end in spans(hidden.shape[1]):

        def summed(which):
            near1, near2, near3 = [h[which, near, at:end].astype(jnp.float32) for h in first]
            total = products[which, 3 * PIECE :, at:end] + near1
            total = total + jnp.where(one, near2 + near3, 0.0)
            return total + sum(h[which, :, at:end].astype(jnp.float32) for h in second)

        gate, up, d_hidden = [summed(which) for which in range(3)]
        sig_gate = jax.nn.sigmoid(gate)
        hidden[:, at:end] = (gate * sig_gate * up).astype(jnp.bfloat16)
        slope = d_hidden * up * sig_gate * (1.0 + gate * (1.0 - sig_gate))
        both[0, :, at:end] = slope.astype(jnp.bfloat16)
        both[1, :, at:end] = (d_hidden * gate * sig_gate).astype(jnp.bfloat16)


def weave_kernel(ins, outs):
    core = Place().core
    for rows, at_core in zip(ins, (core, 1 - core)):
        for piece in range(NY * NX):
            start = pl.multiple_of((piece * NC + at_core) * PIECE, PIECE)
            outs[0][pl.ds(start, PIECE), :] = rows[piece * PIECE : (piece + 1) * PIECE, :]


def pack_kernel(ins, outs):
    own, near1, near2, near3 = ins
    first, second = outs
    core0 = Place().core == 0
    first[:, :PIECE] = own[...]
    first[:, PIECE:] = near1[...]
    second[:, :PIECE] = jnp.where(core0, near2[...], own[...])
    second[:, PIECE:] = jnp.where(core0, near3[...], near1[...])


def layer_kernel(ins, outs, held):
    hidden, *weights = ins
    core = Place().core
    width = weights[0].shape[1]
    for piece in range(NY * NX):
        start = pl.multiple_of((piece * NC + core) * PIECE, PIECE)
        held[piece * PIECE : (piece + 1) * PIECE, :] = hidden[pl.ds(start, PIECE), :]
    for side, weight in enumerate(weights):
        for at, end in spans(width):
            outs[0][:, side * width + at : side * width + end] = product(
                held[...], weight[:, at:end], False
            )


def input_kernel(ins, outs):
    place = Place()
    layer, own, near1, near2, near3, far1, far2, far3 = ins[:8]
    weights = ins[8:]
    *messages, d_set, kept = outs
    core0 = place.core == 0
    pieces = place.gathered()
    values = [own[...], near1[...], far1[:, :PIECE], far1[:, PIECE:], far2[:, :PIECE], far2[:, PIECE:]]
    values.append(jnp.where(core0, near2[...], far3[:, :PIECE]))
    values.append(jnp.where(core0, near3[...], far3[:, PIECE:]))
    for rows_at, value in zip(pieces, values):
        d_set[:, rows_at, :] = value
    depth = weights[0].shape[0]
    block = NX * PIECE
    for side in range(2):
        for at, end in spans(depth):
            gate, up = [weights[2 * side + i][at:end, :] for i in range(2)]
            total = product(d_set[0], gate, True) + product(d_set[1], up, True)
            columns = slice(side * depth + at, side * depth + end)
            for i, term in enumerate((layer[:, columns], total)):
                kept[i, :, columns] = term[:block]
                for k in range(NZ):
                    rows = term[k * block : (k + 1) * block]
                    messages[k][i, :, columns] = rows.astype(jnp.bfloat16)


def send_first(sent):
    return (
        lax.ppermute(sent[0], "row", row_perm(over_x, over_y(1))),
        lax.ppermute(sent[1], "row", row_perm(over_x, over_y(-1))),
        lax.ppermute(sent[2], "row", row_perm(None, over_y(2))),
    )


def send_second(sent):
    return (
        lax.ppermute(sent[0], "row", row_perm(over_y(1), over_x)),
        lax.ppermute(sent[1], "row", row_perm(over_y(-1), over_x)),
        lax.ppermute(sent[2], "row", row_perm(over_y(2), None)),
    )


def body(tokens, gate_weight, up_weight, down_weight, grad_output):
    core = lax.axis_index("row") % NC
    flip = lambda value: lax.ppermute(value, "row", CORE_FLIP)
    after = lambda value, *others: lax.optimization_barrier((value, *others))[0]
    width, ff_width = gate_weight.shape
    half_rows = NY * NX * PIECE
    rows = tokens.shape[0]

    tok_theirs, grad_theirs = flip(tokens), flip(grad_output)
    gate_other, up_other, down_other = flip(gate_weight), flip(up_weight), flip(down_weight)
    (own_block,) = call(
        block_kernel, [tokens, grad_output, tok_theirs, grad_theirs], [shape((2, rows, 2 * width))]
    )
    starts = [own_block, own_block, after(own_block, gate_other), after(own_block, up_other)]
    blocks = [lax.ppermute(starts[step], BOTH, gather_perm(step)) for step in range(NZ)]

    both_weights = [gate_weight, gate_other, up_weight, up_other]
    weights = [*both_weights, down_weight, down_other]
    held = lambda pieces: [pltpu.VMEM((pieces * PIECE, 2 * width), jnp.bfloat16)] * 2
    tok_half, grad_half, *sent = call(
        first_kernel,
        [own_block, *blocks, *weights],
        [shape((half_rows, 2 * width))] * 2 + [shape((3, 2 * PIECE, ff_width))] * 3,
        held(6),
    )
    heard = send_first(sent)
    products, tok_own, grad_own, tok_away, grad_away = call(
        partial_kernel,
        [tok_half, grad_half, *weights],
        [shape((3, 4 * PIECE, ff_width), jnp.float32)] + [shape((half_rows, width))] * 4,
        held(4),
    )
    tok_other, grad_other = flip(tok_away), flip(grad_away)
    (grad_all,) = call(weave_kernel, [grad_own, grad_other], [shape((2 * half_rows, width))])
    *heard, grad_all, tok_other = lax.optimization_barrier((*heard, grad_all, tok_other))
    sent = call(second_kernel, [products, *heard], [shape((3, PIECE, ff_width))] * 3)
    hidden, d_own = call(
        unit_kernel,
        [products, *heard, *send_second(sent)],
        [shape((PIECE, ff_width)), shape((2, PIECE, ff_width))],
    )
    hidden = lax.all_gather(hidden, "row", axis=0, tiled=True)

    near = send_second([d_own] * 3)
    first, second = call(pack_kernel, [d_own, *near], [shape((2, 2 * PIECE, ff_width))] * 2)
    far = send_first([first, second, first])
    hidden = after(hidden, far[0])
    (layer,) = call(
        layer_kernel,
        [hidden, down_weight, down_other],
        [shape((half_rows, 2 * width), jnp.float32)],
        [pltpu.VMEM((half_rows, ff_width), jnp.bfloat16)],
    )
    block = (2, rows, 2 * width)
    *messages, d_set, kept = call(
        input_kernel,
        [layer, d_own, *near, *far, gate_weight, up_weight, gate_other, up_other],
        [shape(block)] * 4 + [shape((2, half_rows, ff_width)), shape(block, jnp.float32)],
    )
    messages = [lax.ppermute(messages[k], BOTH, scatter_perm(k)) for k in range(NZ)]
    d_other = flip(d_set)
    dot = functools.partial(lax.dot_general, preferred_element_type=jnp.float32)
    contract_first = (((0,), (0,)), ((), ()))
    grad_down = dot(hidden, grad_all, contract_first).astype(jnp.bfloat16)

    def weight_gradient(which):
        total = dot(tok_own, d_set[which], contract_first)
        return (total + dot(tok_other, d_other[which], contract_first)).astype(jnp.bfloat16)

    grad_gate, grad_up = weight_gradient(0), weight_gradient(1)
    *messages, grad_gate, grad_up = lax.optimization_barrier((*messages, grad_gate, grad_up))
    total = jnp.where(core == 0, kept, 0.0)
    for message in messages:
        total = total + message.astype(jnp.float32)
    total = (total[:, :, :width] + flip(total[:, :, width:])).astype(jnp.bfloat16)
    return (total[0], total[1], grad_gate, grad_up, grad_down)


def solution(mesh):
    placed = (P("col", "row"), P("row", "col"), P("row", "col"), P("col", "row"), P("col", "row"))
    return jax.shard_map(
        body,
        mesh=mesh,
        in_specs=placed,
        out_specs=(
            P("col", "row"),
            P("col", "row"),
            P("row", "col"),
            P("row", "col"),
            P("col", "row"),
        ),
        check_vma=False,
    )
```

time: 611 us -> 239 us (0.39)
  waiting for transfers between devices: 535 us -> 115 us
  starting transfers between devices: 0.5 us -> 53 us
  matrix products: 41.5 us -> 16.8 us
  Pallas kernels: 0 us -> 20.8 us
  other arithmetic: 12.2 us -> 0.51 us
  local copies, waits for them, and re-layouts: 6.23 us -> 16.5 us
    reduce_scatter x4 -> x0, waiting for transfers between devices: 362 us -> none  [the longest x2 238 us: share_sum(): lax.psum_scatter(term_fn(jnp.int32(0), lax.axis_size('row') * row_count),...]
    all_gather x4 -> x1, waiting for transfers between devices: 171 us -> 0.97 us  [body(): hidden = lax.all_gather(hidden, 'row', axis=0, tiled=True)]
    ppermute x0 -> x29, waiting for transfers between devices: none -> 114 us  [the longest x2 36.1 us: send_first(): lax.ppermute(sent[0], 'row', row_perm(over_x, over_y(1)))]
    ppermute x0 -> x29, starting transfers between devices: none -> 52.9 us  [the longest x4 20.5 us: body(): lax.ppermute(messages[k], BOTH, scatter_perm(k))]
    dot_general x9 -> x5, matrix products: 41.5 us -> 16.8 us  [the longest x2 7.93 us: weight_gradient(): total = dot(tok_own, d_set[which], contract_first)]
    pallas_call x0 -> x9, Pallas kernels: none -> 20.8 us  [call(): pl.pallas_call(run, in_specs=[vmem] * n_in, out_specs=[vmem] * n_out, out...]
    unnamed x14 -> x62, local copies, waits for them, and re-layouts: 6.23 us -> 15.8 us
    concatenate x2 -> x0, other arithmetic: 6.72 us -> none  [the longest x1 5.92 us: gate_terms(): return jnp.concatenate([gate_part, up_part], axis=1)]
  transfers between devices with their start and end apart: 8 -> 30, of which waited for: 8 -> 20; matrix products, arithmetic and copies ran while one was open for 9% -> 7% of each run, Pallas kernels for 0% -> 3%
where the time goes in v7:
time: 239 us; the launch traced here: 237 us
  waiting for transfers between devices  115 us (48%)
  starting transfers between devices  53 us (22%)
  Pallas kernels  20.8 us (9%)
  matrix products  16.8 us (7%)
  local copies, waits for them, and re-layouts  16.5 us (7%)
  between operations  14.4 us (6%)
    ppermute x2, waiting for transfers between devices, send_first(): lax.ppermute(sent[0], 'row', row_perm(over_x, over_y(1)))  36.1 us
    ppermute x4, waiting for transfers between devices, body(): lax.ppermute(starts[step], BOTH, gather_perm(step))  21.1 us
    pallas_call x9, Pallas kernels, call(): pl.pallas_call(run, in_specs=[vmem] * n_in, out_specs=[vmem] * n_out, out...  20.8 us
    ppermute x4, starting transfers between devices, body(): lax.ppermute(messages[k], BOTH, scatter_perm(k))  20.5 us
    unnamed x62, local copies, waits for them, and re-layouts  15.8 us
    ppermute x2, waiting for transfers between devices, send_second(): lax.ppermute(sent[0], 'row', row_perm(over_y(1), over_x))  13.2 us
    ppermute x2, starting transfers between devices, send_first(): lax.ppermute(sent[2], 'row', row_perm(None, over_y(2)))  12 us
    ppermute x2, waiting for transfers between devices, send_second(): lax.ppermute(sent[1], 'row', row_perm(over_y(-1), over_x))  12 us
  transfers between devices with their start and end apart: 30, of which 20 were waited for; matrix products, arithmetic and copies ran while one was open for 7% of the time, Pallas kernels for 3%

profile of v7, /device:TPU:17, one launch (start us, length us, event | category | flops | bytes accessed | tf_op | source)
XLA Modules:
  0.0 237.0 jit_solution(4222717221404771931)
XLA Ops:
  9.0 8.0 %collective-permute-done.refs_2_ = bf16[128,512]{1,0:T(8,128)(2,1)S(1)} collective-permute-done((bf16[128,512]{1,0:T(8,128)(2,1)}, bf16[128,512]{1,0:T(8,128)(2,1)S(1)}, u32[]{:S(2)}, u32[]{:S(2)}) %collective-permute-start) | collective-permute-done | bytes 131104 | tf_op jit(solution)/shard_map/ppermute | solution.py:291
  19.1 4.7 %collective-permute-start.2 = (bf16[2,128,1024]{2,1,0:T(8,128)(2,1)S(1)}, bf16[2,128,1024]{2,1,0:T(8,128)(2,1)S(1)}, u32[]{:S(2)}, u32[]{:S(2)}) collective-permute-start(bf16[2,128,1024]{2,1,0:T(8,128)(2,1)S(1)} %shard_map.92.refs_0_), channel_id=1, source_target_pairs={{12,8},{13,9},{14,10},{15,11},{8,12},{9,13},{10,14},{11,15},{28,24... | collective-permute-start | bytes 1572872 | tf_op jit(solution)/shard_map/ppermute | solution.py:303
  23.7 3.8 %collective-permute-start.3 = (bf16[2,128,1024]{2,1,0:T(8,128)(2,1)S(1)}, bf16[2,128,1024]{2,1,0:T(8,128)(2,1)S(1)}, u32[]{:S(2)}, u32[]{:S(2)}) collective-permute-start(bf16[2,128,1024]{2,1,0:T(8,128)(2,1)S(1)} %shard_map.92.refs_0_), channel_id=1, source_target_pairs={{1,0},{2,1},{3,2},{0,3},{5,4},{6,5},{7,6},{4,7},{13,8},{14,9},{15,... | collective-permute-start | bytes 1572872 | tf_op jit(solution)/shard_map/ppermute | solution.py:303
  30.8 6.8 %collective-permute-done.3.refs_2_ = bf16[2,128,1024]{2,1,0:T(8,128)(2,1)S(1)} collective-permute-done((bf16[2,128,1024]{2,1,0:T(8,128)(2,1)S(1)}, bf16[2,128,1024]{2,1,0:T(8,128)(2,1)S(1)}, u32[]{:S(2)}, u32[]{:S(2)}) %collective-permute-start.3) | collective-permute-done | bytes 524320 | tf_op jit(solution)/shard_map/ppermute | solution.py:303
  37.6 9.4 %collective-permute-done.5.refs_3_ = bf16[2,128,1024]{2,1,0:T(8,128)(2,1)S(1)} collective-permute-done((bf16[2,128,1024]{2,1,0:T(8,128)(2,1)S(1)}, bf16[2,128,1024]{2,1,0:T(8,128)(2,1)S(1)}, u32[]{:S(2)}, u32[]{:S(2)}) %collective-permute-start.5) | collective-permute-done | bytes 524320 | tf_op jit(solution)/shard_map/ppermute | solution.py:303
  47.0 4.8 %collective-permute-done.7.refs_4_ = bf16[2,128,1024]{2,1,0:T(8,128)(2,1)S(1)} collective-permute-done((bf16[2,128,1024]{2,1,0:T(8,128)(2,1)S(1)}, bf16[2,128,1024]{2,1,0:T(8,128)(2,1)S(1)}, u32[]{:S(2)}, u32[]{:S(2)}) %collective-permute-start.7) | collective-permute-done | bytes 524320 | tf_op jit(solution)/shard_map/ppermute | solution.py:303
  56.2 4.5 %shard_map.93 = (bf16[512,1024]{1,0:T(8,128)(2,1)S(1)}, bf16[512,1024]{1,0:T(8,128)(2,1)S(1)}, bf16[3,128,1792]{2,1,0:T(8,128)(2,1)S(1)}, bf16[3,128,1792]{2,1,0:T(8,128)(2,1)S(1)}, bf16[3,128,1792]{2,1,0:T(8,128)(2,1)S(1)}) custom-call(bf16[2,128,1024]{2,1,0:T(8,128)(2,1)S(1)} %shard_map.92.refs_0_, ...), custom_call_target="tpu_custom_call" | custom-call | flops 1 | bytes 1 | tf_op jit(solution)/shard_map/pallas_call | solution.py:78
  61.0 4.5 %collective-permute-start.11 = (bf16[3,128,1792]{2,1,0:T(8,128)(2,1)S(1)}, bf16[3,128,1792]{2,1,0:T(8,128)(2,1)S(1)}, u32[]{:S(2)}, u32[]{:S(2)}) collective-permute-start(bf16[3,128,1792]{2,1,0:T(8,128)(2,1)S(1)} %get-tuple-element.49), channel_id=1, source_target_pairs={{8,72},{24,88},{40,104},{56,120},{72,8},{88,24},{104,40},{120,56},... | collective-permute-start | bytes 4128776 | tf_op jit(solution)/shard_map/ppermute | solution.py:277
  71.5 6.8 %collective-permute-done.10.refs_2_ = bf16[3,128,1792]{2,1,0:T(8,128)(2,1)S(1)} collective-permute-done((bf16[3,128,1792]{2,1,0:T(8,128)(2,1)S(1)}, bf16[3,128,1792]{2,1,0:T(8,128)(2,1)S(1)}, u32[]{:S(2)}, u32[]{:S(2)}) %collective-permute-start.10) | collective-permute-done | bytes 1376288 | tf_op jit(solution)/shard_map/ppermute | solution.py:276
  81.7 16.9 %collective-permute-done.9.refs_1_ = bf16[3,128,1792]{2,1,0:T(8,128)(2,1)S(1)} collective-permute-done((bf16[3,128,1792]{2,1,0:T(8,128)(2,1)S(1)}, bf16[3,128,1792]{2,1,0:T(8,128)(2,1)S(1)}, u32[]{:S(2)}, u32[]{:S(2)}) %collective-permute-start.9) | collective-permute-done | bytes 1376288 | tf_op jit(solution)/shard_map/ppermute | solution.py:275
  101.7 7.7 %collective-permute-done.14.refs_4_ = bf16[3,64,1792]{2,1,0:T(8,128)(2,1)S(1)} collective-permute-done((bf16[3,64,1792]{2,1,0:T(8,128)(2,1)S(1)}, bf16[3,64,1792]{2,1,0:T(8,128)(2,1)S(1)}, u32[]{:S(2)}, u32[]{:S(2)}) %collective-permute-start.14) | collective-permute-done | bytes 688160 | tf_op jit(solution)/shard_map/ppermute | solution.py:283
  109.4 7.4 %collective-permute-done.15.refs_5_ = bf16[3,64,1792]{2,1,0:T(8,128)(2,1)S(1)} collective-permute-done((bf16[3,64,1792]{2,1,0:T(8,128)(2,1)S(1)}, bf16[3,64,1792]{2,1,0:T(8,128)(2,1)S(1)}, u32[]{:S(2)}, u32[]{:S(2)}) %collective-permute-start.15) | collective-permute-done | bytes 688160 | tf_op jit(solution)/shard_map/ppermute | solution.py:284
  120.2 5.5 %collective-permute-done.17.refs_1_.refs_2_ = bf16[2,64,1792]{2,1,0:T(8,128)(2,1)S(1)} collective-permute-done((bf16[2,64,1792]{2,1,0:T(8,128)(2,1)S(1)}, bf16[2,64,1792]{2,1,0:T(8,128)(2,1)S(1)}, u32[]{:S(2)}, u32[]{:S(2)}) %collective-permute-start.17) | collective-permute-done | bytes 458784 | tf_op jit(solution)/shard_map/ppermute | solution.py:283
  125.7 4.6 %collective-permute-done.18.refs_2_.refs_3_ = bf16[2,64,1792]{2,1,0:T(8,128)(2,1)S(1)} collective-permute-done((bf16[2,64,1792]{2,1,0:T(8,128)(2,1)S(1)}, bf16[2,64,1792]{2,1,0:T(8,128)(2,1)S(1)}, u32[]{:S(2)}, u32[]{:S(2)}) %collective-permute-start.18) | collective-permute-done | bytes 458784 | tf_op jit(solution)/shard_map/ppermute | solution.py:284
  133.9 7.5 %collective-permute-start.22 = (bf16[2,128,1792]{2,1,0:T(8,128)(2,1)}, bf16[2,128,1792]{2,1,0:T(8,128)(2,1)}, u32[]{:S(2)}, u32[]{:S(2)}) collective-permute-start(bf16[2,128,1792]{2,1,0:T(8,128)(2,1)} %get-tuple-element.61), channel_id=1, source_target_pairs={{8,72},{24,88},{40,104},{56,120},{72,8},{88,24},{104,40},{120,56},... | collective-permute-start | bytes 2752520 | tf_op jit(solution)/shard_map/ppermute | solution.py:277
  141.5 19.2 %collective-permute-done.20.refs_5_ = bf16[2,128,1792]{2,1,0:T(8,128)(2,1)S(1)} collective-permute-done((bf16[2,128,1792]{2,1,0:T(8,128)(2,1)}, bf16[2,128,1792]{2,1,0:T(8,128)(2,1)S(1)}, u32[]{:S(2)}, u32[]{:S(2)}) %collective-permute-start.20) | collective-permute-done | bytes 917536 | tf_op jit(solution)/shard_map/ppermute | solution.py:275
  168.2 3.4 %collective-permute-done.22.refs_7_ = bf16[2,128,1792]{2,1,0:T(8,128)(2,1)} collective-permute-done((bf16[2,128,1792]{2,1,0:T(8,128)(2,1)}, bf16[2,128,1792]{2,1,0:T(8,128)(2,1)}, u32[]{:S(2)}, u32[]{:S(2)}) %collective-permute-start.22) | collective-permute-done | bytes 917536 | tf_op jit(solution)/shard_map/ppermute | solution.py:277
  171.7 7.8 %shard_map.100 = (bf16[2,128,1024]{2,1,0:T(8,128)(2,1)S(1)}, bf16[2,128,1024]{2,1,0:T(8,128)(2,1)S(1)}, bf16[2,128,1024]{2,1,0:T(8,128)(2,1)S(1)}, bf16[2,128,10...) custom-call(f32[512,1024]{1,0:T(8,128)S(1)} %shard_map.99.refs_0_, ...), custom_call_target="tpu_custom_call" | custom-call | flops 1 | bytes 1 | tf_op jit(solution)/shard_map/pallas_call | solution.py:78
  181.8 4.5 %collective-permute-start.23 = (bf16[2,128,1024]{2,1,0:T(8,128)(2,1)}, bf16[2,128,1024]{2,1,0:T(8,128)(2,1)S(1)}, u32[]{:S(2)}, u32[]{:S(2)}) collective-permute-start(bf16[2,128,1024]{2,1,0:T(8,128)(2,1)} %copy-done.28), channel_id=1, source_target_pairs={{8,12},{9,13},{10,14},{11,15},{12,8},{13,9},{14,10},{15,11},{24,28... | collective-permute-start | bytes 1572872 | tf_op jit(solution)/shard_map/ppermute | solution.py:348
  186.7 11.2 %collective-permute-start.25 = (bf16[2,128,1024]{2,1,0:T(8,128)(2,1)}, bf16[2,128,1024]{2,1,0:T(8,128)(2,1)S(1)}, u32[]{:S(2)}, u32[]{:S(2)}) collective-permute-start(bf16[2,128,1024]{2,1,0:T(8,128)(2,1)} %copy-done.26), channel_id=1, source_target_pairs={{0,2},{1,3},{2,0},{3,1},{4,6},{5,7},{6,4},{7,5},{8,14},{9,15},{10,... | collective-permute-start | bytes 1572872 | tf_op jit(solution)/shard_map/ppermute | solution.py:348
  197.9 4.4 %collective-permute-start.26 = (bf16[2,128,1024]{2,1,0:T(8,128)(2,1)S(1)}, bf16[2,128,1024]{2,1,0:T(8,128)(2,1)S(1)}, u32[]{:S(2)}, u32[]{:S(2)}) collective-permute-start(bf16[2,128,1024]{2,1,0:T(8,128)(2,1)S(1)} %get-tuple-element.68), channel_id=1, source_target_pairs={{0,3},{1,0},{2,1},{3,2},{4,7},{5,4},{6,5},{7,6},{8,15},{9,12},{10,... | collective-permute-start | bytes 1572872 | tf_op jit(solution)/shard_map/ppermute | solution.py:348
  205.1 4.0 %add_convert_fusion = bf16[512,1792]{1,0:T(8,128)(2,1)} fusion(f32[512,1792]{1,0:T(8,128)S(1)} %fusion, bf16[512,512]{1,0:T(8,128)(2,1)S(1)} %get-tuple-element.69, bf16[2,512,1792]{2,1,0:T(8,128)(2,1)} %get-tuple-element.70), kind=kOutput, calls=%fused_computation | convolution fusion | flops 941359104 | bytes 7864320 | tf_op jit(solution)/shard_map/dot_general | solution.py:355
  211.8 3.9 %add_convert_fusion.1 = bf16[512,1792]{1,0:T(8,128)(2,1)} fusion(f32[512,1792]{1,0:T(8,128)S(1)} %fusion.1, bf16[512,512]{1,0:T(8,128)(2,1)S(1)} %get-tuple-element.69, bf16[2,512,1792]{2,1,0:T(8,128)(2,1)} %get-tuple-element.70), kind=kOutput, calls=%fused_computation.1 | convolution fusion | flops 941359104 | bytes 7864320 | tf_op jit(solution)/shard_map/dot_general | solution.py:355
  215.9 7.7 %collective-permute-done.26 = bf16[2,128,1024]{2,1,0:T(8,128)(2,1)S(1)} collective-permute-done((bf16[2,128,1024]{2,1,0:T(8,128)(2,1)S(1)}, bf16[2,128,1024]{2,1,0:T(8,128)(2,1)S(1)}, u32[]{:S(2)}, u32[]{:S(2)}) %collective-permute-start.26) | collective-permute-done | bytes 524320 | tf_op jit(solution)/shard_map/ppermute | solution.py:348
  (117 shorter events, 53.6 us)
Async XLA Ops:
  7.2 155.4 %all-gather.2.cloned.1.call-start = ((), (), s32[]{:S(2)}) async-start(), calls=%async_computation | async-start | bytes 3899392 | tf_op jit(solution)/shard_map/all_gather | solution.py:330
  7.2 20.3 %collective-permute-start.4 = (bf16[512,1792]{1,0:T(8,128)(2,1)}, bf16[512,1792]{1,0:T(8,128)(2,1)S(1)}, u32[]{:S(2)}, u32[]{:S(2)}) collective-permute-start(bf16[512,1792]{1,0:T(8,128)(2,1)} %refs_8_.1), channel_id=1, source_target_pairs={{0,8},{8,0},{16,24},{24,16},{32,40},{40,32},{48,56},{56,48},{64,72... | collective-permute-start | bytes 5505032 | tf_op jit(solution)/shard_map/ppermute | solution.py:291
  8.0 21.7 %collective-permute-start.6 = (bf16[512,1792]{1,0:T(8,128)(2,1)}, bf16[512,1792]{1,0:T(8,128)(2,1)S(1)}, u32[]{:S(2)}, u32[]{:S(2)}) collective-permute-start(bf16[512,1792]{1,0:T(8,128)(2,1)} %refs_9_.3), channel_id=1, source_target_pairs={{0,8},{8,0},{16,24},{24,16},{32,40},{40,32},{48,56},{56,48},{64,72... | collective-permute-start | bytes 5505032 | tf_op jit(solution)/shard_map/ppermute | solution.py:291
  8.1 29.5 %collective-permute-start.8 = (bf16[1792,512]{1,0:T(8,128)(2,1)}, bf16[1792,512]{1,0:T(8,128)(2,1)S(1)}, u32[]{:S(2)}, u32[]{:S(2)}) collective-permute-start(bf16[1792,512]{1,0:T(8,128)(2,1)} %refs_1_.3), channel_id=1, source_target_pairs={{0,8},{8,0},{16,24},{24,16},{32,40},{40,32},{48,56},{56,48},{64,72... | collective-permute-start | bytes 5505032 | tf_op jit(solution)/shard_map/ppermute | solution.py:291
  19.1 11.7 %collective-permute-start.2 = (bf16[2,128,1024]{2,1,0:T(8,128)(2,1)S(1)}, bf16[2,128,1024]{2,1,0:T(8,128)(2,1)S(1)}, u32[]{:S(2)}, u32[]{:S(2)}) collective-permute-start(bf16[2,128,1024]{2,1,0:T(8,128)(2,1)S(1)} %shard_map.92.refs_0_), channel_id=1, source_target_pairs={{12,8},{13,9},{14,10},{15,11},{8,12},{9,13},{10,14},{11,15},{28,24... | collective-permute-start | bytes 1572872 | tf_op jit(solution)/shard_map/ppermute | solution.py:303
  23.7 13.8 %collective-permute-start.3 = (bf16[2,128,1024]{2,1,0:T(8,128)(2,1)S(1)}, bf16[2,128,1024]{2,1,0:T(8,128)(2,1)S(1)}, u32[]{:S(2)}, u32[]{:S(2)}) collective-permute-start(bf16[2,128,1024]{2,1,0:T(8,128)(2,1)S(1)} %shard_map.92.refs_0_), channel_id=1, source_target_pairs={{1,0},{2,1},{3,2},{0,3},{5,4},{6,5},{7,6},{4,7},{13,8},{14,9},{15,... | collective-permute-start | bytes 1572872 | tf_op jit(solution)/shard_map/ppermute | solution.py:303
  27.5 19.5 %collective-permute-start.5 = (bf16[2,128,1024]{2,1,0:T(8,128)(2,1)S(1)}, bf16[2,128,1024]{2,1,0:T(8,128)(2,1)S(1)}, u32[]{:S(2)}, u32[]{:S(2)}) collective-permute-start(bf16[2,128,1024]{2,1,0:T(8,128)(2,1)S(1)} %shard_map.92.refs_0_), channel_id=1, source_target_pairs={{2,0},{3,1},{0,2},{1,3},{6,4},{7,5},{4,6},{5,7},{14,8},{15,9},{12,... | collective-permute-start | bytes 1572872 | tf_op jit(solution)/shard_map/ppermute | solution.py:303
  29.6 22.1 %collective-permute-start.7 = (bf16[2,128,1024]{2,1,0:T(8,128)(2,1)S(1)}, bf16[2,128,1024]{2,1,0:T(8,128)(2,1)S(1)}, u32[]{:S(2)}, u32[]{:S(2)}) collective-permute-start(bf16[2,128,1024]{2,1,0:T(8,128)(2,1)S(1)} %shard_map.92.refs_0_), channel_id=1, source_target_pairs={{3,0},{0,1},{1,2},{2,3},{7,4},{4,5},{5,6},{6,7},{15,8},{12,9},{13,... | collective-permute-start | bytes 1572872 | tf_op jit(solution)/shard_map/ppermute | solution.py:303
  60.8 17.5 %collective-permute-start.10 = (bf16[3,128,1792]{2,1,0:T(8,128)(2,1)S(1)}, bf16[3,128,1792]{2,1,0:T(8,128)(2,1)S(1)}, u32[]{:S(2)}, u32[]{:S(2)}) collective-permute-start(bf16[3,128,1792]{2,1,0:T(8,128)(2,1)S(1)} %get-tuple-element.48), channel_id=1, source_target_pairs={{0,16},{8,104},{16,0},{24,120},{32,48},{40,8},{48,32},{56,24},{64,... | collective-permute-start | bytes 4128776 | tf_op jit(solution)/shard_map/ppermute | solution.py:276
  61.0 20.7 %collective-permute-start.11 = (bf16[3,128,1792]{2,1,0:T(8,128)(2,1)S(1)}, bf16[3,128,1792]{2,1,0:T(8,128)(2,1)S(1)}, u32[]{:S(2)}, u32[]{:S(2)}) collective-permute-start(bf16[3,128,1792]{2,1,0:T(8,128)(2,1)S(1)} %get-tuple-element.49), channel_id=1, source_target_pairs={{8,72},{24,88},{40,104},{56,120},{72,8},{88,24},{104,40},{120,56},... | collective-permute-start | bytes 4128776 | tf_op jit(solution)/shard_map/ppermute | solution.py:277
  65.5 33.0 %collective-permute-start.9 = (bf16[3,128,1792]{2,1,0:T(8,128)(2,1)S(1)}, bf16[3,128,1792]{2,1,0:T(8,128)(2,1)S(1)}, u32[]{:S(2)}, u32[]{:S(2)}) collective-permute-start(bf16[3,128,1792]{2,1,0:T(8,128)(2,1)S(1)} %get-tuple-element.47), channel_id=1, source_target_pairs={{0,16},{8,40},{16,0},{24,56},{32,48},{40,72},{48,32},{56,88},{64,8... | collective-permute-start | bytes 4128776 | tf_op jit(solution)/shard_map/ppermute | solution.py:275
  99.3 10.2 %collective-permute-start.14 = (bf16[3,64,1792]{2,1,0:T(8,128)(2,1)S(1)}, bf16[3,64,1792]{2,1,0:T(8,128)(2,1)S(1)}, u32[]{:S(2)}, u32[]{:S(2)}) collective-permute-start(bf16[3,64,1792]{2,1,0:T(8,128)(2,1)S(1)} %get-tuple-element.56), channel_id=1, source_target_pairs={{0,32},{8,24},{16,48},{24,8},{32,64},{40,56},{48,80},{56,40},{64,9... | collective-permute-start | bytes 2064392 | tf_op jit(solution)/shard_map/ppermute | solution.py:283
  100.5 16.3 %collective-permute-start.15 = (bf16[3,64,1792]{2,1,0:T(8,128)(2,1)S(1)}, bf16[3,64,1792]{2,1,0:T(8,128)(2,1)S(1)}, u32[]{:S(2)}, u32[]{:S(2)}) collective-permute-start(bf16[3,64,1792]{2,1,0:T(8,128)(2,1)S(1)} %get-tuple-element.57), channel_id=1, source_target_pairs={{0,96},{8,24},{16,112},{24,8},{32,0},{40,56},{48,16},{56,40},{64,3... | collective-permute-start | bytes 2064392 | tf_op jit(solution)/shard_map/ppermute | solution.py:284
  100.8 16.0 %collective-permute-start.16 = (bf16[3,64,1792]{2,1,0:T(8,128)(2,1)S(1)}, bf16[3,64,1792]{2,1,0:T(8,128)(2,1)S(1)}, u32[]{:S(2)}, u32[]{:S(2)}) collective-permute-start(bf16[3,64,1792]{2,1,0:T(8,128)(2,1)S(1)} %get-tuple-element.58), channel_id=1, source_target_pairs={{0,64},{16,80},{32,96},{48,112},{64,0},{80,16},{96,32},{112,48},{1... | collective-permute-start | bytes 2064392 | tf_op jit(solution)/shard_map/ppermute | solution.py:285
  119.2 11.1 %collective-permute-start.18 = (bf16[2,64,1792]{2,1,0:T(8,128)(2,1)S(1)}, bf16[2,64,1792]{2,1,0:T(8,128)(2,1)S(1)}, u32[]{:S(2)}, u32[]{:S(2)}) collective-permute-start(bf16[2,64,1792]{2,1,0:T(8,128)(2,1)S(1)} %get-tuple-element.60.refs_0_.refs_1_), channel_id=1, source_target_pairs={{0,96},{8,24},{16,112},{24,8},{32,0},{40,56},{48,16},{56,40},{64,3... | collective-permute-start | bytes 1376264 | tf_op jit(solution)/shard_map/ppermute | solution.py:284
  119.5 10.8 %collective-permute-start.19 = (bf16[2,64,1792]{2,1,0:T(8,128)(2,1)S(1)}, bf16[2,64,1792]{2,1,0:T(8,128)(2,1)S(1)}, u32[]{:S(2)}, u32[]{:S(2)}) collective-permute-start(bf16[2,64,1792]{2,1,0:T(8,128)(2,1)S(1)} %get-tuple-element.60.refs_0_.refs_1_), channel_id=1, source_target_pairs={{0,64},{16,80},{32,96},{48,112},{64,0},{80,16},{96,32},{112,48},{1... | collective-permute-start | bytes 1376264 | tf_op jit(solution)/shard_map/ppermute | solution.py:285
  132.5 28.2 %collective-permute-start.20 = (bf16[2,128,1792]{2,1,0:T(8,128)(2,1)}, bf16[2,128,1792]{2,1,0:T(8,128)(2,1)S(1)}, u32[]{:S(2)}, u32[]{:S(2)}) collective-permute-start(bf16[2,128,1792]{2,1,0:T(8,128)(2,1)} %get-tuple-element.61), channel_id=1, source_target_pairs={{0,16},{8,40},{16,0},{24,56},{32,48},{40,72},{48,32},{56,88},{64,8... | collective-permute-start | bytes 2752520 | tf_op jit(solution)/shard_map/ppermute | solution.py:275
  133.9 34.3 %collective-permute-start.21 = (bf16[2,128,1792]{2,1,0:T(8,128)(2,1)}, bf16[2,128,1792]{2,1,0:T(8,128)(2,1)}, u32[]{:S(2)}, u32[]{:S(2)}) collective-permute-start(bf16[2,128,1792]{2,1,0:T(8,128)(2,1)} %get-tuple-element.63), channel_id=1, source_target_pairs={{0,16},{8,104},{16,0},{24,120},{32,48},{40,8},{48,32},{56,24},{64,... | collective-permute-start | bytes 2752520 | tf_op jit(solution)/shard_map/ppermute | solution.py:276
  133.9 37.7 %collective-permute-start.22 = (bf16[2,128,1792]{2,1,0:T(8,128)(2,1)}, bf16[2,128,1792]{2,1,0:T(8,128)(2,1)}, u32[]{:S(2)}, u32[]{:S(2)}) collective-permute-start(bf16[2,128,1792]{2,1,0:T(8,128)(2,1)} %get-tuple-element.61), channel_id=1, source_target_pairs={{8,72},{24,88},{40,104},{56,120},{72,8},{88,24},{104,40},{120,56},... | collective-permute-start | bytes 2752520 | tf_op jit(solution)/shard_map/ppermute | solution.py:277
  181.8 20.5 %collective-permute-start.27 = (bf16[2,512,1792]{2,1,0:T(8,128)(2,1)}, bf16[2,512,1792]{2,1,0:T(8,128)(2,1)}, u32[]{:S(2)}, u32[]{:S(2)}) collective-permute-start(bf16[2,512,1792]{2,1,0:T(8,128)(2,1)} %get-tuple-element.70), channel_id=1, source_target_pairs={{0,8},{8,0},{16,24},{24,16},{32,40},{40,32},{48,56},{56,48},{64,72... | collective-permute-start | bytes 11010056 | tf_op jit(solution)/shard_map/ppermute | solution.py:291
  181.8 33.9 %collective-permute-start.23 = (bf16[2,128,1024]{2,1,0:T(8,128)(2,1)}, bf16[2,128,1024]{2,1,0:T(8,128)(2,1)S(1)}, u32[]{:S(2)}, u32[]{:S(2)}) collective-permute-start(bf16[2,128,1024]{2,1,0:T(8,128)(2,1)} %copy-done.28), channel_id=1, source_target_pairs={{8,12},{9,13},{10,14},{11,15},{12,8},{13,9},{14,10},{15,11},{24,28... | collective-permute-start | bytes 1572872 | tf_op jit(solution)/shard_map/ppermute | solution.py:348
  186.4 29.4 %collective-permute-start.24 = (bf16[2,128,1024]{2,1,0:T(8,128)(2,1)}, bf16[2,128,1024]{2,1,0:T(8,128)(2,1)S(1)}, u32[]{:S(2)}, u32[]{:S(2)}) collective-permute-start(bf16[2,128,1024]{2,1,0:T(8,128)(2,1)} %copy-done.27), channel_id=1, source_target_pairs={{0,1},{1,2},{2,3},{3,0},{4,5},{5,6},{6,7},{7,4},{8,13},{9,14},{10,... | collective-permute-start | bytes 1572872 | tf_op jit(solution)/shard_map/ppermute | solution.py:348
  186.7 29.2 %collective-permute-start.25 = (bf16[2,128,1024]{2,1,0:T(8,128)(2,1)}, bf16[2,128,1024]{2,1,0:T(8,128)(2,1)S(1)}, u32[]{:S(2)}, u32[]{:S(2)}) collective-permute-start(bf16[2,128,1024]{2,1,0:T(8,128)(2,1)} %copy-done.26), channel_id=1, source_target_pairs={{0,2},{1,3},{2,0},{3,1},{4,6},{5,7},{6,4},{7,5},{8,14},{9,15},{10,... | collective-permute-start | bytes 1572872 | tf_op jit(solution)/shard_map/ppermute | solution.py:348
  197.9 25.7 %collective-permute-start.26 = (bf16[2,128,1024]{2,1,0:T(8,128)(2,1)S(1)}, bf16[2,128,1024]{2,1,0:T(8,128)(2,1)S(1)}, u32[]{:S(2)}, u32[]{:S(2)}) collective-permute-start(bf16[2,128,1024]{2,1,0:T(8,128)(2,1)S(1)} %get-tuple-element.68), channel_id=1, source_target_pairs={{0,3},{1,0},{2,1},{3,2},{4,7},{5,4},{6,5},{7,6},{8,15},{9,12},{10,... | collective-permute-start | bytes 1572872 | tf_op jit(solution)/shard_map/ppermute | solution.py:348
  (37 other events, 283.2 us)
Sparse Core Ops, SparseCore 0:
  118.1 44.4 all-gather.1

commit v8 on v7

--- a/solution.py
+++ b/solution.py
@@ -124,12 +124,37 @@
     return product(held[:, :half], own, transposed) + product(held[:, half:], other, transposed)
 
 
+def mine_kernel(ins, outs):
+    for i in range(2):
+        outs[0][i] = ins[i][...]
+
+
 def block_kernel(ins, outs):
+    mine, *theirs = ins
     (block,) = outs
     half = block.shape[2] // 2
     for i in range(2):
-        block[i, :, :half] = ins[i][...]
-        block[i, :, half:] = ins[2 + i][...]
+        block[i, :, :half] = mine[i]
+        block[i, :, half:] = theirs[i][...]
+
+
+def keep_kernel(ins, outs):
+    for source, out in zip(ins, outs):
+        out[...] = source[...]
+
+
+def gradient_kernel(ins, outs):
+    tok_own, tok_other, d_own, d_other = ins
+    dims = (((0,), (0,)), ((), ()))
+    for i, out in enumerate(outs):
+        for at, end in spans(out.shape[1]):
+            total = lax.dot_general(
+                tok_own[...], d_own[i, :, at:end], dims, preferred_element_type=jnp.float32
+            )
+            total += lax.dot_general(
+                tok_other[...], d_other[i, :, at:end], dims, preferred_element_type=jnp.float32
+            )
+            out[:, at:end] = total.astype(jnp.bfloat16)
 
 
 def first_kernel(ins, outs, tok_held, grad_held):
@@ -295,15 +320,20 @@
     rows = tokens.shape[0]
 
     tok_theirs, grad_theirs = flip(tokens), flip(grad_output)
-    gate_other, up_other, down_other = flip(gate_weight), flip(up_weight), flip(down_weight)
+    (mine,) = call(mine_kernel, [tokens, grad_output], [shape((2, rows, width))])
     (own_block,) = call(
-        block_kernel, [tokens, grad_output, tok_theirs, grad_theirs], [shape((2, rows, 2 * width))]
-    )
-    starts = [own_block, own_block, after(own_block, gate_other), after(own_block, up_other)]
+        block_kernel, [mine, tok_theirs, grad_theirs], [shape((2, rows, 2 * width))]
+    )
+    to_flip = lax.optimization_barrier((gate_weight, up_weight, down_weight, tok_theirs, grad_theirs))
+    gate_other, up_other, down_other = [flip(weight) for weight in to_flip[:3]]
+    own = lax.optimization_barrier((gate_weight, up_weight, down_weight, own_block))[:3]
+    gate_own, up_own, down_own = call(keep_kernel, own, [shape(weight.shape) for weight in own])
+    early = own_block
+    late = [after(own_block, gate_other, gate_own), after(own_block, up_other, gate_own)]
+    starts = [late[1], early, late[0], early]
     blocks = [lax.ppermute(starts[step], BOTH, gather_perm(step)) for step in range(NZ)]
 
-    both_weights = [gate_weight, gate_other, up_weight, up_other]
-    weights = [*both_weights, down_weight, down_other]
+    weights = [gate_own, gate_other, up_own, up_other, down_own, down_other]
     held = lambda pieces: [pltpu.VMEM((pieces * PIECE, 2 * width), jnp.bfloat16)] * 2
     tok_half, grad_half, *sent = call(
         first_kernel,
@@ -346,16 +376,14 @@
         [shape(block)] * 4 + [shape((2, half_rows, ff_width)), shape(block, jnp.float32)],
     )
     messages = [lax.ppermute(messages[k], BOTH, scatter_perm(k)) for k in range(NZ)]
-    d_other = flip(d_set)
-    dot = functools.partial(lax.dot_general, preferred_element_type=jnp.float32)
-    contract_first = (((0,), (0,)), ((), ()))
-    grad_down = dot(hidden, grad_all, contract_first).astype(jnp.bfloat16)
-
-    def weight_gradient(which):
-        total = dot(tok_own, d_set[which], contract_first)
-        return (total + dot(tok_other, d_other[which], contract_first)).astype(jnp.bfloat16)
-
-    grad_gate, grad_up = weight_gradient(0), weight_gradient(1)
+    grad_gate, grad_up = call(
+        gradient_kernel,
+        [tok_own, tok_other, d_set, flip(d_set)],
+        [shape((width, ff_width))] * 2,
+    )
+    grad_down = lax.dot_general(
+        hidden, grad_all, (((0,), (0,)), ((), ())), preferred_element_type=jnp.float32
+    ).astype(jnp.bfloat16)
     *messages, grad_gate, grad_up = lax.optimization_barrier((*messages, grad_gate, grad_up))
     total = jnp.where(core == 0, kept, 0.0)
     for message in messages:

time: 239 us -> 215 us (0.90)
  waiting for transfers between devices: 115 us -> 96.7 us
  matrix products: 16.8 us -> 3.39 us
  Pallas kernels: 20.8 us -> 30.4 us
    dot_general x5 -> x1, matrix products: 16.8 us -> 3.39 us  [body(): lax.dot_general(hidden, grad_all, (((0,), (0,)), ((), ())), preferred_ele...]
    pallas_call x9 -> x12, Pallas kernels: 20.8 us -> 30.4 us  [call(): pl.pallas_call(run, in_specs=[vmem] * n_in, out_specs=[vmem] * n_out, out...]
    ppermute x4, waiting for transfers between devices: 21.1 us -> 13 us  [body(): lax.ppermute(starts[step], BOTH, gather_perm(step))]
    ppermute x9, waiting for transfers between devices: 10.3 us -> 3.53 us  [body(): flip = lambda value: lax.ppermute(value, 'row', CORE_FLIP)]
    ppermute x2, waiting for transfers between devices: 36.1 us -> 30.7 us  [send_first(): lax.ppermute(sent[0], 'row', row_perm(over_x, over_y(1)))]
    ppermute x4, waiting for transfers between devices: 7.85 us -> 11.7 us  [body(): lax.ppermute(messages[k], BOTH, scatter_perm(k))]
    ppermute x4, starting transfers between devices: 20.5 us -> 17.7 us  [body(): lax.ppermute(messages[k], BOTH, scatter_perm(k))]
    ppermute x2, starting transfers between devices: 1.5 us -> 3.92 us  [send_first(): lax.ppermute(sent[0], 'row', row_perm(over_x, over_y(1)))]
  transfers between devices with their start and end apart: 30 -> 30, of which waited for: 20 -> 18; matrix products, arithmetic and copies ran while one was open for 7% -> 2% of each run, Pallas kernels for 3% -> 7%
where the time goes in v8:
time: 215 us
  waiting for transfers between devices  96.7 us (45%)
  starting transfers between devices  53.7 us (25%)
  Pallas kernels  30.4 us (14%)
  local copies, waits for them, and re-layouts  14.9 us (7%)
  between operations  14.4 us (7%)
  matrix products  3.39 us (2%)
    ppermute x2, waiting for transfers between devices, send_first(): lax.ppermute(sent[0], 'row', row_perm(over_x, over_y(1)))  30.7 us
    pallas_call x12, Pallas kernels, call(): pl.pallas_call(run, in_specs=[vmem] * n_in, out_specs=[vmem] * n_out, out...  30.4 us
    ppermute x4, starting transfers between devices, body(): lax.ppermute(messages[k], BOTH, scatter_perm(k))  17.7 us
    unnamed x52, local copies, waits for them, and re-layouts  14.1 us
    ppermute x2, waiting for transfers between devices, send_second(): lax.ppermute(sent[0], 'row', row_perm(over_y(1), over_x))  13.3 us
    ppermute x4, waiting for transfers between devices, body(): lax.ppermute(starts[step], BOTH, gather_perm(step))  13 us
    ppermute x2, starting transfers between devices, send_first(): lax.ppermute(sent[2], 'row', row_perm(None, over_y(2)))  12.8 us
    ppermute x4, starting transfers between devices, body(): lax.ppermute(starts[step], BOTH, gather_perm(step))  12.2 us
  transfers between devices with their start and end apart: 30, of which 18 were waited for; matrix products, arithmetic and copies ran while one was open for 2% of the time, Pallas kernels for 7%

profile of v8, /device:TPU:17, one launch (start us, length us, event | category | flops | bytes accessed | tf_op | source)
XLA Modules:
  0.0 215.1 jit_solution(16609456413915794527)
XLA Ops:
  12.1 6.3 %collective-permute-start.4 = (bf16[2,128,1024]{2,1,0:T(8,128)(2,1)S(1)}, bf16[2,128,1024]{2,1,0:T(8,128)(2,1)S(1)}, u32[]{:S(2)}, u32[]{:S(2)}) collective-permute-start(bf16[2,128,1024]{2,1,0:T(8,128)(2,1)S(1)} %shard_map.93.refs_0_), channel_id=1, source_target_pairs={{1,0},{2,1},{3,2},{0,3},{5,4},{6,5},{7,6},{4,7},{13,8},{14,9},{15,... | collective-permute-start | bytes 1572872 | tf_op jit(solution)/shard_map/ppermute | solution.py:334
  23.3 3.8 %collective-permute-start.6 = (bf16[2,128,1024]{2,1,0:T(8,128)(2,1)S(1)}, bf16[2,128,1024]{2,1,0:T(8,128)(2,1)S(1)}, u32[]{:S(2)}, u32[]{:S(2)}) collective-permute-start(bf16[2,128,1024]{2,1,0:T(8,128)(2,1)S(1)} %shard_map.93.refs_0_), channel_id=1, source_target_pairs={{2,0},{3,1},{0,2},{1,3},{6,4},{7,5},{4,6},{5,7},{14,8},{15,9},{12,... | collective-permute-start | bytes 1572872 | tf_op jit(solution)/shard_map/ppermute | solution.py:334
  31.1 5.3 %collective-permute-done.6.refs_3_ = bf16[2,128,1024]{2,1,0:T(8,128)(2,1)S(1)} collective-permute-done((bf16[2,128,1024]{2,1,0:T(8,128)(2,1)S(1)}, bf16[2,128,1024]{2,1,0:T(8,128)(2,1)S(1)}, u32[]{:S(2)}, u32[]{:S(2)}) %collective-permute-start.6) | collective-permute-done | bytes 524320 | tf_op jit(solution)/shard_map/ppermute | solution.py:334
  36.5 5.8 %collective-permute-done.3.refs_1_ = bf16[2,128,1024]{2,1,0:T(8,128)(2,1)S(1)} collective-permute-done((bf16[2,128,1024]{2,1,0:T(8,128)(2,1)S(1)}, bf16[2,128,1024]{2,1,0:T(8,128)(2,1)S(1)}, u32[]{:S(2)}, u32[]{:S(2)}) %collective-permute-start.3) | collective-permute-done | bytes 524320 | tf_op jit(solution)/shard_map/ppermute | solution.py:334
  42.3 4.5 %shard_map.95 = (bf16[512,1024]{1,0:T(8,128)(2,1)S(1)}, bf16[512,1024]{1,0:T(8,128)(2,1)S(1)}, bf16[3,128,1792]{2,1,0:T(8,128)(2,1)S(1)}, bf16[3,128,1792]{2,1,0:T(8,128)(2,1)S(1)}, bf16[3,128,1792]{2,1,0:T(8,128)(2,1)S(1)}) custom-call(bf16[2,128,1024]{2,1,0:T(8,128)(2,1)S(1)} %shard_map.93.refs_0_, ...), custom_call_target="tpu_custom_call" | custom-call | flops 1 | bytes 1 | tf_op jit(solution)/shard_map/pallas_call | solution.py:78
  47.0 4.5 %collective-permute-start.11 = (bf16[3,128,1792]{2,1,0:T(8,128)(2,1)S(1)}, bf16[3,128,1792]{2,1,0:T(8,128)(2,1)S(1)}, u32[]{:S(2)}, u32[]{:S(2)}) collective-permute-start(bf16[3,128,1792]{2,1,0:T(8,128)(2,1)S(1)} %get-tuple-element.69), channel_id=1, source_target_pairs={{8,72},{24,88},{40,104},{56,120},{72,8},{88,24},{104,40},{120,56},... | collective-permute-start | bytes 4128776 | tf_op jit(solution)/shard_map/ppermute | solution.py:302
  58.3 6.0 %collective-permute-done.10.refs_2_ = bf16[3,128,1792]{2,1,0:T(8,128)(2,1)S(1)} collective-permute-done((bf16[3,128,1792]{2,1,0:T(8,128)(2,1)S(1)}, bf16[3,128,1792]{2,1,0:T(8,128)(2,1)S(1)}, u32[]{:S(2)}, u32[]{:S(2)}) %collective-permute-start.10) | collective-permute-done | bytes 1376288 | tf_op jit(solution)/shard_map/ppermute | solution.py:301
  64.3 3.4 %collective-permute-done.11.refs_3_ = bf16[3,128,1792]{2,1,0:T(8,128)(2,1)S(1)} collective-permute-done((bf16[3,128,1792]{2,1,0:T(8,128)(2,1)S(1)}, bf16[3,128,1792]{2,1,0:T(8,128)(2,1)S(1)}, u32[]{:S(2)}, u32[]{:S(2)}) %collective-permute-start.11) | collective-permute-done | bytes 1376288 | tf_op jit(solution)/shard_map/ppermute | solution.py:302
  67.7 14.6 %collective-permute-done.9.refs_1_ = bf16[3,128,1792]{2,1,0:T(8,128)(2,1)S(1)} collective-permute-done((bf16[3,128,1792]{2,1,0:T(8,128)(2,1)S(1)}, bf16[3,128,1792]{2,1,0:T(8,128)(2,1)S(1)}, u32[]{:S(2)}, u32[]{:S(2)}) %collective-permute-start.9) | collective-permute-done | bytes 1376288 | tf_op jit(solution)/shard_map/ppermute | solution.py:300
  85.4 7.8 %collective-permute-done.14.refs_4_ = bf16[3,64,1792]{2,1,0:T(8,128)(2,1)S(1)} collective-permute-done((bf16[3,64,1792]{2,1,0:T(8,128)(2,1)S(1)}, bf16[3,64,1792]{2,1,0:T(8,128)(2,1)S(1)}, u32[]{:S(2)}, u32[]{:S(2)}) %collective-permute-start.14) | collective-permute-done | bytes 688160 | tf_op jit(solution)/shard_map/ppermute | solution.py:308
  93.2 7.1 %collective-permute-done.15.refs_5_ = bf16[3,64,1792]{2,1,0:T(8,128)(2,1)S(1)} collective-permute-done((bf16[3,64,1792]{2,1,0:T(8,128)(2,1)S(1)}, bf16[3,64,1792]{2,1,0:T(8,128)(2,1)S(1)}, u32[]{:S(2)}, u32[]{:S(2)}) %collective-permute-start.15) | collective-permute-done | bytes 688160 | tf_op jit(solution)/shard_map/ppermute | solution.py:309
  103.6 5.5 %collective-permute-done.17.refs_1_.refs_2_ = bf16[2,64,1792]{2,1,0:T(8,128)(2,1)S(1)} collective-permute-done((bf16[2,64,1792]{2,1,0:T(8,128)(2,1)S(1)}, bf16[2,64,1792]{2,1,0:T(8,128)(2,1)S(1)}, u32[]{:S(2)}, u32[]{:S(2)}) %collective-permute-start.17) | collective-permute-done | bytes 458784 | tf_op jit(solution)/shard_map/ppermute | solution.py:308
  109.1 5.0 %collective-permute-done.18.refs_2_.refs_3_ = bf16[2,64,1792]{2,1,0:T(8,128)(2,1)S(1)} collective-permute-done((bf16[2,64,1792]{2,1,0:T(8,128)(2,1)S(1)}, bf16[2,64,1792]{2,1,0:T(8,128)(2,1)S(1)}, u32[]{:S(2)}, u32[]{:S(2)}) %collective-permute-start.18) | collective-permute-done | bytes 458784 | tf_op jit(solution)/shard_map/ppermute | solution.py:309
  116.3 3.9 %collective-permute-start.20 = (bf16[2,128,1792]{2,1,0:T(8,128)(2,1)}, bf16[2,128,1792]{2,1,0:T(8,128)(2,1)S(1)}, u32[]{:S(2)}, u32[]{:S(2)}) collective-permute-start(bf16[2,128,1792]{2,1,0:T(8,128)(2,1)} %get-tuple-element.81), channel_id=1, source_target_pairs={{0,16},{8,40},{16,0},{24,56},{32,48},{40,72},{48,32},{56,88},{64,8... | collective-permute-start | bytes 2752520 | tf_op jit(solution)/shard_map/ppermute | solution.py:300
  120.2 8.3 %collective-permute-start.22 = (bf16[2,128,1792]{2,1,0:T(8,128)(2,1)}, bf16[2,128,1792]{2,1,0:T(8,128)(2,1)}, u32[]{:S(2)}, u32[]{:S(2)}) collective-permute-start(bf16[2,128,1792]{2,1,0:T(8,128)(2,1)} %get-tuple-element.81), channel_id=1, source_target_pairs={{8,72},{24,88},{40,104},{56,120},{72,8},{88,24},{104,40},{120,56},... | collective-permute-start | bytes 2752520 | tf_op jit(solution)/shard_map/ppermute | solution.py:302
  128.5 16.0 %collective-permute-done.20.refs_5_ = bf16[2,128,1792]{2,1,0:T(8,128)(2,1)S(1)} collective-permute-done((bf16[2,128,1792]{2,1,0:T(8,128)(2,1)}, bf16[2,128,1792]{2,1,0:T(8,128)(2,1)S(1)}, u32[]{:S(2)}, u32[]{:S(2)}) %collective-permute-start.20) | collective-permute-done | bytes 917536 | tf_op jit(solution)/shard_map/ppermute | solution.py:300
  154.1 8.1 %shard_map.102 = (bf16[2,128,1024]{2,1,0:T(8,128)(2,1)}, bf16[2,128,1024]{2,1,0:T(8,128)(2,1)}, bf16[2,128,1024]{2,1,0:T(8,128)(2,1)}, bf16[2,128,1024]{2,1,0:T(...) custom-call(f32[512,1024]{1,0:T(8,128)S(1)} %shard_map.101.refs_0_, ...), custom_call_target="tpu_custom_call" | custom-call | flops 1 | bytes 1 | tf_op jit(solution)/shard_map/pallas_call | solution.py:78
  163.2 4.8 %collective-permute-start.23 = (bf16[2,128,1024]{2,1,0:T(8,128)(2,1)}, bf16[2,128,1024]{2,1,0:T(8,128)(2,1)S(1)}, u32[]{:S(2)}, u32[]{:S(2)}) collective-permute-start(bf16[2,128,1024]{2,1,0:T(8,128)(2,1)} %get-tuple-element.85), channel_id=1, source_target_pairs={{8,12},{9,13},{10,14},{11,15},{12,8},{13,9},{14,10},{15,11},{24,28... | collective-permute-start | bytes 1572872 | tf_op jit(solution)/shard_map/ppermute | solution.py:378
  168.0 8.5 %collective-permute-start.25 = (bf16[2,128,1024]{2,1,0:T(8,128)(2,1)}, bf16[2,128,1024]{2,1,0:T(8,128)(2,1)S(1)}, u32[]{:S(2)}, u32[]{:S(2)}) collective-permute-start(bf16[2,128,1024]{2,1,0:T(8,128)(2,1)} %get-tuple-element.87), channel_id=1, source_target_pairs={{0,2},{1,3},{2,0},{3,1},{4,6},{5,7},{6,4},{7,5},{8,14},{9,15},{10,... | collective-permute-start | bytes 1572872 | tf_op jit(solution)/shard_map/ppermute | solution.py:378
  176.5 4.4 %collective-permute-start.26 = (bf16[2,128,1024]{2,1,0:T(8,128)(2,1)S(1)}, bf16[2,128,1024]{2,1,0:T(8,128)(2,1)}, u32[]{:S(2)}, u32[]{:S(2)}) collective-permute-start(bf16[2,128,1024]{2,1,0:T(8,128)(2,1)S(1)} %get-tuple-element.88), channel_id=1, source_target_pairs={{0,3},{1,0},{2,1},{3,2},{4,7},{5,4},{6,5},{7,6},{8,15},{9,12},{10,... | collective-permute-start | bytes 1572872 | tf_op jit(solution)/shard_map/ppermute | solution.py:378
  180.9 8.9 %shard_map.103 = (bf16[512,1792]{1,0:T(8,128)(2,1)}, bf16[512,1792]{1,0:T(8,128)(2,1)}) custom-call(bf16[512,512]{1,0:T(8,128)(2,1)S(1)} %copy-done.21, bf16[512,512]{1,0:T(8,128)(2,1)S(1)} %copy-done.23, bf16[2,512,1792]{2,1,0:T(8,128)(2,1)} %get-tuple-element.91.refs_2_, bf16[2,512,1792]{2,1,0:T(8,128)(2,1)} %collective-permute-done.27.refs_3_), custom_call_target="tpu_custom_call" | custom-call | flops 1 | bytes 1 | tf_op jit(solution)/shard_map/pallas_call | solution.py:78
  189.8 4.6 %collective-permute-done.25 = bf16[2,128,1024]{2,1,0:T(8,128)(2,1)S(1)} collective-permute-done((bf16[2,128,1024]{2,1,0:T(8,128)(2,1)}, bf16[2,128,1024]{2,1,0:T(8,128)(2,1)S(1)}, u32[]{:S(2)}, u32[]{:S(2)}) %collective-permute-start.25) | collective-permute-done | bytes 524320 | tf_op jit(solution)/shard_map/ppermute | solution.py:378
  194.4 7.1 %collective-permute-done.26 = bf16[2,128,1024]{2,1,0:T(8,128)(2,1)} collective-permute-done((bf16[2,128,1024]{2,1,0:T(8,128)(2,1)S(1)}, bf16[2,128,1024]{2,1,0:T(8,128)(2,1)}, u32[]{:S(2)}, u32[]{:S(2)}) %collective-permute-start.26) | collective-permute-done | bytes 524320 | tf_op jit(solution)/shard_map/ppermute | solution.py:378
  204.0 3.4 %convolution_convert_fusion = bf16[1792,512]{1,0:T(8,128)(2,1)} fusion(bf16[1024,1792]{1,0:T(8,128)(2,1)S(1)} %copy-done.11, bf16[1024,512]{1,0:T(8,128)(2,1)S(1)} %copy-done.17), kind=kOutput, calls=%fused_computation | convolution fusion | flops 1879965696 | bytes 6553600 | tf_op jit(solution)/shard_map/dot_general | solution.py:384
  (106 shorter events, 43.2 us)
Async XLA Ops:
  7.2 138.2 %all-gather.2.cloned.1.call-start = ((), (), s32[]{:S(2)}) async-start(), calls=%async_computation | async-start | bytes 3899392 | tf_op jit(solution)/shard_map/all_gather | solution.py:360
  9.5 13.7 %collective-permute-start.5 = (bf16[512,1792]{1,0:T(8,128)(2,1)}, bf16[512,1792]{1,0:T(8,128)(2,1)S(1)}, u32[]{:S(2)}, u32[]{:S(2)}) collective-permute-start(bf16[512,1792]{1,0:T(8,128)(2,1)} %refs_8_.1), channel_id=1, source_target_pairs={{0,8},{8,0},{16,24},{24,16},{32,40},{40,32},{48,56},{56,48},{64,72... | collective-permute-start | bytes 5505032 | tf_op jit(solution)/shard_map/ppermute | solution.py:316
  9.7 17.3 %collective-permute-start.2 = (bf16[512,1792]{1,0:T(8,128)(2,1)}, bf16[512,1792]{1,0:T(8,128)(2,1)S(1)}, u32[]{:S(2)}, u32[]{:S(2)}) collective-permute-start(bf16[512,1792]{1,0:T(8,128)(2,1)} %refs_9_.1), channel_id=1, source_target_pairs={{0,8},{8,0},{16,24},{24,16},{32,40},{40,32},{48,56},{56,48},{64,72... | collective-permute-start | bytes 5505032 | tf_op jit(solution)/shard_map/ppermute | solution.py:316
  10.0 21.1 %collective-permute-start.8 = (bf16[1792,512]{1,0:T(8,128)(2,1)}, bf16[1792,512]{1,0:T(8,128)(2,1)S(1)}, u32[]{:S(2)}, u32[]{:S(2)}) collective-permute-start(bf16[1792,512]{1,0:T(8,128)(2,1)} %refs_1_.4), channel_id=1, source_target_pairs={{0,8},{8,0},{16,24},{24,16},{32,40},{40,32},{48,56},{56,48},{64,72... | collective-permute-start | bytes 5505032 | tf_op jit(solution)/shard_map/ppermute | solution.py:316
  12.1 17.1 %collective-permute-start.4 = (bf16[2,128,1024]{2,1,0:T(8,128)(2,1)S(1)}, bf16[2,128,1024]{2,1,0:T(8,128)(2,1)S(1)}, u32[]{:S(2)}, u32[]{:S(2)}) collective-permute-start(bf16[2,128,1024]{2,1,0:T(8,128)(2,1)S(1)} %shard_map.93.refs_0_), channel_id=1, source_target_pairs={{1,0},{2,1},{3,2},{0,3},{5,4},{6,5},{7,6},{4,7},{13,8},{14,9},{15,... | collective-permute-start | bytes 1572872 | tf_op jit(solution)/shard_map/ppermute | solution.py:334
  18.4 12.7 %collective-permute-start.7 = (bf16[2,128,1024]{2,1,0:T(8,128)(2,1)S(1)}, bf16[2,128,1024]{2,1,0:T(8,128)(2,1)S(1)}, u32[]{:S(2)}, u32[]{:S(2)}) collective-permute-start(bf16[2,128,1024]{2,1,0:T(8,128)(2,1)S(1)} %shard_map.93.refs_0_), channel_id=1, source_target_pairs={{3,0},{0,1},{1,2},{2,3},{7,4},{4,5},{5,6},{6,7},{15,8},{12,9},{13,... | collective-permute-start | bytes 1572872 | tf_op jit(solution)/shard_map/ppermute | solution.py:334
  23.3 13.2 %collective-permute-start.6 = (bf16[2,128,1024]{2,1,0:T(8,128)(2,1)S(1)}, bf16[2,128,1024]{2,1,0:T(8,128)(2,1)S(1)}, u32[]{:S(2)}, u32[]{:S(2)}) collective-permute-start(bf16[2,128,1024]{2,1,0:T(8,128)(2,1)S(1)} %shard_map.93.refs_0_), channel_id=1, source_target_pairs={{2,0},{3,1},{0,2},{1,3},{6,4},{7,5},{4,6},{5,7},{14,8},{15,9},{12,... | collective-permute-start | bytes 1572872 | tf_op jit(solution)/shard_map/ppermute | solution.py:334
  27.1 15.2 %collective-permute-start.3 = (bf16[2,128,1024]{2,1,0:T(8,128)(2,1)S(1)}, bf16[2,128,1024]{2,1,0:T(8,128)(2,1)S(1)}, u32[]{:S(2)}, u32[]{:S(2)}) collective-permute-start(bf16[2,128,1024]{2,1,0:T(8,128)(2,1)S(1)} %shard_map.93.refs_0_), channel_id=1, source_target_pairs={{12,8},{13,9},{14,10},{15,11},{8,12},{9,13},{10,14},{11,15},{28,24... | collective-permute-start | bytes 1572872 | tf_op jit(solution)/shard_map/ppermute | solution.py:334
  46.8 17.5 %collective-permute-start.10 = (bf16[3,128,1792]{2,1,0:T(8,128)(2,1)S(1)}, bf16[3,128,1792]{2,1,0:T(8,128)(2,1)S(1)}, u32[]{:S(2)}, u32[]{:S(2)}) collective-permute-start(bf16[3,128,1792]{2,1,0:T(8,128)(2,1)S(1)} %get-tuple-element.68), channel_id=1, source_target_pairs={{0,16},{8,104},{16,0},{24,120},{32,48},{40,8},{48,32},{56,24},{64,... | collective-permute-start | bytes 4128776 | tf_op jit(solution)/shard_map/ppermute | solution.py:301
  47.0 20.7 %collective-permute-start.11 = (bf16[3,128,1792]{2,1,0:T(8,128)(2,1)S(1)}, bf16[3,128,1792]{2,1,0:T(8,128)(2,1)S(1)}, u32[]{:S(2)}, u32[]{:S(2)}) collective-permute-start(bf16[3,128,1792]{2,1,0:T(8,128)(2,1)S(1)} %get-tuple-element.69), channel_id=1, source_target_pairs={{8,72},{24,88},{40,104},{56,120},{72,8},{88,24},{104,40},{120,56},... | collective-permute-start | bytes 4128776 | tf_op jit(solution)/shard_map/ppermute | solution.py:302
  51.5 30.8 %collective-permute-start.9 = (bf16[3,128,1792]{2,1,0:T(8,128)(2,1)S(1)}, bf16[3,128,1792]{2,1,0:T(8,128)(2,1)S(1)}, u32[]{:S(2)}, u32[]{:S(2)}) collective-permute-start(bf16[3,128,1792]{2,1,0:T(8,128)(2,1)S(1)} %get-tuple-element.67), channel_id=1, source_target_pairs={{0,16},{8,40},{16,0},{24,56},{32,48},{40,72},{48,32},{56,88},{64,8... | collective-permute-start | bytes 4128776 | tf_op jit(solution)/shard_map/ppermute | solution.py:300
  83.0 10.2 %collective-permute-start.14 = (bf16[3,64,1792]{2,1,0:T(8,128)(2,1)S(1)}, bf16[3,64,1792]{2,1,0:T(8,128)(2,1)S(1)}, u32[]{:S(2)}, u32[]{:S(2)}) collective-permute-start(bf16[3,64,1792]{2,1,0:T(8,128)(2,1)S(1)} %get-tuple-element.76), channel_id=1, source_target_pairs={{0,32},{8,24},{16,48},{24,8},{32,64},{40,56},{48,80},{56,40},{64,9... | collective-permute-start | bytes 2064392 | tf_op jit(solution)/shard_map/ppermute | solution.py:308
  84.4 15.8 %collective-permute-start.15 = (bf16[3,64,1792]{2,1,0:T(8,128)(2,1)S(1)}, bf16[3,64,1792]{2,1,0:T(8,128)(2,1)S(1)}, u32[]{:S(2)}, u32[]{:S(2)}) collective-permute-start(bf16[3,64,1792]{2,1,0:T(8,128)(2,1)S(1)} %get-tuple-element.77), channel_id=1, source_target_pairs={{0,96},{8,24},{16,112},{24,8},{32,0},{40,56},{48,16},{56,40},{64,3... | collective-permute-start | bytes 2064392 | tf_op jit(solution)/shard_map/ppermute | solution.py:309
  84.7 15.6 %collective-permute-start.16 = (bf16[3,64,1792]{2,1,0:T(8,128)(2,1)S(1)}, bf16[3,64,1792]{2,1,0:T(8,128)(2,1)S(1)}, u32[]{:S(2)}, u32[]{:S(2)}) collective-permute-start(bf16[3,64,1792]{2,1,0:T(8,128)(2,1)S(1)} %get-tuple-element.78), channel_id=1, source_target_pairs={{0,64},{16,80},{32,96},{48,112},{64,0},{80,16},{96,32},{112,48},{1... | collective-permute-start | bytes 2064392 | tf_op jit(solution)/shard_map/ppermute | solution.py:310
  102.8 11.3 %collective-permute-start.18 = (bf16[2,64,1792]{2,1,0:T(8,128)(2,1)S(1)}, bf16[2,64,1792]{2,1,0:T(8,128)(2,1)S(1)}, u32[]{:S(2)}, u32[]{:S(2)}) collective-permute-start(bf16[2,64,1792]{2,1,0:T(8,128)(2,1)S(1)} %get-tuple-element.80.refs_0_.refs_1_), channel_id=1, source_target_pairs={{0,96},{8,24},{16,112},{24,8},{32,0},{40,56},{48,16},{56,40},{64,3... | collective-permute-start | bytes 1376264 | tf_op jit(solution)/shard_map/ppermute | solution.py:309
  103.0 11.2 %collective-permute-start.19 = (bf16[2,64,1792]{2,1,0:T(8,128)(2,1)S(1)}, bf16[2,64,1792]{2,1,0:T(8,128)(2,1)S(1)}, u32[]{:S(2)}, u32[]{:S(2)}) collective-permute-start(bf16[2,64,1792]{2,1,0:T(8,128)(2,1)S(1)} %get-tuple-element.80.refs_0_.refs_1_), channel_id=1, source_target_pairs={{0,64},{16,80},{32,96},{48,112},{64,0},{80,16},{96,32},{112,48},{1... | collective-permute-start | bytes 1376264 | tf_op jit(solution)/shard_map/ppermute | solution.py:310
  116.3 28.1 %collective-permute-start.20 = (bf16[2,128,1792]{2,1,0:T(8,128)(2,1)}, bf16[2,128,1792]{2,1,0:T(8,128)(2,1)S(1)}, u32[]{:S(2)}, u32[]{:S(2)}) collective-permute-start(bf16[2,128,1792]{2,1,0:T(8,128)(2,1)} %get-tuple-element.81), channel_id=1, source_target_pairs={{0,16},{8,40},{16,0},{24,56},{32,48},{40,72},{48,32},{56,88},{64,8... | collective-permute-start | bytes 2752520 | tf_op jit(solution)/shard_map/ppermute | solution.py:300
  120.2 30.9 %collective-permute-start.21 = (bf16[2,128,1792]{2,1,0:T(8,128)(2,1)}, bf16[2,128,1792]{2,1,0:T(8,128)(2,1)}, u32[]{:S(2)}, u32[]{:S(2)}) collective-permute-start(bf16[2,128,1792]{2,1,0:T(8,128)(2,1)} %get-tuple-element.83), channel_id=1, source_target_pairs={{0,16},{8,104},{16,0},{24,120},{32,48},{40,8},{48,32},{56,24},{64,... | collective-permute-start | bytes 2752520 | tf_op jit(solution)/shard_map/ppermute | solution.py:301
  120.2 33.8 %collective-permute-start.22 = (bf16[2,128,1792]{2,1,0:T(8,128)(2,1)}, bf16[2,128,1792]{2,1,0:T(8,128)(2,1)}, u32[]{:S(2)}, u32[]{:S(2)}) collective-permute-start(bf16[2,128,1792]{2,1,0:T(8,128)(2,1)} %get-tuple-element.81), channel_id=1, source_target_pairs={{8,72},{24,88},{40,104},{56,120},{72,8},{88,24},{104,40},{120,56},... | collective-permute-start | bytes 2752520 | tf_op jit(solution)/shard_map/ppermute | solution.py:302
  163.1 17.8 %collective-permute-start.27 = (bf16[2,512,1792]{2,1,0:T(8,128)(2,1)}, bf16[2,512,1792]{2,1,0:T(8,128)(2,1)}, u32[]{:S(2)}, u32[]{:S(2)}) collective-permute-start(bf16[2,512,1792]{2,1,0:T(8,128)(2,1)} %get-tuple-element.91.refs_2_), channel_id=1, source_target_pairs={{0,8},{8,0},{16,24},{24,16},{32,40},{40,32},{48,56},{56,48},{64,72... | collective-permute-start | bytes 11010056 | tf_op jit(solution)/shard_map/ppermute | solution.py:316
  163.2 26.7 %collective-permute-start.23 = (bf16[2,128,1024]{2,1,0:T(8,128)(2,1)}, bf16[2,128,1024]{2,1,0:T(8,128)(2,1)S(1)}, u32[]{:S(2)}, u32[]{:S(2)}) collective-permute-start(bf16[2,128,1024]{2,1,0:T(8,128)(2,1)} %get-tuple-element.85), channel_id=1, source_target_pairs={{8,12},{9,13},{10,14},{11,15},{12,8},{13,9},{14,10},{15,11},{24,28... | collective-permute-start | bytes 1572872 | tf_op jit(solution)/shard_map/ppermute | solution.py:378
  167.9 21.9 %collective-permute-start.24 = (bf16[2,128,1024]{2,1,0:T(8,128)(2,1)}, bf16[2,128,1024]{2,1,0:T(8,128)(2,1)S(1)}, u32[]{:S(2)}, u32[]{:S(2)}) collective-permute-start(bf16[2,128,1024]{2,1,0:T(8,128)(2,1)} %get-tuple-element.86), channel_id=1, source_target_pairs={{0,1},{1,2},{2,3},{3,0},{4,5},{5,6},{6,7},{7,4},{8,13},{9,14},{10,... | collective-permute-start | bytes 1572872 | tf_op jit(solution)/shard_map/ppermute | solution.py:378
  168.0 26.4 %collective-permute-start.25 = (bf16[2,128,1024]{2,1,0:T(8,128)(2,1)}, bf16[2,128,1024]{2,1,0:T(8,128)(2,1)S(1)}, u32[]{:S(2)}, u32[]{:S(2)}) collective-permute-start(bf16[2,128,1024]{2,1,0:T(8,128)(2,1)} %get-tuple-element.87), channel_id=1, source_target_pairs={{0,2},{1,3},{2,0},{3,1},{4,6},{5,7},{6,4},{7,5},{8,14},{9,15},{10,... | collective-permute-start | bytes 1572872 | tf_op jit(solution)/shard_map/ppermute | solution.py:378
  176.5 25.0 %collective-permute-start.26 = (bf16[2,128,1024]{2,1,0:T(8,128)(2,1)S(1)}, bf16[2,128,1024]{2,1,0:T(8,128)(2,1)}, u32[]{:S(2)}, u32[]{:S(2)}) collective-permute-start(bf16[2,128,1024]{2,1,0:T(8,128)(2,1)S(1)} %get-tuple-element.88), channel_id=1, source_target_pairs={{0,3},{1,0},{2,1},{3,2},{4,7},{5,4},{6,5},{7,6},{8,15},{9,12},{10,... | collective-permute-start | bytes 1572872 | tf_op jit(solution)/shard_map/ppermute | solution.py:378
  (32 other events, 255.7 us)
Sparse Core Ops, SparseCore 0:
  101.5 41.5 all-gather.1

commit v9 on v8

--- a/solution.py
+++ b/solution.py
@@ -143,18 +143,22 @@
         out[...] = source[...]
 
 
-def gradient_kernel(ins, outs):
+def gradient_kernel(ins, outs, own_turned, other_turned):
     tok_own, tok_other, d_own, d_other = ins
-    dims = (((0,), (0,)), ((), ()))
+    own_turned[...] = tok_own[...].T
+    other_turned[...] = tok_other[...].T
     for i, out in enumerate(outs):
         for at, end in spans(out.shape[1]):
-            total = lax.dot_general(
-                tok_own[...], d_own[i, :, at:end], dims, preferred_element_type=jnp.float32
-            )
-            total += lax.dot_general(
-                tok_other[...], d_other[i, :, at:end], dims, preferred_element_type=jnp.float32
-            )
+            total = product(own_turned[...], d_own[i, :, at:end], False)
+            total += product(other_turned[...], d_other[i, :, at:end], False)
             out[:, at:end] = total.astype(jnp.bfloat16)
+
+
+def down_kernel(ins, outs):
+    hidden, grad_all = ins
+    for at, end in spans(hidden.shape[1]):
+        total = product(hidden[:, at:end].T, grad_all[...], False)
+        outs[0][at:end, :] = total.astype(jnp.bfloat16)
 
 
 def first_kernel(ins, outs, tok_held, grad_held):
@@ -304,11 +308,9 @@
 
 
 def send_second(sent):
-    return (
-        lax.ppermute(sent[0], "row", row_perm(over_y(1), over_x)),
-        lax.ppermute(sent[1], "row", row_perm(over_y(-1), over_x)),
-        lax.ppermute(sent[2], "row", row_perm(over_y(2), None)),
-    )
+    third = lax.ppermute(sent[2], "row", row_perm(over_y(2), None))
+    first = lax.ppermute(sent[0], "row", row_perm(over_y(1), over_x))
+    return first, lax.ppermute(sent[1], "row", row_perm(over_y(-1), over_x)), third
 
 
 def body(tokens, gate_weight, up_weight, down_weight, grad_output):
@@ -375,16 +377,18 @@
         [layer, d_own, *near, *far, gate_weight, up_weight, gate_other, up_other],
         [shape(block)] * 4 + [shape((2, half_rows, ff_width)), shape(block, jnp.float32)],
     )
-    messages = [lax.ppermute(messages[k], BOTH, scatter_perm(k)) for k in range(NZ)]
+    heard = {k: lax.ppermute(messages[k], BOTH, scatter_perm(k)) for k in (2, 1, 3, 0)}
+    messages = [heard[k] for k in range(NZ)]
     grad_gate, grad_up = call(
         gradient_kernel,
         [tok_own, tok_other, d_set, flip(d_set)],
         [shape((width, ff_width))] * 2,
-    )
-    grad_down = lax.dot_general(
-        hidden, grad_all, (((0,), (0,)), ((), ())), preferred_element_type=jnp.float32
-    ).astype(jnp.bfloat16)
-    *messages, grad_gate, grad_up = lax.optimization_barrier((*messages, grad_gate, grad_up))
+        [pltpu.VMEM((width, half_rows), jnp.bfloat16)] * 2,
+    )
+    (grad_down,) = call(down_kernel, [hidden, grad_all], [shape((ff_width, width))])
+    *messages, grad_gate, grad_up, grad_down = lax.optimization_barrier(
+        (*messages, grad_gate, grad_up, grad_down)
+    )
     total = jnp.where(core == 0, kept, 0.0)
     for message in messages:
         total = total + message.astype(jnp.float32)

time: 215 us -> 214 us (level)
  matrix products: 3.39 us -> 0 us
  Pallas kernels: 30.4 us -> 33.2 us
  waiting for transfers between devices: 96.7 us -> 94.4 us
    ppermute x4, waiting for transfers between devices: 11.7 us -> 6.76 us  [body(): lax.ppermute(messages[k], BOTH, scatter_perm(k))]
    dot_general x1 -> x0, matrix products: 3.39 us -> none  [body(): lax.dot_general(hidden, grad_all, (((0,), (0,)), ((), ())), preferred_ele...]
    pallas_call x12 -> x13, Pallas kernels: 30.4 us -> 33.2 us  [call(): pl.pallas_call(run, in_specs=[vmem] * n_in, out_specs=[vmem] * n_out, out...]
    unnamed x52 -> x58, local copies, waits for them, and re-layouts: 14.1 us -> 15.5 us
  transfers between devices with their start and end apart: 30 -> 30, of which waited for: 18 -> 18; matrix products, arithmetic and copies ran while one was open for 2% -> 0% of each run, Pallas kernels for 7% -> 9%
where the time goes in v9:
time: 214 us
  waiting for transfers between devices  94.4 us (44%)
  starting transfers between devices  53.7 us (25%)
  Pallas kernels  33.2 us (16%)
  local copies, waits for them, and re-layouts  16.2 us (8%)
  between operations  14.4 us (7%)
    pallas_call x13, Pallas kernels, call(): pl.pallas_call(run, in_specs=[vmem] * n_in, out_specs=[vmem] * n_out, out...  33.2 us
    ppermute x2, waiting for transfers between devices, send_first(): lax.ppermute(sent[0], 'row', row_perm(over_x, over_y(1)))  30.5 us
    ppermute x4, starting transfers between devices, body(): lax.ppermute(messages[k], BOTH, scatter_perm(k))  17.8 us
    unnamed x58, local copies, waits for them, and re-layouts  15.5 us
    ppermute x2, waiting for transfers between devices, send_second(): first = lax.ppermute(sent[0], 'row', row_perm(over_y(1), over_x))  13.3 us
    ppermute x4, waiting for transfers between devices, body(): lax.ppermute(starts[step], BOTH, gather_perm(step))  13 us
    ppermute x2, starting transfers between devices, send_first(): lax.ppermute(sent[2], 'row', row_perm(None, over_y(2)))  12.8 us
    ppermute x4, starting transfers between devices, body(): lax.ppermute(starts[step], BOTH, gather_perm(step))  12.2 us
  transfers between devices with their start and end apart: 30, of which 18 were waited for; matrix products, arithmetic and copies ran while one was open for 0% of the time, Pallas kernels for 9%

profile of v9, /device:TPU:17, one launch (start us, length us, event | category | flops | bytes accessed | tf_op | source)
XLA Modules:
  0.0 213.8 jit_solution(17824551547649328880)
XLA Ops:
  12.1 6.3 %collective-permute-start.4 = (bf16[2,128,1024]{2,1,0:T(8,128)(2,1)S(1)}, bf16[2,128,1024]{2,1,0:T(8,128)(2,1)S(1)}, u32[]{:S(2)}, u32[]{:S(2)}) collective-permute-start(bf16[2,128,1024]{2,1,0:T(8,128)(2,1)S(1)} %shard_map.93.refs_0_), channel_id=1, source_target_pairs={{1,0},{2,1},{3,2},{0,3},{5,4},{6,5},{7,6},{4,7},{13,8},{14,9},{15,... | collective-permute-start | bytes 1572872 | tf_op jit(solution)/shard_map/ppermute | solution.py:336
  23.3 3.8 %collective-permute-start.6 = (bf16[2,128,1024]{2,1,0:T(8,128)(2,1)S(1)}, bf16[2,128,1024]{2,1,0:T(8,128)(2,1)S(1)}, u32[]{:S(2)}, u32[]{:S(2)}) collective-permute-start(bf16[2,128,1024]{2,1,0:T(8,128)(2,1)S(1)} %shard_map.93.refs_0_), channel_id=1, source_target_pairs={{2,0},{3,1},{0,2},{1,3},{6,4},{7,5},{4,6},{5,7},{14,8},{15,9},{12,... | collective-permute-start | bytes 1572872 | tf_op jit(solution)/shard_map/ppermute | solution.py:336
  31.1 5.3 %collective-permute-done.6.refs_3_ = bf16[2,128,1024]{2,1,0:T(8,128)(2,1)S(1)} collective-permute-done((bf16[2,128,1024]{2,1,0:T(8,128)(2,1)S(1)}, bf16[2,128,1024]{2,1,0:T(8,128)(2,1)S(1)}, u32[]{:S(2)}, u32[]{:S(2)}) %collective-permute-start.6) | collective-permute-done | bytes 524320 | tf_op jit(solution)/shard_map/ppermute | solution.py:336
  36.5 5.8 %collective-permute-done.3.refs_1_ = bf16[2,128,1024]{2,1,0:T(8,128)(2,1)S(1)} collective-permute-done((bf16[2,128,1024]{2,1,0:T(8,128)(2,1)S(1)}, bf16[2,128,1024]{2,1,0:T(8,128)(2,1)S(1)}, u32[]{:S(2)}, u32[]{:S(2)}) %collective-permute-start.3) | collective-permute-done | bytes 524320 | tf_op jit(solution)/shard_map/ppermute | solution.py:336
  42.3 4.5 %shard_map.95 = (bf16[512,1024]{1,0:T(8,128)(2,1)S(1)}, bf16[512,1024]{1,0:T(8,128)(2,1)S(1)}, bf16[3,128,1792]{2,1,0:T(8,128)(2,1)S(1)}, bf16[3,128,1792]{2,1,0:T(8,128)(2,1)S(1)}, bf16[3,128,1792]{2,1,0:T(8,128)(2,1)S(1)}) custom-call(bf16[2,128,1024]{2,1,0:T(8,128)(2,1)S(1)} %shard_map.93.refs_0_, ...), custom_call_target="tpu_custom_call" | custom-call | flops 1 | bytes 1 | tf_op jit(solution)/shard_map/pallas_call | solution.py:78
  47.0 4.5 %collective-permute-start.11 = (bf16[3,128,1792]{2,1,0:T(8,128)(2,1)S(1)}, bf16[3,128,1792]{2,1,0:T(8,128)(2,1)S(1)}, u32[]{:S(2)}, u32[]{:S(2)}) collective-permute-start(bf16[3,128,1792]{2,1,0:T(8,128)(2,1)S(1)} %get-tuple-element.70), channel_id=1, source_target_pairs={{8,72},{24,88},{40,104},{56,120},{72,8},{88,24},{104,40},{120,56},... | collective-permute-start | bytes 4128776 | tf_op jit(solution)/shard_map/ppermute | solution.py:306
  51.6 3.1 %shard_map.96 = (f32[3,256,1792]{2,1,0:T(8,128)S(1)}, bf16[512,512]{1,0:T(8,128)(2,1)S(1)}, bf16[512,512]{1,0:T(8,128)(2,1)S(1)}, bf16[512,512]{1,0:T(8,128)(2,1)S(1)}, bf16[512,512]{1,0:T(8,128)(2,1)S(1)}) custom-call(bf16[512,1024]{1,0:T(8,128)(2,1)S(1)} %get-tuple-element.65.refs_0_, bf16[512,1024]{1,0:T(8,128)(2,1)S(1)} %get-tuple-element.66.refs_1_, ...), custom_call_target="tpu_custom_call" | custom-call | flops 1 | bytes 1 | tf_op jit(solution)/shard_map/pallas_call | solution.py:78
  57.5 6.8 %collective-permute-done.10.refs_2_ = bf16[3,128,1792]{2,1,0:T(8,128)(2,1)S(1)} collective-permute-done((bf16[3,128,1792]{2,1,0:T(8,128)(2,1)S(1)}, bf16[3,128,1792]{2,1,0:T(8,128)(2,1)S(1)}, u32[]{:S(2)}, u32[]{:S(2)}) %collective-permute-start.10) | collective-permute-done | bytes 1376288 | tf_op jit(solution)/shard_map/ppermute | solution.py:305
  64.3 3.4 %collective-permute-done.11.refs_3_ = bf16[3,128,1792]{2,1,0:T(8,128)(2,1)S(1)} collective-permute-done((bf16[3,128,1792]{2,1,0:T(8,128)(2,1)S(1)}, bf16[3,128,1792]{2,1,0:T(8,128)(2,1)S(1)}, u32[]{:S(2)}, u32[]{:S(2)}) %collective-permute-start.11) | collective-permute-done | bytes 1376288 | tf_op jit(solution)/shard_map/ppermute | solution.py:306
  67.7 14.6 %collective-permute-done.9.refs_1_ = bf16[3,128,1792]{2,1,0:T(8,128)(2,1)S(1)} collective-permute-done((bf16[3,128,1792]{2,1,0:T(8,128)(2,1)S(1)}, bf16[3,128,1792]{2,1,0:T(8,128)(2,1)S(1)}, u32[]{:S(2)}, u32[]{:S(2)}) %collective-permute-start.9) | collective-permute-done | bytes 1376288 | tf_op jit(solution)/shard_map/ppermute | solution.py:304
  85.4 7.8 %collective-permute-done.14.refs_4_ = bf16[3,64,1792]{2,1,0:T(8,128)(2,1)S(1)} collective-permute-done((bf16[3,64,1792]{2,1,0:T(8,128)(2,1)S(1)}, bf16[3,64,1792]{2,1,0:T(8,128)(2,1)S(1)}, u32[]{:S(2)}, u32[]{:S(2)}) %collective-permute-start.14) | collective-permute-done | bytes 688160 | tf_op jit(solution)/shard_map/ppermute | solution.py:312
  93.2 7.1 %collective-permute-done.15.refs_5_ = bf16[3,64,1792]{2,1,0:T(8,128)(2,1)S(1)} collective-permute-done((bf16[3,64,1792]{2,1,0:T(8,128)(2,1)S(1)}, bf16[3,64,1792]{2,1,0:T(8,128)(2,1)S(1)}, u32[]{:S(2)}, u32[]{:S(2)}) %collective-permute-start.15) | collective-permute-done | bytes 688160 | tf_op jit(solution)/shard_map/ppermute | solution.py:313
  104.0 5.5 %collective-permute-done.17.refs_1_.refs_2_ = bf16[2,64,1792]{2,1,0:T(8,128)(2,1)S(1)} collective-permute-done((bf16[2,64,1792]{2,1,0:T(8,128)(2,1)S(1)}, bf16[2,64,1792]{2,1,0:T(8,128)(2,1)S(1)}, u32[]{:S(2)}, u32[]{:S(2)}) %collective-permute-start.17) | collective-permute-done | bytes 458784 | tf_op jit(solution)/shard_map/ppermute | solution.py:312
  109.5 5.0 %collective-permute-done.18.refs_2_.refs_3_ = bf16[2,64,1792]{2,1,0:T(8,128)(2,1)S(1)} collective-permute-done((bf16[2,64,1792]{2,1,0:T(8,128)(2,1)S(1)}, bf16[2,64,1792]{2,1,0:T(8,128)(2,1)S(1)}, u32[]{:S(2)}, u32[]{:S(2)}) %collective-permute-start.18) | collective-permute-done | bytes 458784 | tf_op jit(solution)/shard_map/ppermute | solution.py:313
  116.8 3.9 %collective-permute-start.20 = (bf16[2,128,1792]{2,1,0:T(8,128)(2,1)}, bf16[2,128,1792]{2,1,0:T(8,128)(2,1)S(1)}, u32[]{:S(2)}, u32[]{:S(2)}) collective-permute-start(bf16[2,128,1792]{2,1,0:T(8,128)(2,1)} %get-tuple-element.82), channel_id=1, source_target_pairs={{0,16},{8,40},{16,0},{24,56},{32,48},{40,72},{48,32},{56,88},{64,8... | collective-permute-start | bytes 2752520 | tf_op jit(solution)/shard_map/ppermute | solution.py:304
  120.7 8.3 %collective-permute-start.22 = (bf16[2,128,1792]{2,1,0:T(8,128)(2,1)}, bf16[2,128,1792]{2,1,0:T(8,128)(2,1)}, u32[]{:S(2)}, u32[]{:S(2)}) collective-permute-start(bf16[2,128,1792]{2,1,0:T(8,128)(2,1)} %get-tuple-element.82), channel_id=1, source_target_pairs={{8,72},{24,88},{40,104},{56,120},{72,8},{88,24},{104,40},{120,56},... | collective-permute-start | bytes 2752520 | tf_op jit(solution)/shard_map/ppermute | solution.py:306
  128.9 15.9 %collective-permute-done.20.refs_5_ = bf16[2,128,1792]{2,1,0:T(8,128)(2,1)S(1)} collective-permute-done((bf16[2,128,1792]{2,1,0:T(8,128)(2,1)}, bf16[2,128,1792]{2,1,0:T(8,128)(2,1)S(1)}, u32[]{:S(2)}, u32[]{:S(2)}) %collective-permute-start.20) | collective-permute-done | bytes 917536 | tf_op jit(solution)/shard_map/ppermute | solution.py:304
  155.7 8.3 %shard_map.102 = (bf16[2,128,1024]{2,1,0:T(8,128)(2,1)}, bf16[2,128,1024]{2,1,0:T(8,128)(2,1)}, bf16[2,128,1024]{2,1,0:T(8,128)(2,1)}, bf16[2,128,1024]{2,1,0:T(...) custom-call(f32[512,1024]{1,0:T(8,128)S(1)} %shard_map.101.refs_0_, ...), custom_call_target="tpu_custom_call" | custom-call | flops 1 | bytes 1 | tf_op jit(solution)/shard_map/pallas_call | solution.py:78
  164.0 4.7 %collective-permute-start.23 = (bf16[2,128,1024]{2,1,0:T(8,128)(2,1)}, bf16[2,128,1024]{2,1,0:T(8,128)(2,1)S(1)}, u32[]{:S(2)}, u32[]{:S(2)}) collective-permute-start(bf16[2,128,1024]{2,1,0:T(8,128)(2,1)} %get-tuple-element.86), channel_id=1, source_target_pairs={{8,12},{9,13},{10,14},{11,15},{12,8},{13,9},{14,10},{15,11},{24,28... | collective-permute-start | bytes 1572872 | tf_op jit(solution)/shard_map/ppermute | solution.py:380
  168.8 8.6 %collective-permute-start.25 = (bf16[2,128,1024]{2,1,0:T(8,128)(2,1)}, bf16[2,128,1024]{2,1,0:T(8,128)(2,1)}, u32[]{:S(2)}, u32[]{:S(2)}) collective-permute-start(bf16[2,128,1024]{2,1,0:T(8,128)(2,1)} %get-tuple-element.88), channel_id=1, source_target_pairs={{0,2},{1,3},{2,0},{3,1},{4,6},{5,7},{6,4},{7,5},{8,14},{9,15},{10,... | collective-permute-start | bytes 1572872 | tf_op jit(solution)/shard_map/ppermute | solution.py:380
  177.4 4.4 %collective-permute-start.26 = (bf16[2,128,1024]{2,1,0:T(8,128)(2,1)}, bf16[2,128,1024]{2,1,0:T(8,128)(2,1)}, u32[]{:S(2)}, u32[]{:S(2)}) collective-permute-start(bf16[2,128,1024]{2,1,0:T(8,128)(2,1)} %get-tuple-element.89), channel_id=1, source_target_pairs={{0,3},{1,0},{2,1},{3,2},{4,7},{5,4},{6,5},{7,6},{8,15},{9,12},{10,... | collective-permute-start | bytes 1572872 | tf_op jit(solution)/shard_map/ppermute | solution.py:380
  183.8 3.3 %shard_map.104 = bf16[1792,512]{1,0:T(8,128)(2,1)} custom-call(bf16[1024,1792]{1,0:T(8,128)(2,1)S(1)} %copy-done.5, bf16[1024,512]{1,0:T(8,128)(2,1)S(1)} %shard_map.97.refs_1_), custom_call_target="tpu_custom_call" | custom-call | flops 1 | bytes 1 | tf_op jit(solution)/shard_map/pallas_call | solution.py:78
  187.2 8.5 %shard_map.103 = (bf16[512,1792]{1,0:T(8,128)(2,1)}, bf16[512,1792]{1,0:T(8,128)(2,1)}) custom-call(bf16[512,512]{1,0:T(8,128)(2,1)S(1)} %copy-done.23, bf16[512,512]{1,0:T(8,128)(2,1)S(1)} %copy-done.25, bf16[2,512,1792]{2,1,0:T(8,128)(2,1)} %get-tuple-element.92.refs_2_, bf16[2,512,1792]{2,1,0:T(8,128)(2,1)} %collective-permute-done.27.refs_3_), custom_call_target="tpu_custom_call" | custom-call | flops 1 | bytes 1 | tf_op jit(solution)/shard_map/pallas_call | solution.py:78
  195.6 6.7 %collective-permute-done.26 = bf16[2,128,1024]{2,1,0:T(8,128)(2,1)} collective-permute-done((bf16[2,128,1024]{2,1,0:T(8,128)(2,1)}, bf16[2,128,1024]{2,1,0:T(8,128)(2,1)}, u32[]{:S(2)}, u32[]{:S(2)}) %collective-permute-start.26) | collective-permute-done | bytes 524320 | tf_op jit(solution)/shard_map/ppermute | solution.py:380
  (112 shorter events, 43.5 us)
Async XLA Ops:
  7.2 138.6 %all-gather.2.cloned.1.call-start = ((), (), s32[]{:S(2)}) async-start(), calls=%async_computation | async-start | bytes 3899392 | tf_op jit(solution)/shard_map/all_gather | solution.py:362
  9.5 13.7 %collective-permute-start.5 = (bf16[512,1792]{1,0:T(8,128)(2,1)}, bf16[512,1792]{1,0:T(8,128)(2,1)S(1)}, u32[]{:S(2)}, u32[]{:S(2)}) collective-permute-start(bf16[512,1792]{1,0:T(8,128)(2,1)} %refs_8_.1), channel_id=1, source_target_pairs={{0,8},{8,0},{16,24},{24,16},{32,40},{40,32},{48,56},{56,48},{64,72... | collective-permute-start | bytes 5505032 | tf_op jit(solution)/shard_map/ppermute | solution.py:318
  9.7 17.3 %collective-permute-start.2 = (bf16[512,1792]{1,0:T(8,128)(2,1)}, bf16[512,1792]{1,0:T(8,128)(2,1)S(1)}, u32[]{:S(2)}, u32[]{:S(2)}) collective-permute-start(bf16[512,1792]{1,0:T(8,128)(2,1)} %refs_9_.1), channel_id=1, source_target_pairs={{0,8},{8,0},{16,24},{24,16},{32,40},{40,32},{48,56},{56,48},{64,72... | collective-permute-start | bytes 5505032 | tf_op jit(solution)/shard_map/ppermute | solution.py:318
  10.0 21.1 %collective-permute-start.8 = (bf16[1792,512]{1,0:T(8,128)(2,1)}, bf16[1792,512]{1,0:T(8,128)(2,1)S(1)}, u32[]{:S(2)}, u32[]{:S(2)}) collective-permute-start(bf16[1792,512]{1,0:T(8,128)(2,1)} %refs_1_.4), channel_id=1, source_target_pairs={{0,8},{8,0},{16,24},{24,16},{32,40},{40,32},{48,56},{56,48},{64,72... | collective-permute-start | bytes 5505032 | tf_op jit(solution)/shard_map/ppermute | solution.py:318
  12.1 17.1 %collective-permute-start.4 = (bf16[2,128,1024]{2,1,0:T(8,128)(2,1)S(1)}, bf16[2,128,1024]{2,1,0:T(8,128)(2,1)S(1)}, u32[]{:S(2)}, u32[]{:S(2)}) collective-permute-start(bf16[2,128,1024]{2,1,0:T(8,128)(2,1)S(1)} %shard_map.93.refs_0_), channel_id=1, source_target_pairs={{1,0},{2,1},{3,2},{0,3},{5,4},{6,5},{7,6},{4,7},{13,8},{14,9},{15,... | collective-permute-start | bytes 1572872 | tf_op jit(solution)/shard_map/ppermute | solution.py:336
  18.4 12.7 %collective-permute-start.7 = (bf16[2,128,1024]{2,1,0:T(8,128)(2,1)S(1)}, bf16[2,128,1024]{2,1,0:T(8,128)(2,1)S(1)}, u32[]{:S(2)}, u32[]{:S(2)}) collective-permute-start(bf16[2,128,1024]{2,1,0:T(8,128)(2,1)S(1)} %shard_map.93.refs_0_), channel_id=1, source_target_pairs={{3,0},{0,1},{1,2},{2,3},{7,4},{4,5},{5,6},{6,7},{15,8},{12,9},{13,... | collective-permute-start | bytes 1572872 | tf_op jit(solution)/shard_map/ppermute | solution.py:336
  23.3 13.2 %collective-permute-start.6 = (bf16[2,128,1024]{2,1,0:T(8,128)(2,1)S(1)}, bf16[2,128,1024]{2,1,0:T(8,128)(2,1)S(1)}, u32[]{:S(2)}, u32[]{:S(2)}) collective-permute-start(bf16[2,128,1024]{2,1,0:T(8,128)(2,1)S(1)} %shard_map.93.refs_0_), channel_id=1, source_target_pairs={{2,0},{3,1},{0,2},{1,3},{6,4},{7,5},{4,6},{5,7},{14,8},{15,9},{12,... | collective-permute-start | bytes 1572872 | tf_op jit(solution)/shard_map/ppermute | solution.py:336
  27.1 15.2 %collective-permute-start.3 = (bf16[2,128,1024]{2,1,0:T(8,128)(2,1)S(1)}, bf16[2,128,1024]{2,1,0:T(8,128)(2,1)S(1)}, u32[]{:S(2)}, u32[]{:S(2)}) collective-permute-start(bf16[2,128,1024]{2,1,0:T(8,128)(2,1)S(1)} %shard_map.93.refs_0_), channel_id=1, source_target_pairs={{12,8},{13,9},{14,10},{15,11},{8,12},{9,13},{10,14},{11,15},{28,24... | collective-permute-start | bytes 1572872 | tf_op jit(solution)/shard_map/ppermute | solution.py:336
  46.8 17.5 %collective-permute-start.10 = (bf16[3,128,1792]{2,1,0:T(8,128)(2,1)S(1)}, bf16[3,128,1792]{2,1,0:T(8,128)(2,1)S(1)}, u32[]{:S(2)}, u32[]{:S(2)}) collective-permute-start(bf16[3,128,1792]{2,1,0:T(8,128)(2,1)S(1)} %get-tuple-element.69), channel_id=1, source_target_pairs={{0,16},{8,104},{16,0},{24,120},{32,48},{40,8},{48,32},{56,24},{64,... | collective-permute-start | bytes 4128776 | tf_op jit(solution)/shard_map/ppermute | solution.py:305
  47.0 20.7 %collective-permute-start.11 = (bf16[3,128,1792]{2,1,0:T(8,128)(2,1)S(1)}, bf16[3,128,1792]{2,1,0:T(8,128)(2,1)S(1)}, u32[]{:S(2)}, u32[]{:S(2)}) collective-permute-start(bf16[3,128,1792]{2,1,0:T(8,128)(2,1)S(1)} %get-tuple-element.70), channel_id=1, source_target_pairs={{8,72},{24,88},{40,104},{56,120},{72,8},{88,24},{104,40},{120,56},... | collective-permute-start | bytes 4128776 | tf_op jit(solution)/shard_map/ppermute | solution.py:306
  51.5 30.8 %collective-permute-start.9 = (bf16[3,128,1792]{2,1,0:T(8,128)(2,1)S(1)}, bf16[3,128,1792]{2,1,0:T(8,128)(2,1)S(1)}, u32[]{:S(2)}, u32[]{:S(2)}) collective-permute-start(bf16[3,128,1792]{2,1,0:T(8,128)(2,1)S(1)} %get-tuple-element.68), channel_id=1, source_target_pairs={{0,16},{8,40},{16,0},{24,56},{32,48},{40,72},{48,32},{56,88},{64,8... | collective-permute-start | bytes 4128776 | tf_op jit(solution)/shard_map/ppermute | solution.py:304
  83.0 10.2 %collective-permute-start.14 = (bf16[3,64,1792]{2,1,0:T(8,128)(2,1)S(1)}, bf16[3,64,1792]{2,1,0:T(8,128)(2,1)S(1)}, u32[]{:S(2)}, u32[]{:S(2)}) collective-permute-start(bf16[3,64,1792]{2,1,0:T(8,128)(2,1)S(1)} %get-tuple-element.77), channel_id=1, source_target_pairs={{0,32},{8,24},{16,48},{24,8},{32,64},{40,56},{48,80},{56,40},{64,9... | collective-permute-start | bytes 2064392 | tf_op jit(solution)/shard_map/ppermute | solution.py:312
  84.4 15.8 %collective-permute-start.15 = (bf16[3,64,1792]{2,1,0:T(8,128)(2,1)S(1)}, bf16[3,64,1792]{2,1,0:T(8,128)(2,1)S(1)}, u32[]{:S(2)}, u32[]{:S(2)}) collective-permute-start(bf16[3,64,1792]{2,1,0:T(8,128)(2,1)S(1)} %get-tuple-element.78), channel_id=1, source_target_pairs={{0,96},{8,24},{16,112},{24,8},{32,0},{40,56},{48,16},{56,40},{64,3... | collective-permute-start | bytes 2064392 | tf_op jit(solution)/shard_map/ppermute | solution.py:313
  84.7 15.6 %collective-permute-start.16 = (bf16[3,64,1792]{2,1,0:T(8,128)(2,1)S(1)}, bf16[3,64,1792]{2,1,0:T(8,128)(2,1)S(1)}, u32[]{:S(2)}, u32[]{:S(2)}) collective-permute-start(bf16[3,64,1792]{2,1,0:T(8,128)(2,1)S(1)} %get-tuple-element.79), channel_id=1, source_target_pairs={{0,64},{16,80},{32,96},{48,112},{64,0},{80,16},{96,32},{112,48},{1... | collective-permute-start | bytes 2064392 | tf_op jit(solution)/shard_map/ppermute | solution.py:311
  103.2 11.3 %collective-permute-start.18 = (bf16[2,64,1792]{2,1,0:T(8,128)(2,1)S(1)}, bf16[2,64,1792]{2,1,0:T(8,128)(2,1)S(1)}, u32[]{:S(2)}, u32[]{:S(2)}) collective-permute-start(bf16[2,64,1792]{2,1,0:T(8,128)(2,1)S(1)} %get-tuple-element.81.refs_0_.refs_1_), channel_id=1, source_target_pairs={{0,96},{8,24},{16,112},{24,8},{32,0},{40,56},{48,16},{56,40},{64,3... | collective-permute-start | bytes 1376264 | tf_op jit(solution)/shard_map/ppermute | solution.py:313
  103.3 11.2 %collective-permute-start.19 = (bf16[2,64,1792]{2,1,0:T(8,128)(2,1)S(1)}, bf16[2,64,1792]{2,1,0:T(8,128)(2,1)S(1)}, u32[]{:S(2)}, u32[]{:S(2)}) collective-permute-start(bf16[2,64,1792]{2,1,0:T(8,128)(2,1)S(1)} %get-tuple-element.81.refs_0_.refs_1_), channel_id=1, source_target_pairs={{0,64},{16,80},{32,96},{48,112},{64,0},{80,16},{96,32},{112,48},{1... | collective-permute-start | bytes 1376264 | tf_op jit(solution)/shard_map/ppermute | solution.py:311
  116.8 28.0 %collective-permute-start.20 = (bf16[2,128,1792]{2,1,0:T(8,128)(2,1)}, bf16[2,128,1792]{2,1,0:T(8,128)(2,1)S(1)}, u32[]{:S(2)}, u32[]{:S(2)}) collective-permute-start(bf16[2,128,1792]{2,1,0:T(8,128)(2,1)} %get-tuple-element.82), channel_id=1, source_target_pairs={{0,16},{8,40},{16,0},{24,56},{32,48},{40,72},{48,32},{56,88},{64,8... | collective-permute-start | bytes 2752520 | tf_op jit(solution)/shard_map/ppermute | solution.py:304
  120.7 30.7 %collective-permute-start.21 = (bf16[2,128,1792]{2,1,0:T(8,128)(2,1)}, bf16[2,128,1792]{2,1,0:T(8,128)(2,1)}, u32[]{:S(2)}, u32[]{:S(2)}) collective-permute-start(bf16[2,128,1792]{2,1,0:T(8,128)(2,1)} %get-tuple-element.84), channel_id=1, source_target_pairs={{0,16},{8,104},{16,0},{24,120},{32,48},{40,8},{48,32},{56,24},{64,... | collective-permute-start | bytes 2752520 | tf_op jit(solution)/shard_map/ppermute | solution.py:305
  120.7 33.8 %collective-permute-start.22 = (bf16[2,128,1792]{2,1,0:T(8,128)(2,1)}, bf16[2,128,1792]{2,1,0:T(8,128)(2,1)}, u32[]{:S(2)}, u32[]{:S(2)}) collective-permute-start(bf16[2,128,1792]{2,1,0:T(8,128)(2,1)} %get-tuple-element.82), channel_id=1, source_target_pairs={{8,72},{24,88},{40,104},{56,120},{72,8},{88,24},{104,40},{120,56},... | collective-permute-start | bytes 2752520 | tf_op jit(solution)/shard_map/ppermute | solution.py:306
  164.0 23.1 %collective-permute-start.27 = (bf16[2,512,1792]{2,1,0:T(8,128)(2,1)}, bf16[2,512,1792]{2,1,0:T(8,128)(2,1)}, u32[]{:S(2)}, u32[]{:S(2)}) collective-permute-start(bf16[2,512,1792]{2,1,0:T(8,128)(2,1)} %get-tuple-element.92.refs_2_), channel_id=1, source_target_pairs={{0,8},{8,0},{16,24},{24,16},{32,40},{40,32},{48,56},{56,48},{64,72... | collective-permute-start | bytes 11010056 | tf_op jit(solution)/shard_map/ppermute | solution.py:318
  164.0 31.6 %collective-permute-start.23 = (bf16[2,128,1024]{2,1,0:T(8,128)(2,1)}, bf16[2,128,1024]{2,1,0:T(8,128)(2,1)S(1)}, u32[]{:S(2)}, u32[]{:S(2)}) collective-permute-start(bf16[2,128,1024]{2,1,0:T(8,128)(2,1)} %get-tuple-element.86), channel_id=1, source_target_pairs={{8,12},{9,13},{10,14},{11,15},{12,8},{13,9},{14,10},{15,11},{24,28... | collective-permute-start | bytes 1572872 | tf_op jit(solution)/shard_map/ppermute | solution.py:380
  168.7 26.9 %collective-permute-start.24 = (bf16[2,128,1024]{2,1,0:T(8,128)(2,1)}, bf16[2,128,1024]{2,1,0:T(8,128)(2,1)}, u32[]{:S(2)}, u32[]{:S(2)}) collective-permute-start(bf16[2,128,1024]{2,1,0:T(8,128)(2,1)} %get-tuple-element.87), channel_id=1, source_target_pairs={{0,1},{1,2},{2,3},{3,0},{4,5},{5,6},{6,7},{7,4},{8,13},{9,14},{10,... | collective-permute-start | bytes 1572872 | tf_op jit(solution)/shard_map/ppermute | solution.py:380
  168.8 26.8 %collective-permute-start.25 = (bf16[2,128,1024]{2,1,0:T(8,128)(2,1)}, bf16[2,128,1024]{2,1,0:T(8,128)(2,1)}, u32[]{:S(2)}, u32[]{:S(2)}) collective-permute-start(bf16[2,128,1024]{2,1,0:T(8,128)(2,1)} %get-tuple-element.88), channel_id=1, source_target_pairs={{0,2},{1,3},{2,0},{3,1},{4,6},{5,7},{6,4},{7,5},{8,14},{9,15},{10,... | collective-permute-start | bytes 1572872 | tf_op jit(solution)/shard_map/ppermute | solution.py:380
  177.4 25.0 %collective-permute-start.26 = (bf16[2,128,1024]{2,1,0:T(8,128)(2,1)}, bf16[2,128,1024]{2,1,0:T(8,128)(2,1)}, u32[]{:S(2)}, u32[]{:S(2)}) collective-permute-start(bf16[2,128,1024]{2,1,0:T(8,128)(2,1)} %get-tuple-element.89), channel_id=1, source_target_pairs={{0,3},{1,0},{2,1},{3,2},{4,7},{5,4},{6,5},{7,6},{8,15},{9,12},{10,... | collective-permute-start | bytes 1572872 | tf_op jit(solution)/shard_map/ppermute | solution.py:380
  (35 other events, 224.6 us)
Sparse Core Ops, SparseCore 0:
  101.9 41.5 all-gather.1

commit v10 on v9

--- a/solution.py
+++ b/solution.py
@@ -251,10 +251,11 @@
 
 def pack_kernel(ins, outs):
     own, near1, near2, near3 = ins
-    first, second = outs
+    first, second, third = outs
     core0 = Place().core == 0
-    first[:, :PIECE] = own[...]
-    first[:, PIECE:] = near1[...]
+    for out in (first, third):
+        out[:, :PIECE] = own[...]
+        out[:, PIECE:] = near1[...]
     second[:, :PIECE] = jnp.where(core0, near2[...], own[...])
     second[:, PIECE:] = jnp.where(core0, near3[...], near1[...])
 
@@ -307,10 +308,10 @@
     )
 
 
-def send_second(sent):
+def send_second(sent, core1=over_x):
     third = lax.ppermute(sent[2], "row", row_perm(over_y(2), None))
     first = lax.ppermute(sent[0], "row", row_perm(over_y(1), over_x))
-    return first, lax.ppermute(sent[1], "row", row_perm(over_y(-1), over_x)), third
+    return first, lax.ppermute(sent[1], "row", row_perm(over_y(-1), core1)), third
 
 
 def body(tokens, gate_weight, up_weight, down_weight, grad_output):
@@ -361,9 +362,9 @@
     )
     hidden = lax.all_gather(hidden, "row", axis=0, tiled=True)
 
-    near = send_second([d_own] * 3)
-    first, second = call(pack_kernel, [d_own, *near], [shape((2, 2 * PIECE, ff_width))] * 2)
-    far = send_first([first, second, first])
+    near = send_second([d_own] * 3, None)
+    packed = call(pack_kernel, [d_own, *near], [shape((2, 2 * PIECE, ff_width))] * 3)
+    far = send_first(packed)
     hidden = after(hidden, far[0])
     (layer,) = call(
         layer_kernel,

time: 214 us -> 216 us (level); the launches traced: 214 us -> 213 us
  starting transfers between devices: 53.7 us -> 43.2 us
  waiting for transfers between devices: 94.4 us -> 103 us
    ppermute x2, waiting for transfers between devices: 30.5 us -> 50.4 us  [send_first(): lax.ppermute(sent[0], 'row', row_perm(over_x, over_y(1)))]
    ppermute x4, starting transfers between devices: 17.8 us -> 7.06 us  [body(): lax.ppermute(messages[k], BOTH, scatter_perm(k))]
    ppermute x2, waiting for transfers between devices: 12.1 us -> 7.08 us  [send_second(): lax.ppermute(sent[1], 'row', row_perm(over_y(-1), core1))]
    ppermute x9, starting transfers between devices: 2.21 us -> 6.73 us  [body(): flip = lambda value: lax.ppermute(value, 'row', CORE_FLIP)]
    ppermute x2, waiting for transfers between devices: 6.45 us -> 3.37 us  [send_first(): lax.ppermute(sent[2], 'row', row_perm(None, over_y(2)))]
    ppermute x2, starting transfers between devices: 12.8 us -> 10.2 us  [send_first(): lax.ppermute(sent[2], 'row', row_perm(None, over_y(2)))]
    ppermute x4, waiting for transfers between devices: 6.76 us -> 4.26 us  [body(): lax.ppermute(messages[k], BOTH, scatter_perm(k))]
    ppermute x2, starting transfers between devices: 3.92 us -> 1.52 us  [send_first(): lax.ppermute(sent[0], 'row', row_perm(over_x, over_y(1)))]
  transfers between devices with their start and end apart: 30 -> 30, of which waited for: 18 -> 16; matrix products, arithmetic and copies ran while one was open for 0% -> 0% of each run, Pallas kernels for 9% -> 9%
where the time goes in v10:
time: 216 us; the launch traced here: 213 us
  waiting for transfers between devices  103 us (48%)
  starting transfers between devices  43.2 us (20%)
  Pallas kernels  33.3 us (15%)
  local copies, waits for them, and re-layouts  17.5 us (8%)
  between operations  14.4 us (7%)
    ppermute x2, waiting for transfers between devices, send_first(): lax.ppermute(sent[0], 'row', row_perm(over_x, over_y(1)))  50.4 us
    pallas_call x13, Pallas kernels, call(): pl.pallas_call(run, in_specs=[vmem] * n_in, out_specs=[vmem] * n_out, out...  33.3 us
    unnamed x58, local copies, waits for them, and re-layouts  16.8 us
    ppermute x4, waiting for transfers between devices, body(): lax.ppermute(starts[step], BOTH, gather_perm(step))  13 us
    ppermute x2, waiting for transfers between devices, send_second(): first = lax.ppermute(sent[0], 'row', row_perm(over_y(1), over_x))  12.7 us
    ppermute x4, starting transfers between devices, body(): lax.ppermute(starts[step], BOTH, gather_perm(step))  12.2 us
    ppermute x2, starting transfers between devices, send_first(): lax.ppermute(sent[2], 'row', row_perm(None, over_y(2)))  10.2 us
    ppermute x2, waiting for transfers between devices, send_second(): lax.ppermute(sent[1], 'row', row_perm(over_y(-1), core1))  7.08 us
  transfers between devices with their start and end apart: 30, of which 16 were waited for; matrix products, arithmetic and copies ran while one was open for 0% of the time, Pallas kernels for 9%

profile of v10, /device:TPU:17, one launch (start us, length us, event | category | flops | bytes accessed | tf_op | source)
XLA Modules:
  0.0 213.0 jit_solution(11140005835271589200)
XLA Ops:
  12.1 6.3 %collective-permute-start.4 = (bf16[2,128,1024]{2,1,0:T(8,128)(2,1)S(1)}, bf16[2,128,1024]{2,1,0:T(8,128)(2,1)S(1)}, u32[]{:S(2)}, u32[]{:S(2)}) collective-permute-start(bf16[2,128,1024]{2,1,0:T(8,128)(2,1)S(1)} %shard_map.93.refs_0_), channel_id=1, source_target_pairs={{1,0},{2,1},{3,2},{0,3},{5,4},{6,5},{7,6},{4,7},{13,8},{14,9},{15,... | collective-permute-start | bytes 1572872 | tf_op jit(solution)/shard_map/ppermute | solution.py:337
  23.3 3.8 %collective-permute-start.6 = (bf16[2,128,1024]{2,1,0:T(8,128)(2,1)S(1)}, bf16[2,128,1024]{2,1,0:T(8,128)(2,1)S(1)}, u32[]{:S(2)}, u32[]{:S(2)}) collective-permute-start(bf16[2,128,1024]{2,1,0:T(8,128)(2,1)S(1)} %shard_map.93.refs_0_), channel_id=1, source_target_pairs={{2,0},{3,1},{0,2},{1,3},{6,4},{7,5},{4,6},{5,7},{14,8},{15,9},{12,... | collective-permute-start | bytes 1572872 | tf_op jit(solution)/shard_map/ppermute | solution.py:337
  27.1 2.1 %collective-permute-start.3 = (bf16[2,128,1024]{2,1,0:T(8,128)(2,1)S(1)}, bf16[2,128,1024]{2,1,0:T(8,128)(2,1)S(1)}, u32[]{:S(2)}, u32[]{:S(2)}) collective-permute-start(bf16[2,128,1024]{2,1,0:T(8,128)(2,1)S(1)} %shard_map.93.refs_0_), channel_id=1, source_target_pairs={{12,8},{13,9},{14,10},{15,11},{8,12},{9,13},{10,14},{11,15},{28,24... | collective-permute-start | bytes 1572872 | tf_op jit(solution)/shard_map/ppermute | solution.py:337
  31.1 5.3 %collective-permute-done.6.refs_3_ = bf16[2,128,1024]{2,1,0:T(8,128)(2,1)S(1)} collective-permute-done((bf16[2,128,1024]{2,1,0:T(8,128)(2,1)S(1)}, bf16[2,128,1024]{2,1,0:T(8,128)(2,1)S(1)}, u32[]{:S(2)}, u32[]{:S(2)}) %collective-permute-start.6) | collective-permute-done | bytes 524320 | tf_op jit(solution)/shard_map/ppermute | solution.py:337
  36.5 5.8 %collective-permute-done.3.refs_1_ = bf16[2,128,1024]{2,1,0:T(8,128)(2,1)S(1)} collective-permute-done((bf16[2,128,1024]{2,1,0:T(8,128)(2,1)S(1)}, bf16[2,128,1024]{2,1,0:T(8,128)(2,1)S(1)}, u32[]{:S(2)}, u32[]{:S(2)}) %collective-permute-start.3) | collective-permute-done | bytes 524320 | tf_op jit(solution)/shard_map/ppermute | solution.py:337
  42.3 4.5 %shard_map.95 = (bf16[512,1024]{1,0:T(8,128)(2,1)S(1)}, bf16[512,1024]{1,0:T(8,128)(2,1)S(1)}, bf16[3,128,1792]{2,1,0:T(8,128)(2,1)S(1)}, bf16[3,128,1792]{2,1,0:T(8,128)(2,1)S(1)}, bf16[3,128,1792]{2,1,0:T(8,128)(2,1)S(1)}) custom-call(bf16[2,128,1024]{2,1,0:T(8,128)(2,1)S(1)} %shard_map.93.refs_0_, ...), custom_call_target="tpu_custom_call" | custom-call | flops 1 | bytes 1 | tf_op jit(solution)/shard_map/pallas_call | solution.py:78
  47.0 4.5 %collective-permute-start.11 = (bf16[3,128,1792]{2,1,0:T(8,128)(2,1)S(1)}, bf16[3,128,1792]{2,1,0:T(8,128)(2,1)S(1)}, u32[]{:S(2)}, u32[]{:S(2)}) collective-permute-start(bf16[3,128,1792]{2,1,0:T(8,128)(2,1)S(1)} %get-tuple-element.71), channel_id=1, source_target_pairs={{8,72},{24,88},{40,104},{56,120},{72,8},{88,24},{104,40},{120,56},... | collective-permute-start | bytes 4128776 | tf_op jit(solution)/shard_map/ppermute | solution.py:307
  51.6 3.1 %shard_map.96 = (f32[3,256,1792]{2,1,0:T(8,128)S(1)}, bf16[512,512]{1,0:T(8,128)(2,1)S(1)}, bf16[512,512]{1,0:T(8,128)(2,1)S(1)}, bf16[512,512]{1,0:T(8,128)(2,1)S(1)}, bf16[512,512]{1,0:T(8,128)(2,1)S(1)}) custom-call(bf16[512,1024]{1,0:T(8,128)(2,1)S(1)} %get-tuple-element.66.refs_0_, bf16[512,1024]{1,0:T(8,128)(2,1)S(1)} %get-tuple-element.67.refs_1_, ...), custom_call_target="tpu_custom_call" | custom-call | flops 1 | bytes 1 | tf_op jit(solution)/shard_map/pallas_call | solution.py:78
  57.5 6.8 %collective-permute-done.10.refs_2_ = bf16[3,128,1792]{2,1,0:T(8,128)(2,1)S(1)} collective-permute-done((bf16[3,128,1792]{2,1,0:T(8,128)(2,1)S(1)}, bf16[3,128,1792]{2,1,0:T(8,128)(2,1)S(1)}, u32[]{:S(2)}, u32[]{:S(2)}) %collective-permute-start.10) | collective-permute-done | bytes 1376288 | tf_op jit(solution)/shard_map/ppermute | solution.py:306
  64.3 3.4 %collective-permute-done.11.refs_3_ = bf16[3,128,1792]{2,1,0:T(8,128)(2,1)S(1)} collective-permute-done((bf16[3,128,1792]{2,1,0:T(8,128)(2,1)S(1)}, bf16[3,128,1792]{2,1,0:T(8,128)(2,1)S(1)}, u32[]{:S(2)}, u32[]{:S(2)}) %collective-permute-start.11) | collective-permute-done | bytes 1376288 | tf_op jit(solution)/shard_map/ppermute | solution.py:307
  67.7 14.6 %collective-permute-done.9.refs_1_ = bf16[3,128,1792]{2,1,0:T(8,128)(2,1)S(1)} collective-permute-done((bf16[3,128,1792]{2,1,0:T(8,128)(2,1)S(1)}, bf16[3,128,1792]{2,1,0:T(8,128)(2,1)S(1)}, u32[]{:S(2)}, u32[]{:S(2)}) %collective-permute-start.9) | collective-permute-done | bytes 1376288 | tf_op jit(solution)/shard_map/ppermute | solution.py:305
  85.4 7.8 %collective-permute-done.14.refs_4_ = bf16[3,64,1792]{2,1,0:T(8,128)(2,1)S(1)} collective-permute-done((bf16[3,64,1792]{2,1,0:T(8,128)(2,1)S(1)}, bf16[3,64,1792]{2,1,0:T(8,128)(2,1)S(1)}, u32[]{:S(2)}, u32[]{:S(2)}) %collective-permute-start.14) | collective-permute-done | bytes 688160 | tf_op jit(solution)/shard_map/ppermute | solution.py:313
  93.2 7.1 %collective-permute-done.15.refs_5_ = bf16[3,64,1792]{2,1,0:T(8,128)(2,1)S(1)} collective-permute-done((bf16[3,64,1792]{2,1,0:T(8,128)(2,1)S(1)}, bf16[3,64,1792]{2,1,0:T(8,128)(2,1)S(1)}, u32[]{:S(2)}, u32[]{:S(2)}) %collective-permute-start.15) | collective-permute-done | bytes 688160 | tf_op jit(solution)/shard_map/ppermute | solution.py:314
  104.6 4.9 %collective-permute-done.17.refs_1_.refs_2_ = bf16[2,64,1792]{2,1,0:T(8,128)(2,1)S(1)} collective-permute-done((bf16[2,64,1792]{2,1,0:T(8,128)(2,1)S(1)}, bf16[2,64,1792]{2,1,0:T(8,128)(2,1)S(1)}, u32[]{:S(2)}, u32[]{:S(2)}) %collective-permute-start.17) | collective-permute-done | bytes 458784 | tf_op jit(solution)/shard_map/ppermute | solution.py:313
  113.3 5.7 %collective-permute-start.22 = (bf16[2,128,1792]{2,1,0:T(8,128)(2,1)}, bf16[2,128,1792]{2,1,0:T(8,128)(2,1)}, u32[]{:S(2)}, u32[]{:S(2)}) collective-permute-start(bf16[2,128,1792]{2,1,0:T(8,128)(2,1)} %get-tuple-element.86), channel_id=1, source_target_pairs={{8,72},{24,88},{40,104},{56,120},{72,8},{88,24},{104,40},{120,56},... | collective-permute-start | bytes 2752520 | tf_op jit(solution)/shard_map/ppermute | solution.py:307
  119.0 35.8 %collective-permute-done.20.refs_5_ = bf16[2,128,1792]{2,1,0:T(8,128)(2,1)S(1)} collective-permute-done((bf16[2,128,1792]{2,1,0:T(8,128)(2,1)S(1)}, bf16[2,128,1792]{2,1,0:T(8,128)(2,1)S(1)}, u32[]{:S(2)}, u32[]{:S(2)}) %collective-permute-start.20) | collective-permute-done | bytes 917536 | tf_op jit(solution)/shard_map/ppermute | solution.py:305
  155.7 2.0 copy-done.4
  159.3 2.1 shard_map.101.refs_0_
  163.9 8.3 %shard_map.102 = (bf16[2,128,1024]{2,1,0:T(8,128)(2,1)}, bf16[2,128,1024]{2,1,0:T(8,128)(2,1)}, bf16[2,128,1024]{2,1,0:T(8,128)(2,1)}, bf16[2,128,1024]{2,1,0:T(...) custom-call(f32[512,1024]{1,0:T(8,128)S(1)} %shard_map.101.refs_0_, ...), custom_call_target="tpu_custom_call" | custom-call | flops 1 | bytes 1 | tf_op jit(solution)/shard_map/pallas_call | solution.py:78
  174.3 5.0 %collective-permute-start.26 = (bf16[2,128,1024]{2,1,0:T(8,128)(2,1)}, bf16[2,128,1024]{2,1,0:T(8,128)(2,1)}, u32[]{:S(2)}, u32[]{:S(2)}) collective-permute-start(bf16[2,128,1024]{2,1,0:T(8,128)(2,1)} %get-tuple-element.91), channel_id=1, source_target_pairs={{0,3},{1,0},{2,1},{3,2},{4,7},{5,4},{6,5},{7,6},{8,15},{9,12},{10,... | collective-permute-start | bytes 1572872 | tf_op jit(solution)/shard_map/ppermute | solution.py:381
  181.3 3.3 %shard_map.104 = bf16[1792,512]{1,0:T(8,128)(2,1)} custom-call(bf16[1024,1792]{1,0:T(8,128)(2,1)S(1)} %copy-done.5, bf16[1024,512]{1,0:T(8,128)(2,1)S(1)} %shard_map.97.refs_1_), custom_call_target="tpu_custom_call" | custom-call | flops 1 | bytes 1 | tf_op jit(solution)/shard_map/pallas_call | solution.py:78
  184.6 8.5 %shard_map.103 = (bf16[512,1792]{1,0:T(8,128)(2,1)}, bf16[512,1792]{1,0:T(8,128)(2,1)}) custom-call(bf16[512,512]{1,0:T(8,128)(2,1)S(1)} %copy-done.23, bf16[512,512]{1,0:T(8,128)(2,1)S(1)} %copy-done.25, bf16[2,512,1792]{2,1,0:T(8,128)(2,1)} %get-tuple-element.94.refs_2_, bf16[2,512,1792]{2,1,0:T(8,128)(2,1)} %collective-permute-done.27.refs_3_), custom_call_target="tpu_custom_call" | custom-call | flops 1 | bytes 1 | tf_op jit(solution)/shard_map/pallas_call | solution.py:78
  193.1 4.3 %collective-permute-done.26 = bf16[2,128,1024]{2,1,0:T(8,128)(2,1)} collective-permute-done((bf16[2,128,1024]{2,1,0:T(8,128)(2,1)}, bf16[2,128,1024]{2,1,0:T(8,128)(2,1)}, u32[]{:S(2)}, u32[]{:S(2)}) %collective-permute-start.26) | collective-permute-done | bytes 524320 | tf_op jit(solution)/shard_map/ppermute | solution.py:381
  199.2 4.6 %collective-permute-start.28 = (f32[2,128,512]{2,1,0:T(8,128)S(1)}, f32[2,128,512]{2,1,0:T(8,128)S(1)}, u32[]{:S(2)}, u32[]{:S(2)}) collective-permute-start(f32[2,128,512]{2,1,0:T(8,128)S(1)} %slice.17), channel_id=1, source_target_pairs={{0,8},{8,0},{16,24},{24,16},{32,40},{40,32},{48,56},{56,48},{64,72... | collective-permute-start | bytes 1572872 | tf_op jit(solution)/shard_map/ppermute | solution.py:319
  (112 shorter events, 39.1 us)
Async XLA Ops:
  7.2 148.6 %all-gather.2.cloned.1.call-start = ((), (), s32[]{:S(2)}) async-start(), calls=%async_computation | async-start | bytes 3899392 | tf_op jit(solution)/shard_map/all_gather | solution.py:363
  9.5 13.7 %collective-permute-start.5 = (bf16[512,1792]{1,0:T(8,128)(2,1)}, bf16[512,1792]{1,0:T(8,128)(2,1)S(1)}, u32[]{:S(2)}, u32[]{:S(2)}) collective-permute-start(bf16[512,1792]{1,0:T(8,128)(2,1)} %refs_8_.1), channel_id=1, source_target_pairs={{0,8},{8,0},{16,24},{24,16},{32,40},{40,32},{48,56},{56,48},{64,72... | collective-permute-start | bytes 5505032 | tf_op jit(solution)/shard_map/ppermute | solution.py:319
  9.7 17.3 %collective-permute-start.2 = (bf16[512,1792]{1,0:T(8,128)(2,1)}, bf16[512,1792]{1,0:T(8,128)(2,1)S(1)}, u32[]{:S(2)}, u32[]{:S(2)}) collective-permute-start(bf16[512,1792]{1,0:T(8,128)(2,1)} %refs_9_.1), channel_id=1, source_target_pairs={{0,8},{8,0},{16,24},{24,16},{32,40},{40,32},{48,56},{56,48},{64,72... | collective-permute-start | bytes 5505032 | tf_op jit(solution)/shard_map/ppermute | solution.py:319
  10.0 21.1 %collective-permute-start.8 = (bf16[1792,512]{1,0:T(8,128)(2,1)}, bf16[1792,512]{1,0:T(8,128)(2,1)S(1)}, u32[]{:S(2)}, u32[]{:S(2)}) collective-permute-start(bf16[1792,512]{1,0:T(8,128)(2,1)} %refs_1_.4), channel_id=1, source_target_pairs={{0,8},{8,0},{16,24},{24,16},{32,40},{40,32},{48,56},{56,48},{64,72... | collective-permute-start | bytes 5505032 | tf_op jit(solution)/shard_map/ppermute | solution.py:319
  12.1 17.1 %collective-permute-start.4 = (bf16[2,128,1024]{2,1,0:T(8,128)(2,1)S(1)}, bf16[2,128,1024]{2,1,0:T(8,128)(2,1)S(1)}, u32[]{:S(2)}, u32[]{:S(2)}) collective-permute-start(bf16[2,128,1024]{2,1,0:T(8,128)(2,1)S(1)} %shard_map.93.refs_0_), channel_id=1, source_target_pairs={{1,0},{2,1},{3,2},{0,3},{5,4},{6,5},{7,6},{4,7},{13,8},{14,9},{15,... | collective-permute-start | bytes 1572872 | tf_op jit(solution)/shard_map/ppermute | solution.py:337
  18.4 12.7 %collective-permute-start.7 = (bf16[2,128,1024]{2,1,0:T(8,128)(2,1)S(1)}, bf16[2,128,1024]{2,1,0:T(8,128)(2,1)S(1)}, u32[]{:S(2)}, u32[]{:S(2)}) collective-permute-start(bf16[2,128,1024]{2,1,0:T(8,128)(2,1)S(1)} %shard_map.93.refs_0_), channel_id=1, source_target_pairs={{3,0},{0,1},{1,2},{2,3},{7,4},{4,5},{5,6},{6,7},{15,8},{12,9},{13,... | collective-permute-start | bytes 1572872 | tf_op jit(solution)/shard_map/ppermute | solution.py:337
  23.3 13.2 %collective-permute-start.6 = (bf16[2,128,1024]{2,1,0:T(8,128)(2,1)S(1)}, bf16[2,128,1024]{2,1,0:T(8,128)(2,1)S(1)}, u32[]{:S(2)}, u32[]{:S(2)}) collective-permute-start(bf16[2,128,1024]{2,1,0:T(8,128)(2,1)S(1)} %shard_map.93.refs_0_), channel_id=1, source_target_pairs={{2,0},{3,1},{0,2},{1,3},{6,4},{7,5},{4,6},{5,7},{14,8},{15,9},{12,... | collective-permute-start | bytes 1572872 | tf_op jit(solution)/shard_map/ppermute | solution.py:337
  27.1 15.2 %collective-permute-start.3 = (bf16[2,128,1024]{2,1,0:T(8,128)(2,1)S(1)}, bf16[2,128,1024]{2,1,0:T(8,128)(2,1)S(1)}, u32[]{:S(2)}, u32[]{:S(2)}) collective-permute-start(bf16[2,128,1024]{2,1,0:T(8,128)(2,1)S(1)} %shard_map.93.refs_0_), channel_id=1, source_target_pairs={{12,8},{13,9},{14,10},{15,11},{8,12},{9,13},{10,14},{11,15},{28,24... | collective-permute-start | bytes 1572872 | tf_op jit(solution)/shard_map/ppermute | solution.py:337
  46.8 17.5 %collective-permute-start.10 = (bf16[3,128,1792]{2,1,0:T(8,128)(2,1)S(1)}, bf16[3,128,1792]{2,1,0:T(8,128)(2,1)S(1)}, u32[]{:S(2)}, u32[]{:S(2)}) collective-permute-start(bf16[3,128,1792]{2,1,0:T(8,128)(2,1)S(1)} %get-tuple-element.70), channel_id=1, source_target_pairs={{0,16},{8,104},{16,0},{24,120},{32,48},{40,8},{48,32},{56,24},{64,... | collective-permute-start | bytes 4128776 | tf_op jit(solution)/shard_map/ppermute | solution.py:306
  47.0 20.7 %collective-permute-start.11 = (bf16[3,128,1792]{2,1,0:T(8,128)(2,1)S(1)}, bf16[3,128,1792]{2,1,0:T(8,128)(2,1)S(1)}, u32[]{:S(2)}, u32[]{:S(2)}) collective-permute-start(bf16[3,128,1792]{2,1,0:T(8,128)(2,1)S(1)} %get-tuple-element.71), channel_id=1, source_target_pairs={{8,72},{24,88},{40,104},{56,120},{72,8},{88,24},{104,40},{120,56},... | collective-permute-start | bytes 4128776 | tf_op jit(solution)/shard_map/ppermute | solution.py:307
  51.5 30.8 %collective-permute-start.9 = (bf16[3,128,1792]{2,1,0:T(8,128)(2,1)S(1)}, bf16[3,128,1792]{2,1,0:T(8,128)(2,1)S(1)}, u32[]{:S(2)}, u32[]{:S(2)}) collective-permute-start(bf16[3,128,1792]{2,1,0:T(8,128)(2,1)S(1)} %get-tuple-element.69), channel_id=1, source_target_pairs={{0,16},{8,40},{16,0},{24,56},{32,48},{40,72},{48,32},{56,88},{64,8... | collective-permute-start | bytes 4128776 | tf_op jit(solution)/shard_map/ppermute | solution.py:305
  83.0 10.2 %collective-permute-start.14 = (bf16[3,64,1792]{2,1,0:T(8,128)(2,1)S(1)}, bf16[3,64,1792]{2,1,0:T(8,128)(2,1)S(1)}, u32[]{:S(2)}, u32[]{:S(2)}) collective-permute-start(bf16[3,64,1792]{2,1,0:T(8,128)(2,1)S(1)} %get-tuple-element.78), channel_id=1, source_target_pairs={{0,32},{8,24},{16,48},{24,8},{32,64},{40,56},{48,80},{56,40},{64,9... | collective-permute-start | bytes 2064392 | tf_op jit(solution)/shard_map/ppermute | solution.py:313
  84.4 15.8 %collective-permute-start.15 = (bf16[3,64,1792]{2,1,0:T(8,128)(2,1)S(1)}, bf16[3,64,1792]{2,1,0:T(8,128)(2,1)S(1)}, u32[]{:S(2)}, u32[]{:S(2)}) collective-permute-start(bf16[3,64,1792]{2,1,0:T(8,128)(2,1)S(1)} %get-tuple-element.79), channel_id=1, source_target_pairs={{0,96},{8,24},{16,112},{24,8},{32,0},{40,56},{48,16},{56,40},{64,3... | collective-permute-start | bytes 2064392 | tf_op jit(solution)/shard_map/ppermute | solution.py:314
  84.7 15.6 %collective-permute-start.16 = (bf16[3,64,1792]{2,1,0:T(8,128)(2,1)S(1)}, bf16[3,64,1792]{2,1,0:T(8,128)(2,1)S(1)}, u32[]{:S(2)}, u32[]{:S(2)}) collective-permute-start(bf16[3,64,1792]{2,1,0:T(8,128)(2,1)S(1)} %get-tuple-element.80), channel_id=1, source_target_pairs={{0,64},{16,80},{32,96},{48,112},{64,0},{80,16},{96,32},{112,48},{1... | collective-permute-start | bytes 2064392 | tf_op jit(solution)/shard_map/ppermute | solution.py:312
  101.8 7.7 %collective-permute-start.17 = (bf16[2,64,1792]{2,1,0:T(8,128)(2,1)S(1)}, bf16[2,64,1792]{2,1,0:T(8,128)(2,1)S(1)}, u32[]{:S(2)}, u32[]{:S(2)}) collective-permute-start(bf16[2,64,1792]{2,1,0:T(8,128)(2,1)S(1)} %get-tuple-element.82.refs_0_.refs_1_), channel_id=1, source_target_pairs={{0,32},{8,24},{16,48},{24,8},{32,64},{40,56},{48,80},{56,40},{64,9... | collective-permute-start | bytes 1376264 | tf_op jit(solution)/shard_map/ppermute | solution.py:313
  103.2 6.3 %collective-permute-start.18 = (bf16[2,64,1792]{2,1,0:T(8,128)(2,1)S(1)}, bf16[2,64,1792]{2,1,0:T(8,128)(2,1)S(1)}, u32[]{:S(2)}, u32[]{:S(2)}) collective-permute-start(bf16[2,64,1792]{2,1,0:T(8,128)(2,1)S(1)} %get-tuple-element.82.refs_0_.refs_1_), channel_id=1, source_target_pairs={{0,96},{16,112},{32,0},{48,16},{64,32},{80,48},{96,64},{112,80},{1... | collective-permute-start | bytes 1376264 | tf_op jit(solution)/shard_map/ppermute | solution.py:314
  111.8 42.9 %collective-permute-start.20 = (bf16[2,128,1792]{2,1,0:T(8,128)(2,1)S(1)}, bf16[2,128,1792]{2,1,0:T(8,128)(2,1)S(1)}, u32[]{:S(2)}, u32[]{:S(2)}) collective-permute-start(bf16[2,128,1792]{2,1,0:T(8,128)(2,1)S(1)} %get-tuple-element.83), channel_id=1, source_target_pairs={{0,16},{8,40},{16,0},{24,56},{32,48},{40,72},{48,32},{56,88},{64,8... | collective-permute-start | bytes 2752520 | tf_op jit(solution)/shard_map/ppermute | solution.py:305
  113.3 48.1 %collective-permute-start.21 = (bf16[2,128,1792]{2,1,0:T(8,128)(2,1)}, bf16[2,128,1792]{2,1,0:T(8,128)(2,1)}, u32[]{:S(2)}, u32[]{:S(2)}) collective-permute-start(bf16[2,128,1792]{2,1,0:T(8,128)(2,1)} %get-tuple-element.85), channel_id=1, source_target_pairs={{0,16},{8,104},{16,0},{24,120},{32,48},{40,8},{48,32},{56,24},{64,... | collective-permute-start | bytes 2752520 | tf_op jit(solution)/shard_map/ppermute | solution.py:306
  113.3 48.1 %collective-permute-start.22 = (bf16[2,128,1792]{2,1,0:T(8,128)(2,1)}, bf16[2,128,1792]{2,1,0:T(8,128)(2,1)}, u32[]{:S(2)}, u32[]{:S(2)}) collective-permute-start(bf16[2,128,1792]{2,1,0:T(8,128)(2,1)} %get-tuple-element.86), channel_id=1, source_target_pairs={{8,72},{24,88},{40,104},{56,120},{72,8},{88,24},{104,40},{120,56},... | collective-permute-start | bytes 2752520 | tf_op jit(solution)/shard_map/ppermute | solution.py:307
  172.1 12.5 %collective-permute-start.27 = (bf16[2,512,1792]{2,1,0:T(8,128)(2,1)}, bf16[2,512,1792]{2,1,0:T(8,128)(2,1)}, u32[]{:S(2)}, u32[]{:S(2)}) collective-permute-start(bf16[2,512,1792]{2,1,0:T(8,128)(2,1)} %get-tuple-element.94.refs_2_), channel_id=1, source_target_pairs={{0,8},{8,0},{16,24},{24,16},{32,40},{40,32},{48,56},{56,48},{64,72... | collective-permute-start | bytes 11010056 | tf_op jit(solution)/shard_map/ppermute | solution.py:319
  172.2 20.9 %collective-permute-start.23 = (bf16[2,128,1024]{2,1,0:T(8,128)(2,1)}, bf16[2,128,1024]{2,1,0:T(8,128)(2,1)S(1)}, u32[]{:S(2)}, u32[]{:S(2)}) collective-permute-start(bf16[2,128,1024]{2,1,0:T(8,128)(2,1)} %get-tuple-element.88), channel_id=1, source_target_pairs={{8,12},{9,13},{10,14},{11,15},{12,8},{13,9},{14,10},{15,11},{24,28... | collective-permute-start | bytes 1572872 | tf_op jit(solution)/shard_map/ppermute | solution.py:381
  174.1 19.0 %collective-permute-start.24 = (bf16[2,128,1024]{2,1,0:T(8,128)(2,1)}, bf16[2,128,1024]{2,1,0:T(8,128)(2,1)}, u32[]{:S(2)}, u32[]{:S(2)}) collective-permute-start(bf16[2,128,1024]{2,1,0:T(8,128)(2,1)} %get-tuple-element.89), channel_id=1, source_target_pairs={{0,1},{1,2},{2,3},{3,0},{4,5},{5,6},{6,7},{7,4},{8,13},{9,14},{10,... | collective-permute-start | bytes 1572872 | tf_op jit(solution)/shard_map/ppermute | solution.py:381
  174.2 18.9 %collective-permute-start.25 = (bf16[2,128,1024]{2,1,0:T(8,128)(2,1)}, bf16[2,128,1024]{2,1,0:T(8,128)(2,1)}, u32[]{:S(2)}, u32[]{:S(2)}) collective-permute-start(bf16[2,128,1024]{2,1,0:T(8,128)(2,1)} %get-tuple-element.90), channel_id=1, source_target_pairs={{0,2},{1,3},{2,0},{3,1},{4,6},{5,7},{6,4},{7,5},{8,14},{9,15},{10,... | collective-permute-start | bytes 1572872 | tf_op jit(solution)/shard_map/ppermute | solution.py:381
  174.3 23.1 %collective-permute-start.26 = (bf16[2,128,1024]{2,1,0:T(8,128)(2,1)}, bf16[2,128,1024]{2,1,0:T(8,128)(2,1)}, u32[]{:S(2)}, u32[]{:S(2)}) collective-permute-start(bf16[2,128,1024]{2,1,0:T(8,128)(2,1)} %get-tuple-element.91), channel_id=1, source_target_pairs={{0,3},{1,0},{2,1},{3,2},{4,7},{5,4},{6,5},{7,6},{8,15},{9,12},{10,... | collective-permute-start | bytes 1572872 | tf_op jit(solution)/shard_map/ppermute | solution.py:381
  (35 other events, 197.0 us)
Sparse Core Ops, SparseCore 0:
  101.9 44.9 all-gather.1

commit v11 on v10

--- a/solution.py
+++ b/solution.py
@@ -122,11 +122,6 @@
     chunk = (slice(at, end), slice(None)) if transposed else (slice(None), slice(at, end))
     own, other = [ref[chunk] for ref in pair]
     return product(held[:, :half], own, transposed) + product(held[:, half:], other, transposed)
-
-
-def mine_kernel(ins, outs):
-    for i in range(2):
-        outs[0][i] = ins[i][...]
 
 
 def block_kernel(ins, outs):
@@ -262,22 +257,28 @@
 
 def layer_kernel(ins, outs, held):
     hidden, *weights = ins
+    messages, kept = outs[:NZ], outs[NZ]
     core = Place().core
+    block = kept.shape[0]
     width = weights[0].shape[1]
     for piece in range(NY * NX):
         start = pl.multiple_of((piece * NC + core) * PIECE, PIECE)
         held[piece * PIECE : (piece + 1) * PIECE, :] = hidden[pl.ds(start, PIECE), :]
     for side, weight in enumerate(weights):
         for at, end in spans(width):
-            outs[0][:, side * width + at : side * width + end] = product(
-                held[...], weight[:, at:end], False
-            )
+            term = product(held[...], weight[:, at:end], False)
+            columns = slice(side * width + at, side * width + end)
+            kept[:, columns] = term[:block]
+            for k in range(NZ):
+                rows = term[k * block : (k + 1) * block]
+                messages[k][:, columns] = rows.astype(jnp.bfloat16)
 
 
 def input_kernel(ins, outs):
     place = Place()
-    layer, own, near1, near2, near3, far1, far2, far3 = ins[:8]
-    weights = ins[8:]
+    layer, layer_kept = ins[:NZ], ins[NZ]
+    own, near1, near2, near3, far1, far2, far3 = ins[NZ + 1 : NZ + 8]
+    weights = ins[NZ + 8 :]
     *messages, d_set, kept = outs
     core0 = place.core == 0
     pieces = place.gathered()
@@ -288,16 +289,31 @@
         d_set[:, rows_at, :] = value
     depth = weights[0].shape[0]
     block = NX * PIECE
+    kept[0] = layer_kept[...]
+    for k in range(NZ):
+        messages[k][0] = layer[k][...]
     for side in range(2):
         for at, end in spans(depth):
             gate, up = [weights[2 * side + i][at:end, :] for i in range(2)]
             total = product(d_set[0], gate, True) + product(d_set[1], up, True)
             columns = slice(side * depth + at, side * depth + end)
-            for i, term in enumerate((layer[:, columns], total)):
-                kept[i, :, columns] = term[:block]
-                for k in range(NZ):
-                    rows = term[k * block : (k + 1) * block]
-                    messages[k][i, :, columns] = rows.astype(jnp.bfloat16)
+            kept[1, :, columns] = total[:block]
+            for k in range(NZ):
+                rows = total[k * block : (k + 1) * block]
+                messages[k][1, :, columns] = rows.astype(jnp.bfloat16)
+
+
+def last_kernel(ins, outs):
+    kept, *messages = ins
+    own, away = outs
+    width = own.shape[2]
+    core0 = Place().core == 0
+    for i in range(2):
+        total = jnp.where(core0, kept[i], 0.0)
+        for message in messages:
+            total = total + message[i].astype(jnp.float32)
+        own[i] = total[:, :width]
+        away[i] = total[:, width:]
 
 
 def send_first(sent):
@@ -315,7 +331,6 @@
 
 
 def body(tokens, gate_weight, up_weight, down_weight, grad_output):
-    core = lax.axis_index("row") % NC
     flip = lambda value: lax.ppermute(value, "row", CORE_FLIP)
     after = lambda value, *others: lax.optimization_barrier((value, *others))[0]
     width, ff_width = gate_weight.shape
@@ -323,9 +338,10 @@
     rows = tokens.shape[0]
 
     tok_theirs, grad_theirs = flip(tokens), flip(grad_output)
-    (mine,) = call(mine_kernel, [tokens, grad_output], [shape((2, rows, width))])
     (own_block,) = call(
-        block_kernel, [mine, tok_theirs, grad_theirs], [shape((2, rows, 2 * width))]
+        block_kernel,
+        [jnp.stack([tokens, grad_output]), tok_theirs, grad_theirs],
+        [shape((2, rows, 2 * width))],
     )
     to_flip = lax.optimization_barrier((gate_weight, up_weight, down_weight, tok_theirs, grad_theirs))
     gate_other, up_other, down_other = [flip(weight) for weight in to_flip[:3]]
@@ -366,16 +382,16 @@
     packed = call(pack_kernel, [d_own, *near], [shape((2, 2 * PIECE, ff_width))] * 3)
     far = send_first(packed)
     hidden = after(hidden, far[0])
-    (layer,) = call(
+    layer = call(
         layer_kernel,
         [hidden, down_weight, down_other],
-        [shape((half_rows, 2 * width), jnp.float32)],
+        [shape((rows, 2 * width))] * NZ + [shape((rows, 2 * width), jnp.float32)],
         [pltpu.VMEM((half_rows, ff_width), jnp.bfloat16)],
     )
     block = (2, rows, 2 * width)
     *messages, d_set, kept = call(
         input_kernel,
-        [layer, d_own, *near, *far, gate_weight, up_weight, gate_other, up_other],
+        [*layer, d_own, *near, *far, gate_weight, up_weight, gate_other, up_other],
         [shape(block)] * 4 + [shape((2, half_rows, ff_width)), shape(block, jnp.float32)],
     )
     heard = {k: lax.ppermute(messages[k], BOTH, scatter_perm(k)) for k in (2, 1, 3, 0)}
@@ -390,10 +406,10 @@
     *messages, grad_gate, grad_up, grad_down = lax.optimization_barrier(
         (*messages, grad_gate, grad_up, grad_down)
     )
-    total = jnp.where(core == 0, kept, 0.0)
-    for message in messages:
-        total = total + message.astype(jnp.float32)
-    total = (total[:, :, :width] + flip(total[:, :, width:])).astype(jnp.bfloat16)
+    own, away = call(
+        last_kernel, [kept, *messages], [shape((2, rows, width), jnp.float32)] * 2
+    )
+    total = (own + flip(away)).astype(jnp.bfloat16)
     return (total[0], total[1], grad_gate, grad_up, grad_down)
 
 

time: 216 us -> 217 us (level)
  the two profiles are of different devices: /device:TPU:17 before, /device:TPU:5 now
where the time goes in v11:
time: 217 us
  waiting for transfers between devices  110 us (51%)
  starting transfers between devices  49.8 us (23%)
  Pallas kernels  28.3 us (13%)
  between operations  14.3 us (7%)
  local copies, waits for them, and re-layouts  13.9 us (6%)
    pallas_call x13, Pallas kernels, call(): pl.pallas_call(run, in_specs=[vmem] * n_in, out_specs=[vmem] * n_out, out...  28.3 us
    ppermute x2, waiting for transfers between devices, send_first(): lax.ppermute(sent[0], 'row', row_perm(over_x, over_y(1)))  26.2 us
    ppermute x4, waiting for transfers between devices, body(): lax.ppermute(messages[k], BOTH, scatter_perm(k))  19.9 us
    ppermute x4, starting transfers between devices, body(): lax.ppermute(messages[k], BOTH, scatter_perm(k))  17.6 us
    ppermute x2, waiting for transfers between devices, send_second(): first = lax.ppermute(sent[0], 'row', row_perm(over_y(1), over_x))  14.8 us
    ppermute x4, waiting for transfers between devices, body(): lax.ppermute(starts[step], BOTH, gather_perm(step))  13.8 us
    unnamed x50, local copies, waits for them, and re-layouts  13.2 us
    ppermute x2, waiting for transfers between devices, send_first(): lax.ppermute(sent[1], 'row', row_perm(over_x, over_y(-1)))  13 us
  transfers between devices with their start and end apart: 30, of which 19 were waited for; matrix products, arithmetic and copies ran while one was open for 0% of the time, Pallas kernels for 7%

profile of v11, /device:TPU:5, one launch (start us, length us, event | category | flops | bytes accessed | tf_op | source)
XLA Modules:
  0.0 217.0 jit_solution(13686460707486080205)
XLA Ops:
  12.9 3.5 %collective-permute-start.4 = (bf16[2,128,1024]{2,1,0:T(8,128)(2,1)S(1)}, bf16[2,128,1024]{2,1,0:T(8,128)(2,1)S(1)}, u32[]{:S(2)}, u32[]{:S(2)}) collective-permute-start(bf16[2,128,1024]{2,1,0:T(8,128)(2,1)S(1)} %shard_map.92.refs_0_), channel_id=1, source_target_pairs={{1,0},{2,1},{3,2},{0,3},{5,4},{6,5},{7,6},{4,7},{13,8},{14,9},{15,... | collective-permute-start | bytes 1572872 | tf_op jit(solution)/shard_map/ppermute | solution.py:353
  21.3 3.4 %collective-permute-start.3 = (bf16[2,128,1024]{2,1,0:T(8,128)(2,1)S(1)}, bf16[2,128,1024]{2,1,0:T(8,128)(2,1)S(1)}, u32[]{:S(2)}, u32[]{:S(2)}) collective-permute-start(bf16[2,128,1024]{2,1,0:T(8,128)(2,1)S(1)} %shard_map.92.refs_0_), channel_id=1, source_target_pairs={{12,8},{13,9},{14,10},{15,11},{8,12},{9,13},{10,14},{11,15},{28,24... | collective-permute-start | bytes 1572872 | tf_op jit(solution)/shard_map/ppermute | solution.py:353
  24.7 3.7 %collective-permute-start.6 = (bf16[2,128,1024]{2,1,0:T(8,128)(2,1)S(1)}, bf16[2,128,1024]{2,1,0:T(8,128)(2,1)S(1)}, u32[]{:S(2)}, u32[]{:S(2)}) collective-permute-start(bf16[2,128,1024]{2,1,0:T(8,128)(2,1)S(1)} %shard_map.92.refs_0_), channel_id=1, source_target_pairs={{2,0},{3,1},{0,2},{1,3},{6,4},{7,5},{4,6},{5,7},{14,8},{15,9},{12,... | collective-permute-start | bytes 1572872 | tf_op jit(solution)/shard_map/ppermute | solution.py:353
  29.3 4.5 %collective-permute-done.3.refs_1_ = bf16[2,128,1024]{2,1,0:T(8,128)(2,1)S(1)} collective-permute-done((bf16[2,128,1024]{2,1,0:T(8,128)(2,1)S(1)}, bf16[2,128,1024]{2,1,0:T(8,128)(2,1)S(1)}, u32[]{:S(2)}, u32[]{:S(2)}) %collective-permute-start.3) | collective-permute-done | bytes 524320 | tf_op jit(solution)/shard_map/ppermute | solution.py:353
  33.9 8.3 %collective-permute-done.6.refs_3_ = bf16[2,128,1024]{2,1,0:T(8,128)(2,1)S(1)} collective-permute-done((bf16[2,128,1024]{2,1,0:T(8,128)(2,1)S(1)}, bf16[2,128,1024]{2,1,0:T(8,128)(2,1)S(1)}, u32[]{:S(2)}, u32[]{:S(2)}) %collective-permute-start.6) | collective-permute-done | bytes 524320 | tf_op jit(solution)/shard_map/ppermute | solution.py:353
  42.1 4.5 %shard_map.94 = (bf16[512,1024]{1,0:T(8,128)(2,1)S(1)}, bf16[512,1024]{1,0:T(8,128)(2,1)S(1)}, bf16[3,128,1792]{2,1,0:T(8,128)(2,1)S(1)}, bf16[3,128,1792]{2,1,0:T(8,128)(2,1)S(1)}, bf16[3,128,1792]{2,1,0:T(8,128)(2,1)S(1)}) custom-call(bf16[2,128,1024]{2,1,0:T(8,128)(2,1)S(1)} %shard_map.92.refs_0_, ...), custom_call_target="tpu_custom_call" | custom-call | flops 1 | bytes 1 | tf_op jit(solution)/shard_map/pallas_call | solution.py:78
  49.6 3.5 %collective-permute-start.11 = (bf16[3,128,1792]{2,1,0:T(8,128)(2,1)S(1)}, bf16[3,128,1792]{2,1,0:T(8,128)(2,1)S(1)}, u32[]{:S(2)}, u32[]{:S(2)}) collective-permute-start(bf16[3,128,1792]{2,1,0:T(8,128)(2,1)S(1)} %get-tuple-element.78), channel_id=1, source_target_pairs={{8,72},{24,88},{40,104},{56,120},{72,8},{88,24},{104,40},{120,56},... | collective-permute-start | bytes 4128776 | tf_op jit(solution)/shard_map/ppermute | solution.py:323
  53.1 3.1 %shard_map.95 = (f32[3,256,1792]{2,1,0:T(8,128)S(1)}, bf16[512,512]{1,0:T(8,128)(2,1)S(1)}, bf16[512,512]{1,0:T(8,128)(2,1)S(1)}, bf16[512,512]{1,0:T(8,128)(2,1)S(1)}, bf16[512,512]{1,0:T(8,128)(2,1)S(1)}) custom-call(bf16[512,1024]{1,0:T(8,128)(2,1)S(1)} %get-tuple-element.73.refs_0_, bf16[512,1024]{1,0:T(8,128)(2,1)S(1)} %get-tuple-element.74.refs_1_, ...), custom_call_target="tpu_custom_call" | custom-call | flops 1 | bytes 1 | tf_op jit(solution)/shard_map/pallas_call | solution.py:78
  58.9 6.3 %collective-permute-done.9.refs_1_ = bf16[3,128,1792]{2,1,0:T(8,128)(2,1)S(1)} collective-permute-done((bf16[3,128,1792]{2,1,0:T(8,128)(2,1)S(1)}, bf16[3,128,1792]{2,1,0:T(8,128)(2,1)S(1)}, u32[]{:S(2)}, u32[]{:S(2)}) %collective-permute-start.9) | collective-permute-done | bytes 1376288 | tf_op jit(solution)/shard_map/ppermute | solution.py:321
  65.2 13.0 %collective-permute-done.10.refs_2_ = bf16[3,128,1792]{2,1,0:T(8,128)(2,1)S(1)} collective-permute-done((bf16[3,128,1792]{2,1,0:T(8,128)(2,1)S(1)}, bf16[3,128,1792]{2,1,0:T(8,128)(2,1)S(1)}, u32[]{:S(2)}, u32[]{:S(2)}) %collective-permute-start.10) | collective-permute-done | bytes 1376288 | tf_op jit(solution)/shard_map/ppermute | solution.py:322
  78.2 4.6 %collective-permute-done.11.refs_3_ = bf16[3,128,1792]{2,1,0:T(8,128)(2,1)S(1)} collective-permute-done((bf16[3,128,1792]{2,1,0:T(8,128)(2,1)S(1)}, bf16[3,128,1792]{2,1,0:T(8,128)(2,1)S(1)}, u32[]{:S(2)}, u32[]{:S(2)}) %collective-permute-start.11) | collective-permute-done | bytes 1376288 | tf_op jit(solution)/shard_map/ppermute | solution.py:323
  85.8 7.9 %collective-permute-done.14.refs_4_ = bf16[3,64,1792]{2,1,0:T(8,128)(2,1)S(1)} collective-permute-done((bf16[3,64,1792]{2,1,0:T(8,128)(2,1)S(1)}, bf16[3,64,1792]{2,1,0:T(8,128)(2,1)S(1)}, u32[]{:S(2)}, u32[]{:S(2)}) %collective-permute-start.14) | collective-permute-done | bytes 688160 | tf_op jit(solution)/shard_map/ppermute | solution.py:329
  93.7 7.1 %collective-permute-done.15.refs_5_ = bf16[3,64,1792]{2,1,0:T(8,128)(2,1)S(1)} collective-permute-done((bf16[3,64,1792]{2,1,0:T(8,128)(2,1)S(1)}, bf16[3,64,1792]{2,1,0:T(8,128)(2,1)S(1)}, u32[]{:S(2)}, u32[]{:S(2)}) %collective-permute-start.15) | collective-permute-done | bytes 688160 | tf_op jit(solution)/shard_map/ppermute | solution.py:330
  104.7 6.9 %collective-permute-done.17.refs_1_.refs_6_ = bf16[2,64,1792]{2,1,0:T(8,128)(2,1)S(1)} collective-permute-done((bf16[2,64,1792]{2,1,0:T(8,128)(2,1)S(1)}, bf16[2,64,1792]{2,1,0:T(8,128)(2,1)S(1)}, u32[]{:S(2)}, u32[]{:S(2)}) %collective-permute-start.17) | collective-permute-done | bytes 458784 | tf_op jit(solution)/shard_map/ppermute | solution.py:329
  114.3 2.3 %collective-permute-start.21 = (bf16[2,128,1792]{2,1,0:T(8,128)(2,1)}, bf16[2,128,1792]{2,1,0:T(8,128)(2,1)}, u32[]{:S(2)}, u32[]{:S(2)}) collective-permute-start(bf16[2,128,1792]{2,1,0:T(8,128)(2,1)} %get-tuple-element.97), channel_id=1, source_target_pairs={{0,16},{8,104},{16,0},{24,120},{32,48},{40,8},{48,32},{56,24},{64,... | collective-permute-start | bytes 2752520 | tf_op jit(solution)/shard_map/ppermute | solution.py:322
  118.5 20.0 %collective-permute-done.20.refs_9_ = bf16[2,128,1792]{2,1,0:T(8,128)(2,1)S(1)} collective-permute-done((bf16[2,128,1792]{2,1,0:T(8,128)(2,1)S(1)}, bf16[2,128,1792]{2,1,0:T(8,128)(2,1)S(1)}, u32[]{:S(2)}, u32[]{:S(2)}) %collective-permute-start.20) | collective-permute-done | bytes 917536 | tf_op jit(solution)/shard_map/ppermute | solution.py:321
  148.4 2.8 %collective-permute-done.22.refs_11_ = bf16[2,128,1792]{2,1,0:T(8,128)(2,1)} collective-permute-done((bf16[2,128,1792]{2,1,0:T(8,128)(2,1)}, bf16[2,128,1792]{2,1,0:T(8,128)(2,1)}, u32[]{:S(2)}, u32[]{:S(2)}) %collective-permute-start.22) | collective-permute-done | bytes 917536 | tf_op jit(solution)/shard_map/ppermute | solution.py:323
  152.4 6.1 %shard_map.101 = (bf16[2,128,1024]{2,1,0:T(8,128)(2,1)S(1)}, bf16[2,128,1024]{2,1,0:T(8,128)(2,1)S(1)}, bf16[2,128,1024]{2,1,0:T(8,128)(2,1)S(1)}, bf16[2,128,10...) custom-call(bf16[128,1024]{1,0:T(8,128)(2,1)S(1)} %get-tuple-element.92.refs_0_, ...), custom_call_target="tpu_custom_call" | custom-call | flops 1 | bytes 1 | tf_op jit(solution)/shard_map/pallas_call | solution.py:78
  162.6 13.3 %collective-permute-start.24 = (bf16[2,128,1024]{2,1,0:T(8,128)(2,1)S(1)}, bf16[2,128,1024]{2,1,0:T(8,128)(2,1)S(1)}, u32[]{:S(2)}, u32[]{:S(2)}) collective-permute-start(bf16[2,128,1024]{2,1,0:T(8,128)(2,1)S(1)} %get-tuple-element.101), channel_id=1, source_target_pairs={{0,1},{1,2},{2,3},{3,0},{4,5},{5,6},{6,7},{7,4},{8,13},{9,14},{10,... | collective-permute-start | bytes 1572872 | tf_op jit(solution)/shard_map/ppermute | solution.py:397
  175.9 2.4 %collective-permute-start.26 = (bf16[2,128,1024]{2,1,0:T(8,128)(2,1)S(1)}, bf16[2,128,1024]{2,1,0:T(8,128)(2,1)S(1)}, u32[]{:S(2)}, u32[]{:S(2)}) collective-permute-start(bf16[2,128,1024]{2,1,0:T(8,128)(2,1)S(1)} %get-tuple-element.103), channel_id=1, source_target_pairs={{0,3},{1,0},{2,1},{3,2},{4,7},{5,4},{6,5},{7,6},{8,15},{9,12},{10,... | collective-permute-start | bytes 1572872 | tf_op jit(solution)/shard_map/ppermute | solution.py:397
  178.3 3.3 %shard_map.103 = bf16[1792,512]{1,0:T(8,128)(2,1)} custom-call(bf16[1024,1792]{1,0:T(8,128)(2,1)S(1)} %copy-done.5, bf16[1024,512]{1,0:T(8,128)(2,1)S(1)} %shard_map.96.refs_1_), custom_call_target="tpu_custom_call" | custom-call | flops 1 | bytes 1 | tf_op jit(solution)/shard_map/pallas_call | solution.py:78
  181.7 5.5 %shard_map.102 = (bf16[512,1792]{1,0:T(8,128)(2,1)}, bf16[512,1792]{1,0:T(8,128)(2,1)}) custom-call(bf16[512,512]{1,0:T(8,128)(2,1)S(1)} %copy-done.21, bf16[512,512]{1,0:T(8,128)(2,1)S(1)} %copy-done.23, bf16[2,512,1792]{2,1,0:T(8,128)(2,1)S(1)} %get-tuple-element.106.refs_2_, bf16[2,512,1792]{2,1,0:T(8,128)(2,1)S(1)} %collective-permute-done.27.refs_3_), custom_call_target="tpu_custom_call" | custom-call | flops 1 | bytes 1 | tf_op jit(solution)/shard_map/pallas_call | solution.py:78
  187.1 3.0 %collective-permute-done.25.refs_3_ = bf16[2,128,1024]{2,1,0:T(8,128)(2,1)S(1)} collective-permute-done((bf16[2,128,1024]{2,1,0:T(8,128)(2,1)S(1)}, bf16[2,128,1024]{2,1,0:T(8,128)(2,1)S(1)}, u32[]{:S(2)}, u32[]{:S(2)}) %collective-permute-start.25) | collective-permute-done | bytes 524320 | tf_op jit(solution)/shard_map/ppermute | solution.py:397
  190.1 17.0 %collective-permute-done.26.refs_4_ = bf16[2,128,1024]{2,1,0:T(8,128)(2,1)S(1)} collective-permute-done((bf16[2,128,1024]{2,1,0:T(8,128)(2,1)S(1)}, bf16[2,128,1024]{2,1,0:T(8,128)(2,1)S(1)}, u32[]{:S(2)}, u32[]{:S(2)}) %collective-permute-start.26) | collective-permute-done | bytes 524320 | tf_op jit(solution)/shard_map/ppermute | solution.py:397
  (103 shorter events, 46.9 us)
Async XLA Ops:
  7.2 134.1 %all-gather.2.cloned.1.call-start = ((), (), s32[]{:S(2)}) async-start(), calls=%async_computation | async-start | bytes 3899392 | tf_op jit(solution)/shard_map/all_gather | solution.py:379
  9.5 11.7 %collective-permute-start.5 = (bf16[512,1792]{1,0:T(8,128)(2,1)}, bf16[512,1792]{1,0:T(8,128)(2,1)S(1)}, u32[]{:S(2)}, u32[]{:S(2)}) collective-permute-start(bf16[512,1792]{1,0:T(8,128)(2,1)} %refs_12_.1), channel_id=1, source_target_pairs={{0,8},{8,0},{16,24},{24,16},{32,40},{40,32},{48,56},{56,48},{64,72... | collective-permute-start | bytes 5505032 | tf_op jit(solution)/shard_map/ppermute | solution.py:334
  9.7 11.6 %collective-permute-start.2 = (bf16[512,1792]{1,0:T(8,128)(2,1)}, bf16[512,1792]{1,0:T(8,128)(2,1)S(1)}, u32[]{:S(2)}, u32[]{:S(2)}) collective-permute-start(bf16[512,1792]{1,0:T(8,128)(2,1)} %refs_13_.1), channel_id=1, source_target_pairs={{0,8},{8,0},{16,24},{24,16},{32,40},{40,32},{48,56},{56,48},{64,72... | collective-permute-start | bytes 5505032 | tf_op jit(solution)/shard_map/ppermute | solution.py:334
  10.0 19.3 %collective-permute-start.8 = (bf16[1792,512]{1,0:T(8,128)(2,1)}, bf16[1792,512]{1,0:T(8,128)(2,1)S(1)}, u32[]{:S(2)}, u32[]{:S(2)}) collective-permute-start(bf16[1792,512]{1,0:T(8,128)(2,1)} %refs_1_.2), channel_id=1, source_target_pairs={{0,8},{8,0},{16,24},{24,16},{32,40},{40,32},{48,56},{56,48},{64,72... | collective-permute-start | bytes 5505032 | tf_op jit(solution)/shard_map/ppermute | solution.py:334
  11.3 17.1 %collective-permute-start.7 = (bf16[2,128,1024]{2,1,0:T(8,128)(2,1)S(1)}, bf16[2,128,1024]{2,1,0:T(8,128)(2,1)S(1)}, u32[]{:S(2)}, u32[]{:S(2)}) collective-permute-start(bf16[2,128,1024]{2,1,0:T(8,128)(2,1)S(1)} %shard_map.92.refs_0_), channel_id=1, source_target_pairs={{3,0},{0,1},{1,2},{2,3},{7,4},{4,5},{5,6},{6,7},{15,8},{12,9},{13,... | collective-permute-start | bytes 1572872 | tf_op jit(solution)/shard_map/ppermute | solution.py:353
  12.9 16.4 %collective-permute-start.4 = (bf16[2,128,1024]{2,1,0:T(8,128)(2,1)S(1)}, bf16[2,128,1024]{2,1,0:T(8,128)(2,1)S(1)}, u32[]{:S(2)}, u32[]{:S(2)}) collective-permute-start(bf16[2,128,1024]{2,1,0:T(8,128)(2,1)S(1)} %shard_map.92.refs_0_), channel_id=1, source_target_pairs={{1,0},{2,1},{3,2},{0,3},{5,4},{6,5},{7,6},{4,7},{13,8},{14,9},{15,... | collective-permute-start | bytes 1572872 | tf_op jit(solution)/shard_map/ppermute | solution.py:353
  21.3 12.6 %collective-permute-start.3 = (bf16[2,128,1024]{2,1,0:T(8,128)(2,1)S(1)}, bf16[2,128,1024]{2,1,0:T(8,128)(2,1)S(1)}, u32[]{:S(2)}, u32[]{:S(2)}) collective-permute-start(bf16[2,128,1024]{2,1,0:T(8,128)(2,1)S(1)} %shard_map.92.refs_0_), channel_id=1, source_target_pairs={{12,8},{13,9},{14,10},{15,11},{8,12},{9,13},{10,14},{11,15},{28,24... | collective-permute-start | bytes 1572872 | tf_op jit(solution)/shard_map/ppermute | solution.py:353
  24.7 17.5 %collective-permute-start.6 = (bf16[2,128,1024]{2,1,0:T(8,128)(2,1)S(1)}, bf16[2,128,1024]{2,1,0:T(8,128)(2,1)S(1)}, u32[]{:S(2)}, u32[]{:S(2)}) collective-permute-start(bf16[2,128,1024]{2,1,0:T(8,128)(2,1)S(1)} %shard_map.92.refs_0_), channel_id=1, source_target_pairs={{2,0},{3,1},{0,2},{1,3},{6,4},{7,5},{4,6},{5,7},{14,8},{15,9},{12,... | collective-permute-start | bytes 1572872 | tf_op jit(solution)/shard_map/ppermute | solution.py:353
  46.7 18.5 %collective-permute-start.9 = (bf16[3,128,1792]{2,1,0:T(8,128)(2,1)S(1)}, bf16[3,128,1792]{2,1,0:T(8,128)(2,1)S(1)}, u32[]{:S(2)}, u32[]{:S(2)}) collective-permute-start(bf16[3,128,1792]{2,1,0:T(8,128)(2,1)S(1)} %get-tuple-element.76), channel_id=1, source_target_pairs={{0,16},{8,40},{16,0},{24,56},{32,48},{40,72},{48,32},{56,88},{64,8... | collective-permute-start | bytes 4128776 | tf_op jit(solution)/shard_map/ppermute | solution.py:321
  48.1 30.2 %collective-permute-start.10 = (bf16[3,128,1792]{2,1,0:T(8,128)(2,1)S(1)}, bf16[3,128,1792]{2,1,0:T(8,128)(2,1)S(1)}, u32[]{:S(2)}, u32[]{:S(2)}) collective-permute-start(bf16[3,128,1792]{2,1,0:T(8,128)(2,1)S(1)} %get-tuple-element.77), channel_id=1, source_target_pairs={{0,16},{8,104},{16,0},{24,120},{32,48},{40,8},{48,32},{56,24},{64,... | collective-permute-start | bytes 4128776 | tf_op jit(solution)/shard_map/ppermute | solution.py:322
  49.6 33.3 %collective-permute-start.11 = (bf16[3,128,1792]{2,1,0:T(8,128)(2,1)S(1)}, bf16[3,128,1792]{2,1,0:T(8,128)(2,1)S(1)}, u32[]{:S(2)}, u32[]{:S(2)}) collective-permute-start(bf16[3,128,1792]{2,1,0:T(8,128)(2,1)S(1)} %get-tuple-element.78), channel_id=1, source_target_pairs={{8,72},{24,88},{40,104},{56,120},{72,8},{88,24},{104,40},{120,56},... | collective-permute-start | bytes 4128776 | tf_op jit(solution)/shard_map/ppermute | solution.py:323
  56.3 2.6 %collective-permute-start.13 = (bf16[512,512]{1,0:T(8,128)(2,1)S(1)}, bf16[512,512]{1,0:T(8,128)(2,1)S(1)}, u32[]{:S(2)}, u32[]{:S(2)}) collective-permute-start(bf16[512,512]{1,0:T(8,128)(2,1)S(1)} %get-tuple-element.81), channel_id=1, source_target_pairs={{0,8},{8,0},{16,24},{24,16},{32,40},{40,32},{48,56},{56,48},{64,72... | collective-permute-start | bytes 1572872 | tf_op jit(solution)/shard_map/ppermute | solution.py:334
  83.6 10.2 %collective-permute-start.14 = (bf16[3,64,1792]{2,1,0:T(8,128)(2,1)S(1)}, bf16[3,64,1792]{2,1,0:T(8,128)(2,1)S(1)}, u32[]{:S(2)}, u32[]{:S(2)}) collective-permute-start(bf16[3,64,1792]{2,1,0:T(8,128)(2,1)S(1)} %get-tuple-element.85), channel_id=1, source_target_pairs={{0,32},{8,24},{16,48},{24,8},{32,64},{40,56},{48,80},{56,40},{64,9... | collective-permute-start | bytes 2064392 | tf_op jit(solution)/shard_map/ppermute | solution.py:329
  84.5 16.3 %collective-permute-start.15 = (bf16[3,64,1792]{2,1,0:T(8,128)(2,1)S(1)}, bf16[3,64,1792]{2,1,0:T(8,128)(2,1)S(1)}, u32[]{:S(2)}, u32[]{:S(2)}) collective-permute-start(bf16[3,64,1792]{2,1,0:T(8,128)(2,1)S(1)} %get-tuple-element.86), channel_id=1, source_target_pairs={{0,96},{8,24},{16,112},{24,8},{32,0},{40,56},{48,16},{56,40},{64,3... | collective-permute-start | bytes 2064392 | tf_op jit(solution)/shard_map/ppermute | solution.py:330
  85.1 15.7 %collective-permute-start.16 = (bf16[3,64,1792]{2,1,0:T(8,128)(2,1)S(1)}, bf16[3,64,1792]{2,1,0:T(8,128)(2,1)S(1)}, u32[]{:S(2)}, u32[]{:S(2)}) collective-permute-start(bf16[3,64,1792]{2,1,0:T(8,128)(2,1)S(1)} %get-tuple-element.87), channel_id=1, source_target_pairs={{0,64},{16,80},{32,96},{48,112},{64,0},{80,16},{96,32},{112,48},{1... | collective-permute-start | bytes 2064392 | tf_op jit(solution)/shard_map/ppermute | solution.py:328
  103.7 7.9 %collective-permute-start.17 = (bf16[2,64,1792]{2,1,0:T(8,128)(2,1)S(1)}, bf16[2,64,1792]{2,1,0:T(8,128)(2,1)S(1)}, u32[]{:S(2)}, u32[]{:S(2)}) collective-permute-start(bf16[2,64,1792]{2,1,0:T(8,128)(2,1)S(1)} %get-tuple-element.89.refs_0_.refs_5_), channel_id=1, source_target_pairs={{0,32},{8,24},{16,48},{24,8},{32,64},{40,56},{48,80},{56,40},{64,9... | collective-permute-start | bytes 1376264 | tf_op jit(solution)/shard_map/ppermute | solution.py:329
  113.9 24.6 %collective-permute-start.20 = (bf16[2,128,1792]{2,1,0:T(8,128)(2,1)S(1)}, bf16[2,128,1792]{2,1,0:T(8,128)(2,1)S(1)}, u32[]{:S(2)}, u32[]{:S(2)}) collective-permute-start(bf16[2,128,1792]{2,1,0:T(8,128)(2,1)S(1)} %get-tuple-element.90), channel_id=1, source_target_pairs={{0,16},{8,40},{16,0},{24,56},{32,48},{40,72},{48,32},{56,88},{64,8... | collective-permute-start | bytes 2752520 | tf_op jit(solution)/shard_map/ppermute | solution.py:321
  114.3 34.1 %collective-permute-start.21 = (bf16[2,128,1792]{2,1,0:T(8,128)(2,1)}, bf16[2,128,1792]{2,1,0:T(8,128)(2,1)}, u32[]{:S(2)}, u32[]{:S(2)}) collective-permute-start(bf16[2,128,1792]{2,1,0:T(8,128)(2,1)} %get-tuple-element.97), channel_id=1, source_target_pairs={{0,16},{8,104},{16,0},{24,120},{32,48},{40,8},{48,32},{56,24},{64,... | collective-permute-start | bytes 2752520 | tf_op jit(solution)/shard_map/ppermute | solution.py:322
  116.6 34.6 %collective-permute-start.22 = (bf16[2,128,1792]{2,1,0:T(8,128)(2,1)}, bf16[2,128,1792]{2,1,0:T(8,128)(2,1)}, u32[]{:S(2)}, u32[]{:S(2)}) collective-permute-start(bf16[2,128,1792]{2,1,0:T(8,128)(2,1)} %get-tuple-element.98), channel_id=1, source_target_pairs={{8,72},{24,88},{40,104},{56,120},{72,8},{88,24},{104,40},{120,56},... | collective-permute-start | bytes 2752520 | tf_op jit(solution)/shard_map/ppermute | solution.py:323
  158.4 23.2 %collective-permute-start.27 = (bf16[2,512,1792]{2,1,0:T(8,128)(2,1)S(1)}, bf16[2,512,1792]{2,1,0:T(8,128)(2,1)S(1)}, u32[]{:S(2)}, u32[]{:S(2)}) collective-permute-start(bf16[2,512,1792]{2,1,0:T(8,128)(2,1)S(1)} %get-tuple-element.106.refs_2_), channel_id=1, source_target_pairs={{0,8},{8,0},{16,24},{24,16},{32,40},{40,32},{48,56},{56,48},{64,72... | collective-permute-start | bytes 11010056 | tf_op jit(solution)/shard_map/ppermute | solution.py:334
  160.7 26.4 %collective-permute-start.23 = (bf16[2,128,1024]{2,1,0:T(8,128)(2,1)S(1)}, bf16[2,128,1024]{2,1,0:T(8,128)(2,1)S(1)}, u32[]{:S(2)}, u32[]{:S(2)}) collective-permute-start(bf16[2,128,1024]{2,1,0:T(8,128)(2,1)S(1)} %get-tuple-element.100), channel_id=1, source_target_pairs={{8,12},{9,13},{10,14},{11,15},{12,8},{13,9},{14,10},{15,11},{24,28... | collective-permute-start | bytes 1572872 | tf_op jit(solution)/shard_map/ppermute | solution.py:397
  162.6 24.5 %collective-permute-start.24 = (bf16[2,128,1024]{2,1,0:T(8,128)(2,1)S(1)}, bf16[2,128,1024]{2,1,0:T(8,128)(2,1)S(1)}, u32[]{:S(2)}, u32[]{:S(2)}) collective-permute-start(bf16[2,128,1024]{2,1,0:T(8,128)(2,1)S(1)} %get-tuple-element.101), channel_id=1, source_target_pairs={{0,1},{1,2},{2,3},{3,0},{4,5},{5,6},{6,7},{7,4},{8,13},{9,14},{10,... | collective-permute-start | bytes 1572872 | tf_op jit(solution)/shard_map/ppermute | solution.py:397
  175.9 14.2 %collective-permute-start.25 = (bf16[2,128,1024]{2,1,0:T(8,128)(2,1)S(1)}, bf16[2,128,1024]{2,1,0:T(8,128)(2,1)S(1)}, u32[]{:S(2)}, u32[]{:S(2)}) collective-permute-start(bf16[2,128,1024]{2,1,0:T(8,128)(2,1)S(1)} %get-tuple-element.102), channel_id=1, source_target_pairs={{0,2},{1,3},{2,0},{3,1},{4,6},{5,7},{6,4},{7,5},{8,14},{9,15},{10,... | collective-permute-start | bytes 1572872 | tf_op jit(solution)/shard_map/ppermute | solution.py:397
  175.9 31.1 %collective-permute-start.26 = (bf16[2,128,1024]{2,1,0:T(8,128)(2,1)S(1)}, bf16[2,128,1024]{2,1,0:T(8,128)(2,1)S(1)}, u32[]{:S(2)}, u32[]{:S(2)}) collective-permute-start(bf16[2,128,1024]{2,1,0:T(8,128)(2,1)S(1)} %get-tuple-element.103), channel_id=1, source_target_pairs={{0,3},{1,0},{2,1},{3,2},{4,7},{5,4},{6,5},{7,6},{8,15},{9,12},{10,... | collective-permute-start | bytes 1572872 | tf_op jit(solution)/shard_map/ppermute | solution.py:397
  (31 other events, 209.6 us)
Sparse Core Ops, SparseCore 0:
  102.4 38.7 all-gather.1

commit v12 on v11

--- a/solution.py
+++ b/solution.py
@@ -303,19 +303,6 @@
                 messages[k][1, :, columns] = rows.astype(jnp.bfloat16)
 
 
-def last_kernel(ins, outs):
-    kept, *messages = ins
-    own, away = outs
-    width = own.shape[2]
-    core0 = Place().core == 0
-    for i in range(2):
-        total = jnp.where(core0, kept[i], 0.0)
-        for message in messages:
-            total = total + message[i].astype(jnp.float32)
-        own[i] = total[:, :width]
-        away[i] = total[:, width:]
-
-
 def send_first(sent):
     return (
         lax.ppermute(sent[0], "row", row_perm(over_x, over_y(1))),
@@ -378,7 +365,7 @@
     )
     hidden = lax.all_gather(hidden, "row", axis=0, tiled=True)
 
-    near = send_second([d_own] * 3, None)
+    near = send_second([d_own] * 3)
     packed = call(pack_kernel, [d_own, *near], [shape((2, 2 * PIECE, ff_width))] * 3)
     far = send_first(packed)
     hidden = after(hidden, far[0])
@@ -406,10 +393,10 @@
     *messages, grad_gate, grad_up, grad_down = lax.optimization_barrier(
         (*messages, grad_gate, grad_up, grad_down)
     )
-    own, away = call(
-        last_kernel, [kept, *messages], [shape((2, rows, width), jnp.float32)] * 2
-    )
-    total = (own + flip(away)).astype(jnp.bfloat16)
+    total = jnp.where(lax.axis_index("row") % NC == 0, kept, 0.0)
+    for message in messages:
+        total = total + message.astype(jnp.float32)
+    total = (total[:, :, :width] + flip(total[:, :, width:])).astype(jnp.bfloat16)
     return (total[0], total[1], grad_gate, grad_up, grad_down)
 
 

time: 217 us -> 216 us (level)
  the two profiles are of different devices: /device:TPU:5 before, /device:TPU:17 now
where the time goes in v12:
time: 216 us
  waiting for transfers between devices  93.5 us (43%)
  starting transfers between devices  54.7 us (25%)
  Pallas kernels  33.3 us (15%)
  local copies, waits for them, and re-layouts  16.9 us (8%)
  between operations  14.4 us (7%)
  other arithmetic  2.85 us (1%)
    pallas_call x12, Pallas kernels, call(): pl.pallas_call(run, in_specs=[vmem] * n_in, out_specs=[vmem] * n_out, out...  33.3 us
    ppermute x2, waiting for transfers between devices, send_first(): lax.ppermute(sent[0], 'row', row_perm(over_x, over_y(1)))  30.5 us
    ppermute x4, starting transfers between devices, body(): lax.ppermute(messages[k], BOTH, scatter_perm(k))  18.7 us
    unnamed x54, local copies, waits for them, and re-layouts  16.2 us
    ppermute x2, waiting for transfers between devices, send_second(): first = lax.ppermute(sent[0], 'row', row_perm(over_y(1), over_x))  13.3 us
    ppermute x4, waiting for transfers between devices, body(): lax.ppermute(starts[step], BOTH, gather_perm(step))  13 us
    ppermute x2, starting transfers between devices, send_first(): lax.ppermute(sent[2], 'row', row_perm(None, over_y(2)))  12.8 us
    ppermute x4, starting transfers between devices, body(): lax.ppermute(starts[step], BOTH, gather_perm(step))  12.2 us
  transfers between devices with their start and end apart: 30, of which 18 were waited for; matrix products, arithmetic and copies ran while one was open for 0% of the time, Pallas kernels for 9%

profile of v12, /device:TPU:17, one launch (start us, length us, event | category | flops | bytes accessed | tf_op | source)
XLA Modules:
  0.0 215.5 jit_solution(10461631801068162882)
XLA Ops:
  11.3 6.3 %collective-permute-start.4 = (bf16[2,128,1024]{2,1,0:T(8,128)(2,1)S(1)}, bf16[2,128,1024]{2,1,0:T(8,128)(2,1)S(1)}, u32[]{:S(2)}, u32[]{:S(2)}) collective-permute-start(bf16[2,128,1024]{2,1,0:T(8,128)(2,1)S(1)} %shard_map.92.refs_0_), channel_id=1, source_target_pairs={{1,0},{2,1},{3,2},{0,3},{5,4},{6,5},{7,6},{4,7},{13,8},{14,9},{15,... | collective-permute-start | bytes 1572872 | tf_op jit(solution)/shard_map/ppermute | solution.py:340
  22.4 3.8 %collective-permute-start.6 = (bf16[2,128,1024]{2,1,0:T(8,128)(2,1)S(1)}, bf16[2,128,1024]{2,1,0:T(8,128)(2,1)S(1)}, u32[]{:S(2)}, u32[]{:S(2)}) collective-permute-start(bf16[2,128,1024]{2,1,0:T(8,128)(2,1)S(1)} %shard_map.92.refs_0_), channel_id=1, source_target_pairs={{2,0},{3,1},{0,2},{1,3},{6,4},{7,5},{4,6},{5,7},{14,8},{15,9},{12,... | collective-permute-start | bytes 1572872 | tf_op jit(solution)/shard_map/ppermute | solution.py:340
  30.3 5.3 %collective-permute-done.6.refs_3_ = bf16[2,128,1024]{2,1,0:T(8,128)(2,1)S(1)} collective-permute-done((bf16[2,128,1024]{2,1,0:T(8,128)(2,1)S(1)}, bf16[2,128,1024]{2,1,0:T(8,128)(2,1)S(1)}, u32[]{:S(2)}, u32[]{:S(2)}) %collective-permute-start.6) | collective-permute-done | bytes 524320 | tf_op jit(solution)/shard_map/ppermute | solution.py:340
  35.6 5.8 %collective-permute-done.3.refs_1_ = bf16[2,128,1024]{2,1,0:T(8,128)(2,1)S(1)} collective-permute-done((bf16[2,128,1024]{2,1,0:T(8,128)(2,1)S(1)}, bf16[2,128,1024]{2,1,0:T(8,128)(2,1)S(1)}, u32[]{:S(2)}, u32[]{:S(2)}) %collective-permute-start.3) | collective-permute-done | bytes 524320 | tf_op jit(solution)/shard_map/ppermute | solution.py:340
  41.4 4.5 %shard_map.94 = (bf16[512,1024]{1,0:T(8,128)(2,1)S(1)}, bf16[512,1024]{1,0:T(8,128)(2,1)S(1)}, bf16[3,128,1792]{2,1,0:T(8,128)(2,1)S(1)}, bf16[3,128,1792]{2,1,0:T(8,128)(2,1)S(1)}, bf16[3,128,1792]{2,1,0:T(8,128)(2,1)S(1)}) custom-call(bf16[2,128,1024]{2,1,0:T(8,128)(2,1)S(1)} %shard_map.92.refs_0_, ...), custom_call_target="tpu_custom_call" | custom-call | flops 1 | bytes 1 | tf_op jit(solution)/shard_map/pallas_call | solution.py:78
  46.2 4.5 %collective-permute-start.11 = (bf16[3,128,1792]{2,1,0:T(8,128)(2,1)S(1)}, bf16[3,128,1792]{2,1,0:T(8,128)(2,1)S(1)}, u32[]{:S(2)}, u32[]{:S(2)}) collective-permute-start(bf16[3,128,1792]{2,1,0:T(8,128)(2,1)S(1)} %get-tuple-element.76), channel_id=1, source_target_pairs={{8,72},{24,88},{40,104},{56,120},{72,8},{88,24},{104,40},{120,56},... | collective-permute-start | bytes 4128776 | tf_op jit(solution)/shard_map/ppermute | solution.py:310
  50.8 3.1 %shard_map.95 = (f32[3,256,1792]{2,1,0:T(8,128)S(1)}, bf16[512,512]{1,0:T(8,128)(2,1)S(1)}, bf16[512,512]{1,0:T(8,128)(2,1)S(1)}, bf16[512,512]{1,0:T(8,128)(2,1)S(1)}, bf16[512,512]{1,0:T(8,128)(2,1)S(1)}) custom-call(bf16[512,1024]{1,0:T(8,128)(2,1)S(1)} %get-tuple-element.71.refs_0_, bf16[512,1024]{1,0:T(8,128)(2,1)S(1)} %get-tuple-element.72.refs_1_, ...), custom_call_target="tpu_custom_call" | custom-call | flops 1 | bytes 1 | tf_op jit(solution)/shard_map/pallas_call | solution.py:78
  56.7 6.8 %collective-permute-done.10.refs_2_ = bf16[3,128,1792]{2,1,0:T(8,128)(2,1)S(1)} collective-permute-done((bf16[3,128,1792]{2,1,0:T(8,128)(2,1)S(1)}, bf16[3,128,1792]{2,1,0:T(8,128)(2,1)S(1)}, u32[]{:S(2)}, u32[]{:S(2)}) %collective-permute-start.10) | collective-permute-done | bytes 1376288 | tf_op jit(solution)/shard_map/ppermute | solution.py:309
  63.5 3.4 %collective-permute-done.11.refs_3_ = bf16[3,128,1792]{2,1,0:T(8,128)(2,1)S(1)} collective-permute-done((bf16[3,128,1792]{2,1,0:T(8,128)(2,1)S(1)}, bf16[3,128,1792]{2,1,0:T(8,128)(2,1)S(1)}, u32[]{:S(2)}, u32[]{:S(2)}) %collective-permute-start.11) | collective-permute-done | bytes 1376288 | tf_op jit(solution)/shard_map/ppermute | solution.py:310
  66.8 14.6 %collective-permute-done.9.refs_1_ = bf16[3,128,1792]{2,1,0:T(8,128)(2,1)S(1)} collective-permute-done((bf16[3,128,1792]{2,1,0:T(8,128)(2,1)S(1)}, bf16[3,128,1792]{2,1,0:T(8,128)(2,1)S(1)}, u32[]{:S(2)}, u32[]{:S(2)}) %collective-permute-start.9) | collective-permute-done | bytes 1376288 | tf_op jit(solution)/shard_map/ppermute | solution.py:308
  84.5 7.8 %collective-permute-done.14.refs_4_ = bf16[3,64,1792]{2,1,0:T(8,128)(2,1)S(1)} collective-permute-done((bf16[3,64,1792]{2,1,0:T(8,128)(2,1)S(1)}, bf16[3,64,1792]{2,1,0:T(8,128)(2,1)S(1)}, u32[]{:S(2)}, u32[]{:S(2)}) %collective-permute-start.14) | collective-permute-done | bytes 688160 | tf_op jit(solution)/shard_map/ppermute | solution.py:316
  92.3 7.1 %collective-permute-done.15.refs_5_ = bf16[3,64,1792]{2,1,0:T(8,128)(2,1)S(1)} collective-permute-done((bf16[3,64,1792]{2,1,0:T(8,128)(2,1)S(1)}, bf16[3,64,1792]{2,1,0:T(8,128)(2,1)S(1)}, u32[]{:S(2)}, u32[]{:S(2)}) %collective-permute-start.15) | collective-permute-done | bytes 688160 | tf_op jit(solution)/shard_map/ppermute | solution.py:317
  103.2 5.5 %collective-permute-done.17.refs_1_.refs_6_ = bf16[2,64,1792]{2,1,0:T(8,128)(2,1)S(1)} collective-permute-done((bf16[2,64,1792]{2,1,0:T(8,128)(2,1)S(1)}, bf16[2,64,1792]{2,1,0:T(8,128)(2,1)S(1)}, u32[]{:S(2)}, u32[]{:S(2)}) %collective-permute-start.17) | collective-permute-done | bytes 458784 | tf_op jit(solution)/shard_map/ppermute | solution.py:316
  108.7 5.0 %collective-permute-done.18.refs_2_.refs_7_ = bf16[2,64,1792]{2,1,0:T(8,128)(2,1)S(1)} collective-permute-done((bf16[2,64,1792]{2,1,0:T(8,128)(2,1)S(1)}, bf16[2,64,1792]{2,1,0:T(8,128)(2,1)S(1)}, u32[]{:S(2)}, u32[]{:S(2)}) %collective-permute-start.18) | collective-permute-done | bytes 458784 | tf_op jit(solution)/shard_map/ppermute | solution.py:317
  116.0 3.8 %collective-permute-start.20 = (bf16[2,128,1792]{2,1,0:T(8,128)(2,1)S(1)}, bf16[2,128,1792]{2,1,0:T(8,128)(2,1)S(1)}, u32[]{:S(2)}, u32[]{:S(2)}) collective-permute-start(bf16[2,128,1792]{2,1,0:T(8,128)(2,1)S(1)} %get-tuple-element.88), channel_id=1, source_target_pairs={{0,16},{8,40},{16,0},{24,56},{32,48},{40,72},{48,32},{56,88},{64,8... | collective-permute-start | bytes 2752520 | tf_op jit(solution)/shard_map/ppermute | solution.py:308
  119.9 8.3 %collective-permute-start.22 = (bf16[2,128,1792]{2,1,0:T(8,128)(2,1)}, bf16[2,128,1792]{2,1,0:T(8,128)(2,1)}, u32[]{:S(2)}, u32[]{:S(2)}) collective-permute-start(bf16[2,128,1792]{2,1,0:T(8,128)(2,1)} %get-tuple-element.96), channel_id=1, source_target_pairs={{8,72},{24,88},{40,104},{56,120},{72,8},{88,24},{104,40},{120,56},... | collective-permute-start | bytes 2752520 | tf_op jit(solution)/shard_map/ppermute | solution.py:310
  128.1 15.9 %collective-permute-done.20.refs_9_ = bf16[2,128,1792]{2,1,0:T(8,128)(2,1)S(1)} collective-permute-done((bf16[2,128,1792]{2,1,0:T(8,128)(2,1)S(1)}, bf16[2,128,1792]{2,1,0:T(8,128)(2,1)S(1)}, u32[]{:S(2)}, u32[]{:S(2)}) %collective-permute-start.20) | collective-permute-done | bytes 917536 | tf_op jit(solution)/shard_map/ppermute | solution.py:308
  154.7 8.3 %shard_map.101 = (bf16[2,128,1024]{2,1,0:T(8,128)(2,1)}, bf16[2,128,1024]{2,1,0:T(8,128)(2,1)}, bf16[2,128,1024]{2,1,0:T(8,128)(2,1)}, bf16[2,128,1024]{2,1,0:T(...) custom-call(bf16[128,1024]{1,0:T(8,128)(2,1)S(1)} %get-tuple-element.90.refs_0_, ...), custom_call_target="tpu_custom_call" | custom-call | flops 1 | bytes 1 | tf_op jit(solution)/shard_map/pallas_call | solution.py:78
  164.0 4.7 %collective-permute-start.23 = (bf16[2,128,1024]{2,1,0:T(8,128)(2,1)}, bf16[2,128,1024]{2,1,0:T(8,128)(2,1)S(1)}, u32[]{:S(2)}, u32[]{:S(2)}) collective-permute-start(bf16[2,128,1024]{2,1,0:T(8,128)(2,1)} %get-tuple-element.98), channel_id=1, source_target_pairs={{8,12},{9,13},{10,14},{11,15},{12,8},{13,9},{14,10},{15,11},{24,28... | collective-permute-start | bytes 1572872 | tf_op jit(solution)/shard_map/ppermute | solution.py:384
  168.8 9.5 %collective-permute-start.25 = (bf16[2,128,1024]{2,1,0:T(8,128)(2,1)}, bf16[2,128,1024]{2,1,0:T(8,128)(2,1)}, u32[]{:S(2)}, u32[]{:S(2)}) collective-permute-start(bf16[2,128,1024]{2,1,0:T(8,128)(2,1)} %get-tuple-element.100), channel_id=1, source_target_pairs={{0,2},{1,3},{2,0},{3,1},{4,6},{5,7},{6,4},{7,5},{8,14},{9,15},{10,... | collective-permute-start | bytes 1572872 | tf_op jit(solution)/shard_map/ppermute | solution.py:384
  178.3 4.4 %collective-permute-start.26 = (bf16[2,128,1024]{2,1,0:T(8,128)(2,1)}, bf16[2,128,1024]{2,1,0:T(8,128)(2,1)}, u32[]{:S(2)}, u32[]{:S(2)}) collective-permute-start(bf16[2,128,1024]{2,1,0:T(8,128)(2,1)} %get-tuple-element.101), channel_id=1, source_target_pairs={{0,3},{1,0},{2,1},{3,2},{4,7},{5,4},{6,5},{7,6},{8,15},{9,12},{10,... | collective-permute-start | bytes 1572872 | tf_op jit(solution)/shard_map/ppermute | solution.py:384
  184.8 3.3 %shard_map.103 = bf16[1792,512]{1,0:T(8,128)(2,1)} custom-call(bf16[1024,1792]{1,0:T(8,128)(2,1)S(1)} %copy-done.5, bf16[1024,512]{1,0:T(8,128)(2,1)S(1)} %shard_map.96.refs_1_), custom_call_target="tpu_custom_call" | custom-call | flops 1 | bytes 1 | tf_op jit(solution)/shard_map/pallas_call | solution.py:78
  188.1 8.5 %shard_map.102 = (bf16[512,1792]{1,0:T(8,128)(2,1)}, bf16[512,1792]{1,0:T(8,128)(2,1)}) custom-call(bf16[512,512]{1,0:T(8,128)(2,1)S(1)} %copy-done.23, bf16[512,512]{1,0:T(8,128)(2,1)S(1)} %copy-done.25, bf16[2,512,1792]{2,1,0:T(8,128)(2,1)} %get-tuple-element.104.refs_2_, bf16[2,512,1792]{2,1,0:T(8,128)(2,1)} %collective-permute-done.27.refs_3_), custom_call_target="tpu_custom_call" | custom-call | flops 1 | bytes 1 | tf_op jit(solution)/shard_map/pallas_call | solution.py:78
  196.6 7.5 %collective-permute-done.26 = bf16[2,128,1024]{2,1,0:T(8,128)(2,1)} collective-permute-done((bf16[2,128,1024]{2,1,0:T(8,128)(2,1)}, bf16[2,128,1024]{2,1,0:T(8,128)(2,1)}, u32[]{:S(2)}, u32[]{:S(2)}) %collective-permute-start.26) | collective-permute-done | bytes 524320 | tf_op jit(solution)/shard_map/ppermute | solution.py:384
  (108 shorter events, 43.6 us)
Async XLA Ops:
  7.2 137.8 %all-gather.2.cloned.1.call-start = ((), (), s32[]{:S(2)}) async-start(), calls=%async_computation | async-start | bytes 3899392 | tf_op jit(solution)/shard_map/all_gather | solution.py:366
  9.5 12.9 %collective-permute-start.5 = (bf16[512,1792]{1,0:T(8,128)(2,1)}, bf16[512,1792]{1,0:T(8,128)(2,1)S(1)}, u32[]{:S(2)}, u32[]{:S(2)}) collective-permute-start(bf16[512,1792]{1,0:T(8,128)(2,1)} %refs_12_.1), channel_id=1, source_target_pairs={{0,8},{8,0},{16,24},{24,16},{32,40},{40,32},{48,56},{56,48},{64,72... | collective-permute-start | bytes 5505032 | tf_op jit(solution)/shard_map/ppermute | solution.py:321
  9.7 16.5 %collective-permute-start.2 = (bf16[512,1792]{1,0:T(8,128)(2,1)}, bf16[512,1792]{1,0:T(8,128)(2,1)S(1)}, u32[]{:S(2)}, u32[]{:S(2)}) collective-permute-start(bf16[512,1792]{1,0:T(8,128)(2,1)} %refs_13_.1), channel_id=1, source_target_pairs={{0,8},{8,0},{16,24},{24,16},{32,40},{40,32},{48,56},{56,48},{64,72... | collective-permute-start | bytes 5505032 | tf_op jit(solution)/shard_map/ppermute | solution.py:321
  10.0 20.3 %collective-permute-start.8 = (bf16[1792,512]{1,0:T(8,128)(2,1)}, bf16[1792,512]{1,0:T(8,128)(2,1)S(1)}, u32[]{:S(2)}, u32[]{:S(2)}) collective-permute-start(bf16[1792,512]{1,0:T(8,128)(2,1)} %refs_1_.2), channel_id=1, source_target_pairs={{0,8},{8,0},{16,24},{24,16},{32,40},{40,32},{48,56},{56,48},{64,72... | collective-permute-start | bytes 5505032 | tf_op jit(solution)/shard_map/ppermute | solution.py:321
  11.3 17.1 %collective-permute-start.4 = (bf16[2,128,1024]{2,1,0:T(8,128)(2,1)S(1)}, bf16[2,128,1024]{2,1,0:T(8,128)(2,1)S(1)}, u32[]{:S(2)}, u32[]{:S(2)}) collective-permute-start(bf16[2,128,1024]{2,1,0:T(8,128)(2,1)S(1)} %shard_map.92.refs_0_), channel_id=1, source_target_pairs={{1,0},{2,1},{3,2},{0,3},{5,4},{6,5},{7,6},{4,7},{13,8},{14,9},{15,... | collective-permute-start | bytes 1572872 | tf_op jit(solution)/shard_map/ppermute | solution.py:340
  17.6 12.7 %collective-permute-start.7 = (bf16[2,128,1024]{2,1,0:T(8,128)(2,1)S(1)}, bf16[2,128,1024]{2,1,0:T(8,128)(2,1)S(1)}, u32[]{:S(2)}, u32[]{:S(2)}) collective-permute-start(bf16[2,128,1024]{2,1,0:T(8,128)(2,1)S(1)} %shard_map.92.refs_0_), channel_id=1, source_target_pairs={{3,0},{0,1},{1,2},{2,3},{7,4},{4,5},{5,6},{6,7},{15,8},{12,9},{13,... | collective-permute-start | bytes 1572872 | tf_op jit(solution)/shard_map/ppermute | solution.py:340
  22.4 13.2 %collective-permute-start.6 = (bf16[2,128,1024]{2,1,0:T(8,128)(2,1)S(1)}, bf16[2,128,1024]{2,1,0:T(8,128)(2,1)S(1)}, u32[]{:S(2)}, u32[]{:S(2)}) collective-permute-start(bf16[2,128,1024]{2,1,0:T(8,128)(2,1)S(1)} %shard_map.92.refs_0_), channel_id=1, source_target_pairs={{2,0},{3,1},{0,2},{1,3},{6,4},{7,5},{4,6},{5,7},{14,8},{15,9},{12,... | collective-permute-start | bytes 1572872 | tf_op jit(solution)/shard_map/ppermute | solution.py:340
  26.2 15.2 %collective-permute-start.3 = (bf16[2,128,1024]{2,1,0:T(8,128)(2,1)S(1)}, bf16[2,128,1024]{2,1,0:T(8,128)(2,1)S(1)}, u32[]{:S(2)}, u32[]{:S(2)}) collective-permute-start(bf16[2,128,1024]{2,1,0:T(8,128)(2,1)S(1)} %shard_map.92.refs_0_), channel_id=1, source_target_pairs={{12,8},{13,9},{14,10},{15,11},{8,12},{9,13},{10,14},{11,15},{28,24... | collective-permute-start | bytes 1572872 | tf_op jit(solution)/shard_map/ppermute | solution.py:340
  46.0 17.5 %collective-permute-start.10 = (bf16[3,128,1792]{2,1,0:T(8,128)(2,1)S(1)}, bf16[3,128,1792]{2,1,0:T(8,128)(2,1)S(1)}, u32[]{:S(2)}, u32[]{:S(2)}) collective-permute-start(bf16[3,128,1792]{2,1,0:T(8,128)(2,1)S(1)} %get-tuple-element.75), channel_id=1, source_target_pairs={{0,16},{8,104},{16,0},{24,120},{32,48},{40,8},{48,32},{56,24},{64,... | collective-permute-start | bytes 4128776 | tf_op jit(solution)/shard_map/ppermute | solution.py:309
  46.2 20.7 %collective-permute-start.11 = (bf16[3,128,1792]{2,1,0:T(8,128)(2,1)S(1)}, bf16[3,128,1792]{2,1,0:T(8,128)(2,1)S(1)}, u32[]{:S(2)}, u32[]{:S(2)}) collective-permute-start(bf16[3,128,1792]{2,1,0:T(8,128)(2,1)S(1)} %get-tuple-element.76), channel_id=1, source_target_pairs={{8,72},{24,88},{40,104},{56,120},{72,8},{88,24},{104,40},{120,56},... | collective-permute-start | bytes 4128776 | tf_op jit(solution)/shard_map/ppermute | solution.py:310
  50.7 30.8 %collective-permute-start.9 = (bf16[3,128,1792]{2,1,0:T(8,128)(2,1)S(1)}, bf16[3,128,1792]{2,1,0:T(8,128)(2,1)S(1)}, u32[]{:S(2)}, u32[]{:S(2)}) collective-permute-start(bf16[3,128,1792]{2,1,0:T(8,128)(2,1)S(1)} %get-tuple-element.74), channel_id=1, source_target_pairs={{0,16},{8,40},{16,0},{24,56},{32,48},{40,72},{48,32},{56,88},{64,8... | collective-permute-start | bytes 4128776 | tf_op jit(solution)/shard_map/ppermute | solution.py:308
  82.2 10.2 %collective-permute-start.14 = (bf16[3,64,1792]{2,1,0:T(8,128)(2,1)S(1)}, bf16[3,64,1792]{2,1,0:T(8,128)(2,1)S(1)}, u32[]{:S(2)}, u32[]{:S(2)}) collective-permute-start(bf16[3,64,1792]{2,1,0:T(8,128)(2,1)S(1)} %get-tuple-element.83), channel_id=1, source_target_pairs={{0,32},{8,24},{16,48},{24,8},{32,64},{40,56},{48,80},{56,40},{64,9... | collective-permute-start | bytes 2064392 | tf_op jit(solution)/shard_map/ppermute | solution.py:316
  83.6 15.8 %collective-permute-start.15 = (bf16[3,64,1792]{2,1,0:T(8,128)(2,1)S(1)}, bf16[3,64,1792]{2,1,0:T(8,128)(2,1)S(1)}, u32[]{:S(2)}, u32[]{:S(2)}) collective-permute-start(bf16[3,64,1792]{2,1,0:T(8,128)(2,1)S(1)} %get-tuple-element.84), channel_id=1, source_target_pairs={{0,96},{8,24},{16,112},{24,8},{32,0},{40,56},{48,16},{56,40},{64,3... | collective-permute-start | bytes 2064392 | tf_op jit(solution)/shard_map/ppermute | solution.py:317
  83.8 15.6 %collective-permute-start.16 = (bf16[3,64,1792]{2,1,0:T(8,128)(2,1)S(1)}, bf16[3,64,1792]{2,1,0:T(8,128)(2,1)S(1)}, u32[]{:S(2)}, u32[]{:S(2)}) collective-permute-start(bf16[3,64,1792]{2,1,0:T(8,128)(2,1)S(1)} %get-tuple-element.85), channel_id=1, source_target_pairs={{0,64},{16,80},{32,96},{48,112},{64,0},{80,16},{96,32},{112,48},{1... | collective-permute-start | bytes 2064392 | tf_op jit(solution)/shard_map/ppermute | solution.py:315
  102.4 11.3 %collective-permute-start.18 = (bf16[2,64,1792]{2,1,0:T(8,128)(2,1)S(1)}, bf16[2,64,1792]{2,1,0:T(8,128)(2,1)S(1)}, u32[]{:S(2)}, u32[]{:S(2)}) collective-permute-start(bf16[2,64,1792]{2,1,0:T(8,128)(2,1)S(1)} %get-tuple-element.87.refs_0_.refs_5_), channel_id=1, source_target_pairs={{0,96},{8,24},{16,112},{24,8},{32,0},{40,56},{48,16},{56,40},{64,3... | collective-permute-start | bytes 1376264 | tf_op jit(solution)/shard_map/ppermute | solution.py:317
  102.5 11.2 %collective-permute-start.19 = (bf16[2,64,1792]{2,1,0:T(8,128)(2,1)S(1)}, bf16[2,64,1792]{2,1,0:T(8,128)(2,1)S(1)}, u32[]{:S(2)}, u32[]{:S(2)}) collective-permute-start(bf16[2,64,1792]{2,1,0:T(8,128)(2,1)S(1)} %get-tuple-element.87.refs_0_.refs_5_), channel_id=1, source_target_pairs={{0,64},{16,80},{32,96},{48,112},{64,0},{80,16},{96,32},{112,48},{1... | collective-permute-start | bytes 1376264 | tf_op jit(solution)/shard_map/ppermute | solution.py:315
  116.0 28.0 %collective-permute-start.20 = (bf16[2,128,1792]{2,1,0:T(8,128)(2,1)S(1)}, bf16[2,128,1792]{2,1,0:T(8,128)(2,1)S(1)}, u32[]{:S(2)}, u32[]{:S(2)}) collective-permute-start(bf16[2,128,1792]{2,1,0:T(8,128)(2,1)S(1)} %get-tuple-element.88), channel_id=1, source_target_pairs={{0,16},{8,40},{16,0},{24,56},{32,48},{40,72},{48,32},{56,88},{64,8... | collective-permute-start | bytes 2752520 | tf_op jit(solution)/shard_map/ppermute | solution.py:308
  119.9 32.2 %collective-permute-start.21 = (bf16[2,128,1792]{2,1,0:T(8,128)(2,1)}, bf16[2,128,1792]{2,1,0:T(8,128)(2,1)}, u32[]{:S(2)}, u32[]{:S(2)}) collective-permute-start(bf16[2,128,1792]{2,1,0:T(8,128)(2,1)} %get-tuple-element.95), channel_id=1, source_target_pairs={{0,16},{8,104},{16,0},{24,120},{32,48},{40,8},{48,32},{56,24},{64,... | collective-permute-start | bytes 2752520 | tf_op jit(solution)/shard_map/ppermute | solution.py:309
  119.9 33.6 %collective-permute-start.22 = (bf16[2,128,1792]{2,1,0:T(8,128)(2,1)}, bf16[2,128,1792]{2,1,0:T(8,128)(2,1)}, u32[]{:S(2)}, u32[]{:S(2)}) collective-permute-start(bf16[2,128,1792]{2,1,0:T(8,128)(2,1)} %get-tuple-element.96), channel_id=1, source_target_pairs={{8,72},{24,88},{40,104},{56,120},{72,8},{88,24},{104,40},{120,56},... | collective-permute-start | bytes 2752520 | tf_op jit(solution)/shard_map/ppermute | solution.py:310
  164.0 24.1 %collective-permute-start.27 = (bf16[2,512,1792]{2,1,0:T(8,128)(2,1)}, bf16[2,512,1792]{2,1,0:T(8,128)(2,1)}, u32[]{:S(2)}, u32[]{:S(2)}) collective-permute-start(bf16[2,512,1792]{2,1,0:T(8,128)(2,1)} %get-tuple-element.104.refs_2_), channel_id=1, source_target_pairs={{0,8},{8,0},{16,24},{24,16},{32,40},{40,32},{48,56},{56,48},{64,72... | collective-permute-start | bytes 11010056 | tf_op jit(solution)/shard_map/ppermute | solution.py:321
  164.0 32.6 %collective-permute-start.23 = (bf16[2,128,1024]{2,1,0:T(8,128)(2,1)}, bf16[2,128,1024]{2,1,0:T(8,128)(2,1)S(1)}, u32[]{:S(2)}, u32[]{:S(2)}) collective-permute-start(bf16[2,128,1024]{2,1,0:T(8,128)(2,1)} %get-tuple-element.98), channel_id=1, source_target_pairs={{8,12},{9,13},{10,14},{11,15},{12,8},{13,9},{14,10},{15,11},{24,28... | collective-permute-start | bytes 1572872 | tf_op jit(solution)/shard_map/ppermute | solution.py:384
  168.7 27.8 %collective-permute-start.24 = (bf16[2,128,1024]{2,1,0:T(8,128)(2,1)}, bf16[2,128,1024]{2,1,0:T(8,128)(2,1)}, u32[]{:S(2)}, u32[]{:S(2)}) collective-permute-start(bf16[2,128,1024]{2,1,0:T(8,128)(2,1)} %get-tuple-element.99), channel_id=1, source_target_pairs={{0,1},{1,2},{2,3},{3,0},{4,5},{5,6},{6,7},{7,4},{8,13},{9,14},{10,... | collective-permute-start | bytes 1572872 | tf_op jit(solution)/shard_map/ppermute | solution.py:384
  168.8 27.7 %collective-permute-start.25 = (bf16[2,128,1024]{2,1,0:T(8,128)(2,1)}, bf16[2,128,1024]{2,1,0:T(8,128)(2,1)}, u32[]{:S(2)}, u32[]{:S(2)}) collective-permute-start(bf16[2,128,1024]{2,1,0:T(8,128)(2,1)} %get-tuple-element.100), channel_id=1, source_target_pairs={{0,2},{1,3},{2,0},{3,1},{4,6},{5,7},{6,4},{7,5},{8,14},{9,15},{10,... | collective-permute-start | bytes 1572872 | tf_op jit(solution)/shard_map/ppermute | solution.py:384
  178.3 25.7 %collective-permute-start.26 = (bf16[2,128,1024]{2,1,0:T(8,128)(2,1)}, bf16[2,128,1024]{2,1,0:T(8,128)(2,1)}, u32[]{:S(2)}, u32[]{:S(2)}) collective-permute-start(bf16[2,128,1024]{2,1,0:T(8,128)(2,1)} %get-tuple-element.101), channel_id=1, source_target_pairs={{0,3},{1,0},{2,1},{3,2},{4,7},{5,4},{6,5},{7,6},{8,15},{9,12},{10,... | collective-permute-start | bytes 1572872 | tf_op jit(solution)/shard_map/ppermute | solution.py:384
  (33 other events, 180.0 us)
Sparse Core Ops, SparseCore 0:
  101.1 41.4 all-gather.1

commit v13 on v11

--- a/solution.py
+++ b/solution.py
@@ -378,7 +378,7 @@
     )
     hidden = lax.all_gather(hidden, "row", axis=0, tiled=True)
 
-    near = send_second([d_own] * 3, None)
+    near = send_second([d_own] * 3)
     packed = call(pack_kernel, [d_own, *near], [shape((2, 2 * PIECE, ff_width))] * 3)
     far = send_first(packed)
     hidden = after(hidden, far[0])

time: 217 us -> 214 us (0.986)
  the two profiles are of different devices: /device:TPU:5 before, /device:TPU:21 now
where the time goes in v13:
time: 214 us
  waiting for transfers between devices  103 us (48%)
  starting transfers between devices  53.6 us (25%)
  Pallas kernels  28.3 us (13%)
  between operations  14.3 us (7%)
  local copies, waits for them, and re-layouts  13.9 us (6%)
    ppermute x2, waiting for transfers between devices, send_first(): lax.ppermute(sent[0], 'row', row_perm(over_x, over_y(1)))  29.5 us
    pallas_call x13, Pallas kernels, call(): pl.pallas_call(run, in_specs=[vmem] * n_in, out_specs=[vmem] * n_out, out...  28.3 us
    ppermute x4, waiting for transfers between devices, body(): lax.ppermute(messages[k], BOTH, scatter_perm(k))  20.3 us
    ppermute x4, starting transfers between devices, body(): lax.ppermute(messages[k], BOTH, scatter_perm(k))  14.4 us
    ppermute x4, waiting for transfers between devices, body(): lax.ppermute(starts[step], BOTH, gather_perm(step))  13.8 us
    ppermute x2, waiting for transfers between devices, send_second(): lax.ppermute(sent[1], 'row', row_perm(over_y(-1), core1))  13.2 us
    unnamed x50, local copies, waits for them, and re-layouts  13.2 us
    ppermute x2, waiting for transfers between devices, send_second(): first = lax.ppermute(sent[0], 'row', row_perm(over_y(1), over_x))  12.9 us
  transfers between devices with their start and end apart: 30, of which 18 were waited for; matrix products, arithmetic and copies ran while one was open for 0% of the time, Pallas kernels for 7%

profile of v13, /device:TPU:21, one launch (start us, length us, event | category | flops | bytes accessed | tf_op | source)
XLA Modules:
  0.0 213.9 jit_solution(1592845450038635130)
XLA Ops:
  12.9 3.5 %collective-permute-start.4 = (bf16[2,128,1024]{2,1,0:T(8,128)(2,1)S(1)}, bf16[2,128,1024]{2,1,0:T(8,128)(2,1)S(1)}, u32[]{:S(2)}, u32[]{:S(2)}) collective-permute-start(bf16[2,128,1024]{2,1,0:T(8,128)(2,1)S(1)} %shard_map.92.refs_0_), channel_id=1, source_target_pairs={{1,0},{2,1},{3,2},{0,3},{5,4},{6,5},{7,6},{4,7},{13,8},{14,9},{15,... | collective-permute-start | bytes 1572872 | tf_op jit(solution)/shard_map/ppermute | solution.py:353
  21.3 3.4 %collective-permute-start.3 = (bf16[2,128,1024]{2,1,0:T(8,128)(2,1)S(1)}, bf16[2,128,1024]{2,1,0:T(8,128)(2,1)S(1)}, u32[]{:S(2)}, u32[]{:S(2)}) collective-permute-start(bf16[2,128,1024]{2,1,0:T(8,128)(2,1)S(1)} %shard_map.92.refs_0_), channel_id=1, source_target_pairs={{12,8},{13,9},{14,10},{15,11},{8,12},{9,13},{10,14},{11,15},{28,24... | collective-permute-start | bytes 1572872 | tf_op jit(solution)/shard_map/ppermute | solution.py:353
  24.7 3.7 %collective-permute-start.6 = (bf16[2,128,1024]{2,1,0:T(8,128)(2,1)S(1)}, bf16[2,128,1024]{2,1,0:T(8,128)(2,1)S(1)}, u32[]{:S(2)}, u32[]{:S(2)}) collective-permute-start(bf16[2,128,1024]{2,1,0:T(8,128)(2,1)S(1)} %shard_map.92.refs_0_), channel_id=1, source_target_pairs={{2,0},{3,1},{0,2},{1,3},{6,4},{7,5},{4,6},{5,7},{14,8},{15,9},{12,... | collective-permute-start | bytes 1572872 | tf_op jit(solution)/shard_map/ppermute | solution.py:353
  29.3 4.5 %collective-permute-done.3.refs_1_ = bf16[2,128,1024]{2,1,0:T(8,128)(2,1)S(1)} collective-permute-done((bf16[2,128,1024]{2,1,0:T(8,128)(2,1)S(1)}, bf16[2,128,1024]{2,1,0:T(8,128)(2,1)S(1)}, u32[]{:S(2)}, u32[]{:S(2)}) %collective-permute-start.3) | collective-permute-done | bytes 524320 | tf_op jit(solution)/shard_map/ppermute | solution.py:353
  33.9 8.3 %collective-permute-done.6.refs_3_ = bf16[2,128,1024]{2,1,0:T(8,128)(2,1)S(1)} collective-permute-done((bf16[2,128,1024]{2,1,0:T(8,128)(2,1)S(1)}, bf16[2,128,1024]{2,1,0:T(8,128)(2,1)S(1)}, u32[]{:S(2)}, u32[]{:S(2)}) %collective-permute-start.6) | collective-permute-done | bytes 524320 | tf_op jit(solution)/shard_map/ppermute | solution.py:353
  42.1 4.5 %shard_map.94 = (bf16[512,1024]{1,0:T(8,128)(2,1)S(1)}, bf16[512,1024]{1,0:T(8,128)(2,1)S(1)}, bf16[3,128,1792]{2,1,0:T(8,128)(2,1)S(1)}, bf16[3,128,1792]{2,1,0:T(8,128)(2,1)S(1)}, bf16[3,128,1792]{2,1,0:T(8,128)(2,1)S(1)}) custom-call(bf16[2,128,1024]{2,1,0:T(8,128)(2,1)S(1)} %shard_map.92.refs_0_, ...), custom_call_target="tpu_custom_call" | custom-call | flops 1 | bytes 1 | tf_op jit(solution)/shard_map/pallas_call | solution.py:78
  48.2 3.3 %collective-permute-start.11 = (bf16[3,128,1792]{2,1,0:T(8,128)(2,1)S(1)}, bf16[3,128,1792]{2,1,0:T(8,128)(2,1)S(1)}, u32[]{:S(2)}, u32[]{:S(2)}) collective-permute-start(bf16[3,128,1792]{2,1,0:T(8,128)(2,1)S(1)} %get-tuple-element.78), channel_id=1, source_target_pairs={{8,72},{24,88},{40,104},{56,120},{72,8},{88,24},{104,40},{120,56},... | collective-permute-start | bytes 4128776 | tf_op jit(solution)/shard_map/ppermute | solution.py:323
  51.5 3.1 %shard_map.95 = (f32[3,256,1792]{2,1,0:T(8,128)S(1)}, bf16[512,512]{1,0:T(8,128)(2,1)S(1)}, bf16[512,512]{1,0:T(8,128)(2,1)S(1)}, bf16[512,512]{1,0:T(8,128)(2,1)S(1)}, bf16[512,512]{1,0:T(8,128)(2,1)S(1)}) custom-call(bf16[512,1024]{1,0:T(8,128)(2,1)S(1)} %get-tuple-element.73.refs_0_, bf16[512,1024]{1,0:T(8,128)(2,1)S(1)} %get-tuple-element.74.refs_1_, ...), custom_call_target="tpu_custom_call" | custom-call | flops 1 | bytes 1 | tf_op jit(solution)/shard_map/pallas_call | solution.py:78
  57.4 19.5 %collective-permute-done.9.refs_1_ = bf16[3,128,1792]{2,1,0:T(8,128)(2,1)S(1)} collective-permute-done((bf16[3,128,1792]{2,1,0:T(8,128)(2,1)S(1)}, bf16[3,128,1792]{2,1,0:T(8,128)(2,1)S(1)}, u32[]{:S(2)}, u32[]{:S(2)}) %collective-permute-start.9) | collective-permute-done | bytes 1376288 | tf_op jit(solution)/shard_map/ppermute | solution.py:321
  76.9 3.5 %collective-permute-done.11.refs_3_ = bf16[3,128,1792]{2,1,0:T(8,128)(2,1)S(1)} collective-permute-done((bf16[3,128,1792]{2,1,0:T(8,128)(2,1)S(1)}, bf16[3,128,1792]{2,1,0:T(8,128)(2,1)S(1)}, u32[]{:S(2)}, u32[]{:S(2)}) %collective-permute-start.11) | collective-permute-done | bytes 1376288 | tf_op jit(solution)/shard_map/ppermute | solution.py:323
  83.3 7.9 %collective-permute-done.14.refs_4_ = bf16[3,64,1792]{2,1,0:T(8,128)(2,1)S(1)} collective-permute-done((bf16[3,64,1792]{2,1,0:T(8,128)(2,1)S(1)}, bf16[3,64,1792]{2,1,0:T(8,128)(2,1)S(1)}, u32[]{:S(2)}, u32[]{:S(2)}) %collective-permute-start.14) | collective-permute-done | bytes 688160 | tf_op jit(solution)/shard_map/ppermute | solution.py:329
  91.2 7.1 %collective-permute-done.15.refs_5_ = bf16[3,64,1792]{2,1,0:T(8,128)(2,1)S(1)} collective-permute-done((bf16[3,64,1792]{2,1,0:T(8,128)(2,1)S(1)}, bf16[3,64,1792]{2,1,0:T(8,128)(2,1)S(1)}, u32[]{:S(2)}, u32[]{:S(2)}) %collective-permute-start.15) | collective-permute-done | bytes 688160 | tf_op jit(solution)/shard_map/ppermute | solution.py:330
  102.1 6.2 %collective-permute-done.18.refs_2_.refs_7_ = bf16[2,64,1792]{2,1,0:T(8,128)(2,1)S(1)} collective-permute-done((bf16[2,64,1792]{2,1,0:T(8,128)(2,1)S(1)}, bf16[2,64,1792]{2,1,0:T(8,128)(2,1)S(1)}, u32[]{:S(2)}, u32[]{:S(2)}) %collective-permute-start.18) | collective-permute-done | bytes 458784 | tf_op jit(solution)/shard_map/ppermute | solution.py:330
  108.2 5.0 %collective-permute-done.17.refs_1_.refs_6_ = bf16[2,64,1792]{2,1,0:T(8,128)(2,1)S(1)} collective-permute-done((bf16[2,64,1792]{2,1,0:T(8,128)(2,1)S(1)}, bf16[2,64,1792]{2,1,0:T(8,128)(2,1)S(1)}, u32[]{:S(2)}, u32[]{:S(2)}) %collective-permute-start.17) | collective-permute-done | bytes 458784 | tf_op jit(solution)/shard_map/ppermute | solution.py:329
  115.6 7.8 %collective-permute-start.20 = (bf16[2,128,1792]{2,1,0:T(8,128)(2,1)S(1)}, bf16[2,128,1792]{2,1,0:T(8,128)(2,1)S(1)}, u32[]{:S(2)}, u32[]{:S(2)}) collective-permute-start(bf16[2,128,1792]{2,1,0:T(8,128)(2,1)S(1)} %get-tuple-element.90), channel_id=1, source_target_pairs={{0,16},{8,40},{16,0},{24,56},{32,48},{40,72},{48,32},{56,88},{64,8... | collective-permute-start | bytes 2752520 | tf_op jit(solution)/shard_map/ppermute | solution.py:321
  123.3 7.7 %collective-permute-start.22 = (bf16[2,128,1792]{2,1,0:T(8,128)(2,1)}, bf16[2,128,1792]{2,1,0:T(8,128)(2,1)}, u32[]{:S(2)}, u32[]{:S(2)}) collective-permute-start(bf16[2,128,1792]{2,1,0:T(8,128)(2,1)} %get-tuple-element.98), channel_id=1, source_target_pairs={{8,72},{24,88},{40,104},{56,120},{72,8},{88,24},{104,40},{120,56},... | collective-permute-start | bytes 2752520 | tf_op jit(solution)/shard_map/ppermute | solution.py:323
  131.0 10.0 %collective-permute-done.20.refs_9_ = bf16[2,128,1792]{2,1,0:T(8,128)(2,1)S(1)} collective-permute-done((bf16[2,128,1792]{2,1,0:T(8,128)(2,1)S(1)}, bf16[2,128,1792]{2,1,0:T(8,128)(2,1)S(1)}, u32[]{:S(2)}, u32[]{:S(2)}) %collective-permute-start.20) | collective-permute-done | bytes 917536 | tf_op jit(solution)/shard_map/ppermute | solution.py:321
  149.1 3.9 %collective-permute-done.22.refs_11_ = bf16[2,128,1792]{2,1,0:T(8,128)(2,1)} collective-permute-done((bf16[2,128,1792]{2,1,0:T(8,128)(2,1)}, bf16[2,128,1792]{2,1,0:T(8,128)(2,1)}, u32[]{:S(2)}, u32[]{:S(2)}) %collective-permute-start.22) | collective-permute-done | bytes 917536 | tf_op jit(solution)/shard_map/ppermute | solution.py:323
  154.2 6.1 %shard_map.101 = (bf16[2,128,1024]{2,1,0:T(8,128)(2,1)S(1)}, bf16[2,128,1024]{2,1,0:T(8,128)(2,1)S(1)}, bf16[2,128,1024]{2,1,0:T(8,128)(2,1)S(1)}, bf16[2,128,10...) custom-call(bf16[128,1024]{1,0:T(8,128)(2,1)S(1)} %get-tuple-element.92.refs_0_, ...), custom_call_target="tpu_custom_call" | custom-call | flops 1 | bytes 1 | tf_op jit(solution)/shard_map/pallas_call | solution.py:78
  162.7 9.9 %collective-permute-start.24 = (bf16[2,128,1024]{2,1,0:T(8,128)(2,1)S(1)}, bf16[2,128,1024]{2,1,0:T(8,128)(2,1)S(1)}, u32[]{:S(2)}, u32[]{:S(2)}) collective-permute-start(bf16[2,128,1024]{2,1,0:T(8,128)(2,1)S(1)} %get-tuple-element.101), channel_id=1, source_target_pairs={{0,1},{1,2},{2,3},{3,0},{4,5},{5,6},{6,7},{7,4},{8,13},{9,14},{10,... | collective-permute-start | bytes 1572872 | tf_op jit(solution)/shard_map/ppermute | solution.py:397
  174.8 3.3 %shard_map.103 = bf16[1792,512]{1,0:T(8,128)(2,1)} custom-call(bf16[1024,1792]{1,0:T(8,128)(2,1)S(1)} %copy-done.5, bf16[1024,512]{1,0:T(8,128)(2,1)S(1)} %shard_map.96.refs_1_), custom_call_target="tpu_custom_call" | custom-call | flops 1 | bytes 1 | tf_op jit(solution)/shard_map/pallas_call | solution.py:78
  178.1 5.5 %shard_map.102 = (bf16[512,1792]{1,0:T(8,128)(2,1)}, bf16[512,1792]{1,0:T(8,128)(2,1)}) custom-call(bf16[512,512]{1,0:T(8,128)(2,1)S(1)} %copy-done.21, bf16[512,512]{1,0:T(8,128)(2,1)S(1)} %copy-done.23, bf16[2,512,1792]{2,1,0:T(8,128)(2,1)S(1)} %get-tuple-element.106.refs_2_, bf16[2,512,1792]{2,1,0:T(8,128)(2,1)S(1)} %collective-permute-done.27.refs_3_), custom_call_target="tpu_custom_call" | custom-call | flops 1 | bytes 1 | tf_op jit(solution)/shard_map/pallas_call | solution.py:78
  183.6 2.3 %collective-permute-done.25.refs_3_ = bf16[2,128,1024]{2,1,0:T(8,128)(2,1)S(1)} collective-permute-done((bf16[2,128,1024]{2,1,0:T(8,128)(2,1)S(1)}, bf16[2,128,1024]{2,1,0:T(8,128)(2,1)S(1)}, u32[]{:S(2)}, u32[]{:S(2)}) %collective-permute-start.25) | collective-permute-done | bytes 524320 | tf_op jit(solution)/shard_map/ppermute | solution.py:397
  185.9 18.0 %collective-permute-done.26.refs_4_ = bf16[2,128,1024]{2,1,0:T(8,128)(2,1)S(1)} collective-permute-done((bf16[2,128,1024]{2,1,0:T(8,128)(2,1)S(1)}, bf16[2,128,1024]{2,1,0:T(8,128)(2,1)S(1)}, u32[]{:S(2)}, u32[]{:S(2)}) %collective-permute-start.26) | collective-permute-done | bytes 524320 | tf_op jit(solution)/shard_map/ppermute | solution.py:397
  (103 shorter events, 41.7 us)
Async XLA Ops:
  7.2 134.8 %all-gather.2.cloned.1.call-start = ((), (), s32[]{:S(2)}) async-start(), calls=%async_computation | async-start | bytes 3899392 | tf_op jit(solution)/shard_map/all_gather | solution.py:379
  9.5 11.7 %collective-permute-start.5 = (bf16[512,1792]{1,0:T(8,128)(2,1)}, bf16[512,1792]{1,0:T(8,128)(2,1)S(1)}, u32[]{:S(2)}, u32[]{:S(2)}) collective-permute-start(bf16[512,1792]{1,0:T(8,128)(2,1)} %refs_12_.1), channel_id=1, source_target_pairs={{0,8},{8,0},{16,24},{24,16},{32,40},{40,32},{48,56},{56,48},{64,72... | collective-permute-start | bytes 5505032 | tf_op jit(solution)/shard_map/ppermute | solution.py:334
  9.7 11.6 %collective-permute-start.2 = (bf16[512,1792]{1,0:T(8,128)(2,1)}, bf16[512,1792]{1,0:T(8,128)(2,1)S(1)}, u32[]{:S(2)}, u32[]{:S(2)}) collective-permute-start(bf16[512,1792]{1,0:T(8,128)(2,1)} %refs_13_.1), channel_id=1, source_target_pairs={{0,8},{8,0},{16,24},{24,16},{32,40},{40,32},{48,56},{56,48},{64,72... | collective-permute-start | bytes 5505032 | tf_op jit(solution)/shard_map/ppermute | solution.py:334
  10.0 19.3 %collective-permute-start.8 = (bf16[1792,512]{1,0:T(8,128)(2,1)}, bf16[1792,512]{1,0:T(8,128)(2,1)S(1)}, u32[]{:S(2)}, u32[]{:S(2)}) collective-permute-start(bf16[1792,512]{1,0:T(8,128)(2,1)} %refs_1_.2), channel_id=1, source_target_pairs={{0,8},{8,0},{16,24},{24,16},{32,40},{40,32},{48,56},{56,48},{64,72... | collective-permute-start | bytes 5505032 | tf_op jit(solution)/shard_map/ppermute | solution.py:334
  11.3 17.1 %collective-permute-start.7 = (bf16[2,128,1024]{2,1,0:T(8,128)(2,1)S(1)}, bf16[2,128,1024]{2,1,0:T(8,128)(2,1)S(1)}, u32[]{:S(2)}, u32[]{:S(2)}) collective-permute-start(bf16[2,128,1024]{2,1,0:T(8,128)(2,1)S(1)} %shard_map.92.refs_0_), channel_id=1, source_target_pairs={{3,0},{0,1},{1,2},{2,3},{7,4},{4,5},{5,6},{6,7},{15,8},{12,9},{13,... | collective-permute-start | bytes 1572872 | tf_op jit(solution)/shard_map/ppermute | solution.py:353
  12.9 16.4 %collective-permute-start.4 = (bf16[2,128,1024]{2,1,0:T(8,128)(2,1)S(1)}, bf16[2,128,1024]{2,1,0:T(8,128)(2,1)S(1)}, u32[]{:S(2)}, u32[]{:S(2)}) collective-permute-start(bf16[2,128,1024]{2,1,0:T(8,128)(2,1)S(1)} %shard_map.92.refs_0_), channel_id=1, source_target_pairs={{1,0},{2,1},{3,2},{0,3},{5,4},{6,5},{7,6},{4,7},{13,8},{14,9},{15,... | collective-permute-start | bytes 1572872 | tf_op jit(solution)/shard_map/ppermute | solution.py:353
  21.3 12.6 %collective-permute-start.3 = (bf16[2,128,1024]{2,1,0:T(8,128)(2,1)S(1)}, bf16[2,128,1024]{2,1,0:T(8,128)(2,1)S(1)}, u32[]{:S(2)}, u32[]{:S(2)}) collective-permute-start(bf16[2,128,1024]{2,1,0:T(8,128)(2,1)S(1)} %shard_map.92.refs_0_), channel_id=1, source_target_pairs={{12,8},{13,9},{14,10},{15,11},{8,12},{9,13},{10,14},{11,15},{28,24... | collective-permute-start | bytes 1572872 | tf_op jit(solution)/shard_map/ppermute | solution.py:353
  24.7 17.5 %collective-permute-start.6 = (bf16[2,128,1024]{2,1,0:T(8,128)(2,1)S(1)}, bf16[2,128,1024]{2,1,0:T(8,128)(2,1)S(1)}, u32[]{:S(2)}, u32[]{:S(2)}) collective-permute-start(bf16[2,128,1024]{2,1,0:T(8,128)(2,1)S(1)} %shard_map.92.refs_0_), channel_id=1, source_target_pairs={{2,0},{3,1},{0,2},{1,3},{6,4},{7,5},{4,6},{5,7},{14,8},{15,9},{12,... | collective-permute-start | bytes 1572872 | tf_op jit(solution)/shard_map/ppermute | solution.py:353
  46.7 30.2 %collective-permute-start.9 = (bf16[3,128,1792]{2,1,0:T(8,128)(2,1)S(1)}, bf16[3,128,1792]{2,1,0:T(8,128)(2,1)S(1)}, u32[]{:S(2)}, u32[]{:S(2)}) collective-permute-start(bf16[3,128,1792]{2,1,0:T(8,128)(2,1)S(1)} %get-tuple-element.76), channel_id=1, source_target_pairs={{0,16},{8,40},{16,0},{24,56},{32,48},{40,72},{48,32},{56,88},{64,8... | collective-permute-start | bytes 4128776 | tf_op jit(solution)/shard_map/ppermute | solution.py:321
  47.8 29.1 %collective-permute-start.10 = (bf16[3,128,1792]{2,1,0:T(8,128)(2,1)S(1)}, bf16[3,128,1792]{2,1,0:T(8,128)(2,1)S(1)}, u32[]{:S(2)}, u32[]{:S(2)}) collective-permute-start(bf16[3,128,1792]{2,1,0:T(8,128)(2,1)S(1)} %get-tuple-element.77), channel_id=1, source_target_pairs={{0,16},{8,104},{16,0},{24,120},{32,48},{40,8},{48,32},{56,24},{64,... | collective-permute-start | bytes 4128776 | tf_op jit(solution)/shard_map/ppermute | solution.py:322
  48.2 32.2 %collective-permute-start.11 = (bf16[3,128,1792]{2,1,0:T(8,128)(2,1)S(1)}, bf16[3,128,1792]{2,1,0:T(8,128)(2,1)S(1)}, u32[]{:S(2)}, u32[]{:S(2)}) collective-permute-start(bf16[3,128,1792]{2,1,0:T(8,128)(2,1)S(1)} %get-tuple-element.78), channel_id=1, source_target_pairs={{8,72},{24,88},{40,104},{56,120},{72,8},{88,24},{104,40},{120,56},... | collective-permute-start | bytes 4128776 | tf_op jit(solution)/shard_map/ppermute | solution.py:323
  81.1 10.2 %collective-permute-start.14 = (bf16[3,64,1792]{2,1,0:T(8,128)(2,1)S(1)}, bf16[3,64,1792]{2,1,0:T(8,128)(2,1)S(1)}, u32[]{:S(2)}, u32[]{:S(2)}) collective-permute-start(bf16[3,64,1792]{2,1,0:T(8,128)(2,1)S(1)} %get-tuple-element.85), channel_id=1, source_target_pairs={{0,32},{8,24},{16,48},{24,8},{32,64},{40,56},{48,80},{56,40},{64,9... | collective-permute-start | bytes 2064392 | tf_op jit(solution)/shard_map/ppermute | solution.py:329
  82.0 16.3 %collective-permute-start.15 = (bf16[3,64,1792]{2,1,0:T(8,128)(2,1)S(1)}, bf16[3,64,1792]{2,1,0:T(8,128)(2,1)S(1)}, u32[]{:S(2)}, u32[]{:S(2)}) collective-permute-start(bf16[3,64,1792]{2,1,0:T(8,128)(2,1)S(1)} %get-tuple-element.86), channel_id=1, source_target_pairs={{0,96},{8,24},{16,112},{24,8},{32,0},{40,56},{48,16},{56,40},{64,3... | collective-permute-start | bytes 2064392 | tf_op jit(solution)/shard_map/ppermute | solution.py:330
  82.6 15.7 %collective-permute-start.16 = (bf16[3,64,1792]{2,1,0:T(8,128)(2,1)S(1)}, bf16[3,64,1792]{2,1,0:T(8,128)(2,1)S(1)}, u32[]{:S(2)}, u32[]{:S(2)}) collective-permute-start(bf16[3,64,1792]{2,1,0:T(8,128)(2,1)S(1)} %get-tuple-element.87), channel_id=1, source_target_pairs={{0,64},{16,80},{32,96},{48,112},{64,0},{80,16},{96,32},{112,48},{1... | collective-permute-start | bytes 2064392 | tf_op jit(solution)/shard_map/ppermute | solution.py:328
  100.5 7.7 %collective-permute-start.18 = (bf16[2,64,1792]{2,1,0:T(8,128)(2,1)S(1)}, bf16[2,64,1792]{2,1,0:T(8,128)(2,1)S(1)}, u32[]{:S(2)}, u32[]{:S(2)}) collective-permute-start(bf16[2,64,1792]{2,1,0:T(8,128)(2,1)S(1)} %get-tuple-element.89.refs_0_.refs_5_), channel_id=1, source_target_pairs={{0,96},{8,24},{16,112},{24,8},{32,0},{40,56},{48,16},{56,40},{64,3... | collective-permute-start | bytes 1376264 | tf_op jit(solution)/shard_map/ppermute | solution.py:330
  101.5 11.8 %collective-permute-start.17 = (bf16[2,64,1792]{2,1,0:T(8,128)(2,1)S(1)}, bf16[2,64,1792]{2,1,0:T(8,128)(2,1)S(1)}, u32[]{:S(2)}, u32[]{:S(2)}) collective-permute-start(bf16[2,64,1792]{2,1,0:T(8,128)(2,1)S(1)} %get-tuple-element.89.refs_0_.refs_5_), channel_id=1, source_target_pairs={{0,32},{8,24},{16,48},{24,8},{32,64},{40,56},{48,80},{56,40},{64,9... | collective-permute-start | bytes 1376264 | tf_op jit(solution)/shard_map/ppermute | solution.py:329
  115.6 25.5 %collective-permute-start.20 = (bf16[2,128,1792]{2,1,0:T(8,128)(2,1)S(1)}, bf16[2,128,1792]{2,1,0:T(8,128)(2,1)S(1)}, u32[]{:S(2)}, u32[]{:S(2)}) collective-permute-start(bf16[2,128,1792]{2,1,0:T(8,128)(2,1)S(1)} %get-tuple-element.90), channel_id=1, source_target_pairs={{0,16},{8,40},{16,0},{24,56},{32,48},{40,72},{48,32},{56,88},{64,8... | collective-permute-start | bytes 2752520 | tf_op jit(solution)/shard_map/ppermute | solution.py:321
  123.3 25.8 %collective-permute-start.21 = (bf16[2,128,1792]{2,1,0:T(8,128)(2,1)}, bf16[2,128,1792]{2,1,0:T(8,128)(2,1)}, u32[]{:S(2)}, u32[]{:S(2)}) collective-permute-start(bf16[2,128,1792]{2,1,0:T(8,128)(2,1)} %get-tuple-element.97), channel_id=1, source_target_pairs={{0,16},{8,104},{16,0},{24,120},{32,48},{40,8},{48,32},{56,24},{64,... | collective-permute-start | bytes 2752520 | tf_op jit(solution)/shard_map/ppermute | solution.py:322
  123.3 29.7 %collective-permute-start.22 = (bf16[2,128,1792]{2,1,0:T(8,128)(2,1)}, bf16[2,128,1792]{2,1,0:T(8,128)(2,1)}, u32[]{:S(2)}, u32[]{:S(2)}) collective-permute-start(bf16[2,128,1792]{2,1,0:T(8,128)(2,1)} %get-tuple-element.98), channel_id=1, source_target_pairs={{8,72},{24,88},{40,104},{56,120},{72,8},{88,24},{104,40},{120,56},... | collective-permute-start | bytes 2752520 | tf_op jit(solution)/shard_map/ppermute | solution.py:323
  160.3 17.8 %collective-permute-start.27 = (bf16[2,512,1792]{2,1,0:T(8,128)(2,1)S(1)}, bf16[2,512,1792]{2,1,0:T(8,128)(2,1)S(1)}, u32[]{:S(2)}, u32[]{:S(2)}) collective-permute-start(bf16[2,512,1792]{2,1,0:T(8,128)(2,1)S(1)} %get-tuple-element.106.refs_2_), channel_id=1, source_target_pairs={{0,8},{8,0},{16,24},{24,16},{32,40},{40,32},{48,56},{56,48},{64,72... | collective-permute-start | bytes 11010056 | tf_op jit(solution)/shard_map/ppermute | solution.py:334
  160.4 23.2 %collective-permute-start.23 = (bf16[2,128,1024]{2,1,0:T(8,128)(2,1)S(1)}, bf16[2,128,1024]{2,1,0:T(8,128)(2,1)S(1)}, u32[]{:S(2)}, u32[]{:S(2)}) collective-permute-start(bf16[2,128,1024]{2,1,0:T(8,128)(2,1)S(1)} %get-tuple-element.100), channel_id=1, source_target_pairs={{8,12},{9,13},{10,14},{11,15},{12,8},{13,9},{14,10},{15,11},{24,28... | collective-permute-start | bytes 1572872 | tf_op jit(solution)/shard_map/ppermute | solution.py:397
  162.7 20.9 %collective-permute-start.24 = (bf16[2,128,1024]{2,1,0:T(8,128)(2,1)S(1)}, bf16[2,128,1024]{2,1,0:T(8,128)(2,1)S(1)}, u32[]{:S(2)}, u32[]{:S(2)}) collective-permute-start(bf16[2,128,1024]{2,1,0:T(8,128)(2,1)S(1)} %get-tuple-element.101), channel_id=1, source_target_pairs={{0,1},{1,2},{2,3},{3,0},{4,5},{5,6},{6,7},{7,4},{8,13},{9,14},{10,... | collective-permute-start | bytes 1572872 | tf_op jit(solution)/shard_map/ppermute | solution.py:397
  172.6 13.3 %collective-permute-start.25 = (bf16[2,128,1024]{2,1,0:T(8,128)(2,1)S(1)}, bf16[2,128,1024]{2,1,0:T(8,128)(2,1)S(1)}, u32[]{:S(2)}, u32[]{:S(2)}) collective-permute-start(bf16[2,128,1024]{2,1,0:T(8,128)(2,1)S(1)} %get-tuple-element.102), channel_id=1, source_target_pairs={{0,2},{1,3},{2,0},{3,1},{4,6},{5,7},{6,4},{7,5},{8,14},{9,15},{10,... | collective-permute-start | bytes 1572872 | tf_op jit(solution)/shard_map/ppermute | solution.py:397
  172.6 31.3 %collective-permute-start.26 = (bf16[2,128,1024]{2,1,0:T(8,128)(2,1)S(1)}, bf16[2,128,1024]{2,1,0:T(8,128)(2,1)S(1)}, u32[]{:S(2)}, u32[]{:S(2)}) collective-permute-start(bf16[2,128,1024]{2,1,0:T(8,128)(2,1)S(1)} %get-tuple-element.103), channel_id=1, source_target_pairs={{0,3},{1,0},{2,1},{3,2},{4,7},{5,4},{6,5},{7,6},{8,15},{9,12},{10,... | collective-permute-start | bytes 1572872 | tf_op jit(solution)/shard_map/ppermute | solution.py:397
  (31 other events, 204.4 us)
Sparse Core Ops, SparseCore 0:
  100.0 39.1 all-gather.1

commit v14 on v9

--- a/solution.py
+++ b/solution.py
@@ -359,9 +359,9 @@
         [products, *heard, *send_second(sent)],
         [shape((PIECE, ff_width)), shape((2, PIECE, ff_width))],
     )
-    hidden = lax.all_gather(hidden, "row", axis=0, tiled=True)
 
     near = send_second([d_own] * 3)
+    hidden = lax.all_gather(after(hidden, near[0]), "row", axis=0, tiled=True)
     first, second = call(pack_kernel, [d_own, *near], [shape((2, 2 * PIECE, ff_width))] * 2)
     far = send_first([first, second, first])
     hidden = after(hidden, far[0])

time: 214 us -> 224 us (1.047); the launches traced: 214 us -> 222 us
  waiting for transfers between devices: 94.4 us -> 110 us
  starting transfers between devices: 53.7 us -> 43.9 us
  local copies, waits for them, and re-layouts: 16.2 us -> 18.8 us
    ppermute x4, starting transfers between devices: 17.8 us -> 7.04 us  [body(): lax.ppermute(messages[k], BOTH, scatter_perm(k))]
    all_gather x1, waiting for transfers between devices: 0.01 us -> 10 us  [body(): hidden = lax.all_gather(after(hidden, near[0]), 'row', axis=0, tiled=True)]
    ppermute x2, waiting for transfers between devices: 30.5 us -> 40.1 us  [send_first(): lax.ppermute(sent[0], 'row', row_perm(over_x, over_y(1)))]
    ppermute x9, starting transfers between devices: 2.21 us -> 6.75 us  [body(): flip = lambda value: lax.ppermute(value, 'row', CORE_FLIP)]
    ppermute x2, waiting for transfers between devices: 6.45 us -> 3.37 us  [send_first(): lax.ppermute(sent[2], 'row', row_perm(None, over_y(2)))]
    unnamed x58 -> x56, local copies, waits for them, and re-layouts: 15.5 us -> 18 us
    ppermute x2, starting transfers between devices: 12.8 us -> 10.3 us  [send_first(): lax.ppermute(sent[2], 'row', row_perm(None, over_y(2)))]
    ppermute x2, starting transfers between devices: 3.92 us -> 1.52 us  [send_first(): lax.ppermute(sent[0], 'row', row_perm(over_x, over_y(1)))]
where the time goes in v14:
time: 224 us; the launch traced here: 222 us
  waiting for transfers between devices  110 us (49%)
  starting transfers between devices  43.9 us (20%)
  Pallas kernels  33.1 us (15%)
  local copies, waits for them, and re-layouts  18.8 us (8%)
  between operations  14.3 us (6%)
    ppermute x2, waiting for transfers between devices, send_first(): lax.ppermute(sent[0], 'row', row_perm(over_x, over_y(1)))  40.1 us
    pallas_call x13, Pallas kernels, call(): pl.pallas_call(run, in_specs=[vmem] * n_in, out_specs=[vmem] * n_out, out...  33.1 us
    unnamed x56, local copies, waits for them, and re-layouts  18 us
    ppermute x2, waiting for transfers between devices, send_second(): first = lax.ppermute(sent[0], 'row', row_perm(over_y(1), over_x))  14.1 us
    ppermute x4, waiting for transfers between devices, body(): lax.ppermute(starts[step], BOTH, gather_perm(step))  13 us
    ppermute x2, waiting for transfers between devices, send_second(): lax.ppermute(sent[1], 'row', row_perm(over_y(-1), over_x))  12.7 us
    ppermute x4, starting transfers between devices, body(): lax.ppermute(starts[step], BOTH, gather_perm(step))  12.2 us
    ppermute x2, starting transfers between devices, send_first(): lax.ppermute(sent[2], 'row', row_perm(None, over_y(2)))  10.3 us
  transfers between devices with their start and end apart: 30, of which 18 were waited for; matrix products, arithmetic and copies ran while one was open for 0% of the time, Pallas kernels for 9%

profile of v14, /device:TPU:17, one launch (start us, length us, event | category | flops | bytes accessed | tf_op | source)
XLA Modules:
  0.0 221.5 jit_solution(14165671887147138048)
XLA Ops:
  12.1 6.3 %collective-permute-start.4 = (bf16[2,128,1024]{2,1,0:T(8,128)(2,1)S(1)}, bf16[2,128,1024]{2,1,0:T(8,128)(2,1)S(1)}, u32[]{:S(2)}, u32[]{:S(2)}) collective-permute-start(bf16[2,128,1024]{2,1,0:T(8,128)(2,1)S(1)} %shard_map.93.refs_0_), channel_id=1, source_target_pairs={{1,0},{2,1},{3,2},{0,3},{5,4},{6,5},{7,6},{4,7},{13,8},{14,9},{15,... | collective-permute-start | bytes 1572872 | tf_op jit(solution)/shard_map/ppermute | solution.py:336
  23.3 3.8 %collective-permute-start.6 = (bf16[2,128,1024]{2,1,0:T(8,128)(2,1)S(1)}, bf16[2,128,1024]{2,1,0:T(8,128)(2,1)S(1)}, u32[]{:S(2)}, u32[]{:S(2)}) collective-permute-start(bf16[2,128,1024]{2,1,0:T(8,128)(2,1)S(1)} %shard_map.93.refs_0_), channel_id=1, source_target_pairs={{2,0},{3,1},{0,2},{1,3},{6,4},{7,5},{4,6},{5,7},{14,8},{15,9},{12,... | collective-permute-start | bytes 1572872 | tf_op jit(solution)/shard_map/ppermute | solution.py:336
  27.1 2.1 collective-permute-start.3
  31.1 5.3 %collective-permute-done.6.refs_3_ = bf16[2,128,1024]{2,1,0:T(8,128)(2,1)S(1)} collective-permute-done((bf16[2,128,1024]{2,1,0:T(8,128)(2,1)S(1)}, bf16[2,128,1024]{2,1,0:T(8,128)(2,1)S(1)}, u32[]{:S(2)}, u32[]{:S(2)}) %collective-permute-start.6) | collective-permute-done | bytes 524320 | tf_op jit(solution)/shard_map/ppermute | solution.py:336
  36.5 5.8 %collective-permute-done.3.refs_1_ = bf16[2,128,1024]{2,1,0:T(8,128)(2,1)S(1)} collective-permute-done((bf16[2,128,1024]{2,1,0:T(8,128)(2,1)S(1)}, bf16[2,128,1024]{2,1,0:T(8,128)(2,1)S(1)}, u32[]{:S(2)}, u32[]{:S(2)}) %collective-permute-start.3) | collective-permute-done | bytes 524320 | tf_op jit(solution)/shard_map/ppermute | solution.py:336
  42.3 4.5 %shard_map.95 = (bf16[512,1024]{1,0:T(8,128)(2,1)S(1)}, bf16[512,1024]{1,0:T(8,128)(2,1)S(1)}, bf16[3,128,1792]{2,1,0:T(8,128)(2,1)S(1)}, bf16[3,128,1792]{2,1,0:T(8,128)(2,1)S(1)}, bf16[3,128,1792]{2,1,0:T(8,128)(2,1)S(1)}) custom-call(bf16[2,128,1024]{2,1,0:T(8,128)(2,1)S(1)} %shard_map.93.refs_0_, ...), custom_call_target="tpu_custom_call" | custom-call | flops 1 | bytes 1 | tf_op jit(solution)/shard_map/pallas_call | solution.py:78
  47.0 4.5 %collective-permute-start.11 = (bf16[3,128,1792]{2,1,0:T(8,128)(2,1)S(1)}, bf16[3,128,1792]{2,1,0:T(8,128)(2,1)S(1)}, u32[]{:S(2)}, u32[]{:S(2)}) collective-permute-start(bf16[3,128,1792]{2,1,0:T(8,128)(2,1)S(1)} %get-tuple-element.71), channel_id=1, source_target_pairs={{8,72},{24,88},{40,104},{56,120},{72,8},{88,24},{104,40},{120,56},... | collective-permute-start | bytes 4128776 | tf_op jit(solution)/shard_map/ppermute | solution.py:306
  51.6 3.1 %shard_map.96 = (f32[3,256,1792]{2,1,0:T(8,128)S(1)}, bf16[512,512]{1,0:T(8,128)(2,1)S(1)}, bf16[512,512]{1,0:T(8,128)(2,1)S(1)}, bf16[512,512]{1,0:T(8,128)(2,1)S(1)}, bf16[512,512]{1,0:T(8,128)(2,1)S(1)}) custom-call(bf16[512,1024]{1,0:T(8,128)(2,1)S(1)} %get-tuple-element.66.refs_0_, bf16[512,1024]{1,0:T(8,128)(2,1)S(1)} %get-tuple-element.67.refs_1_, ...), custom_call_target="tpu_custom_call" | custom-call | flops 1 | bytes 1 | tf_op jit(solution)/shard_map/pallas_call | solution.py:78
  57.5 6.8 %collective-permute-done.10.refs_2_ = bf16[3,128,1792]{2,1,0:T(8,128)(2,1)S(1)} collective-permute-done((bf16[3,128,1792]{2,1,0:T(8,128)(2,1)S(1)}, bf16[3,128,1792]{2,1,0:T(8,128)(2,1)S(1)}, u32[]{:S(2)}, u32[]{:S(2)}) %collective-permute-start.10) | collective-permute-done | bytes 1376288 | tf_op jit(solution)/shard_map/ppermute | solution.py:305
  64.3 3.4 %collective-permute-done.11.refs_3_ = bf16[3,128,1792]{2,1,0:T(8,128)(2,1)S(1)} collective-permute-done((bf16[3,128,1792]{2,1,0:T(8,128)(2,1)S(1)}, bf16[3,128,1792]{2,1,0:T(8,128)(2,1)S(1)}, u32[]{:S(2)}, u32[]{:S(2)}) %collective-permute-start.11) | collective-permute-done | bytes 1376288 | tf_op jit(solution)/shard_map/ppermute | solution.py:306
  67.7 14.6 %collective-permute-done.9.refs_1_ = bf16[3,128,1792]{2,1,0:T(8,128)(2,1)S(1)} collective-permute-done((bf16[3,128,1792]{2,1,0:T(8,128)(2,1)S(1)}, bf16[3,128,1792]{2,1,0:T(8,128)(2,1)S(1)}, u32[]{:S(2)}, u32[]{:S(2)}) %collective-permute-start.9) | collective-permute-done | bytes 1376288 | tf_op jit(solution)/shard_map/ppermute | solution.py:304
  85.4 7.8 %collective-permute-done.14.refs_4_ = bf16[3,64,1792]{2,1,0:T(8,128)(2,1)S(1)} collective-permute-done((bf16[3,64,1792]{2,1,0:T(8,128)(2,1)S(1)}, bf16[3,64,1792]{2,1,0:T(8,128)(2,1)S(1)}, u32[]{:S(2)}, u32[]{:S(2)}) %collective-permute-start.14) | collective-permute-done | bytes 688160 | tf_op jit(solution)/shard_map/ppermute | solution.py:312
  93.2 7.1 %collective-permute-done.15.refs_5_ = bf16[3,64,1792]{2,1,0:T(8,128)(2,1)S(1)} collective-permute-done((bf16[3,64,1792]{2,1,0:T(8,128)(2,1)S(1)}, bf16[3,64,1792]{2,1,0:T(8,128)(2,1)S(1)}, u32[]{:S(2)}, u32[]{:S(2)}) %collective-permute-start.15) | collective-permute-done | bytes 688160 | tf_op jit(solution)/shard_map/ppermute | solution.py:313
  103.1 6.3 %collective-permute-done.17.refs_1_.refs_2_ = bf16[2,64,1792]{2,1,0:T(8,128)(2,1)S(1)} collective-permute-done((bf16[2,64,1792]{2,1,0:T(8,128)(2,1)S(1)}, bf16[2,64,1792]{2,1,0:T(8,128)(2,1)S(1)}, u32[]{:S(2)}, u32[]{:S(2)}) %collective-permute-start.17) | collective-permute-done | bytes 458784 | tf_op jit(solution)/shard_map/ppermute | solution.py:312
  112.3 5.6 %collective-permute-done.18.refs_2_.refs_3_ = bf16[2,64,1792]{2,1,0:T(8,128)(2,1)S(1)} collective-permute-done((bf16[2,64,1792]{2,1,0:T(8,128)(2,1)S(1)}, bf16[2,64,1792]{2,1,0:T(8,128)(2,1)S(1)}, u32[]{:S(2)}, u32[]{:S(2)}) %collective-permute-start.18) | collective-permute-done | bytes 458784 | tf_op jit(solution)/shard_map/ppermute | solution.py:313
  122.0 5.8 %collective-permute-start.22 = (bf16[2,128,1792]{2,1,0:T(8,128)(2,1)}, bf16[2,128,1792]{2,1,0:T(8,128)(2,1)}, u32[]{:S(2)}, u32[]{:S(2)}) collective-permute-start(bf16[2,128,1792]{2,1,0:T(8,128)(2,1)} %get-tuple-element.84), channel_id=1, source_target_pairs={{8,72},{24,88},{40,104},{56,120},{72,8},{88,24},{104,40},{120,56},... | collective-permute-start | bytes 2752520 | tf_op jit(solution)/shard_map/ppermute | solution.py:306
  127.9 25.5 %collective-permute-done.20.refs_5_ = bf16[2,128,1792]{2,1,0:T(8,128)(2,1)S(1)} collective-permute-done((bf16[2,128,1792]{2,1,0:T(8,128)(2,1)}, bf16[2,128,1792]{2,1,0:T(8,128)(2,1)S(1)}, u32[]{:S(2)}, u32[]{:S(2)}) %collective-permute-start.20) | collective-permute-done | bytes 917536 | tf_op jit(solution)/shard_map/ppermute | solution.py:304
  154.3 10.0 %all-gather.2.cloned.1.call-done.refs_0_ = bf16[1024,1792]{1,0:T(8,128)(2,1)} async-done(((bf16[64,1792]{1,0:T(8,128)(2,1)}), bf16[1024,1792]{1,0:T(8,128)(2,1)}) %all-gather.2.cloned.1.call-update) | async-done | bytes 3670032 | tf_op jit(solution)/shard_map/all_gather | solution.py:364
  172.5 8.2 %shard_map.102 = (bf16[2,128,1024]{2,1,0:T(8,128)(2,1)}, bf16[2,128,1024]{2,1,0:T(8,128)(2,1)}, bf16[2,128,1024]{2,1,0:T(8,128)(2,1)}, bf16[2,128,1024]{2,1,0:T(...) custom-call(f32[512,1024]{1,0:T(8,128)S(1)} %shard_map.101.refs_0_, ...), custom_call_target="tpu_custom_call" | custom-call | flops 1 | bytes 1 | tf_op jit(solution)/shard_map/pallas_call | solution.py:78
  183.1 5.0 %collective-permute-start.26 = (bf16[2,128,1024]{2,1,0:T(8,128)(2,1)}, bf16[2,128,1024]{2,1,0:T(8,128)(2,1)}, u32[]{:S(2)}, u32[]{:S(2)}) collective-permute-start(bf16[2,128,1024]{2,1,0:T(8,128)(2,1)} %get-tuple-element.91), channel_id=1, source_target_pairs={{0,3},{1,0},{2,1},{3,2},{4,7},{5,4},{6,5},{7,6},{8,15},{9,12},{10,... | collective-permute-start | bytes 1572872 | tf_op jit(solution)/shard_map/ppermute | solution.py:380
  190.1 3.3 %shard_map.104 = bf16[1792,512]{1,0:T(8,128)(2,1)} custom-call(bf16[1024,1792]{1,0:T(8,128)(2,1)S(1)} %copy-done.5, bf16[1024,512]{1,0:T(8,128)(2,1)S(1)} %shard_map.97.refs_1_), custom_call_target="tpu_custom_call" | custom-call | flops 1 | bytes 1 | tf_op jit(solution)/shard_map/pallas_call | solution.py:78
  193.4 8.4 %shard_map.103 = (bf16[512,1792]{1,0:T(8,128)(2,1)}, bf16[512,1792]{1,0:T(8,128)(2,1)}) custom-call(bf16[512,512]{1,0:T(8,128)(2,1)S(1)} %copy-done.22, bf16[512,512]{1,0:T(8,128)(2,1)S(1)} %copy-done.24, bf16[2,512,1792]{2,1,0:T(8,128)(2,1)} %get-tuple-element.94.refs_2_, bf16[2,512,1792]{2,1,0:T(8,128)(2,1)} %collective-permute-done.27.refs_3_), custom_call_target="tpu_custom_call" | custom-call | flops 1 | bytes 1 | tf_op jit(solution)/shard_map/pallas_call | solution.py:78
  201.8 4.4 %collective-permute-done.26 = bf16[2,128,1024]{2,1,0:T(8,128)(2,1)} collective-permute-done((bf16[2,128,1024]{2,1,0:T(8,128)(2,1)}, bf16[2,128,1024]{2,1,0:T(8,128)(2,1)}, u32[]{:S(2)}, u32[]{:S(2)}) %collective-permute-start.26) | collective-permute-done | bytes 524320 | tf_op jit(solution)/shard_map/ppermute | solution.py:380
  208.0 4.4 %collective-permute-start.28 = (f32[2,128,512]{2,1,0:T(8,128)S(1)}, f32[2,128,512]{2,1,0:T(8,128)S(1)}, u32[]{:S(2)}, u32[]{:S(2)}) collective-permute-start(f32[2,128,512]{2,1,0:T(8,128)S(1)} %slice.17), channel_id=1, source_target_pairs={{0,8},{8,0},{16,24},{24,16},{32,40},{40,32},{48,56},{56,48},{64,72... | collective-permute-start | bytes 1572872 | tf_op jit(solution)/shard_map/ppermute | solution.py:318
  (110 shorter events, 45.2 us)
Async XLA Ops:
  7.2 157.1 %all-gather.2.cloned.1.call-start = ((), (), s32[]{:S(2)}) async-start(), calls=%async_computation | async-start | bytes 3899392 | tf_op jit(solution)/shard_map/all_gather | solution.py:364
  9.5 13.7 %collective-permute-start.5 = (bf16[512,1792]{1,0:T(8,128)(2,1)}, bf16[512,1792]{1,0:T(8,128)(2,1)S(1)}, u32[]{:S(2)}, u32[]{:S(2)}) collective-permute-start(bf16[512,1792]{1,0:T(8,128)(2,1)} %refs_8_.1), channel_id=1, source_target_pairs={{0,8},{8,0},{16,24},{24,16},{32,40},{40,32},{48,56},{56,48},{64,72... | collective-permute-start | bytes 5505032 | tf_op jit(solution)/shard_map/ppermute | solution.py:318
  9.7 17.3 %collective-permute-start.2 = (bf16[512,1792]{1,0:T(8,128)(2,1)}, bf16[512,1792]{1,0:T(8,128)(2,1)S(1)}, u32[]{:S(2)}, u32[]{:S(2)}) collective-permute-start(bf16[512,1792]{1,0:T(8,128)(2,1)} %refs_9_.1), channel_id=1, source_target_pairs={{0,8},{8,0},{16,24},{24,16},{32,40},{40,32},{48,56},{56,48},{64,72... | collective-permute-start | bytes 5505032 | tf_op jit(solution)/shard_map/ppermute | solution.py:318
  10.0 21.1 %collective-permute-start.8 = (bf16[1792,512]{1,0:T(8,128)(2,1)}, bf16[1792,512]{1,0:T(8,128)(2,1)S(1)}, u32[]{:S(2)}, u32[]{:S(2)}) collective-permute-start(bf16[1792,512]{1,0:T(8,128)(2,1)} %refs_1_.4), channel_id=1, source_target_pairs={{0,8},{8,0},{16,24},{24,16},{32,40},{40,32},{48,56},{56,48},{64,72... | collective-permute-start | bytes 5505032 | tf_op jit(solution)/shard_map/ppermute | solution.py:318
  12.1 17.1 %collective-permute-start.4 = (bf16[2,128,1024]{2,1,0:T(8,128)(2,1)S(1)}, bf16[2,128,1024]{2,1,0:T(8,128)(2,1)S(1)}, u32[]{:S(2)}, u32[]{:S(2)}) collective-permute-start(bf16[2,128,1024]{2,1,0:T(8,128)(2,1)S(1)} %shard_map.93.refs_0_), channel_id=1, source_target_pairs={{1,0},{2,1},{3,2},{0,3},{5,4},{6,5},{7,6},{4,7},{13,8},{14,9},{15,... | collective-permute-start | bytes 1572872 | tf_op jit(solution)/shard_map/ppermute | solution.py:336
  18.4 12.7 %collective-permute-start.7 = (bf16[2,128,1024]{2,1,0:T(8,128)(2,1)S(1)}, bf16[2,128,1024]{2,1,0:T(8,128)(2,1)S(1)}, u32[]{:S(2)}, u32[]{:S(2)}) collective-permute-start(bf16[2,128,1024]{2,1,0:T(8,128)(2,1)S(1)} %shard_map.93.refs_0_), channel_id=1, source_target_pairs={{3,0},{0,1},{1,2},{2,3},{7,4},{4,5},{5,6},{6,7},{15,8},{12,9},{13,... | collective-permute-start | bytes 1572872 | tf_op jit(solution)/shard_map/ppermute | solution.py:336
  23.3 13.2 %collective-permute-start.6 = (bf16[2,128,1024]{2,1,0:T(8,128)(2,1)S(1)}, bf16[2,128,1024]{2,1,0:T(8,128)(2,1)S(1)}, u32[]{:S(2)}, u32[]{:S(2)}) collective-permute-start(bf16[2,128,1024]{2,1,0:T(8,128)(2,1)S(1)} %shard_map.93.refs_0_), channel_id=1, source_target_pairs={{2,0},{3,1},{0,2},{1,3},{6,4},{7,5},{4,6},{5,7},{14,8},{15,9},{12,... | collective-permute-start | bytes 1572872 | tf_op jit(solution)/shard_map/ppermute | solution.py:336
  27.1 15.2 %collective-permute-start.3 = (bf16[2,128,1024]{2,1,0:T(8,128)(2,1)S(1)}, bf16[2,128,1024]{2,1,0:T(8,128)(2,1)S(1)}, u32[]{:S(2)}, u32[]{:S(2)}) collective-permute-start(bf16[2,128,1024]{2,1,0:T(8,128)(2,1)S(1)} %shard_map.93.refs_0_), channel_id=1, source_target_pairs={{12,8},{13,9},{14,10},{15,11},{8,12},{9,13},{10,14},{11,15},{28,24... | collective-permute-start | bytes 1572872 | tf_op jit(solution)/shard_map/ppermute | solution.py:336
  46.8 17.5 %collective-permute-start.10 = (bf16[3,128,1792]{2,1,0:T(8,128)(2,1)S(1)}, bf16[3,128,1792]{2,1,0:T(8,128)(2,1)S(1)}, u32[]{:S(2)}, u32[]{:S(2)}) collective-permute-start(bf16[3,128,1792]{2,1,0:T(8,128)(2,1)S(1)} %get-tuple-element.70), channel_id=1, source_target_pairs={{0,16},{8,104},{16,0},{24,120},{32,48},{40,8},{48,32},{56,24},{64,... | collective-permute-start | bytes 4128776 | tf_op jit(solution)/shard_map/ppermute | solution.py:305
  47.0 20.7 %collective-permute-start.11 = (bf16[3,128,1792]{2,1,0:T(8,128)(2,1)S(1)}, bf16[3,128,1792]{2,1,0:T(8,128)(2,1)S(1)}, u32[]{:S(2)}, u32[]{:S(2)}) collective-permute-start(bf16[3,128,1792]{2,1,0:T(8,128)(2,1)S(1)} %get-tuple-element.71), channel_id=1, source_target_pairs={{8,72},{24,88},{40,104},{56,120},{72,8},{88,24},{104,40},{120,56},... | collective-permute-start | bytes 4128776 | tf_op jit(solution)/shard_map/ppermute | solution.py:306
  51.5 30.8 %collective-permute-start.9 = (bf16[3,128,1792]{2,1,0:T(8,128)(2,1)S(1)}, bf16[3,128,1792]{2,1,0:T(8,128)(2,1)S(1)}, u32[]{:S(2)}, u32[]{:S(2)}) collective-permute-start(bf16[3,128,1792]{2,1,0:T(8,128)(2,1)S(1)} %get-tuple-element.69), channel_id=1, source_target_pairs={{0,16},{8,40},{16,0},{24,56},{32,48},{40,72},{48,32},{56,88},{64,8... | collective-permute-start | bytes 4128776 | tf_op jit(solution)/shard_map/ppermute | solution.py:304
  83.0 10.2 %collective-permute-start.14 = (bf16[3,64,1792]{2,1,0:T(8,128)(2,1)S(1)}, bf16[3,64,1792]{2,1,0:T(8,128)(2,1)S(1)}, u32[]{:S(2)}, u32[]{:S(2)}) collective-permute-start(bf16[3,64,1792]{2,1,0:T(8,128)(2,1)S(1)} %get-tuple-element.78), channel_id=1, source_target_pairs={{0,32},{8,24},{16,48},{24,8},{32,64},{40,56},{48,80},{56,40},{64,9... | collective-permute-start | bytes 2064392 | tf_op jit(solution)/shard_map/ppermute | solution.py:312
  84.4 15.8 %collective-permute-start.15 = (bf16[3,64,1792]{2,1,0:T(8,128)(2,1)S(1)}, bf16[3,64,1792]{2,1,0:T(8,128)(2,1)S(1)}, u32[]{:S(2)}, u32[]{:S(2)}) collective-permute-start(bf16[3,64,1792]{2,1,0:T(8,128)(2,1)S(1)} %get-tuple-element.79), channel_id=1, source_target_pairs={{0,96},{8,24},{16,112},{24,8},{32,0},{40,56},{48,16},{56,40},{64,3... | collective-permute-start | bytes 2064392 | tf_op jit(solution)/shard_map/ppermute | solution.py:313
  84.7 15.6 %collective-permute-start.16 = (bf16[3,64,1792]{2,1,0:T(8,128)(2,1)S(1)}, bf16[3,64,1792]{2,1,0:T(8,128)(2,1)S(1)}, u32[]{:S(2)}, u32[]{:S(2)}) collective-permute-start(bf16[3,64,1792]{2,1,0:T(8,128)(2,1)S(1)} %get-tuple-element.80), channel_id=1, source_target_pairs={{0,64},{16,80},{32,96},{48,112},{64,0},{80,16},{96,32},{112,48},{1... | collective-permute-start | bytes 2064392 | tf_op jit(solution)/shard_map/ppermute | solution.py:311
  101.8 7.6 %collective-permute-start.17 = (bf16[2,64,1792]{2,1,0:T(8,128)(2,1)S(1)}, bf16[2,64,1792]{2,1,0:T(8,128)(2,1)S(1)}, u32[]{:S(2)}, u32[]{:S(2)}) collective-permute-start(bf16[2,64,1792]{2,1,0:T(8,128)(2,1)S(1)} %get-tuple-element.82.refs_0_.refs_1_), channel_id=1, source_target_pairs={{0,32},{8,24},{16,48},{24,8},{32,64},{40,56},{48,80},{56,40},{64,9... | collective-permute-start | bytes 1376264 | tf_op jit(solution)/shard_map/ppermute | solution.py:312
  110.2 7.7 %collective-permute-start.18 = (bf16[2,64,1792]{2,1,0:T(8,128)(2,1)S(1)}, bf16[2,64,1792]{2,1,0:T(8,128)(2,1)S(1)}, u32[]{:S(2)}, u32[]{:S(2)}) collective-permute-start(bf16[2,64,1792]{2,1,0:T(8,128)(2,1)S(1)} %get-tuple-element.82.refs_0_.refs_1_), channel_id=1, source_target_pairs={{0,96},{8,24},{16,112},{24,8},{32,0},{40,56},{48,16},{56,40},{64,3... | collective-permute-start | bytes 1376264 | tf_op jit(solution)/shard_map/ppermute | solution.py:313
  120.6 32.8 %collective-permute-start.20 = (bf16[2,128,1792]{2,1,0:T(8,128)(2,1)}, bf16[2,128,1792]{2,1,0:T(8,128)(2,1)S(1)}, u32[]{:S(2)}, u32[]{:S(2)}) collective-permute-start(bf16[2,128,1792]{2,1,0:T(8,128)(2,1)} %get-tuple-element.84), channel_id=1, source_target_pairs={{0,16},{8,40},{16,0},{24,56},{32,48},{40,72},{48,32},{56,88},{64,8... | collective-permute-start | bytes 2752520 | tf_op jit(solution)/shard_map/ppermute | solution.py:304
  122.0 47.9 %collective-permute-start.21 = (bf16[2,128,1792]{2,1,0:T(8,128)(2,1)}, bf16[2,128,1792]{2,1,0:T(8,128)(2,1)}, u32[]{:S(2)}, u32[]{:S(2)}) collective-permute-start(bf16[2,128,1792]{2,1,0:T(8,128)(2,1)} %get-tuple-element.86), channel_id=1, source_target_pairs={{0,16},{8,104},{16,0},{24,120},{32,48},{40,8},{48,32},{56,24},{64,... | collective-permute-start | bytes 2752520 | tf_op jit(solution)/shard_map/ppermute | solution.py:305
  122.0 47.9 %collective-permute-start.22 = (bf16[2,128,1792]{2,1,0:T(8,128)(2,1)}, bf16[2,128,1792]{2,1,0:T(8,128)(2,1)}, u32[]{:S(2)}, u32[]{:S(2)}) collective-permute-start(bf16[2,128,1792]{2,1,0:T(8,128)(2,1)} %get-tuple-element.84), channel_id=1, source_target_pairs={{8,72},{24,88},{40,104},{56,120},{72,8},{88,24},{104,40},{120,56},... | collective-permute-start | bytes 2752520 | tf_op jit(solution)/shard_map/ppermute | solution.py:306
  180.7 12.7 %collective-permute-start.27 = (bf16[2,512,1792]{2,1,0:T(8,128)(2,1)}, bf16[2,512,1792]{2,1,0:T(8,128)(2,1)}, u32[]{:S(2)}, u32[]{:S(2)}) collective-permute-start(bf16[2,512,1792]{2,1,0:T(8,128)(2,1)} %get-tuple-element.94.refs_2_), channel_id=1, source_target_pairs={{0,8},{8,0},{16,24},{24,16},{32,40},{40,32},{48,56},{56,48},{64,72... | collective-permute-start | bytes 11010056 | tf_op jit(solution)/shard_map/ppermute | solution.py:318
  181.0 20.8 %collective-permute-start.23 = (bf16[2,128,1024]{2,1,0:T(8,128)(2,1)}, bf16[2,128,1024]{2,1,0:T(8,128)(2,1)S(1)}, u32[]{:S(2)}, u32[]{:S(2)}) collective-permute-start(bf16[2,128,1024]{2,1,0:T(8,128)(2,1)} %get-tuple-element.88), channel_id=1, source_target_pairs={{8,12},{9,13},{10,14},{11,15},{12,8},{13,9},{14,10},{15,11},{24,28... | collective-permute-start | bytes 1572872 | tf_op jit(solution)/shard_map/ppermute | solution.py:380
  182.9 18.9 %collective-permute-start.24 = (bf16[2,128,1024]{2,1,0:T(8,128)(2,1)}, bf16[2,128,1024]{2,1,0:T(8,128)(2,1)}, u32[]{:S(2)}, u32[]{:S(2)}) collective-permute-start(bf16[2,128,1024]{2,1,0:T(8,128)(2,1)} %get-tuple-element.89), channel_id=1, source_target_pairs={{0,1},{1,2},{2,3},{3,0},{4,5},{5,6},{6,7},{7,4},{8,13},{9,14},{10,... | collective-permute-start | bytes 1572872 | tf_op jit(solution)/shard_map/ppermute | solution.py:380
  183.0 18.8 %collective-permute-start.25 = (bf16[2,128,1024]{2,1,0:T(8,128)(2,1)}, bf16[2,128,1024]{2,1,0:T(8,128)(2,1)}, u32[]{:S(2)}, u32[]{:S(2)}) collective-permute-start(bf16[2,128,1024]{2,1,0:T(8,128)(2,1)} %get-tuple-element.90), channel_id=1, source_target_pairs={{0,2},{1,3},{2,0},{3,1},{4,6},{5,7},{6,4},{7,5},{8,14},{9,15},{10,... | collective-permute-start | bytes 1572872 | tf_op jit(solution)/shard_map/ppermute | solution.py:380
  183.1 23.1 %collective-permute-start.26 = (bf16[2,128,1024]{2,1,0:T(8,128)(2,1)}, bf16[2,128,1024]{2,1,0:T(8,128)(2,1)}, u32[]{:S(2)}, u32[]{:S(2)}) collective-permute-start(bf16[2,128,1024]{2,1,0:T(8,128)(2,1)} %get-tuple-element.91), channel_id=1, source_target_pairs={{0,3},{1,0},{2,1},{3,2},{4,7},{5,4},{6,5},{7,6},{8,15},{9,12},{10,... | collective-permute-start | bytes 1572872 | tf_op jit(solution)/shard_map/ppermute | solution.py:380
  (34 other events, 173.8 us)
Sparse Core Ops, SparseCore 0:
  110.3 53.9 all-gather.1
